TPU v7x, 256 devices: a whole 4x4x8 slice. The times are simulated.
256 devices in a mesh: head: 16 (over x, y), key: 8 (over z), row: 2 (over core).
Axes of the slice: x: 4, y: 4, z: 8, core: 2. Of those that a mesh axis runs over, the one named last changes fastest.
Arguments:
- mla_query: bfloat16 [256, 128, 576], P('row', 'head'), may hold values from -48 to 48
- mla_cache: bfloat16 [16, 2048, 576], P(None, 'key'), may hold values from -6 to 6
- index_query: bfloat16 [256, 64, 128], P('row'), may hold values from -24 to 24
- index_keys: bfloat16 [32768, 128], P(('head', 'key')), may hold values from -6 to 6
- index_weight: float32 [256, 64], P('row'), may hold values from -0.75 to 0.75
Outputs:
- query_grad: float32 [256, 64, 128], P('row', 'head')
- key_grad: float32 [32768, 128], P(('head', 'key', 'row'))
- weight_grad: float32 [256, 64], P('row')
All inputs are finite; a program needn't handle non-finite values.
Results may differ from a plain program's by a relative error of at most 0.0029.
Values sent between devices are 32-bit elements; how exact they have to be, the bound alone decides.
No kernel may reach another device: no remote copies, remote signals or barrier semaphores. Data moves between devices by JAX's collectives and lax.ppermute only.
A program may use at most 128 MiB of HBM per device.

v0:
```python
import math

import jax
import jax.numpy as jnp
from jax import lax
from jax.sharding import PartitionSpec as P

MH = 128


def shards(mla_query, mla_cache, index_query, index_keys, index_weight):
    key_count = lax.axis_size("key")
    head_count = lax.axis_size("head")
    block_count = mla_cache.shape[0]
    local_keys = mla_cache.shape[1]
    row_local = mla_query.shape[0]
    cache_rows = mla_cache.reshape(block_count * local_keys, mla_cache.shape[2])
    scores = jnp.einsum(
        "thd,sd->ths", mla_query, cache_rows, preferred_element_type=jnp.float32
    ) * (1.0 / math.sqrt(192.0))
    top_score = lax.pmax(jnp.max(scores, axis=2), "key")
    exp_terms = jnp.exp(scores - top_score[:, :, None])
    sum_terms = lax.psum(jnp.sum(exp_terms, axis=2), "key")
    head_scale = 1.0 / sum_terms
    partial_value = jnp.sum(exp_terms * head_scale[:, :, None], axis=1) / MH
    spread = partial_value.reshape(row_local, block_count, local_keys)
    summed_all = lax.psum(spread, "head")
    target = lax.dynamic_slice_in_dim(summed_all, lax.axis_index("head"), 1, 1).reshape(
        row_local, local_keys
    )
    root_width = math.sqrt(index_keys.shape[1])
    products = jnp.einsum(
        "thd,sd->ths", index_query, index_keys, preferred_element_type=jnp.float32
    )
    active = jnp.maximum(products, 0.0)
    logits = jnp.sum(active * index_weight[:, :, None], axis=1) / root_width
    top_logit = lax.pmax(jnp.max(logits, axis=1), ("head", "key"))
    exp_logit = jnp.exp(logits - top_logit[:, None])
    logit_sum = lax.psum(jnp.sum(exp_logit, axis=1), ("head", "key"))
    soft_probs = exp_logit / logit_sum[:, None]
    key_total = index_keys.shape[0] * head_count * key_count
    dlogits = key_total * (soft_probs - target)
    weight_part = jnp.sum(active * dlogits[:, None, :], axis=2) / root_width
    slope_terms = (
        dlogits[:, None, :]
        * index_weight[:, :, None]
        * jnp.where(products > 0.0, 1.0, 0.0)
        / root_width
    ).astype(jnp.bfloat16)
    query_part = jnp.einsum(
        "ths,sd->thd", slope_terms, index_keys, preferred_element_type=jnp.float32
    )
    keys_part = jnp.einsum(
        "ths,thd->sd", slope_terms, index_query, preferred_element_type=jnp.float32
    )
    key_grad = lax.psum_scatter(keys_part, "row", scatter_dimension=0, tiled=True)
    head_share = query_part.shape[1] // head_count
    query_full, weight_grad = lax.psum((query_part, weight_part), ("head", "key"))
    query_grad = lax.dynamic_slice_in_dim(
        query_full, lax.axis_index("head") * head_share, head_share, 1
    )
    return (query_grad, key_grad, weight_grad)


def solution(mesh):
    placed = (
        P("row", "head", None),
        P(None, "key", None),
        P("row", None, None),
        P(("head", "key"), None),
        P("row", None),
    )
    return jax.shard_map(
        shards,
        mesh=mesh,
        in_specs=placed,
        out_specs=(P("row", "head", None), P(("head", "key", "row"), None), P("row", None)),
        check_vma=False,
    )
```

profile of v0, /device:TPU:32, one launch (start us, length us, event | category | flops | bytes accessed | tf_op | source)
XLA Modules:
  0.0 1493.5 jit_solution(123140552502343702)
XLA Ops:
  7.2 0.0 copy-start
  7.2 0.0 all-reduce.3.cloned.1.call-start
  7.2 7.2 copy.19
  14.4 8.3 reshape.73
  22.7 0.0 copy-done
  22.7 12.6 multiply_reduce_fusion.1
  35.3 17.9 %pmax.15 = f32[128,8]{0,1:T(8,128)S(1)} all-reduce(f32[128,8]{0,1:T(8,128)S(1)} %get-tuple-element.12), channel_id=1, replica_groups=mesh['head'=16,'key'=8,'row'=2] {'key'}, use_global_device_ids=true, to_apply=%region_6.0 | all-reduce | flops 1024 | bytes 8192 | tf_op jit(solution)/shard_map/pmax | solution.py:21
  53.2 8.6 fusion
  61.8 16.4 %psum.36 = f32[128,8]{0,1:T(8,128)S(1)} all-reduce(f32[128,8]{0,1:T(8,128)S(1)} %fusion), channel_id=1, replica_groups=mesh['head'=16,'key'=8,'row'=2] {'key'}, use_global_device_ids=true, to_apply=%region_8.0 | all-reduce | flops 1024 | bytes 8192 | tf_op jit(solution)/shard_map/psum | solution.py:23
  78.2 8.0 multiply_reduce_fusion
  86.2 0.0 copy-start.2
  86.2 0.0 copy-start.3
  86.2 0.2 broadcast_multiply_fusion
  86.4 1.9 copy.20
  88.3 3.0 copy.21
  91.3 0.0 all-reduce.3.cloned.1.call-update
  91.3 0.2 all-reduce.5.cloned.1.call-start
  91.5 0.0 copy-done.2
  91.5 0.0 copy-done.3
  91.5 6.8 multiply_reduce_fusion.3
  98.3 0.1 multiply_reduce_fusion.4
  98.4 342.6 %pmax.14 = f32[128]{0:T(128)S(1)} all-reduce(f32[128]{0:T(128)S(1)} %multiply_reduce_fusion.4), channel_id=1, replica_groups=mesh['head'=16,'key'=8,'row'=2] {'head','key'}, use_global_device_ids=true, to_apply=%region_2.0 | all-reduce | flops 128 | bytes 1024 | tf_op jit(solution)/shard_map/pmax | solution.py:37
  441.0 0.2 exponential_reduce_fusion
  441.2 348.7 %psum.35 = f32[128]{0:T(128)S(1)} all-reduce(f32[128]{0:T(128)S(1)} %exponential_reduce_fusion), channel_id=1, replica_groups=mesh['head'=16,'key'=8,'row'=2] {'head','key'}, use_global_device_ids=true, to_apply=%region_4.0 | all-reduce | flops 128 | bytes 1024 | tf_op jit(solution)/shard_map/psum | solution.py:39
  789.8 0.0 all-reduce.3.cloned.1.call-done
  789.8 1.0 fusion.12
  790.9 5.7 fusion.13
  796.6 0.0 copy-start.1
  796.6 0.0 all-reduce.5.cloned.1.call-update
  796.6 0.0 reduce-scatter.2.cloned.1.call-start
  796.7 4.9 multiply_reduce_fusion.2
  801.6 0.0 copy-done.1
  801.6 7.1 fusion.5
  808.7 0.0 reduce-scatter.2.cloned.1.call-update
  808.7 676.4 %psum.39 = f32[128,64]{0,1:T(8,128)} all-reduce(f32[128,64]{0,1:T(8,128)S(1)} %broadcast_multiply_fusion.1), channel_id=1, replica_groups=mesh['head'=16,'key'=8,'row'=2] {'head','key'}, use_global_device_ids=true, to_apply=%region_14.15 | all-reduce | flops 8192 | bytes 65536 | tf_op jit(solution)/shard_map/psum | solution.py:58
  1485.1 0.0 all-reduce.5.cloned.1.call-done
  1485.1 1.0 constant_dynamic-slice_fusion
  1486.1 0.9 copy.24
  1486.9 0.0 reduce-scatter.2.cloned.1.call-done
  (2 shorter events, 0.0 us)
Async XLA Ops:
  7.2 15.6 %copy-start = (bf16[128,8,576]{0,2,1:T(8,128)(2,1)S(1)}, bf16[128,8,576]{0,2,1:T(8,128)(2,1)}, u32[]{:S(2)}) copy-start(bf16[128,8,576]{0,2,1:T(8,128)(2,1)} %param.5) | copy-start | bytes 3538948
  7.2 782.6 %all-reduce.3.cloned.1.call-start = ((), (), s32[]{:S(2)}) async-start(), calls=%async_computation.1 | async-start | bytes 4194304 | tf_op jit(solution)/shard_map/psum | solution.py:27
  86.2 5.3 copy-start.2
  86.2 5.3 copy-start.3
  91.3 1393.8 %all-reduce.5.cloned.1.call-start = ((), (), s32[]{:S(2)}) async-start(), calls=%async_computation.2 | async-start | bytes 8388608 | tf_op jit(solution)/shard_map/psum | solution.py:58
  796.6 5.0 copy-start.1
  796.6 690.3 %reduce-scatter.2.cloned.1.call-start = ((), (), s32[]{:S(2)}) async-start(), calls=%async_computation.3 | async-start | bytes 196608 | tf_op jit(solution)/shard_map/reduce_scatter | solution.py:56
Sparse Core Ops, SparseCore 0:
  91.4 99.0 all-reduce.2
  796.8 226.1 all-reduce.4
  1026.0 11.2 reduce-scatter.1
where the time goes:
time: 1500 us; the launch traced here: 1490 us
  blocking collectives  1400 us (93%)
  matrix products  32.2 us (2%)
  other arithmetic  23 us (2%)
  local copies, waits for them, and re-layouts  22.2 us (1%)
    psum x1, blocking collectives, shards(): lax.psum((query_part, weight_part), ('head', 'key'))  676 us
    psum x1, blocking collectives, shards(): logit_sum = lax.psum(jnp.sum(exp_logit, axis=1), ('head', 'key'))  349 us
    pmax x1, blocking collectives, shards(): top_logit = lax.pmax(jnp.max(logits, axis=1), ('head', 'key'))  343 us
  transfers between devices with their start and end apart: 3, of which 0 were waited for; matrix products, arithmetic and copies ran while one was open for 1% of the time, Pallas kernels for 0%

commit v1 on v0

v1 whole, which is shorter than its diff:
```python
import math

import jax
import jax.numpy as jnp
from jax import lax
from jax.experimental import pallas as pl
from jax.experimental.pallas import tpu as pltpu
from jax.sharding import PartitionSpec as P

MH = 128
LOG2E = 1.4426950408889634
SCORE2 = LOG2E / math.sqrt(192.0)
LANES = 128
NT = (((1,), (1,)), ((), ()))
TN = (((0,), (0,)), ((), ()))
NN = (((1,), (0,)), ((), ()))


def dot(a, b, dims):
    return lax.dot_general(a, b, dims, preferred_element_type=jnp.float32)


def lane_iota(rows):
    return lax.broadcasted_iota(jnp.int32, (rows, LANES), 1)


def forward_kernel(q_ref, k_ref, w_ref, logits_ref, stats_ref, qh_ref, wide, wpad):
    rows, heads, depth = q_ref.shape
    keys = k_ref.shape[0]
    group = 8
    wide[...] = q_ref[...].astype(jnp.float32).reshape(rows * heads, depth)
    wpad[...] = jnp.zeros_like(wpad)
    wpad[:, 0:heads] = w_ref[...]

    logits_ref[...] = jnp.zeros_like(logits_ref)

    def step(i, carry):
        weights = pltpu.roll(wpad[...], LANES - group * i, 1)
        for j in range(group):
            head = i * group + j
            qh_ref[head] = wide[pl.ds(head, rows, stride=heads), :].astype(jnp.bfloat16)
        chunk = qh_ref[pl.ds(i * group, group)].reshape(group * rows, depth)
        products = dot(chunk, k_ref[...], NT)
        total = logits_ref[...]
        for j in range(group):
            part = products[j * rows : (j + 1) * rows]
            total = total + jnp.maximum(part, 0.0) * weights[:, j : j + 1]
        logits_ref[...] = total
        return carry

    lax.fori_loop(0, heads // group, step, 0)
    logits = logits_ref[...] * (1.0 / math.sqrt(depth))
    logits_ref[...] = logits
    top = jnp.max(logits, axis=1, keepdims=True)
    total = jnp.sum(jnp.exp(logits - top), axis=1, keepdims=True)
    lane = lane_iota(rows)
    packed = jnp.where(lane == 0, top, jnp.where(lane == 1, total, 0.0))
    stats_ref[...] = packed.T[0:8]


def indexer_forward(index_query, index_keys, index_weight):
    rows, heads, depth = index_query.shape
    keys = index_keys.shape[0]
    return pl.pallas_call(
        forward_kernel,
        out_shape=(
            jax.ShapeDtypeStruct((rows, keys), jnp.float32),
            jax.ShapeDtypeStruct((8, rows), jnp.float32),
            jax.ShapeDtypeStruct((heads, rows, depth), jnp.bfloat16),
        ),
        scratch_shapes=[
            pltpu.VMEM((rows * heads, depth), jnp.float32),
            pltpu.VMEM((rows, LANES), jnp.float32),
        ],
        compiler_params=pltpu.CompilerParams(vmem_limit_bytes=40 << 20),
        name="indexer_forward",
    )(index_query, index_keys, index_weight)


def scores_kernel(q_ref, c_ref, lstats_ref, e_ref, tops_ref, send_ref, wide, qh, sums):
    rows, heads, width = q_ref.shape
    step = pl.program_id(0)
    steps = pl.num_programs(0)
    pair = c_ref.shape[0]
    lane = lane_iota(2 * rows)

    @pl.when(step == 0)
    def _():
        for k in range(0, width, LANES):
            size = min(LANES, width - k)
            piece = q_ref[:, :, k : k + size].astype(jnp.float32)
            wide[:, 0:size] = piece.reshape(rows * heads, size)
            for h in range(heads):
                strided = wide[pl.ds(h, rows, stride=heads), :]
                qh[h * rows : (h + 1) * rows, k : k + size] = strided[:, 0:size].astype(jnp.bfloat16)
        tops_ref[...] = jnp.zeros_like(tops_ref)
        sums[...] = jnp.zeros_like(sums)

    for h in range(0, heads, 2):
        span = slice(h * rows, (h + 2) * rows)
        queries = qh[span]
        blocks = [dot(queries, c_ref[j], NT) for j in range(pair)]
        top = blocks[0]
        for block in blocks[1:]:
            top = jnp.maximum(top, block)
        top = jnp.max(top, axis=1, keepdims=True)
        total = None
        for j, block in enumerate(blocks):
            terms = jnp.exp2((block - top) * SCORE2)
            total = terms if total is None else total + terms
            e_ref[j, h : h + 2] = terms.astype(jnp.bfloat16).reshape(2, rows, terms.shape[1])
        total = jnp.sum(total, axis=1, keepdims=True)
        tops_ref[span] = jnp.where(lane == step, top, tops_ref[span])
        sums[span] = jnp.where(lane == step, total, sums[span])

    @pl.when(step == steps - 1)
    def _():
        lane1 = lane_iota(rows)
        used = lane1 < steps
        packed = jnp.zeros((rows, LANES), jnp.float32)
        for h in range(heads):
            tops = tops_ref[h * rows : (h + 1) * rows]
            top = jnp.max(jnp.where(used, tops, -jnp.inf), axis=1, keepdims=True)
            scaled = sums[h * rows : (h + 1) * rows] * jnp.exp2(jnp.where(used, tops - top, 0.0) * SCORE2)
            total = jnp.sum(jnp.where(used, scaled, 0.0), axis=1, keepdims=True)
            packed = jnp.where(lane1 == h, top, packed)
            packed = jnp.where(lane1 == heads + h, total, packed)
        flat = packed.T[0 : 2 * heads]
        for z in range(send_ref.shape[0]):
            send_ref[z, 0 : 2 * heads] = flat
            send_ref[z, 2 * heads :] = lstats_ref[...]


def attention_scores(mla_query, mla_cache, lstats, key_count):
    rows, heads, width = mla_query.shape
    blocks, keys, _ = mla_cache.shape
    pair = 2
    steps = blocks // pair
    return pl.pallas_call(
        scores_kernel,
        grid=(steps,),
        in_specs=[
            pl.BlockSpec((rows, heads, width), lambda i: (0, 0, 0)),
            pl.BlockSpec((pair, keys, width), lambda i: (i, 0, 0)),
            pl.BlockSpec((8, rows), lambda i: (0, 0)),
        ],
        out_specs=(
            pl.BlockSpec((pair, heads, rows, keys), lambda i: (i, 0, 0, 0)),
            pl.BlockSpec((heads * rows, LANES), lambda i: (0, 0)),
            pl.BlockSpec((key_count, 2 * heads + 8, rows), lambda i: (0, 0, 0)),
        ),
        out_shape=(
            jax.ShapeDtypeStruct((blocks, heads, rows, keys), jnp.bfloat16),
            jax.ShapeDtypeStruct((heads * rows, LANES), jnp.float32),
            jax.ShapeDtypeStruct((key_count, 2 * heads + 8, rows), jnp.float32),
        ),
        scratch_shapes=[
            pltpu.VMEM((rows * heads, LANES), jnp.float32),
            pltpu.VMEM((rows * heads, width), jnp.bfloat16),
            pltpu.VMEM((rows * heads, LANES), jnp.float32),
        ],
        compiler_params=pltpu.CompilerParams(vmem_limit_bytes=48 << 20),
        name="attention_scores",
    )(mla_query, mla_cache, lstats)


def headsum_kernel(e_ref, tops_ref, got_ref, out_ref, weights, tail, square):
    pair, heads, rows, keys = e_ref.shape
    step = pl.program_id(0)
    lane = lane_iota(rows)

    @pl.when(step == 0)
    def _():
        tops = got_ref[:, 0:heads]
        top = jnp.max(tops, axis=0)
        total = jnp.sum(got_ref[:, heads : 2 * heads] * jnp.exp2((tops - top[None]) * SCORE2), axis=0)
        square[...] = jnp.zeros_like(square)
        square[0:heads] = top
        square[heads : 2 * heads] = (1.0 / MH) / total
        columns = square[...].T
        for h in range(heads):
            local = tops_ref[h * rows : (h + 1) * rows] - columns[:, h : h + 1]
            scale = columns[:, heads + h : heads + h + 1]
            weights[h] = jnp.exp2(jnp.minimum(local * SCORE2, 0.0)) * scale
        ltops = got_ref[:, 2 * heads : 2 * heads + 1]
        ltop = jnp.max(ltops, axis=0)
        lsum = jnp.sum(got_ref[:, 2 * heads + 1 : 2 * heads + 2] * jnp.exp(ltops - ltop[None]), axis=0)
        tail[...] = jnp.zeros_like(tail)
        tail[0:1, 0:rows] = ltop
        tail[1:2, 0:rows] = lsum

    columns = []
    for h in range(heads):
        columns.append(jnp.sum(jnp.where(lane == step, weights[h], 0.0), axis=1, keepdims=True))
    for j in range(pair):
        total = e_ref[j, 0].astype(jnp.float32) * columns[0]
        for h in range(1, heads):
            total = total + e_ref[j, h].astype(jnp.float32) * columns[h]
        out_ref[j, 0:rows] = total
        out_ref[j, rows:] = tail[...]


def head_sum(terms, tops, got):
    blocks, heads, rows, keys = terms.shape
    pair = 2
    return pl.pallas_call(
        headsum_kernel,
        grid=(blocks // pair,),
        in_specs=[
            pl.BlockSpec((pair, heads, rows, keys), lambda i: (i, 0, 0, 0)),
            pl.BlockSpec((heads * rows, LANES), lambda i: (0, 0)),
            pl.BlockSpec(got.shape, lambda i: (0, 0, 0)),
        ],
        out_specs=pl.BlockSpec((pair, rows + 8, keys), lambda i: (i, 0, 0)),
        out_shape=jax.ShapeDtypeStruct((blocks, rows + 8, keys), jnp.float32),
        scratch_shapes=[
            pltpu.VMEM((heads, rows, LANES), jnp.float32),
            pltpu.VMEM((8, keys), jnp.float32),
            pltpu.VMEM((LANES, rows), jnp.float32),
        ],
        compiler_params=pltpu.CompilerParams(vmem_limit_bytes=40 << 20),
        name="head_sum",
    )(terms, tops, got)


def keys_kernel(key_total, got_ref, logits_ref, qh_ref, k_ref, w_ref, send_ref, keys_ref, wpad, slopes, acc, square):
    copies, _, keys = got_ref.shape
    heads, rows, depth = qh_ref.shape
    group = 8
    root = 1.0 / math.sqrt(depth)
    lane = lane_iota(rows)

    ltops = got_ref[:, rows : rows + 1, 0:rows]
    ltop = jnp.max(ltops, axis=0)
    lsum = jnp.sum(got_ref[:, rows + 1 : rows + 2, 0:rows] * jnp.exp(ltops - ltop[None]), axis=0)
    square[...] = jnp.zeros_like(square)
    square[0:1] = ltop
    square[1:2] = lsum
    columns = square[...].T
    target = got_ref[0, 0:rows]
    for g in range(1, copies):
        target = target + got_ref[g, 0:rows]
    soft = jnp.exp(logits_ref[...] - columns[:, 0:1]) / columns[:, 1:2]
    send_ref[0, 0:rows] = key_total * (soft - target)

    wpad[...] = jnp.zeros_like(wpad)
    wpad[:, 0:heads] = w_ref[...] * root
    keys_ref[...] = jnp.zeros_like(keys_ref)
    acc[...] = jnp.zeros_like(acc)

    def step(i, carry):
        weights = pltpu.roll(wpad[...], LANES - group * i, 1)
        chunk = qh_ref[pl.ds(i * group, group)].reshape(group * rows, depth)
        products = dot(chunk, k_ref[...], NT)
        dlogits = send_ref[0, 0:rows]
        sums = acc[...]
        for j in range(group):
            part = products[j * rows : (j + 1) * rows]
            active = jnp.sum(jnp.maximum(part, 0.0) * dlogits, axis=1, keepdims=True)
            sums = jnp.where(lane == i * group + j, active, sums)
            slope = jnp.where(part > 0.0, dlogits * weights[:, j : j + 1], 0.0)
            slopes[j * rows : (j + 1) * rows] = slope.astype(jnp.bfloat16)
        acc[...] = sums
        keys_ref[...] += dot(slopes[...], chunk, TN)
        return carry

    lax.fori_loop(0, heads // group, step, 0)
    flat = (acc[...] * root).T
    send_ref[0, rows : rows + heads // 2, 0:rows] = flat[0 : heads // 2]
    send_ref[0, rows : rows + heads // 2, rows : 2 * rows] = flat[heads // 2 : heads]
    for g in range(1, copies):
        send_ref[g] = send_ref[0]


def key_gradient(got, logits, qh, index_keys, index_weight, key_total):
    copies, _, keys = got.shape
    heads, rows, depth = qh.shape
    return pl.pallas_call(
        lambda *refs: keys_kernel(key_total, *refs),
        out_shape=(
            jax.ShapeDtypeStruct((copies, rows + heads // 2, keys), jnp.float32),
            jax.ShapeDtypeStruct((keys, depth), jnp.float32),
        ),
        scratch_shapes=[
            pltpu.VMEM((rows, LANES), jnp.float32),
            pltpu.VMEM((8 * rows, keys), jnp.bfloat16),
            pltpu.VMEM((rows, LANES), jnp.float32),
            pltpu.VMEM((LANES, rows), jnp.float32),
        ],
        compiler_params=pltpu.CompilerParams(vmem_limit_bytes=40 << 20),
        name="key_gradient",
    )(got, logits, qh, index_keys, index_weight)


def query_kernel(got_ref, k_ref, q_ref, w_ref, out_ref, slopes, acc, wsum):
    share, rows, depth = q_ref.shape
    step = pl.program_id(0)
    keys = k_ref.shape[1]
    extra = wsum.shape[0]
    pieces = out_ref.shape[0]
    root = 1.0 / math.sqrt(depth)

    @pl.when(step == 0)
    def _():
        acc[...] = jnp.zeros_like(acc)
        wsum[...] = jnp.zeros_like(wsum)

    block = k_ref[0].astype(jnp.bfloat16)
    products = dot(q_ref[...].reshape(share * rows, depth), block, NT)
    dlogits = got_ref[0, 0:rows]
    for j in range(share):
        part = products[j * rows : (j + 1) * rows]
        weight = w_ref[:, j : j + 1] * root
        slope = jnp.where(part > 0.0, dlogits * weight, 0.0)
        slopes[j * rows : (j + 1) * rows] = slope.astype(jnp.bfloat16)
    acc[...] += dot(slopes[...], block, NN)
    wsum[...] += got_ref[0, rows:]

    @pl.when(step == pl.num_programs(0) - 1)
    def _():
        span = rows // pieces
        few = extra // pieces
        for z in range(pieces):
            for j in range(share):
                first = j * rows + z * span
                out_ref[z, pl.ds(j, span, stride=share), :] = acc[first : first + span]
            piece = wsum[z * few : (z + 1) * few]
            out_ref[z, share * span : share * span + few] = piece[:, 0:rows]
            out_ref[z, share * span + few :] = piece[:, rows : 2 * rows]


def query_gradient(got, plane_keys, queries, weights, pieces):
    blocks, height, keys = got.shape
    share, rows, depth = queries.shape
    extra = height - rows
    tall = share * (rows // pieces) + 2 * (extra // pieces)
    return pl.pallas_call(
        query_kernel,
        grid=(blocks,),
        in_specs=[
            pl.BlockSpec((1, height, keys), lambda i: (i, 0, 0)),
            pl.BlockSpec((1, keys, depth), lambda i: (i, 0, 0)),
            pl.BlockSpec((share, rows, depth), lambda i: (0, 0, 0)),
            pl.BlockSpec((rows, share), lambda i: (0, 0)),
        ],
        out_specs=pl.BlockSpec((pieces, tall, depth), lambda i: (0, 0, 0)),
        out_shape=jax.ShapeDtypeStruct((pieces, tall, depth), jnp.float32),
        scratch_shapes=[
            pltpu.VMEM((share * rows, keys), jnp.bfloat16),
            pltpu.VMEM((share * rows, depth), jnp.float32),
            pltpu.VMEM((extra, keys), jnp.float32),
        ],
        compiler_params=pltpu.CompilerParams(vmem_limit_bytes=40 << 20),
        name="query_gradient",
    )(got, plane_keys, queries, weights)


def exchange(x, axis):
    return lax.all_to_all(x, axis, split_axis=0, concat_axis=0, tiled=True)


def shards(mla_query, mla_cache, index_query, index_keys, index_weight):
    key_count = lax.axis_size("key")
    head_count = lax.axis_size("head")
    rows = mla_query.shape[0]
    keys, depth = index_keys.shape
    heads = index_query.shape[1]
    share = heads // head_count
    head_index = lax.axis_index("head")
    row_index = lax.axis_index("row")

    plane_keys = lax.all_gather(index_keys.astype(jnp.float32), "head", axis=0)
    logits, lstats, qh = indexer_forward(index_query, index_keys, index_weight)
    terms, tops, send1 = attention_scores(mla_query, mla_cache, lstats, key_count)
    got1 = exchange(send1, "key")
    send2 = head_sum(terms, tops, got1)
    got2 = exchange(send2, "head")
    key_total = float(keys * head_count * key_count)
    send3, keys_part = key_gradient(got2, logits, qh, index_keys, index_weight, key_total)

    half = keys // 2
    away = lax.dynamic_slice_in_dim(keys_part, (1 - row_index) * half, half, 0)
    near = lax.dynamic_slice_in_dim(keys_part, row_index * half, half, 0)
    key_grad = near + lax.ppermute(away, "row", [(0, 1), (1, 0)])

    got3 = exchange(send3, "head")
    mine = lax.dynamic_slice_in_dim(qh, head_index * share, share, 0)
    my_weights = lax.dynamic_slice_in_dim(index_weight, head_index * share, share, 1)
    send4 = query_gradient(got3, plane_keys, mine, my_weights, key_count)
    got4 = jnp.sum(exchange(send4, "key"), axis=0)
    got5 = exchange(jnp.broadcast_to(got4[None], (key_count, *got4.shape)), "key")
    span = share * (rows // key_count)
    query_grad = got5[:, 0:span].reshape(rows, share, depth)
    few = (got4.shape[0] - span) // 2
    low = got5[:, span : span + few].reshape(heads // 2, rows)
    high = got5[:, span + few :].reshape(heads // 2, rows)
    weight_grad = jnp.concatenate([low, high], axis=0).T
    return (query_grad, key_grad, weight_grad)


def solution(mesh):
    placed = (
        P("row", "head", None),
        P(None, "key", None),
        P("row", None, None),
        P(("head", "key"), None),
        P("row", None),
    )
    return jax.shard_map(
        shards,
        mesh=mesh,
        in_specs=placed,
        out_specs=(P("row", "head", None), P(("head", "key", "row"), None), P("row", None)),
        check_vma=False,
    )
```

time: 1500 us -> 203 us (0.14)
  blocking collectives: 1400 us -> 29.1 us
  waiting for transfers between devices: 0.05 us -> 79.3 us
  Pallas kernels: 0 us -> 35.9 us
  matrix products: 32.2 us -> 0 us
  other arithmetic: 23 us -> 1.94 us
  starting transfers between devices: 0.3 us -> 15.8 us
    psum x3 -> x0, blocking collectives: 1040 us -> none  [the longest x1 676 us: shards(): lax.psum((query_part, weight_part), ('head', 'key'))]
    pmax x2 -> x0, blocking collectives: 360 us -> none  [the longest x1 343 us: shards(): top_logit = lax.pmax(jnp.max(logits, axis=1), ('head', 'key'))]
    all_to_all x0 -> x3, waiting for transfers between devices: none -> 41.9 us  [exchange(): return lax.all_to_all(x, axis, split_axis=0, concat_axis=0, tiled=True)]
    all_gather x0 -> x1, waiting for transfers between devices: none -> 36.2 us  [shards(): plane_keys = lax.all_gather(index_keys.astype(jnp.float32), 'head', axis=0)]
    pallas_call x0 -> x5, Pallas kernels: none -> 35.9 us  [the longest x1 14 us: attention_scores(): pl.pallas_call(scores_kernel, grid=(steps,), in_specs=[pl.BlockSpec((rows...]
    dot_general x4 -> x0, matrix products: 32.2 us -> none  [the longest x1 12.6 us: shards(): jnp.einsum('thd,sd->ths', mla_query, cache_rows, preferred_element_type=j...]
    all_to_all x0 -> x2, blocking collectives: none -> 29.1 us  [exchange(): return lax.all_to_all(x, axis, split_axis=0, concat_axis=0, tiled=True)]
    reduce_sum x4 -> x1, other arithmetic: 21.7 us -> 0.02 us  [shards(): got4 = jnp.sum(exchange(send4, 'key'), axis=0)]
  transfers between devices with their start and end apart: 3 -> 5, of which waited for: 0 -> 5; matrix products, arithmetic and copies ran while one was open for 1% -> 1% of each run, Pallas kernels for 0% -> 4%
where the time goes in v1:
time: 203 us; the launch traced here: 201 us
  waiting for transfers between devices  79.3 us (39%)
  Pallas kernels  35.9 us (18%)
  blocking collectives  29.1 us (14%)
  local copies, waits for them, and re-layouts  24.8 us (12%)
  starting transfers between devices  15.8 us (8%)
  between operations  14.2 us (7%)
    all_to_all x3, waiting for transfers between devices, exchange(): return lax.all_to_all(x, axis, split_axis=0, concat_axis=0, tiled=True)  41.9 us
    all_gather x1, waiting for transfers between devices, shards(): plane_keys = lax.all_gather(index_keys.astype(jnp.float32), 'head', axis=0)  36.2 us
    all_to_all x2, blocking collectives, exchange(): return lax.all_to_all(x, axis, split_axis=0, concat_axis=0, tiled=True)  29.1 us
    unnamed x23, local copies, waits for them, and re-layouts  22.3 us
    all_to_all x3, starting transfers between devices, exchange(): return lax.all_to_all(x, axis, split_axis=0, concat_axis=0, tiled=True)  15.7 us
    pallas_call x1, Pallas kernels, attention_scores(): pl.pallas_call(scores_kernel, grid=(steps,), in_specs=[pl.BlockSpec((rows...  14 us
    pallas_call x1, Pallas kernels, key_gradient(): pl.pallas_call(lambda *refs: keys_kernel(key_total, *refs), out_shape=(ja...  7.55 us
    pallas_call x1, Pallas kernels, query_gradient(): pl.pallas_call(query_kernel, grid=(blocks,), in_specs=[pl.BlockSpec((1, h...  6.58 us
  transfers between devices with their start and end apart: 5, of which 5 were waited for; matrix products, arithmetic and copies ran while one was open for 1% of the time, Pallas kernels for 4%

profile of v1, /device:TPU:32, one launch (start us, length us, event | category | flops | bytes accessed | tf_op | source)
XLA Modules:
  0.0 201.1 jit_solution(4096864908327759192)
XLA Ops:
  7.2 0.8 copy.8.w_ref.refs_4_
  8.0 7.7 %copy.10.c_ref = bf16[16,256,576]{2,1,0:T(8,128)(2,1)} copy(bf16[16,256,576]{1,2,0:T(8,128)(2,1)} %param.6) | data formatting | bytes 9437184 | tf_op args[1]
  15.7 0.0 copy-start.5
  15.7 0.0 copy-start.7
  15.7 2.4 %copy.9.q_ref = bf16[128,8,576]{2,1,0:T(8,128)(2,1)S(1)} copy(bf16[128,8,576]{0,2,1:T(8,128)(2,1)} %param.5) | data formatting | bytes 2359296 | tf_op args[0]
  18.1 0.0 copy-done.5
  18.1 0.0 copy-done.7
  18.1 4.9 %indexer_forward.1 = (f32[128,256]{1,0:T(8,128)S(1)}, f32[8,128]{1,0:T(8,128)S(1)}, bf16[64,128,128]{2,1,0:T(8,128)(2,1)S(1)}) custom-call(bf16[128,64,128]{2,1,0:T(8,128)(2,1)S(1)} %copy-done.5, bf16[256,128]{1,0:T(8,128)(2,1)S(1)} %copy-done.7, f32[128,64]{1,0:T(8,128)S(1)} %copy.8.w_ref.refs_4_), custom_call_target="tpu_custom_call" | custom-call | tf_op jit(solution)/shard_map/indexer_forward/pallas_call | solution.py:64
  23.0 0.0 copy-start.3
  23.0 1.3 copy-done.3
  24.3 0.0 copy-start.8
  24.3 0.7 copy-done.8
  25.0 14.0 %attention_scores.1 = (bf16[16,8,128,256]{3,2,1,0:T(8,128)(2,1)}, f32[1024,128]{1,0:T(8,128)S(1)}, f32[8,24,128]{2,1,0:T(8,128)S(1)}) custom-call(bf16[128,8,576]{2,1,0:T(8,128)(2,1)S(1)} %copy.9.q_ref, bf16[16,256,576]{2,1,0:T(8,128)(2,1)} %copy.10.c_ref, f32[8,128]{1,0:T(8,128)S(1)} %get-tuple-element.11.lstats_ref), custom_call_target="tpu_custom_call" | custom-call | tf_op jit(solution)/shard_map/attention_scores/pallas_call | solution.py:139
  39.0 15.5 %all_to_all.25.got_ref = f32[8,24,128]{2,1,0:T(8,128)S(1)} all-to-all(f32[8,24,128]{2,1,0:T(8,128)S(1)} %get-tuple-element.14), channel_id=1, replica_groups=mesh['head'=16,'key'=8,'row'=2] {'key'}, dimensions={0} | all-to-all | bytes 196608 | tf_op jit(solution)/shard_map/all_to_all | solution.py:359
  54.5 0.0 copy-start.1
  54.5 3.4 %copy-done.1 = bf16[16,8,128,256]{3,2,1,0:T(8,128)(2,1)S(1)} copy-done((bf16[16,8,128,256]{3,2,1,0:T(8,128)(2,1)S(1)}, bf16[16,8,128,256]{3,2,1,0:T(8,128)(2,1)}, u32[]{:S(2)}) %copy-start.1) | copy-done | bytes 8388632
  57.9 2.8 %head_sum.1 = f32[16,136,256]{2,1,0:T(8,128)S(1)} custom-call(bf16[16,8,128,256]{3,2,1,0:T(8,128)(2,1)S(1)} %copy-done.1, f32[1024,128]{1,0:T(8,128)S(1)} %get-tuple-element.13.tops_ref, f32[8,24,128]{2,1,0:T(8,128)S(1)} %all_to_all.25.got_ref), custom_call_target="tpu_custom_call" | custom-call | tf_op jit(solution)/shard_map/head_sum/pallas_call | solution.py:206
  60.7 0.0 copy-start
  60.7 1.4 copy-done
  62.1 0.0 copy-start.9
  62.1 7.2 %all-to-all-start.1 = ((f32[16,136,256]{2,1,0:T(8,128)}), f32[16,136,256]{2,1,0:T(8,128)S(1)}, u32[]{:S(2)}, u32[]{:S(2)}) async-start(f32[16,136,256]{2,1,0:T(8,128)} %copy-done), calls=%async_computation.1 | async-start | bytes 4456448 | tf_op jit(solution)/shard_map/all_to_all | solution.py:359
  69.3 0.0 all-gather.3.cloned.1.call-start
  69.3 0.7 all_gather.12
  70.0 0.0 all-gather.3.cloned.1.call-update
  70.0 30.8 %all-to-all-done.1.refs_0_ = f32[16,136,256]{2,1,0:T(8,128)S(1)} async-done(((f32[16,136,256]{2,1,0:T(8,128)}), f32[16,136,256]{2,1,0:T(8,128)S(1)}, u32[]{:S(2)}, u32[]{:S(2)}) %all-to-all-start.1) | async-done | bytes 2228256 | tf_op jit(solution)/shard_map/all_to_all | solution.py:359
  100.8 0.0 copy-done.9
  100.8 0.0 copy-start.4
  100.8 1.6 copy-done.4
  102.4 7.5 %key_gradient.1 = (f32[16,160,256]{2,1,0:T(8,128)S(1)}, f32[256,128]{1,0:T(8,128)S(1)}) custom-call(f32[16,136,256]{2,1,0:T(8,128)S(1)} %all-to-all-done.1.refs_0_, f32[128,256]{1,0:T(8,128)S(1)} %copy-done.9, bf16[64,128,128]{2,1,0:T(8,128)(2,1)S(1)} %copy-done.4, bf16[256,128]{1,0:T(8,128)(2,1)S(1)} %copy-done.7, f32[128,64]{1,0:T(8,128)S(1)} %copy.8.w_ref.refs_4_), custom_call_target="tpu_custom_call" | custom-call | tf_op jit(solution)/shard_map/key_gradient/pallas_call | solution.py:278
  109.9 0.0 copy-start.2
  110.0 1.5 copy-done.2
  111.4 3.7 %all-to-all-start.2 = ((f32[16,160,256]{2,1,0:T(8,128)}), f32[16,160,256]{2,1,0:T(8,128)S(1)}, u32[]{:S(2)}, u32[]{:S(2)}) async-start(f32[16,160,256]{2,1,0:T(8,128)} %copy-done.2), calls=%async_computation.2 | async-start | bytes 5242880 | tf_op jit(solution)/shard_map/all_to_all | solution.py:359
  115.2 0.1 constant_dynamic-slice_fusion.1.w_ref
  115.3 0.9 constant_dynamic-slice_fusion.2.q_ref
  116.2 36.2 %all-gather.3.cloned.1.call-done = f32[4096,128]{1,0:T(8,128)} async-done(((f32[256,128]{1,0:T(8,128)}), f32[4096,128]{1,0:T(8,128)}) %all-gather.3.cloned.1.call-update) | async-done | bytes 2097168 | tf_op jit(solution)/shard_map/all_gather | solution.py:372
  152.3 4.3 %all-to-all-done.2.got_ref = f32[16,160,256]{2,1,0:T(8,128)S(1)} async-done(((f32[16,160,256]{2,1,0:T(8,128)}), f32[16,160,256]{2,1,0:T(8,128)S(1)}, u32[]{:S(2)}, u32[]{:S(2)}) %all-to-all-start.2) | async-done | bytes 2621472 | tf_op jit(solution)/shard_map/all_to_all | solution.py:359
  156.6 0.0 copy-start.6
  156.6 1.6 copy-done.6
  158.2 6.6 %query_gradient.1 = f32[8,72,128]{2,1,0:T(8,128)S(1)} custom-call(f32[16,160,256]{2,1,0:T(8,128)S(1)} %all-to-all-done.2.got_ref, f32[16,256,128]{2,1,0:T(8,128)S(1)} %bitcast.6, bf16[4,128,128]{2,1,0:T(8,128)(2,1)S(1)} %constant_dynamic-slice_fusion.2.q_ref, f32[128,4]{1,0:T(8,128)S(1)} %constant_dynamic-slice_fusion.1.w_ref), custom_call_target="tpu_custom_call" | custom-call | tf_op jit(solution)/shard_map/query_gradient/pallas_call | solution.py:337
  164.8 13.6 %all_to_all.26 = f32[8,72,128]{2,1,0:T(8,128)S(1)} all-to-all(f32[8,72,128]{2,1,0:T(8,128)S(1)} %query_gradient.1), channel_id=1, replica_groups=mesh['head'=16,'key'=8,'row'=2] {'key'}, dimensions={0} | all-to-all | bytes 589824 | tf_op jit(solution)/shard_map/all_to_all | solution.py:359
  178.5 0.7 broadcast_in_dim.2
  179.2 4.8 %all-to-all-start.4 = ((f32[8,72,128]{2,1,0:T(8,128)}), f32[8,72,128]{2,1,0:T(8,128)S(1)}, u32[]{:S(2)}, u32[]{:S(2)}) async-start(f32[8,72,128]{2,1,0:T(8,128)} %broadcast_in_dim.2), calls=%async_computation.4 | async-start | bytes 589824 | tf_op jit(solution)/shard_map/all_to_all | solution.py:359
  184.0 0.1 collective-permute-start
  184.1 1.2 collective-permute-done
  185.4 0.6 dynamic-slice_add_fusion
  186.0 6.9 %all-to-all-done.4 = f32[8,72,128]{2,1,0:T(8,128)S(1)} async-done(((f32[8,72,128]{2,1,0:T(8,128)}), f32[8,72,128]{2,1,0:T(8,128)S(1)}, u32[]{:S(2)}, u32[]{:S(2)}) %all-to-all-start.4) | async-done | bytes 294944 | tf_op jit(solution)/shard_map/all_to_all | solution.py:359
  192.9 0.6 maximum_bitcast_fusion
  193.5 0.7 slice.12
  (3 shorter events, 0.0 us)
Async XLA Ops:
  15.7 2.4 %copy-start.5 = (bf16[128,64,128]{2,1,0:T(8,128)(2,1)S(1)}, bf16[128,64,128]{2,1,0:T(8,128)(2,1)}, u32[]{:S(2)}) copy-start(bf16[128,64,128]{2,1,0:T(8,128)(2,1)} %q_ref.2) | copy-start | bytes 6291460
  15.7 2.4 %copy-start.7 = (bf16[256,128]{1,0:T(8,128)(2,1)S(1)}, bf16[256,128]{1,0:T(8,128)(2,1)}, u32[]{:S(2)}) copy-start(bf16[256,128]{1,0:T(8,128)(2,1)} %refs_3_.1) | copy-start | bytes 196612
  23.0 1.3 copy-start.3
  24.3 0.7 copy-start.8
  54.5 3.4 %copy-start.1 = (bf16[16,8,128,256]{3,2,1,0:T(8,128)(2,1)S(1)}, bf16[16,8,128,256]{3,2,1,0:T(8,128)(2,1)}, u32[]{:S(2)}) copy-start(bf16[16,8,128,256]{3,2,1,0:T(8,128)(2,1)} %get-tuple-element.12.e_ref) | copy-start | bytes 25165828
  60.7 1.4 copy-start
  62.1 38.7 %copy-start.9 = (f32[128,256]{1,0:T(8,128)S(1)}, f32[128,256]{1,0:T(8,128)}, u32[]{:S(2)}) copy-start(f32[128,256]{1,0:T(8,128)} %copy-done.8) | copy-start | bytes 393220
  62.1 38.7 %all-to-all-start.1 = ((f32[16,136,256]{2,1,0:T(8,128)}), f32[16,136,256]{2,1,0:T(8,128)S(1)}, u32[]{:S(2)}, u32[]{:S(2)}) async-start(f32[16,136,256]{2,1,0:T(8,128)} %copy-done), calls=%async_computation.1 | async-start | bytes 4456448 | tf_op jit(solution)/shard_map/all_to_all | solution.py:359
  69.3 83.1 %all-gather.3.cloned.1.call-start = ((), (), s32[]{:S(2)}) async-start(), calls=%async_computation.5 | async-start | bytes 2228224 | tf_op jit(solution)/shard_map/all_gather | solution.py:372
  100.8 1.6 copy-start.4
  109.9 1.5 copy-start.2
  111.4 45.2 %all-to-all-start.2 = ((f32[16,160,256]{2,1,0:T(8,128)}), f32[16,160,256]{2,1,0:T(8,128)S(1)}, u32[]{:S(2)}, u32[]{:S(2)}) async-start(f32[16,160,256]{2,1,0:T(8,128)} %copy-done.2), calls=%async_computation.2 | async-start | bytes 5242880 | tf_op jit(solution)/shard_map/all_to_all | solution.py:359
  156.6 1.6 copy-start.6
  179.2 13.7 %all-to-all-start.4 = ((f32[8,72,128]{2,1,0:T(8,128)}), f32[8,72,128]{2,1,0:T(8,128)S(1)}, u32[]{:S(2)}, u32[]{:S(2)}) async-start(f32[8,72,128]{2,1,0:T(8,128)} %broadcast_in_dim.2), calls=%async_computation.4 | async-start | bytes 589824 | tf_op jit(solution)/shard_map/all_to_all | solution.py:359
  184.0 1.3 collective-permute-start
Sparse Core Ops, SparseCore 0:
  72.5 79.7 all-gather.2

commit v2 on v1

v2 whole, which is shorter than its diff:
```python
import math

import jax
import jax.numpy as jnp
from jax import lax
from jax.experimental import pallas as pl
from jax.experimental.pallas import tpu as pltpu
from jax.sharding import PartitionSpec as P

MH = 128
LOG2E = 1.4426950408889634
SCORE2 = LOG2E / math.sqrt(192.0)
LANES = 128
NT = (((1,), (1,)), ((), ()))
TN = (((0,), (0,)), ((), ()))
NN = (((1,), (0,)), ((), ()))


def dot(a, b, dims):
    return lax.dot_general(a, b, dims, preferred_element_type=jnp.float32)


def lane_iota(rows):
    return lax.broadcasted_iota(jnp.int32, (rows, LANES), 1)


VMEM_BYTES = 60 << 20


def call(kernel, name, vmem=VMEM_BYTES, **options):
    return pl.pallas_call(
        kernel, name=name, compiler_params=pltpu.CompilerParams(vmem_limit_bytes=vmem), **options
    )


def forward_kernel(q_ref, k_ref, w_ref, logits_ref, stats_ref, qh_ref, qt_ref, wide):
    rows, heads, depth = q_ref.shape
    group = 8
    wide[...] = q_ref[...].astype(jnp.float32).reshape(rows * heads, depth)
    logits_ref[...] = jnp.zeros_like(logits_ref)

    def step(i, carry):
        total = logits_ref[...]
        weights = w_ref[pl.ds(i * group, group)]
        for j in range(group):
            head = i * group + j
            query = wide[pl.ds(head, rows, stride=heads), :]
            qh_ref[head] = query.astype(jnp.bfloat16)
            turned = query.T.astype(jnp.bfloat16)
            qt_ref[head] = turned
            products = dot(k_ref[...], turned, NN)
            total = total + jnp.maximum(products, 0.0) * weights[j : j + 1]
        logits_ref[...] = total
        return carry

    lax.fori_loop(0, heads // group, step, 0)
    logits = logits_ref[...] * (1.0 / math.sqrt(depth))
    logits_ref[...] = logits
    top = jnp.max(logits, axis=0, keepdims=True)
    total = jnp.sum(jnp.exp(logits - top), axis=0, keepdims=True)
    stats_ref[...] = jnp.zeros_like(stats_ref)
    stats_ref[0:1] = top
    stats_ref[1:2] = total


def indexer_forward(index_query, index_keys, weights):
    rows, heads, depth = index_query.shape
    keys = index_keys.shape[0]
    return call(
        forward_kernel,
        "indexer_forward",
        out_shape=(
            jax.ShapeDtypeStruct((keys, rows), jnp.float32),
            jax.ShapeDtypeStruct((8, rows), jnp.float32),
            jax.ShapeDtypeStruct((heads, rows, depth), jnp.bfloat16),
            jax.ShapeDtypeStruct((heads, depth, rows), jnp.bfloat16),
        ),
        scratch_shapes=[pltpu.VMEM((rows * heads, depth), jnp.float32)],
    )(index_query, index_keys, weights)


def scores_kernel(q_ref, c_ref, lstats_ref, e_ref, tops_ref, send_ref, qh, sums):
    heads, width, rows = q_ref.shape
    step = pl.program_id(0)
    steps = pl.num_programs(0)
    part = c_ref.shape[0]
    lane = lane_iota(2 * rows)

    @pl.when(step == 0)
    def _():
        for h in range(heads):
            qh[h * rows : (h + 1) * rows] = q_ref[h].T
        tops_ref[...] = jnp.zeros_like(tops_ref)
        sums[...] = jnp.zeros_like(sums)

    for h in range(0, heads, 2):
        span = slice(h * rows, (h + 2) * rows)
        queries = qh[span]
        blocks = [dot(queries, c_ref[j], NN) for j in range(part)]
        top = blocks[0]
        for block in blocks[1:]:
            top = jnp.maximum(top, block)
        top = jnp.max(top, axis=1, keepdims=True)
        total = None
        for j, block in enumerate(blocks):
            terms = jnp.exp2((block - top) * SCORE2)
            total = terms if total is None else total + terms
            e_ref[j, h : h + 2] = terms.astype(jnp.bfloat16).reshape(2, rows, terms.shape[1])
        total = jnp.sum(total, axis=1, keepdims=True)
        tops_ref[span] = jnp.where(lane == step, top, tops_ref[span])
        sums[span] = jnp.where(lane == step, total, sums[span])

    @pl.when(step == steps - 1)
    def _():
        lane1 = lane_iota(rows)
        used = lane1 < steps
        packed = jnp.zeros((rows, LANES), jnp.float32)
        for h in range(heads):
            tops = tops_ref[h * rows : (h + 1) * rows]
            top = jnp.max(jnp.where(used, tops, -jnp.inf), axis=1, keepdims=True)
            scaled = sums[h * rows : (h + 1) * rows] * jnp.exp2(jnp.where(used, tops - top, 0.0) * SCORE2)
            total = jnp.sum(jnp.where(used, scaled, 0.0), axis=1, keepdims=True)
            packed = jnp.where(lane1 == h, top, packed)
            packed = jnp.where(lane1 == heads + h, total, packed)
        flat = packed.T[0 : 2 * heads]
        for z in range(send_ref.shape[0]):
            send_ref[z, 0 : 2 * heads] = flat
            send_ref[z, 2 * heads :] = lstats_ref[...]


PART = 2


def attention_scores(queries, cache, lstats, key_count):
    heads, width, rows = queries.shape
    blocks, _, keys = cache.shape
    return call(
        scores_kernel,
        "attention_scores",
        grid=(blocks // PART,),
        in_specs=[
            pl.BlockSpec((heads, width, rows), lambda i: (0, 0, 0)),
            pl.BlockSpec((PART, width, keys), lambda i: (i, 0, 0)),
            pl.BlockSpec((8, rows), lambda i: (0, 0)),
        ],
        out_specs=(
            pl.BlockSpec((PART, heads, rows, keys), lambda i: (i, 0, 0, 0)),
            pl.BlockSpec((heads * rows, LANES), lambda i: (0, 0)),
            pl.BlockSpec((key_count, 2 * heads + 8, rows), lambda i: (0, 0, 0)),
        ),
        out_shape=(
            jax.ShapeDtypeStruct((blocks, heads, rows, keys), jnp.bfloat16),
            jax.ShapeDtypeStruct((heads * rows, LANES), jnp.float32),
            jax.ShapeDtypeStruct((key_count, 2 * heads + 8, rows), jnp.float32),
        ),
        scratch_shapes=[
            pltpu.VMEM((rows * heads, width), jnp.bfloat16),
            pltpu.VMEM((rows * heads, LANES), jnp.float32),
        ],
    )(queries, cache, lstats)


def headsum_kernel(e_ref, tops_ref, got_ref, out_ref, weights, tail, square):
    part, heads, rows, keys = e_ref.shape
    step = pl.program_id(0)
    lane = lane_iota(rows)

    @pl.when(step == 0)
    def _():
        tops = got_ref[:, 0:heads]
        top = jnp.max(tops, axis=0)
        total = jnp.sum(got_ref[:, heads : 2 * heads] * jnp.exp2((tops - top[None]) * SCORE2), axis=0)
        square[...] = jnp.zeros_like(square)
        square[0:heads] = top
        square[heads : 2 * heads] = (1.0 / MH) / total
        columns = square[...].T
        for h in range(heads):
            local = tops_ref[h * rows : (h + 1) * rows] - columns[:, h : h + 1]
            scale = columns[:, heads + h : heads + h + 1]
            weights[h] = jnp.exp2(jnp.minimum(local * SCORE2, 0.0)) * scale
        ltops = got_ref[:, 2 * heads : 2 * heads + 1]
        ltop = jnp.max(ltops, axis=0)
        lsum = jnp.sum(got_ref[:, 2 * heads + 1 : 2 * heads + 2] * jnp.exp(ltops - ltop[None]), axis=0)
        tail[...] = jnp.zeros_like(tail)
        tail[0:1, 0:rows] = ltop
        tail[1:2, 0:rows] = lsum

    columns = []
    for h in range(heads):
        columns.append(jnp.sum(jnp.where(lane == step, weights[h], 0.0), axis=1, keepdims=True))
    for j in range(part):
        total = e_ref[j, 0].astype(jnp.float32) * columns[0]
        for h in range(1, heads):
            total = total + e_ref[j, h].astype(jnp.float32) * columns[h]
        out_ref[j, 0:rows] = total
        out_ref[j, rows:] = tail[...]


def head_sum(terms, tops, got):
    blocks, heads, rows, keys = terms.shape
    return call(
        headsum_kernel,
        "head_sum",
        grid=(blocks // PART,),
        in_specs=[
            pl.BlockSpec((PART, heads, rows, keys), lambda i: (i, 0, 0, 0)),
            pl.BlockSpec((heads * rows, LANES), lambda i: (0, 0)),
            pl.BlockSpec(got.shape, lambda i: (0, 0, 0)),
        ],
        out_specs=pl.BlockSpec((PART, rows + 8, keys), lambda i: (i, 0, 0)),
        out_shape=jax.ShapeDtypeStruct((blocks, rows + 8, keys), jnp.float32),
        scratch_shapes=[
            pltpu.VMEM((heads, rows, LANES), jnp.float32),
            pltpu.VMEM((8, keys), jnp.float32),
            pltpu.VMEM((LANES, rows), jnp.float32),
        ],
    )(terms, tops, got)


def keys_kernel(key_total, got_ref, logits_ref, qh_ref, qt_ref, k_ref, w_ref, send_ref, keys_ref, slopes, turned):
    copies, _, keys = got_ref.shape
    heads, rows, depth = qh_ref.shape
    group = 8
    root = 1.0 / math.sqrt(depth)

    ltops = got_ref[:, rows : rows + 1, 0:rows]
    ltop = jnp.max(ltops, axis=0)
    lsum = jnp.sum(got_ref[:, rows + 1 : rows + 2, 0:rows] * jnp.exp(ltops - ltop[None]), axis=0)
    target = got_ref[0, 0:rows]
    for g in range(1, copies):
        target = target + got_ref[g, 0:rows]
    soft = jnp.exp(logits_ref[...] - ltop) * (1.0 / lsum)
    for k in range(0, keys, rows):
        turned[k : k + rows] = key_total * (soft[k : k + rows] - target[:, k : k + rows].T)
        send_ref[0:rows, k : k + rows] = turned[k : k + rows].T
    keys_ref[...] = jnp.zeros_like(keys_ref)

    def step(i, first, column):
        weights = w_ref[pl.ds(i * group, group)] * root
        sums = []
        for j in range(group):
            products = dot(k_ref[...], qt_ref[i * group + j], NN)
            dlogits = turned[...]
            sums.append(jnp.sum(jnp.maximum(products, 0.0) * dlogits, axis=0, keepdims=True) * root)
            slope = jnp.where(products > 0.0, dlogits * weights[j : j + 1], 0.0)
            slopes[:, j * rows : (j + 1) * rows] = slope.astype(jnp.bfloat16)
        place = pl.ds(pl.multiple_of(rows + first, group), group)
        send_ref[place, column : column + rows] = jnp.concatenate(sums, axis=0)
        chunk = qh_ref[pl.ds(i * group, group)].reshape(group * rows, depth)
        keys_ref[...] += dot(slopes[...], chunk, NN)

    half = heads // 2 // group

    def low(i, carry):
        step(i, i * group, 0)
        return carry

    def high(i, carry):
        step(i + half, i * group, rows)
        return carry

    lax.fori_loop(0, half, low, 0)
    lax.fori_loop(0, half, high, 0)


def key_gradient(got, logits, qh, qt, index_keys, weights, key_total):
    copies, _, keys = got.shape
    heads, rows, depth = qh.shape
    return call(
        lambda *refs: keys_kernel(key_total, *refs),
        "key_gradient",
        24 << 20,
        out_shape=(
            jax.ShapeDtypeStruct((rows + heads // 2, keys), jnp.float32),
            jax.ShapeDtypeStruct((keys, depth), jnp.float32),
        ),
        scratch_shapes=[
            pltpu.VMEM((keys, 8 * rows), jnp.bfloat16),
            pltpu.VMEM((keys, rows), jnp.float32),
        ],
    )(got, logits, qh, qt, index_keys, weights)


def query_kernel(place_ref, *refs):
    ring = RING
    got, kept = refs[0:ring], refs[ring : 2 * ring]
    qh_ref, w_ref = refs[2 * ring : 2 * ring + 2]
    outs = refs[2 * ring + 2 : 3 * ring + 2]
    slopes, acc, near, dlogits = refs[3 * ring + 2 :]
    heads, rows, depth = qh_ref.shape
    keys = kept[0].shape[0]
    pieces, tall, _ = outs[0].shape
    extra = got[0].shape[0] - rows
    share = (tall - 2 * extra // pieces) * pieces // rows
    root = 1.0 / math.sqrt(depth)
    x, y = place_ref[0], place_ref[1]
    span = rows // pieces
    few = extra // pieces

    wsum = got[0][rows:]
    for d in range(1, ring):
        wsum = wsum + got[d][rows:]
    for d in range(ring):
        near[d * keys : (d + 1) * keys] = kept[d][...].astype(jnp.bfloat16)
        dlogits[:, d * keys : (d + 1) * keys] = got[d][0:rows] * root
    columns = jnp.concatenate([w_ref[...], jnp.zeros((LANES - heads, rows), jnp.float32)], axis=0).T

    for d in range(ring):
        first = (lax.rem(x + d, ring) * ring + y) * share
        weights = pltpu.roll(columns, LANES - first, 1)
        queries = qh_ref[pl.ds(first, share)].reshape(share * rows, depth)
        for k in range(0, ring * keys, keys):
            products = dot(queries, near[k : k + keys], NT)
            for j in range(share):
                part = products[j * rows : (j + 1) * rows]
                slope = jnp.where(part > 0.0, dlogits[:, k : k + keys] * weights[:, j : j + 1], 0.0)
                slopes[j * rows : (j + 1) * rows, k : k + keys] = slope.astype(jnp.bfloat16)
        acc[...] = dot(slopes[...], near[...], NN)
        for z in range(pieces):
            for j in range(share):
                start = j * rows + z * span
                outs[d][z, pl.ds(j, span, stride=share), :] = acc[start : start + span]
            piece = wsum[z * few : (z + 1) * few]
            outs[d][z, share * span : share * span + few] = piece[:, 0:rows]
            outs[d][z, share * span + few :] = piece[:, rows : 2 * rows]


RING = 4


def query_gradient(place, got, kept, qh, weights, pieces):
    height, keys = got[0].shape
    heads, rows, depth = qh.shape
    share = heads // (RING * RING)
    extra = height - rows
    tall = share * (rows // pieces) + 2 * (extra // pieces)
    vmem = pl.BlockSpec(memory_space=pltpu.VMEM)
    return call(
        query_kernel,
        "query_gradient",
        24 << 20,
        in_specs=[pl.BlockSpec(memory_space=pltpu.SMEM)] + [vmem] * (2 * RING + 2),
        out_specs=[vmem] * RING,
        out_shape=[jax.ShapeDtypeStruct((pieces, tall, depth), jnp.float32)] * RING,
        scratch_shapes=[
            pltpu.VMEM((share * rows, RING * keys), jnp.bfloat16),
            pltpu.VMEM((share * rows, depth), jnp.float32),
            pltpu.VMEM((RING * keys, depth), jnp.bfloat16),
            pltpu.VMEM((rows, RING * keys), jnp.float32),
        ],
    )(place, *got, *kept, qh, weights)


def exchange(x, axis):
    return lax.all_to_all(x, axis, split_axis=0, concat_axis=0, tiled=True)


def shift_y(x, d):
    pairs = [(a * RING + b, a * RING + (b + d) % RING) for a in range(RING) for b in range(RING)]
    return lax.ppermute(x, "head", pairs)


def shift_x(x, d):
    pairs = [(a * RING + b, (a + d) % RING * RING + b) for a in range(RING) for b in range(RING)]
    return lax.ppermute(x, "head", pairs)


def shards(mla_query, mla_cache, index_query, index_keys, index_weight):
    key_count = lax.axis_size("key")
    head_count = lax.axis_size("head")
    rows = mla_query.shape[0]
    keys, depth = index_keys.shape
    heads = index_query.shape[1]
    share = heads // head_count
    head_index = lax.axis_index("head")
    row_index = lax.axis_index("row")
    place = jnp.stack([head_index // RING, head_index % RING]).astype(jnp.int32)

    wide_keys = index_keys.astype(jnp.float32)
    kept = [wide_keys] + [shift_y(wide_keys, d) for d in range(1, RING)]
    weights = index_weight.T
    logits, lstats, qh, qt = indexer_forward(index_query, index_keys, weights)
    queries = jnp.transpose(mla_query, (1, 2, 0))
    cache = jnp.swapaxes(mla_cache, 1, 2)
    terms, tops, send1 = attention_scores(queries, cache, lstats, key_count)
    got1, kept = lax.optimization_barrier((exchange(send1, "key"), kept))
    send2 = head_sum(terms, tops, got1)
    got2 = exchange(send2, "head")
    key_total = float(keys * head_count * key_count)
    send3, keys_part = key_gradient(got2, logits, qh, qt, index_keys, weights, key_total)
    got3 = [send3] + [shift_y(send3, d) for d in range(1, RING)]

    half = keys // 2
    away = lax.dynamic_slice_in_dim(keys_part, (1 - row_index) * half, half, 0)
    near = lax.dynamic_slice_in_dim(keys_part, row_index * half, half, 0)
    key_grad = near + lax.ppermute(away, "row", [(0, 1), (1, 0)])

    parts = query_gradient(place, got3, kept, qh, weights, key_count)
    send4 = parts[0]
    for d in range(1, RING):
        send4 = send4 + shift_x(parts[d], d)
    got4 = jnp.sum(exchange(send4, "key"), axis=0)
    got5 = exchange(jnp.broadcast_to(got4[None], (key_count, *got4.shape)), "key")
    span = share * (rows // key_count)
    query_grad = got5[:, 0:span].reshape(rows, share, depth)
    few = (got4.shape[0] - span) // 2
    low = got5[:, span : span + few].reshape(heads // 2, rows)
    high = got5[:, span + few :].reshape(heads // 2, rows)
    weight_grad = jnp.concatenate([low, high], axis=0).T
    return (query_grad, key_grad, weight_grad)


def solution(mesh):
    placed = (
        P("row", "head", None),
        P(None, "key", None),
        P("row", None, None),
        P(("head", "key"), None),
        P("row", None),
    )
    return jax.shard_map(
        shards,
        mesh=mesh,
        in_specs=placed,
        out_specs=(P("row", "head", None), P(("head", "key", "row"), None), P("row", None)),
        check_vma=False,
    )
```

time: 203 us -> 152 us (0.75)
  waiting for transfers between devices: 79.3 us -> 27.1 us
  local copies, waits for them, and re-layouts: 24.8 us -> 2.14 us
  blocking collectives: 29.1 us -> 51.7 us
  between operations: 14.2 us -> 0.71 us
  starting transfers between devices: 15.8 us -> 27.9 us
  Pallas kernels: 35.9 us -> 39 us
    all_gather x1 -> x0, waiting for transfers between devices: 36.2 us -> none  [shards(): plane_keys = lax.all_gather(index_keys.astype(jnp.float32), 'head', axis=0)]
    all_to_all x3 -> x2, waiting for transfers between devices: 41.9 us -> 7.42 us  [exchange(): return lax.all_to_all(x, axis, split_axis=0, concat_axis=0, tiled=True)]
    all_to_all x2, blocking collectives: 29.1 us -> 51.7 us  [exchange(): return lax.all_to_all(x, axis, split_axis=0, concat_axis=0, tiled=True)]
    unnamed x23 -> x12, local copies, waits for them, and re-layouts: 22.3 us -> 0.66 us
    ppermute x0 -> x9, waiting for transfers between devices: none -> 18.4 us  [the longest x3 9.39 us: shift_x(): return lax.ppermute(x, 'head', pairs)]
    ppermute x0 -> x9, starting transfers between devices: none -> 14.4 us  [the longest x6 10.1 us: shift_y(): return lax.ppermute(x, 'head', pairs)]
    pallas_call x5, Pallas kernels: 35.9 us -> 39 us  [the longest x1 14.2 us: attention_scores(): call(scores_kernel, 'attention_scores', grid=(blocks // PART,), in_specs=...]
    all_to_all x3 -> x2, starting transfers between devices: 15.7 us -> 13.4 us  [exchange(): return lax.all_to_all(x, axis, split_axis=0, concat_axis=0, tiled=True)]
  transfers between devices with their start and end apart: 5 -> 12, of which waited for: 5 -> 8; matrix products, arithmetic and copies ran while one was open for 1% -> 0% of each run, Pallas kernels for 4% -> 0%
where the time goes in v2:
time: 152 us; the launch traced here: 150 us
  blocking collectives  51.7 us (34%)
  Pallas kernels  39 us (26%)
  starting transfers between devices  27.9 us (18%)
  waiting for transfers between devices  27.1 us (18%)
  local copies, waits for them, and re-layouts  2.14 us (1%)
    all_to_all x2, blocking collectives, exchange(): return lax.all_to_all(x, axis, split_axis=0, concat_axis=0, tiled=True)  51.7 us
    pallas_call x1, Pallas kernels, attention_scores(): call(scores_kernel, 'attention_scores', grid=(blocks // PART,), in_specs=...  14.2 us
    all_to_all x2, starting transfers between devices, exchange(): return lax.all_to_all(x, axis, split_axis=0, concat_axis=0, tiled=True)  13.4 us
    ppermute x6, starting transfers between devices, shift_y(): return lax.ppermute(x, 'head', pairs)  10.1 us
    ppermute x3, waiting for transfers between devices, shift_x(): return lax.ppermute(x, 'head', pairs)  9.39 us
    ppermute x6, waiting for transfers between devices, shift_y(): return lax.ppermute(x, 'head', pairs)  9.02 us
    pallas_call x1, Pallas kernels, head_sum(): call(headsum_kernel, 'head_sum', grid=(blocks // PART,), in_specs=[pl.Blo...  8.6 us
    pallas_call x1, Pallas kernels, indexer_forward(): call(forward_kernel, 'indexer_forward', out_shape=(jax.ShapeDtypeStruct((...  8.31 us
  transfers between devices with their start and end apart: 12, of which 8 were waited for; matrix products, arithmetic and copies ran while one was open for 0% of the time, Pallas kernels for 0%

profile of v2, /device:TPU:32, one launch (start us, length us, event | category | flops | bytes accessed | tf_op | source)
XLA Modules:
  0.0 150.0 jit_solution(12644274639068403749)
XLA Ops:
  0.6 8.3 %indexer_forward.1 = (f32[256,128]{1,0:T(8,128)}, f32[8,128]{1,0:T(8,128)}, bf16[64,128,128]{2,1,0:T(8,128)(2,1)}, bf16[64,128,128]{2,1,0:T(8,128)(2,1)}) custom-call(bf16[128,64,128]{2,1,0:T(8,128)(2,1)} %q_ref.1, bf16[256,128]{1,0:T(8,128)(2,1)} %refs_4_.1, f32[64,128]{1,0:T(8,128)} %bitcast.10), custom_call_target="tpu_custom_call" | custom-call | tf_op jit(solution)/shard_map/indexer_forward/pallas_call | solution.py:69
  8.9 0.0 copy-start.2
  8.9 14.2 %attention_scores.1 = (bf16[16,8,128,256]{3,2,1,0:T(8,128)(2,1)}, f32[1024,128]{1,0:T(8,128)}, f32[8,24,128]{2,1,0:T(8,128)}) custom-call(bf16[8,576,128]{2,1,0:T(8,128)(2,1)} %bitcast.14, bf16[16,576,256]{2,1,0:T(8,128)(2,1)} %bitcast.13, f32[8,128]{1,0:T(8,128)} %get-tuple-element.21.lstats_ref), custom_call_target="tpu_custom_call" | custom-call | tf_op jit(solution)/shard_map/attention_scores/pallas_call | solution.py:137
  23.1 8.6 %all-to-all-start = ((f32[8,24,128]{2,1,0:T(8,128)}), f32[8,24,128]{2,1,0:T(8,128)S(1)}, u32[]{:S(2)}, u32[]{:S(2)}) async-start(f32[8,24,128]{2,1,0:T(8,128)} %get-tuple-element.24), calls=%async_computation | async-start | bytes 196608 | tf_op jit(solution)/shard_map/all_to_all | solution.py:355
  31.7 0.0 copy-done.2
  31.7 1.6 %collective-permute-start = (f32[256,128]{1,0:T(8,128)S(1)}, f32[256,128]{1,0:T(8,128)S(1)}, u32[]{:S(2)}, u32[]{:S(2)}) collective-permute-start(f32[256,128]{1,0:T(8,128)S(1)} %convert_element_type.3.refs_4_), channel_id=1, source_target_pairs={{0,16},{16,32},{32,48},{48,0},{64,80},{80,96},{96,112},{112,64},{1... | collective-permute-start | bytes 393224 | tf_op jit(solution)/shard_map/ppermute | solution.py:360
  33.4 2.9 %collective-permute-start.1 = (f32[256,128]{1,0:T(8,128)S(1)}, f32[256,128]{1,0:T(8,128)S(1)}, u32[]{:S(2)}, u32[]{:S(2)}) collective-permute-start(f32[256,128]{1,0:T(8,128)S(1)} %convert_element_type.3.refs_4_), channel_id=1, source_target_pairs={{0,32},{16,48},{32,0},{48,16},{64,96},{80,112},{96,64},{112,80},{1... | collective-permute-start | bytes 393224 | tf_op jit(solution)/shard_map/ppermute | solution.py:360
  36.3 1.3 collective-permute-start.2
  37.6 1.2 collective-permute-done.refs_5_
  38.8 2.9 %collective-permute-done.1.refs_6_ = f32[256,128]{1,0:T(8,128)S(1)} collective-permute-done((f32[256,128]{1,0:T(8,128)S(1)}, f32[256,128]{1,0:T(8,128)S(1)}, u32[]{:S(2)}, u32[]{:S(2)}) %collective-permute-start.1) | collective-permute-done | bytes 131104 | tf_op jit(solution)/shard_map/ppermute | solution.py:360
  41.7 0.0 collective-permute-done.2.refs_7_
  41.7 0.0 all-to-all-done.got_ref
  41.7 0.0 copy-start.5
  41.7 0.6 copy-done.5
  42.4 8.6 %head_sum.1 = f32[16,136,256]{2,1,0:T(8,128)} custom-call(bf16[16,8,128,256]{3,2,1,0:T(8,128)(2,1)} %get-tuple-element.22.e_ref, f32[1024,128]{1,0:T(8,128)} %get-tuple-element.23.tops_ref, f32[8,24,128]{2,1,0:T(8,128)} %copy-done.5), custom_call_target="tpu_custom_call" | custom-call | tf_op jit(solution)/shard_map/head_sum/pallas_call | solution.py:201
  51.0 0.0 copy-start
  51.0 0.0 copy-start.1
  51.0 0.0 copy-start.4
  51.0 35.4 %all_to_all.20.refs_0_ = f32[16,136,256]{2,1,0:T(8,128)S(1)} all-to-all(f32[16,136,256]{2,1,0:T(8,128)} %head_sum.1), channel_id=1, replica_groups=mesh['head'=16,'key'=8,'row'=2] {'head'}, dimensions={0} | all-to-all | bytes 4456448 | tf_op jit(solution)/shard_map/all_to_all | solution.py:355
  86.4 0.0 copy-done
  86.4 0.0 copy-done.1
  86.4 0.0 copy-done.3
  86.5 0.0 copy-done.4
  86.5 4.8 %key_gradient.1 = (f32[160,256]{1,0:T(8,128)S(1)}, f32[256,128]{1,0:T(8,128)S(1)}) custom-call(f32[16,136,256]{2,1,0:T(8,128)S(1)} %all_to_all.20.refs_0_, f32[256,128]{1,0:T(8,128)S(1)} %copy-done.4, bf16[64,128,128]{2,1,0:T(8,128)(2,1)S(1)} %copy-done, bf16[64,128,128]{2,1,0:T(8,128)(2,1)S(1)} %copy-done.1, bf16[256,128]{1,0:T(8,128)(2,1)S(1)} %copy-done.2, ...), custom_call_target="tpu_custom_call" | custom-call | tf_op jit(solution)/shard_map/key_gradient/pallas_call | solution.py:269
  91.2 0.6 collective-permute-start.3
  91.8 2.2 %collective-permute-start.4 = (f32[160,256]{1,0:T(8,128)S(1)}, f32[160,256]{1,0:T(8,128)S(1)}, u32[]{:S(2)}, u32[]{:S(2)}) collective-permute-start(f32[160,256]{1,0:T(8,128)S(1)} %get-tuple-element.29.refs_0_), channel_id=1, source_target_pairs={{0,32},{16,48},{32,0},{48,16},{64,96},{80,112},{96,64},{112,80},{1... | collective-permute-start | bytes 491528 | tf_op jit(solution)/shard_map/ppermute | solution.py:360
  94.0 1.4 collective-permute-start.5
  95.5 0.1 pad_add_fusion.place_ref
  95.5 4.1 %collective-permute-done.3.refs_1_ = f32[160,256]{1,0:T(8,128)S(1)} collective-permute-done((f32[160,256]{1,0:T(8,128)S(1)}, f32[160,256]{1,0:T(8,128)S(1)}, u32[]{:S(2)}, u32[]{:S(2)}) %collective-permute-start.3) | collective-permute-done | bytes 163872 | tf_op jit(solution)/shard_map/ppermute | solution.py:360
  99.6 0.0 collective-permute-done.4.refs_2_
  99.6 0.9 collective-permute-done.5.refs_3_
  100.5 3.1 %query_gradient.1 = (f32[8,72,128]{2,1,0:T(8,128)S(1)}, f32[8,72,128]{2,1,0:T(8,128)S(1)}, f32[8,72,128]{2,1,0:T(8,128)S(1)}, f32[8,72,128]{2,1,0:T(8,128)S(1)}) custom-call(s32[2]{0:T(128)S(1)} %pad_add_fusion.place_ref, f32[160,256]{1,0:T(8,128)S(1)} %get-tuple-element.29.refs_0_, f32[160,256]{1,0:T(8,128)S(1)} %collective-permute-done.3.refs_1_, ...), custom_call_target="tpu_custom_call" | custom-call | tf_op jit(solution)/shard_map/query_gradient/pallas_call | solution.py:338
  103.6 0.7 collective-permute-start.6
  104.3 2.3 %collective-permute-start.7 = (f32[8,72,128]{2,1,0:T(8,128)S(1)}, f32[8,72,128]{2,1,0:T(8,128)S(1)}, u32[]{:S(2)}, u32[]{:S(2)}) collective-permute-start(f32[8,72,128]{2,1,0:T(8,128)S(1)} %get-tuple-element.36), channel_id=1, source_target_pairs={{0,128},{16,144},{32,160},{48,176},{64,192},{80,208},{96,224},{112... | collective-permute-start | bytes 884744 | tf_op jit(solution)/shard_map/ppermute | solution.py:365
  106.6 1.2 collective-permute-start.8
  107.8 8.9 %collective-permute-done.6 = f32[8,72,128]{2,1,0:T(8,128)S(1)} collective-permute-done((f32[8,72,128]{2,1,0:T(8,128)S(1)}, f32[8,72,128]{2,1,0:T(8,128)S(1)}, u32[]{:S(2)}, u32[]{:S(2)}) %collective-permute-start.6) | collective-permute-done | bytes 294944 | tf_op jit(solution)/shard_map/ppermute | solution.py:365
  116.7 0.0 collective-permute-done.7
  116.7 0.5 collective-permute-done.8
  117.2 0.1 add_add_fusion
  117.3 16.3 %all_to_all.21 = f32[8,72,128]{2,1,0:T(8,128)S(1)} all-to-all(f32[8,72,128]{2,1,0:T(8,128)S(1)} %add_add_fusion), channel_id=1, replica_groups=mesh['head'=16,'key'=8,'row'=2] {'key'}, dimensions={0} | all-to-all | bytes 589824 | tf_op jit(solution)/shard_map/all_to_all | solution.py:355
  133.6 0.7 broadcast_in_dim.2
  134.4 4.9 %all-to-all-start.3 = ((f32[8,72,128]{2,1,0:T(8,128)}), f32[8,72,128]{2,1,0:T(8,128)S(1)}, u32[]{:S(2)}, u32[]{:S(2)}) async-start(f32[8,72,128]{2,1,0:T(8,128)} %broadcast_in_dim.2), calls=%async_computation.3 | async-start | bytes 589824 | tf_op jit(solution)/shard_map/all_to_all | solution.py:355
  139.2 0.1 collective-permute-start.9
  139.3 1.2 collective-permute-done.9
  140.6 0.6 dynamic-slice_add_fusion
  141.2 7.4 %all-to-all-done.3 = f32[8,72,128]{2,1,0:T(8,128)S(1)} async-done(((f32[8,72,128]{2,1,0:T(8,128)}), f32[8,72,128]{2,1,0:T(8,128)S(1)}, u32[]{:S(2)}, u32[]{:S(2)}) %all-to-all-start.3) | async-done | bytes 294944 | tf_op jit(solution)/shard_map/all_to_all | solution.py:355
  148.6 0.6 maximum_bitcast_fusion
  149.2 0.7 slice.12
  (5 shorter events, 0.0 us)
Async XLA Ops:
  8.9 22.8 %copy-start.2 = (bf16[256,128]{1,0:T(8,128)(2,1)S(1)}, bf16[256,128]{1,0:T(8,128)(2,1)}, u32[]{:S(2)}) copy-start(bf16[256,128]{1,0:T(8,128)(2,1)} %refs_4_.1) | copy-start | bytes 196612
  23.1 18.6 %all-to-all-start = ((f32[8,24,128]{2,1,0:T(8,128)}), f32[8,24,128]{2,1,0:T(8,128)S(1)}, u32[]{:S(2)}, u32[]{:S(2)}) async-start(f32[8,24,128]{2,1,0:T(8,128)} %get-tuple-element.24), calls=%async_computation | async-start | bytes 196608 | tf_op jit(solution)/shard_map/all_to_all | solution.py:355
  31.7 7.1 %collective-permute-start = (f32[256,128]{1,0:T(8,128)S(1)}, f32[256,128]{1,0:T(8,128)S(1)}, u32[]{:S(2)}, u32[]{:S(2)}) collective-permute-start(f32[256,128]{1,0:T(8,128)S(1)} %convert_element_type.3.refs_4_), channel_id=1, source_target_pairs={{0,16},{16,32},{32,48},{48,0},{64,80},{80,96},{96,112},{112,64},{1... | collective-permute-start | bytes 393224 | tf_op jit(solution)/shard_map/ppermute | solution.py:360
  33.4 8.4 %collective-permute-start.1 = (f32[256,128]{1,0:T(8,128)S(1)}, f32[256,128]{1,0:T(8,128)S(1)}, u32[]{:S(2)}, u32[]{:S(2)}) collective-permute-start(f32[256,128]{1,0:T(8,128)S(1)} %convert_element_type.3.refs_4_), channel_id=1, source_target_pairs={{0,32},{16,48},{32,0},{48,16},{64,96},{80,112},{96,64},{112,80},{1... | collective-permute-start | bytes 393224 | tf_op jit(solution)/shard_map/ppermute | solution.py:360
  36.3 5.5 %collective-permute-start.2 = (f32[256,128]{1,0:T(8,128)S(1)}, f32[256,128]{1,0:T(8,128)S(1)}, u32[]{:S(2)}, u32[]{:S(2)}) collective-permute-start(f32[256,128]{1,0:T(8,128)S(1)} %convert_element_type.3.refs_4_), channel_id=1, source_target_pairs={{0,48},{16,0},{32,16},{48,32},{64,112},{80,64},{96,80},{112,96},{1... | collective-permute-start | bytes 393224 | tf_op jit(solution)/shard_map/ppermute | solution.py:360
  41.7 0.6 copy-start.5
  51.0 35.5 %copy-start = (bf16[64,128,128]{2,1,0:T(8,128)(2,1)S(1)}, bf16[64,128,128]{2,1,0:T(8,128)(2,1)}, u32[]{:S(2)}) copy-start(bf16[64,128,128]{2,1,0:T(8,128)(2,1)} %get-tuple-element.27.refs_2_.refs_8_) | copy-start | bytes 6291460
  51.0 35.5 %copy-start.1 = (bf16[64,128,128]{2,1,0:T(8,128)(2,1)S(1)}, bf16[64,128,128]{2,1,0:T(8,128)(2,1)}, u32[]{:S(2)}) copy-start(bf16[64,128,128]{2,1,0:T(8,128)(2,1)} %get-tuple-element.28.refs_3_) | copy-start | bytes 6291460
  51.0 35.5 %copy-start.3 = (f32[128,64]{0,1:T(8,128)S(1)}, f32[128,64]{0,1:T(8,128)}, u32[]{:S(2)}) copy-start(f32[128,64]{0,1:T(8,128)} %param.9) | copy-start | bytes 98308
  51.0 35.5 %copy-start.4 = (f32[256,128]{1,0:T(8,128)S(1)}, f32[256,128]{1,0:T(8,128)}, u32[]{:S(2)}) copy-start(f32[256,128]{1,0:T(8,128)} %get-tuple-element.26.refs_1_) | copy-start | bytes 393220
  91.2 8.4 %collective-permute-start.3 = (f32[160,256]{1,0:T(8,128)S(1)}, f32[160,256]{1,0:T(8,128)S(1)}, u32[]{:S(2)}, u32[]{:S(2)}) collective-permute-start(f32[160,256]{1,0:T(8,128)S(1)} %get-tuple-element.29.refs_0_), channel_id=1, source_target_pairs={{0,16},{16,32},{32,48},{48,0},{64,80},{80,96},{96,112},{112,64},{1... | collective-permute-start | bytes 491528 | tf_op jit(solution)/shard_map/ppermute | solution.py:360
  91.8 7.8 %collective-permute-start.4 = (f32[160,256]{1,0:T(8,128)S(1)}, f32[160,256]{1,0:T(8,128)S(1)}, u32[]{:S(2)}, u32[]{:S(2)}) collective-permute-start(f32[160,256]{1,0:T(8,128)S(1)} %get-tuple-element.29.refs_0_), channel_id=1, source_target_pairs={{0,32},{16,48},{32,0},{48,16},{64,96},{80,112},{96,64},{112,80},{1... | collective-permute-start | bytes 491528 | tf_op jit(solution)/shard_map/ppermute | solution.py:360
  94.0 6.4 %collective-permute-start.5 = (f32[160,256]{1,0:T(8,128)S(1)}, f32[160,256]{1,0:T(8,128)S(1)}, u32[]{:S(2)}, u32[]{:S(2)}) collective-permute-start(f32[160,256]{1,0:T(8,128)S(1)} %get-tuple-element.29.refs_0_), channel_id=1, source_target_pairs={{0,48},{16,0},{32,16},{48,32},{64,112},{80,64},{96,80},{112,96},{1... | collective-permute-start | bytes 491528 | tf_op jit(solution)/shard_map/ppermute | solution.py:360
  103.6 13.1 %collective-permute-start.6 = (f32[8,72,128]{2,1,0:T(8,128)S(1)}, f32[8,72,128]{2,1,0:T(8,128)S(1)}, u32[]{:S(2)}, u32[]{:S(2)}) collective-permute-start(f32[8,72,128]{2,1,0:T(8,128)S(1)} %get-tuple-element.35), channel_id=1, source_target_pairs={{0,64},{16,80},{32,96},{48,112},{64,128},{80,144},{96,160},{112,17... | collective-permute-start | bytes 884744 | tf_op jit(solution)/shard_map/ppermute | solution.py:365
  104.3 12.4 %collective-permute-start.7 = (f32[8,72,128]{2,1,0:T(8,128)S(1)}, f32[8,72,128]{2,1,0:T(8,128)S(1)}, u32[]{:S(2)}, u32[]{:S(2)}) collective-permute-start(f32[8,72,128]{2,1,0:T(8,128)S(1)} %get-tuple-element.36), channel_id=1, source_target_pairs={{0,128},{16,144},{32,160},{48,176},{64,192},{80,208},{96,224},{112... | collective-permute-start | bytes 884744 | tf_op jit(solution)/shard_map/ppermute | solution.py:365
  106.6 10.6 %collective-permute-start.8 = (f32[8,72,128]{2,1,0:T(8,128)S(1)}, f32[8,72,128]{2,1,0:T(8,128)S(1)}, u32[]{:S(2)}, u32[]{:S(2)}) collective-permute-start(f32[8,72,128]{2,1,0:T(8,128)S(1)} %get-tuple-element.37), channel_id=1, source_target_pairs={{0,192},{16,208},{32,224},{48,240},{64,0},{80,16},{96,32},{112,48}... | collective-permute-start | bytes 884744 | tf_op jit(solution)/shard_map/ppermute | solution.py:365
  134.4 14.3 %all-to-all-start.3 = ((f32[8,72,128]{2,1,0:T(8,128)}), f32[8,72,128]{2,1,0:T(8,128)S(1)}, u32[]{:S(2)}, u32[]{:S(2)}) async-start(f32[8,72,128]{2,1,0:T(8,128)} %broadcast_in_dim.2), calls=%async_computation.3 | async-start | bytes 589824 | tf_op jit(solution)/shard_map/all_to_all | solution.py:355
  139.2 1.3 collective-permute-start.9

commit v3 on v2

v3 whole, which is shorter than its diff:
```python
import math

import jax
import jax.numpy as jnp
from jax import lax
from jax.experimental import pallas as pl
from jax.experimental.pallas import tpu as pltpu
from jax.sharding import PartitionSpec as P

MH = 128
LOG2E = 1.4426950408889634
SCORE2 = LOG2E / math.sqrt(192.0)
LANES = 128
NT = (((1,), (1,)), ((), ()))
TN = (((0,), (0,)), ((), ()))
NN = (((1,), (0,)), ((), ()))


def dot(a, b, dims):
    return lax.dot_general(a, b, dims, preferred_element_type=jnp.float32)


def lane_iota(rows):
    return lax.broadcasted_iota(jnp.int32, (rows, LANES), 1)


RING = 4
PART = 2
VMEM = pl.BlockSpec(memory_space=pltpu.VMEM)
SMEM = pl.BlockSpec(memory_space=pltpu.SMEM)


def call(kernel, name, megabytes=32, **options):
    return pl.pallas_call(
        kernel, name=name, compiler_params=pltpu.CompilerParams(vmem_limit_bytes=megabytes << 20), **options
    )


def f32(*shape):
    return jax.ShapeDtypeStruct(shape, jnp.float32)


def bf16(*shape):
    return jax.ShapeDtypeStruct(shape, jnp.bfloat16)


def forward_kernel(q_ref, k_ref, w_ref, logits_ref, stats_ref, qh_ref, wide, total_ref):
    rows, heads, depth = q_ref.shape
    keys = k_ref.shape[0]
    group = 8
    wide[...] = q_ref[...].astype(jnp.float32).reshape(rows * heads, depth)
    columns = jnp.concatenate([w_ref[...], jnp.zeros((LANES - heads, rows), jnp.float32)], axis=0).T
    total_ref[...] = jnp.zeros_like(total_ref)

    def step(i, carry):
        weights = pltpu.roll(columns, LANES - group * i, 1)
        for j in range(group):
            head = i * group + j
            qh_ref[head] = wide[pl.ds(head, rows, stride=heads), :].astype(jnp.bfloat16)
        chunk = qh_ref[pl.ds(i * group, group)].reshape(group * rows, depth)
        products = dot(chunk, k_ref[...], NT)
        total = total_ref[...]
        for j in range(group):
            part = products[j * rows : (j + 1) * rows]
            total = total + jnp.maximum(part, 0.0) * weights[:, j : j + 1]
        total_ref[...] = total
        return carry

    lax.fori_loop(0, heads // group, step, 0)
    for k in range(0, keys, rows):
        logits_ref[k : k + rows] = total_ref[:, k : k + rows].T * (1.0 / math.sqrt(depth))
    logits = logits_ref[...]
    top = jnp.max(logits, axis=0, keepdims=True)
    total = jnp.sum(jnp.exp(logits - top), axis=0, keepdims=True)
    stats_ref[...] = jnp.zeros_like(stats_ref)
    stats_ref[0:1] = top
    stats_ref[1:2] = total


def indexer_forward(index_query, index_keys, weights):
    rows, heads, depth = index_query.shape
    keys = index_keys.shape[0]
    return call(
        forward_kernel,
        "indexer_forward",
        out_shape=(f32(keys, rows), f32(8, rows), bf16(heads, rows, depth)),
        scratch_shapes=[
            pltpu.VMEM((rows * heads, depth), jnp.float32),
            pltpu.VMEM((rows, keys), jnp.float32),
        ],
    )(index_query, index_keys, weights)


def scores_kernel(q_ref, c_ref, lstats_ref, e_ref, tops_ref, send_ref, qh, sums):
    heads, width, rows = q_ref.shape
    steps = c_ref.shape[0] // PART
    lane2 = lane_iota(2 * rows)
    for h in range(heads):
        qh[h * rows : (h + 1) * rows] = q_ref[h].T
    tops_ref[...] = jnp.zeros_like(tops_ref)
    sums[...] = jnp.zeros_like(sums)

    def body(step, carry):
        for h in range(0, heads, 2):
            span = slice(h * rows, (h + 2) * rows)
            queries = qh[span]
            blocks = [dot(queries, c_ref[step * PART + j], NN) for j in range(PART)]
            top = blocks[0]
            for block in blocks[1:]:
                top = jnp.maximum(top, block)
            top = jnp.max(top, axis=1, keepdims=True)
            total = None
            for j, block in enumerate(blocks):
                terms = jnp.exp2((block - top) * SCORE2)
                total = terms if total is None else total + terms
                e_ref[step * PART + j, h : h + 2] = terms.astype(jnp.bfloat16).reshape(2, rows, terms.shape[1])
            total = jnp.sum(total, axis=1, keepdims=True)
            tops_ref[span] = jnp.where(lane2 == step, top, tops_ref[span])
            sums[span] = jnp.where(lane2 == step, total, sums[span])
        return carry

    lax.fori_loop(0, steps, body, 0)
    lane = lane_iota(rows)
    used = lane < steps
    packed = jnp.zeros((rows, LANES), jnp.float32)
    for h in range(heads):
        tops = tops_ref[h * rows : (h + 1) * rows]
        top = jnp.max(jnp.where(used, tops, -jnp.inf), axis=1, keepdims=True)
        scaled = sums[h * rows : (h + 1) * rows] * jnp.exp2(jnp.where(used, tops - top, 0.0) * SCORE2)
        total = jnp.sum(jnp.where(used, scaled, 0.0), axis=1, keepdims=True)
        packed = jnp.where(lane == h, top, packed)
        packed = jnp.where(lane == heads + h, total, packed)
    flat = packed.T[0 : 2 * heads]
    for z in range(send_ref.shape[0]):
        send_ref[z, 0 : 2 * heads] = flat
        send_ref[z, 2 * heads :] = lstats_ref[...]


def attention_scores(queries, cache, lstats, key_count):
    heads, width, rows = queries.shape
    blocks, _, keys = cache.shape
    return call(
        scores_kernel,
        "attention_scores",
        in_specs=[VMEM] * 3,
        out_specs=[VMEM] * 3,
        out_shape=(
            bf16(blocks, heads, rows, keys),
            f32(heads * rows, LANES),
            f32(key_count, 2 * heads + 8, rows),
        ),
        scratch_shapes=[
            pltpu.VMEM((rows * heads, width), jnp.bfloat16),
            pltpu.VMEM((rows * heads, LANES), jnp.float32),
        ],
    )(queries, cache, lstats)


def headsum_kernel(place_ref, e_ref, tops_ref, got_ref, *refs):
    outs, weights, tail, square = refs[0:RING], *refs[RING:]
    _, heads, rows, keys = e_ref.shape
    lane = lane_iota(rows)
    near, near_stride, far_stride = place_ref[0], place_ref[2], place_ref[3]

    tops = got_ref[:, 0:heads]
    top = jnp.max(tops, axis=0)
    total = jnp.sum(got_ref[:, heads : 2 * heads] * jnp.exp2((tops - top[None]) * SCORE2), axis=0)
    square[...] = jnp.zeros_like(square)
    square[0:heads] = top
    square[heads : 2 * heads] = (1.0 / MH) / total
    columns = square[...].T
    for h in range(heads):
        local = tops_ref[h * rows : (h + 1) * rows] - columns[:, h : h + 1]
        scale = columns[:, heads + h : heads + h + 1]
        weights[h] = jnp.exp2(jnp.minimum(local * SCORE2, 0.0)) * scale
    ltops = got_ref[:, 2 * heads : 2 * heads + 1]
    ltop = jnp.max(ltops, axis=0)
    lsum = jnp.sum(got_ref[:, 2 * heads + 1 : 2 * heads + 2] * jnp.exp(ltops - ltop[None]), axis=0)
    tail[...] = jnp.zeros_like(tail)
    tail[0:1, 0:rows] = ltop
    tail[1:2, 0:rows] = lsum

    for d in range(RING):

        def body(k, carry):
            block = lax.rem(near + d, RING) * near_stride + k * far_stride
            step = block // PART
            total = None
            for h in range(heads):
                column = jnp.sum(jnp.where(lane == step, weights[h], 0.0), axis=1, keepdims=True)
                term = e_ref[block, h].astype(jnp.float32) * column
                total = term if total is None else total + term
            outs[d][k, 0:rows] = total
            outs[d][k, rows:] = tail[...]
            return carry

        lax.fori_loop(0, RING, body, 0)


def head_sum(place, terms, tops, got):
    blocks, heads, rows, keys = terms.shape
    return call(
        headsum_kernel,
        "head_sum",
        in_specs=[SMEM] + [VMEM] * 3,
        out_specs=[VMEM] * RING,
        out_shape=[f32(blocks // RING, rows + 8, keys)] * RING,
        scratch_shapes=[
            pltpu.VMEM((heads, rows, LANES), jnp.float32),
            pltpu.VMEM((8, keys), jnp.float32),
            pltpu.VMEM((LANES, rows), jnp.float32),
        ],
    )(place, terms, tops, got)


def merged_stats(tops, sums):
    top = tops[0]
    for other in tops[1:]:
        top = jnp.maximum(top, other)
    total = sums[0] * jnp.exp(tops[0] - top)
    for other, count in zip(tops[1:], sums[1:]):
        total = total + count * jnp.exp(other - top)
    return top, total


def partial_kernel(place_ref, *refs):
    got, outs = refs[0:RING], refs[RING:]
    rows = outs[0].shape[0] - 8
    top, total = merged_stats([r[0, rows : rows + 1] for r in got], [r[0, rows + 1 : rows + 2] for r in got])
    for d in range(RING):
        k = lax.rem(place_ref[1] + d, RING)
        outs[d][0:rows] = got[0][k, 0:rows] + got[1][k, 0:rows] + (got[2][k, 0:rows] + got[3][k, 0:rows])
        outs[d][rows:] = jnp.zeros_like(outs[d][rows:])
        outs[d][rows : rows + 1] = top
        outs[d][rows + 1 : rows + 2] = total


def partial_sum(place, got):
    _, height, keys = got[0].shape
    return call(
        partial_kernel,
        "partial_sum",
        in_specs=[SMEM] + [VMEM] * RING,
        out_specs=[VMEM] * RING,
        out_shape=[f32(height, keys)] * RING,
    )(place, *got)


def keys_kernel(key_total, *refs):
    got = refs[0:RING]
    logits_ref, qh_ref, k_ref, w_ref, send_ref, keys_ref, slopes, turned = refs[RING:]
    heads, rows, depth = qh_ref.shape
    keys = k_ref.shape[0]
    group = 8
    root = 1.0 / math.sqrt(depth)

    ltop, lsum = merged_stats(
        [r[rows : rows + 1, 0:rows] for r in got], [r[rows + 1 : rows + 2, 0:rows] for r in got]
    )
    target = got[0][0:rows] + got[1][0:rows] + (got[2][0:rows] + got[3][0:rows])
    soft = jnp.exp(logits_ref[...] - ltop) * (1.0 / lsum)
    for k in range(0, keys, rows):
        turned[k : k + rows] = key_total * (soft[k : k + rows] - target[:, k : k + rows].T)
        send_ref[0:rows, k : k + rows] = turned[k : k + rows].T
    keys_ref[...] = jnp.zeros_like(keys_ref)

    def step(i, first, column):
        weights = w_ref[pl.ds(i * group, group)] * root
        sums = []
        for j in range(group):
            products = dot(k_ref[...], qh_ref[i * group + j], NT)
            dlogits = turned[...]
            sums.append(jnp.sum(jnp.maximum(products, 0.0) * dlogits, axis=0, keepdims=True) * root)
            slope = jnp.where(products > 0.0, dlogits * weights[j : j + 1], 0.0)
            slopes[:, j * rows : (j + 1) * rows] = slope.astype(jnp.bfloat16)
        place = pl.ds(pl.multiple_of(rows + first, group), group)
        send_ref[place, column : column + rows] = jnp.concatenate(sums, axis=0)
        chunk = qh_ref[pl.ds(i * group, group)].reshape(group * rows, depth)
        keys_ref[...] += dot(slopes[...], chunk, NN)

    half = heads // 2 // group

    def low(i, carry):
        step(i, i * group, 0)
        return carry

    def high(i, carry):
        step(i + half, i * group, rows)
        return carry

    lax.fori_loop(0, half, low, 0)
    lax.fori_loop(0, half, high, 0)


def key_gradient(got, logits, qh, index_keys, weights, key_total):
    heads, rows, depth = qh.shape
    keys = index_keys.shape[0]
    return call(
        lambda *refs: keys_kernel(key_total, *refs),
        "key_gradient",
        24,
        out_shape=(f32(rows + heads // 2, keys), f32(keys, depth)),
        scratch_shapes=[
            pltpu.VMEM((keys, 8 * rows), jnp.bfloat16),
            pltpu.VMEM((keys, rows), jnp.float32),
        ],
    )(*got, logits, qh, index_keys, weights)


def query_kernel(place_ref, *refs):
    ring = RING
    got, kept = refs[0:ring], refs[ring : 2 * ring]
    qh_ref, w_ref = refs[2 * ring : 2 * ring + 2]
    outs = refs[2 * ring + 2 : 3 * ring + 2]
    slopes, acc, near, dlogits = refs[3 * ring + 2 :]
    heads, rows, depth = qh_ref.shape
    keys = kept[0].shape[0]
    pieces, tall, _ = outs[0].shape
    extra = got[0].shape[0] - rows
    share = (tall - 2 * extra // pieces) * pieces // rows
    root = 1.0 / math.sqrt(depth)
    near_at, far_at, near_stride, far_stride = [place_ref[i] for i in range(4)]
    span = rows // pieces
    few = extra // pieces

    wsum = got[0][rows:]
    for d in range(1, ring):
        wsum = wsum + got[d][rows:]
    for d in range(ring):
        near[d * keys : (d + 1) * keys] = kept[d][...].astype(jnp.bfloat16)
        dlogits[:, d * keys : (d + 1) * keys] = got[d][0:rows] * root
    columns = jnp.concatenate([w_ref[...], jnp.zeros((LANES - heads, rows), jnp.float32)], axis=0).T

    for d in range(ring):
        first = (lax.rem(far_at + d, ring) * far_stride + near_at * near_stride) * share
        weights = pltpu.roll(columns, LANES - first, 1)
        queries = qh_ref[pl.ds(first, share)].reshape(share * rows, depth)
        for k in range(0, ring * keys, keys):
            products = dot(queries, near[k : k + keys], NT)
            for j in range(share):
                part = products[j * rows : (j + 1) * rows]
                slope = jnp.where(part > 0.0, dlogits[:, k : k + keys] * weights[:, j : j + 1], 0.0)
                slopes[j * rows : (j + 1) * rows, k : k + keys] = slope.astype(jnp.bfloat16)
        acc[...] = dot(slopes[...], near[...], NN)
        for z in range(pieces):
            for j in range(share):
                start = j * rows + z * span
                outs[d][z, pl.ds(j, span, stride=share), :] = acc[start : start + span]
            piece = wsum[z * few : (z + 1) * few]
            outs[d][z, share * span : share * span + few] = piece[:, 0:rows]
            outs[d][z, share * span + few :] = piece[:, rows : 2 * rows]


def query_gradient(place, got, kept, qh, weights, pieces):
    height, keys = got[0].shape
    heads, rows, depth = qh.shape
    share = heads // (RING * RING)
    extra = height - rows
    tall = share * (rows // pieces) + 2 * (extra // pieces)
    vmem = pl.BlockSpec(memory_space=pltpu.VMEM)
    return call(
        query_kernel,
        "query_gradient",
        24,
        in_specs=[pl.BlockSpec(memory_space=pltpu.SMEM)] + [vmem] * (2 * RING + 2),
        out_specs=[vmem] * RING,
        out_shape=[jax.ShapeDtypeStruct((pieces, tall, depth), jnp.float32)] * RING,
        scratch_shapes=[
            pltpu.VMEM((share * rows, RING * keys), jnp.bfloat16),
            pltpu.VMEM((share * rows, depth), jnp.float32),
            pltpu.VMEM((RING * keys, depth), jnp.bfloat16),
            pltpu.VMEM((rows, RING * keys), jnp.float32),
        ],
    )(place, *got, *kept, qh, weights)


def exchange(x, axis):
    return lax.all_to_all(x, axis, split_axis=0, concat_axis=0, tiled=True)


def shift(x, d, across):
    pairs = []
    for a in range(RING):
        for b in range(RING):
            for row in range(2):
                if (row == 1) != across:
                    there = (a + d) % RING * RING + b
                else:
                    there = a * RING + (b + d) % RING
                pairs.append(((a * RING + b) * 2 + row, there * 2 + row))
    return lax.ppermute(x, ("head", "row"), pairs)


def shards(mla_query, mla_cache, index_query, index_keys, index_weight):
    key_count = lax.axis_size("key")
    head_count = lax.axis_size("head")
    rows = mla_query.shape[0]
    keys, depth = index_keys.shape
    heads = index_query.shape[1]
    share = heads // head_count
    head_index = lax.axis_index("head")
    row_index = lax.axis_index("row")
    x, y = head_index // RING, head_index % RING
    first = row_index == 0
    place = jnp.stack(
        [jnp.where(first, y, x), jnp.where(first, x, y), jnp.where(first, 1, RING), jnp.where(first, RING, 1)]
    ).astype(jnp.int32)

    weights = index_weight.T
    logits, lstats, qh = indexer_forward(index_query, index_keys, weights)
    queries = jnp.transpose(mla_query, (1, 2, 0))
    cache = jnp.swapaxes(mla_cache, 1, 2)
    terms, tops, send1 = attention_scores(queries, cache, lstats, key_count)
    got1 = exchange(send1, "key")
    send2 = head_sum(place, terms, tops, got1)
    got2 = [send2[0]] + [shift(send2[d], d, False) for d in (1, 3, 2)]
    wide_keys, got2[1] = lax.optimization_barrier((index_keys.astype(jnp.float32), got2[1]))
    kept = [wide_keys] + [shift(wide_keys, d, False) for d in range(1, RING)]
    send2 = partial_sum(place, got2)
    got2 = [send2[0]] + [shift(send2[d], d, True) for d in (1, 3, 2)]
    got2, kept = lax.optimization_barrier((got2, kept))
    key_total = float(keys * head_count * key_count)
    send3, keys_part = key_gradient(got2, logits, qh, index_keys, weights, key_total)
    got3 = [send3] + [shift(send3, d, False) for d in range(1, RING)]

    half = keys // 2
    away = lax.dynamic_slice_in_dim(keys_part, (1 - row_index) * half, half, 0)
    near = lax.dynamic_slice_in_dim(keys_part, row_index * half, half, 0)
    key_grad = near + lax.ppermute(away, "row", [(0, 1), (1, 0)])

    parts = query_gradient(place, got3, kept, qh, weights, key_count)
    send4 = parts[0]
    for d in range(1, RING):
        send4 = send4 + shift(parts[d], d, True)
    got4 = jnp.sum(exchange(send4, "key"), axis=0)
    got5 = exchange(jnp.broadcast_to(got4[None], (key_count, *got4.shape)), "key")
    span = share * (rows // key_count)
    query_grad = got5[:, 0:span].reshape(rows, share, depth)
    few = (got4.shape[0] - span) // 2
    low = got5[:, span : span + few].reshape(heads // 2, rows)
    high = got5[:, span + few :].reshape(heads // 2, rows)
    weight_grad = jnp.concatenate([low, high], axis=0).T
    return (query_grad, key_grad, weight_grad)


def solution(mesh):
    placed = (
        P("row", "head", None),
        P(None, "key", None),
        P("row", None, None),
        P(("head", "key"), None),
        P("row", None),
    )
    return jax.shard_map(
        shards,
        mesh=mesh,
        in_specs=placed,
        out_specs=(P("row", "head", None), P(("head", "key", "row"), None), P("row", None)),
        check_vma=False,
    )
```

time: 152 us -> 143 us (0.941)
  blocking collectives: 51.7 us -> 13.3 us
  waiting for transfers between devices: 27.1 us -> 45.4 us
  local copies, waits for them, and re-layouts: 2.14 us -> 13.6 us
  starting transfers between devices: 27.9 us -> 37.7 us
  Pallas kernels: 39 us -> 29.2 us
    all_to_all x2 -> x1, blocking collectives: 51.7 us -> 13.3 us  [exchange(): return lax.all_to_all(x, axis, split_axis=0, concat_axis=0, tiled=True)]
    unnamed x12 -> x18, local copies, waits for them, and re-layouts: 0.66 us -> 12.2 us
    ppermute x9 -> x15, waiting for transfers between devices: 18.4 us -> 29.7 us  [shift(): return lax.ppermute(x, ('head', 'row'), pairs)]
    ppermute x9 -> x15, starting transfers between devices: 14.4 us -> 24.2 us  [shift(): return lax.ppermute(x, ('head', 'row'), pairs)]
    pallas_call x5 -> x6, Pallas kernels: 39 us -> 29.2 us  [the longest x1 11.1 us: attention_scores(): call(scores_kernel, 'attention_scores', in_specs=[VMEM] * 3, out_specs=[V...]
    all_to_all x2, waiting for transfers between devices: 7.42 us -> 14.5 us  [exchange(): return lax.all_to_all(x, axis, split_axis=0, concat_axis=0, tiled=True)]
  transfers between devices with their start and end apart: 12 -> 18, of which waited for: 8 -> 12; matrix products, arithmetic and copies ran while one was open for 0% -> 1% of each run, Pallas kernels for 0% -> 0%
where the time goes in v3:
time: 143 us; the launch traced here: 141 us
  waiting for transfers between devices  45.4 us (32%)
  starting transfers between devices  37.7 us (26%)
  Pallas kernels  29.2 us (20%)
  local copies, waits for them, and re-layouts  13.6 us (10%)
  blocking collectives  13.3 us (9%)
  other arithmetic  1.43 us (1%)
    ppermute x15, waiting for transfers between devices, shift(): return lax.ppermute(x, ('head', 'row'), pairs)  29.7 us
    ppermute x15, starting transfers between devices, shift(): return lax.ppermute(x, ('head', 'row'), pairs)  24.2 us
    all_to_all x2, waiting for transfers between devices, exchange(): return lax.all_to_all(x, axis, split_axis=0, concat_axis=0, tiled=True)  14.5 us
    all_to_all x2, starting transfers between devices, exchange(): return lax.all_to_all(x, axis, split_axis=0, concat_axis=0, tiled=True)  13.3 us
    all_to_all x1, blocking collectives, exchange(): return lax.all_to_all(x, axis, split_axis=0, concat_axis=0, tiled=True)  13.3 us
    unnamed x18, local copies, waits for them, and re-layouts  12.2 us
    pallas_call x1, Pallas kernels, attention_scores(): call(scores_kernel, 'attention_scores', in_specs=[VMEM] * 3, out_specs=[V...  11.1 us
    pallas_call x1, Pallas kernels, indexer_forward(): call(forward_kernel, 'indexer_forward', out_shape=(f32(keys, rows), f32(8...  4.87 us
  transfers between devices with their start and end apart: 18, of which 12 were waited for; matrix products, arithmetic and copies ran while one was open for 1% of the time, Pallas kernels for 0%

profile of v3, /device:TPU:32, one launch (start us, length us, event | category | flops | bytes accessed | tf_op | source)
XLA Modules:
  0.0 141.4 jit_solution(11457944869983984499)
XLA Ops:
  0.6 1.6 %copy-done.3 = bf16[128,64,128]{2,1,0:T(8,128)(2,1)S(1)} copy-done((bf16[128,64,128]{2,1,0:T(8,128)(2,1)S(1)}, bf16[128,64,128]{2,1,0:T(8,128)(2,1)}, u32[]{:S(2)}) %copy-start.3) | copy-done | bytes 2097176
  2.2 0.8 copy-done.5
  3.1 0.8 copy-done.7
  3.8 4.9 %indexer_forward.1 = (f32[256,128]{1,0:T(8,128)S(1)}, f32[8,128]{1,0:T(8,128)S(1)}, bf16[64,128,128]{2,1,0:T(8,128)(2,1)S(1)}) custom-call(bf16[128,64,128]{2,1,0:T(8,128)(2,1)S(1)} %copy-done.3, bf16[256,128]{1,0:T(8,128)(2,1)S(1)} %copy-done.5, f32[64,128]{1,0:T(8,128)S(1)} %bitcast.14), custom_call_target="tpu_custom_call" | custom-call | tf_op jit(solution)/shard_map/indexer_forward/pallas_call | solution.py:83
  8.7 2.3 %copy-done.2 = bf16[16,256,576]{1,2,0:T(8,128)(2,1)S(1)} copy-done((bf16[16,256,576]{1,2,0:T(8,128)(2,1)S(1)}, bf16[16,256,576]{1,2,0:T(8,128)(2,1)}, u32[]{:S(2)}) %copy-start.2) | copy-done | bytes 4718616
  11.0 11.1 %attention_scores.1 = (bf16[16,8,128,256]{3,2,1,0:T(8,128)(2,1)S(1)}, f32[1024,128]{1,0:T(8,128)S(1)}, f32[8,24,128]{2,1,0:T(8,128)}) custom-call(bf16[8,576,128]{2,1,0:T(8,128)(2,1)S(1)} %bitcast.13, bf16[16,576,256]{2,1,0:T(8,128)(2,1)S(1)} %bitcast.12, f32[8,128]{1,0:T(8,128)S(1)} %get-tuple-element.33.lstats_ref), custom_call_target="tpu_custom_call" | custom-call | tf_op jit(solution)/shard_map/attention_scores/pallas_call | solution.py:142
  22.2 3.3 %copy-done = bf16[16,8,128,256]{3,2,1,0:T(8,128)(2,1)} copy-done((bf16[16,8,128,256]{3,2,1,0:T(8,128)(2,1)}, bf16[16,8,128,256]{3,2,1,0:T(8,128)(2,1)S(1)}, u32[]{:S(2)}) %copy-start) | copy-done | bytes 8388632
  25.5 8.6 %all-to-all-start = ((f32[8,24,128]{2,1,0:T(8,128)}), f32[8,24,128]{2,1,0:T(8,128)S(1)}, u32[]{:S(2)}, u32[]{:S(2)}) async-start(f32[8,24,128]{2,1,0:T(8,128)} %get-tuple-element.36), calls=%async_computation | async-start | bytes 196608 | tf_op jit(solution)/shard_map/all_to_all | solution.py:378
  34.0 0.1 pad_add_fusion.place_ref
  34.1 7.1 %all-to-all-done.got_ref = f32[8,24,128]{2,1,0:T(8,128)S(1)} async-done(((f32[8,24,128]{2,1,0:T(8,128)}), f32[8,24,128]{2,1,0:T(8,128)S(1)}, u32[]{:S(2)}, u32[]{:S(2)}) %all-to-all-start) | async-done | bytes 98336 | tf_op jit(solution)/shard_map/all_to_all | solution.py:378
  41.2 3.4 %copy-done.1 = bf16[16,8,128,256]{3,2,1,0:T(8,128)(2,1)S(1)} copy-done((bf16[16,8,128,256]{3,2,1,0:T(8,128)(2,1)S(1)}, bf16[16,8,128,256]{3,2,1,0:T(8,128)(2,1)}, u32[]{:S(2)}) %copy-start.1) | copy-done | bytes 8388632
  44.6 4.5 %head_sum.1 = (f32[4,136,256]{2,1,0:T(8,128)S(1)}, f32[4,136,256]{2,1,0:T(8,128)S(1)}, f32[4,136,256]{2,1,0:T(8,128)S(1)}, f32[4,136,256]{2,1,0:T(8,128)S(1)}) custom-call(s32[4]{0:T(128)S(1)} %pad_add_fusion.place_ref, bf16[16,8,128,256]{3,2,1,0:T(8,128)(2,1)S(1)} %copy-done.1, f32[1024,128]{1,0:T(8,128)S(1)} %get-tuple-element.35.tops_ref, ...), custom_call_target="tpu_custom_call" | custom-call | tf_op jit(solution)/shard_map/head_sum/pallas_call | solution.py:202
  49.1 1.7 %collective-permute-start = (f32[4,136,256]{2,1,0:T(8,128)S(1)}, f32[4,136,256]{2,1,0:T(8,128)S(1)}, u32[]{:S(2)}, u32[]{:S(2)}) collective-permute-start(f32[4,136,256]{2,1,0:T(8,128)S(1)} %get-tuple-element.38), channel_id=1, source_target_pairs={{0,16},{1,65},{16,32},{17,81},{32,48},{33,97},{48,0},{49,113},{64,... | collective-permute-start | bytes 1671176 | tf_op jit(solution)/shard_map/ppermute | solution.py:391
  50.8 1.7 %collective-permute-start.1 = (f32[4,136,256]{2,1,0:T(8,128)S(1)}, f32[4,136,256]{2,1,0:T(8,128)S(1)}, u32[]{:S(2)}, u32[]{:S(2)}) collective-permute-start(f32[4,136,256]{2,1,0:T(8,128)S(1)} %get-tuple-element.40), channel_id=1, source_target_pairs={{0,48},{1,193},{16,0},{17,209},{32,16},{33,225},{48,32},{49,241},{... | collective-permute-start | bytes 1671176 | tf_op jit(solution)/shard_map/ppermute | solution.py:391
  52.4 2.0 %collective-permute-start.2 = (f32[4,136,256]{2,1,0:T(8,128)S(1)}, f32[4,136,256]{2,1,0:T(8,128)S(1)}, u32[]{:S(2)}, u32[]{:S(2)}) collective-permute-start(f32[4,136,256]{2,1,0:T(8,128)S(1)} %get-tuple-element.41), channel_id=1, source_target_pairs={{0,32},{1,129},{16,48},{17,145},{32,0},{33,161},{48,16},{49,177},{... | collective-permute-start | bytes 1671176 | tf_op jit(solution)/shard_map/ppermute | solution.py:391
  54.4 5.5 %collective-permute-done.refs_1_ = f32[4,136,256]{2,1,0:T(8,128)S(1)} collective-permute-done((f32[4,136,256]{2,1,0:T(8,128)S(1)}, f32[4,136,256]{2,1,0:T(8,128)S(1)}, u32[]{:S(2)}, u32[]{:S(2)}) %collective-permute-start) | collective-permute-done | bytes 557088 | tf_op jit(solution)/shard_map/ppermute | solution.py:391
  59.9 0.4 collective-permute-start.6
  60.3 6.9 %collective-permute-done.2.refs_3_ = f32[4,136,256]{2,1,0:T(8,128)S(1)} collective-permute-done((f32[4,136,256]{2,1,0:T(8,128)S(1)}, f32[4,136,256]{2,1,0:T(8,128)S(1)}, u32[]{:S(2)}, u32[]{:S(2)}) %collective-permute-start.2) | collective-permute-done | bytes 557088 | tf_op jit(solution)/shard_map/ppermute | solution.py:391
  67.2 0.7 partial_sum.1
  67.9 1.6 %collective-permute-start.3 = (f32[136,256]{1,0:T(8,128)S(1)}, f32[136,256]{1,0:T(8,128)S(1)}, u32[]{:S(2)}, u32[]{:S(2)}) collective-permute-start(f32[136,256]{1,0:T(8,128)S(1)} %get-tuple-element.43), channel_id=1, source_target_pairs={{0,64},{1,17},{16,80},{17,33},{32,96},{33,49},{48,112},{49,1},{64,... | collective-permute-start | bytes 417800 | tf_op jit(solution)/shard_map/ppermute | solution.py:391
  69.5 1.7 %collective-permute-start.4 = (f32[136,256]{1,0:T(8,128)S(1)}, f32[136,256]{1,0:T(8,128)S(1)}, u32[]{:S(2)}, u32[]{:S(2)}) collective-permute-start(f32[136,256]{1,0:T(8,128)S(1)} %get-tuple-element.44), channel_id=1, source_target_pairs={{0,192},{1,49},{16,208},{17,1},{32,224},{33,17},{48,240},{49,33},{... | collective-permute-start | bytes 417800 | tf_op jit(solution)/shard_map/ppermute | solution.py:391
  71.2 1.8 %collective-permute-start.5 = (f32[136,256]{1,0:T(8,128)S(1)}, f32[136,256]{1,0:T(8,128)S(1)}, u32[]{:S(2)}, u32[]{:S(2)}) collective-permute-start(f32[136,256]{1,0:T(8,128)S(1)} %get-tuple-element.45), channel_id=1, source_target_pairs={{0,128},{1,33},{16,144},{17,49},{32,160},{33,1},{48,176},{49,17},{... | collective-permute-start | bytes 417800 | tf_op jit(solution)/shard_map/ppermute | solution.py:391
  73.0 0.7 collective-permute-start.7
  73.7 3.3 %collective-permute-start.8 = (f32[256,128]{1,0:T(8,128)S(1)}, f32[256,128]{1,0:T(8,128)S(1)}, u32[]{:S(2)}, u32[]{:S(2)}) collective-permute-start(f32[256,128]{1,0:T(8,128)S(1)} %convert_element_type.3.refs_4_), channel_id=1, source_target_pairs={{0,48},{1,193},{16,0},{17,209},{32,16},{33,225},{48,32},{49,241},{... | collective-permute-start | bytes 393224 | tf_op jit(solution)/shard_map/ppermute | solution.py:391
  77.0 2.5 %collective-permute-done.7.refs_6_ = f32[256,128]{1,0:T(8,128)S(1)} collective-permute-done((f32[256,128]{1,0:T(8,128)S(1)}, f32[256,128]{1,0:T(8,128)S(1)}, u32[]{:S(2)}, u32[]{:S(2)}) %collective-permute-start.7) | collective-permute-done | bytes 131104 | tf_op jit(solution)/shard_map/ppermute | solution.py:391
  79.5 0.6 collective-permute-done.8.refs_7_
  80.2 4.8 %key_gradient.1 = (f32[160,256]{1,0:T(8,128)S(1)}, f32[256,128]{1,0:T(8,128)S(1)}) custom-call(f32[136,256]{1,0:T(8,128)S(1)} %get-tuple-element.47.refs_0_, f32[136,256]{1,0:T(8,128)S(1)} %collective-permute-done.3.refs_1_, f32[136,256]{1,0:T(8,128)S(1)} %collective-permute-done.4.refs_2_, f32[136,256]{1,0:T(8,128)S(1)} %collective-permute-done.5.refs_3_, ...), custom_call_target="tpu_custom_call" | custom-call | tf_op jit(solution)/shard_map/key_gradient/pallas_call | solution.py:298
  85.0 3.0 %collective-permute-start.10 = (f32[160,256]{1,0:T(8,128)S(1)}, f32[160,256]{1,0:T(8,128)S(1)}, u32[]{:S(2)}, u32[]{:S(2)}) collective-permute-start(f32[160,256]{1,0:T(8,128)S(1)} %get-tuple-element.53.refs_0_), channel_id=1, source_target_pairs={{0,32},{1,129},{16,48},{17,145},{32,0},{33,161},{48,16},{49,177},{... | collective-permute-start | bytes 491528 | tf_op jit(solution)/shard_map/ppermute | solution.py:391
  88.0 2.0 %collective-permute-start.11 = (f32[160,256]{1,0:T(8,128)S(1)}, f32[160,256]{1,0:T(8,128)S(1)}, u32[]{:S(2)}, u32[]{:S(2)}) collective-permute-start(f32[160,256]{1,0:T(8,128)S(1)} %get-tuple-element.53.refs_0_), channel_id=1, source_target_pairs={{0,48},{1,193},{16,0},{17,209},{32,16},{33,225},{48,32},{49,241},{... | collective-permute-start | bytes 491528 | tf_op jit(solution)/shard_map/ppermute | solution.py:391
  90.0 0.1 collective-permute-start.9
  90.1 2.0 %collective-permute-done.10.refs_2_ = f32[160,256]{1,0:T(8,128)S(1)} collective-permute-done((f32[160,256]{1,0:T(8,128)S(1)}, f32[160,256]{1,0:T(8,128)S(1)}, u32[]{:S(2)}, u32[]{:S(2)}) %collective-permute-start.10) | collective-permute-done | bytes 163872 | tf_op jit(solution)/shard_map/ppermute | solution.py:391
  92.1 2.1 %collective-permute-done.11.refs_3_ = f32[160,256]{1,0:T(8,128)S(1)} collective-permute-done((f32[160,256]{1,0:T(8,128)S(1)}, f32[160,256]{1,0:T(8,128)S(1)}, u32[]{:S(2)}, u32[]{:S(2)}) %collective-permute-start.11) | collective-permute-done | bytes 163872 | tf_op jit(solution)/shard_map/ppermute | solution.py:391
  94.2 2.3 %collective-permute-done.9.refs_1_ = f32[160,256]{1,0:T(8,128)S(1)} collective-permute-done((f32[160,256]{1,0:T(8,128)S(1)}, f32[160,256]{1,0:T(8,128)S(1)}, u32[]{:S(2)}, u32[]{:S(2)}) %collective-permute-start.9) | collective-permute-done | bytes 163872 | tf_op jit(solution)/shard_map/ppermute | solution.py:391
  96.5 3.1 %query_gradient.1 = (f32[8,72,128]{2,1,0:T(8,128)S(1)}, f32[8,72,128]{2,1,0:T(8,128)S(1)}, f32[8,72,128]{2,1,0:T(8,128)S(1)}, f32[8,72,128]{2,1,0:T(8,128)S(1)}) custom-call(s32[4]{0:T(128)S(1)} %pad_add_fusion.place_ref, f32[160,256]{1,0:T(8,128)S(1)} %get-tuple-element.53.refs_0_, f32[160,256]{1,0:T(8,128)S(1)} %collective-permute-done.9.refs_1_, ...), custom_call_target="tpu_custom_call" | custom-call | tf_op jit(solution)/shard_map/query_gradient/pallas_call | solution.py:361
  99.6 0.7 collective-permute-start.12
  100.3 2.0 %collective-permute-start.13 = (f32[8,72,128]{2,1,0:T(8,128)S(1)}, f32[8,72,128]{2,1,0:T(8,128)S(1)}, u32[]{:S(2)}, u32[]{:S(2)}) collective-permute-start(f32[8,72,128]{2,1,0:T(8,128)S(1)} %get-tuple-element.60), channel_id=1, source_target_pairs={{0,128},{1,33},{16,144},{17,49},{32,160},{33,1},{48,176},{49,17},{... | collective-permute-start | bytes 884744 | tf_op jit(solution)/shard_map/ppermute | solution.py:391
  102.3 1.7 %collective-permute-start.14 = (f32[8,72,128]{2,1,0:T(8,128)S(1)}, f32[8,72,128]{2,1,0:T(8,128)S(1)}, u32[]{:S(2)}, u32[]{:S(2)}) collective-permute-start(f32[8,72,128]{2,1,0:T(8,128)S(1)} %get-tuple-element.61), channel_id=1, source_target_pairs={{0,192},{1,49},{16,208},{17,1},{32,224},{33,17},{48,240},{49,33},{... | collective-permute-start | bytes 884744 | tf_op jit(solution)/shard_map/ppermute | solution.py:391
  104.0 6.7 %collective-permute-done.12 = f32[8,72,128]{2,1,0:T(8,128)S(1)} collective-permute-done((f32[8,72,128]{2,1,0:T(8,128)S(1)}, f32[8,72,128]{2,1,0:T(8,128)S(1)}, u32[]{:S(2)}, u32[]{:S(2)}) %collective-permute-start.12) | collective-permute-done | bytes 294944 | tf_op jit(solution)/shard_map/ppermute | solution.py:391
  110.8 0.9 collective-permute-done.14
  111.8 13.3 %all_to_all.15 = f32[8,72,128]{2,1,0:T(8,128)S(1)} all-to-all(f32[8,72,128]{2,1,0:T(8,128)S(1)} %add_add_fusion), channel_id=1, replica_groups=mesh['head'=16,'key'=8,'row'=2] {'key'}, dimensions={0} | all-to-all | bytes 589824 | tf_op jit(solution)/shard_map/all_to_all | solution.py:378
  125.1 0.7 broadcast_in_dim.2
  125.8 4.8 %all-to-all-start.2 = ((f32[8,72,128]{2,1,0:T(8,128)}), f32[8,72,128]{2,1,0:T(8,128)S(1)}, u32[]{:S(2)}, u32[]{:S(2)}) async-start(f32[8,72,128]{2,1,0:T(8,128)} %broadcast_in_dim.2), calls=%async_computation.2 | async-start | bytes 589824 | tf_op jit(solution)/shard_map/all_to_all | solution.py:378
  130.6 0.1 collective-permute-start.15
  130.7 1.2 collective-permute-done.15
  132.0 0.6 dynamic-slice_add_fusion
  132.6 7.4 %all-to-all-done.2 = f32[8,72,128]{2,1,0:T(8,128)S(1)} async-done(((f32[8,72,128]{2,1,0:T(8,128)}), f32[8,72,128]{2,1,0:T(8,128)S(1)}, u32[]{:S(2)}, u32[]{:S(2)}) %all-to-all-start.2) | async-done | bytes 294944 | tf_op jit(solution)/shard_map/all_to_all | solution.py:378
  140.0 0.6 maximum_bitcast_fusion
  140.7 0.7 slice.12
  (23 shorter events, 0.1 us)
Async XLA Ops:
  0.6 1.6 %copy-start.3 = (bf16[128,64,128]{2,1,0:T(8,128)(2,1)S(1)}, bf16[128,64,128]{2,1,0:T(8,128)(2,1)}, u32[]{:S(2)}) copy-start(bf16[128,64,128]{2,1,0:T(8,128)(2,1)} %q_ref.1) | copy-start | bytes 6291460
  2.2 0.8 copy-start.5
  3.1 0.8 copy-start.7
  3.8 4.9 %copy-start.4 = (bf16[128,8,576]{0,2,1:T(8,128)(2,1)S(1)}, bf16[128,8,576]{0,2,1:T(8,128)(2,1)}, u32[]{:S(2)}) copy-start(bf16[128,8,576]{0,2,1:T(8,128)(2,1)} %param.5) | copy-start | bytes 3538948
  8.7 2.3 %copy-start.2 = (bf16[16,256,576]{1,2,0:T(8,128)(2,1)S(1)}, bf16[16,256,576]{1,2,0:T(8,128)(2,1)}, u32[]{:S(2)}) copy-start(bf16[16,256,576]{1,2,0:T(8,128)(2,1)} %param.6) | copy-start | bytes 14155780
  22.2 3.3 %copy-start = (bf16[16,8,128,256]{3,2,1,0:T(8,128)(2,1)}, bf16[16,8,128,256]{3,2,1,0:T(8,128)(2,1)S(1)}, u32[]{:S(2)}) copy-start(bf16[16,8,128,256]{3,2,1,0:T(8,128)(2,1)S(1)} %get-tuple-element.34.e_ref) | copy-start | bytes 25165828
  25.5 15.7 %all-to-all-start = ((f32[8,24,128]{2,1,0:T(8,128)}), f32[8,24,128]{2,1,0:T(8,128)S(1)}, u32[]{:S(2)}, u32[]{:S(2)}) async-start(f32[8,24,128]{2,1,0:T(8,128)} %get-tuple-element.36), calls=%async_computation | async-start | bytes 196608 | tf_op jit(solution)/shard_map/all_to_all | solution.py:378
  41.2 3.4 %copy-start.1 = (bf16[16,8,128,256]{3,2,1,0:T(8,128)(2,1)S(1)}, bf16[16,8,128,256]{3,2,1,0:T(8,128)(2,1)}, u32[]{:S(2)}) copy-start(bf16[16,8,128,256]{3,2,1,0:T(8,128)(2,1)} %copy-done) | copy-start | bytes 25165828
  44.6 9.9 %copy-start.6 = (bf16[256,128]{1,0:T(8,128)(2,1)S(1)}, bf16[256,128]{1,0:T(8,128)(2,1)}, u32[]{:S(2)}) copy-start(bf16[256,128]{1,0:T(8,128)(2,1)} %refs_6_.1) | copy-start | bytes 196612
  49.1 31.0 %copy-start.8 = (f32[128,64]{0,1:T(8,128)S(1)}, f32[128,64]{0,1:T(8,128)}, u32[]{:S(2)}) copy-start(f32[128,64]{0,1:T(8,128)} %param.9) | copy-start | bytes 98308
  49.1 10.8 %collective-permute-start = (f32[4,136,256]{2,1,0:T(8,128)S(1)}, f32[4,136,256]{2,1,0:T(8,128)S(1)}, u32[]{:S(2)}, u32[]{:S(2)}) collective-permute-start(f32[4,136,256]{2,1,0:T(8,128)S(1)} %get-tuple-element.38), channel_id=1, source_target_pairs={{0,16},{1,65},{16,32},{17,81},{32,48},{33,97},{48,0},{49,113},{64,... | collective-permute-start | bytes 1671176 | tf_op jit(solution)/shard_map/ppermute | solution.py:391
  50.8 9.5 %collective-permute-start.1 = (f32[4,136,256]{2,1,0:T(8,128)S(1)}, f32[4,136,256]{2,1,0:T(8,128)S(1)}, u32[]{:S(2)}, u32[]{:S(2)}) collective-permute-start(f32[4,136,256]{2,1,0:T(8,128)S(1)} %get-tuple-element.40), channel_id=1, source_target_pairs={{0,48},{1,193},{16,0},{17,209},{32,16},{33,225},{48,32},{49,241},{... | collective-permute-start | bytes 1671176 | tf_op jit(solution)/shard_map/ppermute | solution.py:391
  52.4 14.8 %collective-permute-start.2 = (f32[4,136,256]{2,1,0:T(8,128)S(1)}, f32[4,136,256]{2,1,0:T(8,128)S(1)}, u32[]{:S(2)}, u32[]{:S(2)}) collective-permute-start(f32[4,136,256]{2,1,0:T(8,128)S(1)} %get-tuple-element.41), channel_id=1, source_target_pairs={{0,32},{1,129},{16,48},{17,145},{32,0},{33,161},{48,16},{49,177},{... | collective-permute-start | bytes 1671176 | tf_op jit(solution)/shard_map/ppermute | solution.py:391
  59.9 13.8 %collective-permute-start.6 = (f32[256,128]{1,0:T(8,128)S(1)}, f32[256,128]{1,0:T(8,128)S(1)}, u32[]{:S(2)}, u32[]{:S(2)}) collective-permute-start(f32[256,128]{1,0:T(8,128)S(1)} %convert_element_type.3.refs_4_), channel_id=1, source_target_pairs={{0,16},{1,65},{16,32},{17,81},{32,48},{33,97},{48,0},{49,113},{64,... | collective-permute-start | bytes 393224 | tf_op jit(solution)/shard_map/ppermute | solution.py:391
  67.9 12.2 %collective-permute-start.3 = (f32[136,256]{1,0:T(8,128)S(1)}, f32[136,256]{1,0:T(8,128)S(1)}, u32[]{:S(2)}, u32[]{:S(2)}) collective-permute-start(f32[136,256]{1,0:T(8,128)S(1)} %get-tuple-element.43), channel_id=1, source_target_pairs={{0,64},{1,17},{16,80},{17,33},{32,96},{33,49},{48,112},{49,1},{64,... | collective-permute-start | bytes 417800 | tf_op jit(solution)/shard_map/ppermute | solution.py:391
  69.5 10.7 %collective-permute-start.4 = (f32[136,256]{1,0:T(8,128)S(1)}, f32[136,256]{1,0:T(8,128)S(1)}, u32[]{:S(2)}, u32[]{:S(2)}) collective-permute-start(f32[136,256]{1,0:T(8,128)S(1)} %get-tuple-element.44), channel_id=1, source_target_pairs={{0,192},{1,49},{16,208},{17,1},{32,224},{33,17},{48,240},{49,33},{... | collective-permute-start | bytes 417800 | tf_op jit(solution)/shard_map/ppermute | solution.py:391
  71.2 8.9 %collective-permute-start.5 = (f32[136,256]{1,0:T(8,128)S(1)}, f32[136,256]{1,0:T(8,128)S(1)}, u32[]{:S(2)}, u32[]{:S(2)}) collective-permute-start(f32[136,256]{1,0:T(8,128)S(1)} %get-tuple-element.45), channel_id=1, source_target_pairs={{0,128},{1,33},{16,144},{17,49},{32,160},{33,1},{48,176},{49,17},{... | collective-permute-start | bytes 417800 | tf_op jit(solution)/shard_map/ppermute | solution.py:391
  73.0 6.5 %collective-permute-start.7 = (f32[256,128]{1,0:T(8,128)S(1)}, f32[256,128]{1,0:T(8,128)S(1)}, u32[]{:S(2)}, u32[]{:S(2)}) collective-permute-start(f32[256,128]{1,0:T(8,128)S(1)} %convert_element_type.3.refs_4_), channel_id=1, source_target_pairs={{0,32},{1,129},{16,48},{17,145},{32,0},{33,161},{48,16},{49,177},{... | collective-permute-start | bytes 393224 | tf_op jit(solution)/shard_map/ppermute | solution.py:391
  73.7 6.4 %collective-permute-start.8 = (f32[256,128]{1,0:T(8,128)S(1)}, f32[256,128]{1,0:T(8,128)S(1)}, u32[]{:S(2)}, u32[]{:S(2)}) collective-permute-start(f32[256,128]{1,0:T(8,128)S(1)} %convert_element_type.3.refs_4_), channel_id=1, source_target_pairs={{0,48},{1,193},{16,0},{17,209},{32,16},{33,225},{48,32},{49,241},{... | collective-permute-start | bytes 393224 | tf_op jit(solution)/shard_map/ppermute | solution.py:391
  85.0 7.1 %collective-permute-start.10 = (f32[160,256]{1,0:T(8,128)S(1)}, f32[160,256]{1,0:T(8,128)S(1)}, u32[]{:S(2)}, u32[]{:S(2)}) collective-permute-start(f32[160,256]{1,0:T(8,128)S(1)} %get-tuple-element.53.refs_0_), channel_id=1, source_target_pairs={{0,32},{1,129},{16,48},{17,145},{32,0},{33,161},{48,16},{49,177},{... | collective-permute-start | bytes 491528 | tf_op jit(solution)/shard_map/ppermute | solution.py:391
  88.0 6.2 %collective-permute-start.11 = (f32[160,256]{1,0:T(8,128)S(1)}, f32[160,256]{1,0:T(8,128)S(1)}, u32[]{:S(2)}, u32[]{:S(2)}) collective-permute-start(f32[160,256]{1,0:T(8,128)S(1)} %get-tuple-element.53.refs_0_), channel_id=1, source_target_pairs={{0,48},{1,193},{16,0},{17,209},{32,16},{33,225},{48,32},{49,241},{... | collective-permute-start | bytes 491528 | tf_op jit(solution)/shard_map/ppermute | solution.py:391
  90.0 6.5 %collective-permute-start.9 = (f32[160,256]{1,0:T(8,128)S(1)}, f32[160,256]{1,0:T(8,128)S(1)}, u32[]{:S(2)}, u32[]{:S(2)}) collective-permute-start(f32[160,256]{1,0:T(8,128)S(1)} %get-tuple-element.53.refs_0_), channel_id=1, source_target_pairs={{0,16},{1,65},{16,32},{17,81},{32,48},{33,97},{48,0},{49,113},{64,... | collective-permute-start | bytes 491528 | tf_op jit(solution)/shard_map/ppermute | solution.py:391
  99.6 11.2 %collective-permute-start.12 = (f32[8,72,128]{2,1,0:T(8,128)S(1)}, f32[8,72,128]{2,1,0:T(8,128)S(1)}, u32[]{:S(2)}, u32[]{:S(2)}) collective-permute-start(f32[8,72,128]{2,1,0:T(8,128)S(1)} %get-tuple-element.59), channel_id=1, source_target_pairs={{0,64},{1,17},{16,80},{17,33},{32,96},{33,49},{48,112},{49,1},{64,... | collective-permute-start | bytes 884744 | tf_op jit(solution)/shard_map/ppermute | solution.py:391
  100.3 10.5 %collective-permute-start.13 = (f32[8,72,128]{2,1,0:T(8,128)S(1)}, f32[8,72,128]{2,1,0:T(8,128)S(1)}, u32[]{:S(2)}, u32[]{:S(2)}) collective-permute-start(f32[8,72,128]{2,1,0:T(8,128)S(1)} %get-tuple-element.60), channel_id=1, source_target_pairs={{0,128},{1,33},{16,144},{17,49},{32,160},{33,1},{48,176},{49,17},{... | collective-permute-start | bytes 884744 | tf_op jit(solution)/shard_map/ppermute | solution.py:391
  102.3 9.4 %collective-permute-start.14 = (f32[8,72,128]{2,1,0:T(8,128)S(1)}, f32[8,72,128]{2,1,0:T(8,128)S(1)}, u32[]{:S(2)}, u32[]{:S(2)}) collective-permute-start(f32[8,72,128]{2,1,0:T(8,128)S(1)} %get-tuple-element.61), channel_id=1, source_target_pairs={{0,192},{1,49},{16,208},{17,1},{32,224},{33,17},{48,240},{49,33},{... | collective-permute-start | bytes 884744 | tf_op jit(solution)/shard_map/ppermute | solution.py:391
  125.8 14.2 %all-to-all-start.2 = ((f32[8,72,128]{2,1,0:T(8,128)}), f32[8,72,128]{2,1,0:T(8,128)S(1)}, u32[]{:S(2)}, u32[]{:S(2)}) async-start(f32[8,72,128]{2,1,0:T(8,128)} %broadcast_in_dim.2), calls=%async_computation.2 | async-start | bytes 589824 | tf_op jit(solution)/shard_map/all_to_all | solution.py:378
  130.6 1.3 collective-permute-start.15

commit v4 on v3

v4 whole, which is shorter than its diff:
```python
import functools
import math

import jax
import jax.numpy as jnp
from jax import lax
from jax.experimental import pallas as pl
from jax.experimental.pallas import tpu as pltpu
from jax.sharding import PartitionSpec as P

MH = 128
LOG2E = 1.4426950408889634
SCORE2 = LOG2E / math.sqrt(192.0)
LANES = 128
NT = (((1,), (1,)), ((), ()))
TN = (((0,), (0,)), ((), ()))
NN = (((1,), (0,)), ((), ()))


def dot(a, b, dims):
    return lax.dot_general(a, b, dims, preferred_element_type=jnp.float32)


def lane_iota(rows):
    return lax.broadcasted_iota(jnp.int32, (rows, LANES), 1)


RING = 4
PART = 2
VMEM = pl.BlockSpec(memory_space=pltpu.VMEM)
SMEM = pl.BlockSpec(memory_space=pltpu.SMEM)
HBM = pl.BlockSpec(memory_space=pltpu.HBM)


def call(kernel, name, megabytes=32, **options):
    return pl.pallas_call(
        kernel, name=name, compiler_params=pltpu.CompilerParams(vmem_limit_bytes=megabytes << 20), **options
    )


def f32(*shape):
    return jax.ShapeDtypeStruct(shape, jnp.float32)


def bf16(*shape):
    return jax.ShapeDtypeStruct(shape, jnp.bfloat16)


def scores_kernel(
    q_hbm, c_hbm, iq_hbm, k_hbm, w_hbm,
    e_hbm, tops_ref, send_ref, logits_ref, qh_ref,
    e_ref, q_ref, c_ref, iq_ref, k_ref, w_ref, wide, total_ref, queries_ref, sums, sems, out_sems,
):
    heads, width, rows = q_ref.shape
    blocks = c_ref.shape[0]
    steps = blocks // PART
    _, iheads, depth = iq_ref.shape
    keys = k_ref.shape[0]
    group = iheads // steps

    first = pltpu.make_async_copy(q_hbm, q_ref, sems.at[steps])
    first.start()

    def part_copy(step):
        span = pl.ds(step * PART, PART)
        return pltpu.make_async_copy(c_hbm.at[span], c_ref.at[span], sems.at[step])

    def terms_copy(step):
        span = pl.ds(step * PART, PART)
        return pltpu.make_async_copy(e_ref.at[span], e_hbm.at[span], out_sems.at[step])

    for step in range(2):
        part_copy(step).start()
    others = [(iq_hbm, iq_ref), (k_hbm, k_ref), (w_hbm, w_ref)]
    others = [pltpu.make_async_copy(src, dst, sems.at[steps + 1 + i]) for i, (src, dst) in enumerate(others)]
    for copy in others:
        copy.start()
    for step in range(2, steps):
        part_copy(step).start()

    tops_ref[...] = jnp.zeros_like(tops_ref)
    sums[...] = jnp.zeros_like(sums)
    total_ref[...] = jnp.zeros_like(total_ref)
    first.wait()
    for h in range(heads):
        queries_ref[h * rows : (h + 1) * rows] = q_ref[h].T
    for copy in others:
        copy.wait()
    wide[...] = iq_ref[...].astype(jnp.float32).reshape(rows * iheads, depth)
    columns = jnp.concatenate([w_ref[...], jnp.zeros((LANES - iheads, rows), jnp.float32)], axis=0).T
    lane2 = lane_iota(2 * rows)

    def body(step, carry):
        part_copy(step).wait()
        weights = pltpu.roll(columns, LANES - group * step, 1)
        for j in range(group):
            head = step * group + j
            qh_ref[head] = wide[pl.ds(head, rows, stride=iheads), :].astype(jnp.bfloat16)
        chunk = qh_ref[pl.ds(step * group, group)].reshape(group * rows, depth)
        products = dot(chunk, k_ref[...], NT)
        total = total_ref[...]
        for j in range(group):
            part = products[j * rows : (j + 1) * rows]
            total = total + jnp.maximum(part, 0.0) * weights[:, j : j + 1]
        total_ref[...] = total

        for h in range(0, heads, 2):
            span = slice(h * rows, (h + 2) * rows)
            queries = queries_ref[span]
            scores = [dot(queries, c_ref[step * PART + j], NN) for j in range(PART)]
            top = scores[0]
            for score in scores[1:]:
                top = jnp.maximum(top, score)
            top = jnp.max(top, axis=1, keepdims=True)
            total = None
            for j, score in enumerate(scores):
                terms = jnp.exp2((score - top) * SCORE2)
                total = terms if total is None else total + terms
                e_ref[step * PART + j, h : h + 2] = terms.astype(jnp.bfloat16).reshape(2, rows, keys)
            total = jnp.sum(total, axis=1, keepdims=True)
            tops_ref[span] = jnp.where(lane2 == step, top, tops_ref[span])
            sums[span] = jnp.where(lane2 == step, total, sums[span])
        terms_copy(step).start()
        return carry

    lax.fori_loop(0, steps, body, 0)
    lane = lane_iota(rows)
    used = lane < steps
    packed = jnp.zeros((rows, LANES), jnp.float32)
    for h in range(heads):
        tops = tops_ref[h * rows : (h + 1) * rows]
        top = jnp.max(jnp.where(used, tops, -jnp.inf), axis=1, keepdims=True)
        scaled = sums[h * rows : (h + 1) * rows] * jnp.exp2(jnp.where(used, tops - top, 0.0) * SCORE2)
        total = jnp.sum(jnp.where(used, scaled, 0.0), axis=1, keepdims=True)
        packed = jnp.where(lane == h, top, packed)
        packed = jnp.where(lane == heads + h, total, packed)
    flat = packed.T[0 : 2 * heads]
    for k in range(0, keys, rows):
        logits_ref[k : k + rows] = total_ref[:, k : k + rows].T * (1.0 / math.sqrt(depth))
    logits = logits_ref[...]
    ltop = jnp.max(logits, axis=0, keepdims=True)
    lsum = jnp.sum(jnp.exp(logits - ltop), axis=0, keepdims=True)
    for z in range(send_ref.shape[0]):
        send_ref[z, 0 : 2 * heads] = flat
        send_ref[z, 2 * heads :] = jnp.zeros((8, rows), jnp.float32)
        send_ref[z, 2 * heads : 2 * heads + 1] = ltop
        send_ref[z, 2 * heads + 1 : 2 * heads + 2] = lsum
    for step in range(steps):
        terms_copy(step).wait()


def scores_and_logits(queries, cache, index_query, index_keys, weights, key_count):
    heads, width, rows = queries.shape
    blocks, _, keys = cache.shape
    _, iheads, depth = index_query.shape
    steps = blocks // PART
    return call(
        scores_kernel,
        "scores_and_logits",
        60,
        in_specs=[HBM] * 5,
        out_specs=[HBM] + [VMEM] * 4,
        out_shape=(
            bf16(blocks, heads, rows, keys),
            f32(heads * rows, LANES),
            f32(key_count, 2 * heads + 8, rows),
            f32(keys, rows),
            bf16(iheads, rows, depth),
        ),
        scratch_shapes=[
            pltpu.VMEM((blocks, heads, rows, keys), jnp.bfloat16),
            pltpu.VMEM(queries.shape, jnp.bfloat16),
            pltpu.VMEM(cache.shape, jnp.bfloat16),
            pltpu.VMEM(index_query.shape, jnp.bfloat16),
            pltpu.VMEM(index_keys.shape, jnp.bfloat16),
            pltpu.VMEM(weights.shape, jnp.float32),
            pltpu.VMEM((rows * iheads, depth), jnp.float32),
            pltpu.VMEM((rows, keys), jnp.float32),
            pltpu.VMEM((rows * heads, width), jnp.bfloat16),
            pltpu.VMEM((rows * heads, LANES), jnp.float32),
            pltpu.SemaphoreType.DMA((steps + 4,)),
            pltpu.SemaphoreType.DMA((steps,)),
        ],
    )(queries, cache, index_query, index_keys, weights)


def headsum_kernel(offsets, place_ref, e_hbm, tops_ref, got_ref, *refs):
    outs, e_ref, weights, tail, square, sems = refs[0 : len(offsets)], *refs[len(offsets) :]
    _, heads, rows, keys = e_ref.shape
    lane = lane_iota(rows)
    near, near_stride, far_stride = place_ref[0], place_ref[2], place_ref[3]

    def block_of(d, k):
        return lax.rem(near + d, RING) * near_stride + k * far_stride

    def block_copy(i, d, k):
        slot = i * RING + k
        return pltpu.make_async_copy(e_hbm.at[block_of(d, k)], e_ref.at[slot], sems.at[slot])

    for i, d in enumerate(offsets):
        for k in range(RING):
            block_copy(i, d, k).start()

    tops = got_ref[:, 0:heads]
    top = jnp.max(tops, axis=0)
    total = jnp.sum(got_ref[:, heads : 2 * heads] * jnp.exp2((tops - top[None]) * SCORE2), axis=0)
    square[...] = jnp.zeros_like(square)
    square[0:heads] = top
    square[heads : 2 * heads] = (1.0 / MH) / total
    columns = square[...].T
    for h in range(heads):
        local = tops_ref[h * rows : (h + 1) * rows] - columns[:, h : h + 1]
        scale = columns[:, heads + h : heads + h + 1]
        weights[h] = jnp.exp2(jnp.minimum(local * SCORE2, 0.0)) * scale
    ltops = got_ref[:, 2 * heads : 2 * heads + 1]
    ltop = jnp.max(ltops, axis=0)
    lsum = jnp.sum(got_ref[:, 2 * heads + 1 : 2 * heads + 2] * jnp.exp(ltops - ltop[None]), axis=0)
    tail[...] = jnp.zeros_like(tail)
    tail[0:1, 0:rows] = ltop
    tail[1:2, 0:rows] = lsum

    for i, d in enumerate(offsets):

        def body(k, carry):
            step = block_of(d, k) // PART
            block_copy(i, d, k).wait()
            total = None
            for h in range(heads):
                column = jnp.sum(jnp.where(lane == step, weights[h], 0.0), axis=1, keepdims=True)
                term = e_ref[i * RING + k, h].astype(jnp.float32) * column
                total = term if total is None else total + term
            outs[i][k, 0:rows] = total
            outs[i][k, rows:] = tail[...]
            return carry

        lax.fori_loop(0, RING, body, 0)


def head_sum(offsets, place, terms, tops, got):
    blocks, heads, rows, keys = terms.shape
    slots = len(offsets) * RING
    return call(
        functools.partial(headsum_kernel, offsets),
        "head_sum",
        56,
        in_specs=[SMEM, HBM] + [VMEM] * 2,
        out_specs=[VMEM] * len(offsets),
        out_shape=[f32(blocks // RING, rows + 8, keys)] * len(offsets),
        scratch_shapes=[
            pltpu.VMEM((slots, heads, rows, keys), jnp.bfloat16),
            pltpu.VMEM((heads, rows, LANES), jnp.float32),
            pltpu.VMEM((8, keys), jnp.float32),
            pltpu.VMEM((LANES, rows), jnp.float32),
            pltpu.SemaphoreType.DMA((slots,)),
        ],
    )(place, terms, tops, got)


def merged_stats(tops, sums):
    top = tops[0]
    for other in tops[1:]:
        top = jnp.maximum(top, other)
    total = sums[0] * jnp.exp(tops[0] - top)
    for other, count in zip(tops[1:], sums[1:]):
        total = total + count * jnp.exp(other - top)
    return top, total


def partial_kernel(place_ref, *refs):
    got, outs = refs[0:RING], refs[RING:]
    rows = outs[0].shape[0] - 8
    top, total = merged_stats([r[0, rows : rows + 1] for r in got], [r[0, rows + 1 : rows + 2] for r in got])
    for d in range(RING):
        k = lax.rem(place_ref[1] + d, RING)
        outs[d][0:rows] = got[0][k, 0:rows] + got[1][k, 0:rows] + (got[2][k, 0:rows] + got[3][k, 0:rows])
        outs[d][rows:] = jnp.zeros_like(outs[d][rows:])
        outs[d][rows : rows + 1] = top
        outs[d][rows + 1 : rows + 2] = total


def partial_sum(place, got):
    _, height, keys = got[0].shape
    return call(
        partial_kernel,
        "partial_sum",
        in_specs=[SMEM] + [VMEM] * RING,
        out_specs=[VMEM] * RING,
        out_shape=[f32(height, keys)] * RING,
    )(place, *got)


GROUP = 8


def dlogits_kernel(key_total, *refs):
    got = refs[0:RING]
    logits_ref, qh_ref, k_ref, send_ref, turned = refs[RING:]
    heads, rows, depth = qh_ref.shape
    keys = k_ref.shape[0]
    root = 1.0 / math.sqrt(depth)

    ltop, lsum = merged_stats(
        [r[rows : rows + 1, 0:rows] for r in got], [r[rows + 1 : rows + 2, 0:rows] for r in got]
    )
    target = got[0][0:rows] + got[1][0:rows] + (got[2][0:rows] + got[3][0:rows])
    soft = jnp.exp(logits_ref[...] - ltop) * (1.0 / lsum)
    for k in range(0, keys, rows):
        turned[k : k + rows] = key_total * (soft[k : k + rows] - target[:, k : k + rows].T)
        send_ref[0:rows, k : k + rows] = turned[k : k + rows].T

    def step(i, first, column):
        sums = []
        for j in range(GROUP):
            products = dot(k_ref[...], qh_ref[i * GROUP + j], NT)
            sums.append(jnp.sum(jnp.maximum(products, 0.0) * turned[...], axis=0, keepdims=True) * root)
        place = pl.ds(pl.multiple_of(rows + first, GROUP), GROUP)
        send_ref[place, column : column + rows] = jnp.concatenate(sums, axis=0)

    half = heads // 2 // GROUP

    def low(i, carry):
        step(i, i * GROUP, 0)
        return carry

    def high(i, carry):
        step(i + half, i * GROUP, rows)
        return carry

    lax.fori_loop(0, half, low, 0)
    lax.fori_loop(0, half, high, 0)


def dlogits_of(got, logits, qh, index_keys, key_total):
    heads, rows, depth = qh.shape
    keys = index_keys.shape[0]
    return call(
        functools.partial(dlogits_kernel, key_total),
        "dlogits",
        24,
        out_shape=(f32(rows + heads // 2, keys), f32(keys, rows)),
    )(*got, logits, qh, index_keys)


def keys_kernel(turned_ref, qh_ref, k_ref, w_ref, keys_ref, slopes):
    heads, rows, depth = qh_ref.shape
    root = 1.0 / math.sqrt(depth)
    keys_ref[...] = jnp.zeros_like(keys_ref)

    def step(i, carry):
        weights = w_ref[pl.ds(i * GROUP, GROUP)] * root
        for j in range(GROUP):
            products = dot(k_ref[...], qh_ref[i * GROUP + j], NT)
            slope = jnp.where(products > 0.0, turned_ref[...] * weights[j : j + 1], 0.0)
            slopes[:, j * rows : (j + 1) * rows] = slope.astype(jnp.bfloat16)
        chunk = qh_ref[pl.ds(i * GROUP, GROUP)].reshape(GROUP * rows, depth)
        keys_ref[...] += dot(slopes[...], chunk, NN)
        return carry

    lax.fori_loop(0, heads // GROUP, step, 0)


def key_gradient(turned, qh, index_keys, weights):
    heads, rows, depth = qh.shape
    keys = index_keys.shape[0]
    return call(
        keys_kernel,
        "key_gradient",
        24,
        out_shape=f32(keys, depth),
        scratch_shapes=[pltpu.VMEM((keys, GROUP * rows), jnp.bfloat16)],
    )(turned, qh, index_keys, weights)


def query_kernel(offsets, place_ref, *refs):
    ring, count = RING, len(offsets)
    got, kept = refs[0:ring], refs[ring : 2 * ring]
    qh_ref, w_ref = refs[2 * ring : 2 * ring + 2]
    outs = refs[2 * ring + 2 : 2 * ring + 2 + count]
    slopes, acc, near, dlogits = refs[2 * ring + 2 + count :]
    heads, rows, depth = qh_ref.shape
    keys = kept[0].shape[0]
    pieces, tall, _ = outs[0].shape
    extra = got[0].shape[0] - rows
    share = (tall - 2 * extra // pieces) * pieces // rows
    root = 1.0 / math.sqrt(depth)
    near_at, far_at, near_stride, far_stride = [place_ref[i] for i in range(4)]
    span = rows // pieces
    few = extra // pieces

    wsum = got[0][rows:]
    for d in range(1, ring):
        wsum = wsum + got[d][rows:]
    for d in range(ring):
        near[d * keys : (d + 1) * keys] = kept[d][...].astype(jnp.bfloat16)
        dlogits[:, d * keys : (d + 1) * keys] = got[d][0:rows] * root
    columns = jnp.concatenate([w_ref[...], jnp.zeros((LANES - heads, rows), jnp.float32)], axis=0).T

    for i, d in enumerate(offsets):
        first = (lax.rem(far_at + d, ring) * far_stride + near_at * near_stride) * share
        weights = pltpu.roll(columns, LANES - first, 1)
        queries = qh_ref[pl.ds(first, share)].reshape(share * rows, depth)
        for k in range(0, ring * keys, keys):
            products = dot(queries, near[k : k + keys], NT)
            for j in range(share):
                part = products[j * rows : (j + 1) * rows]
                slope = jnp.where(part > 0.0, dlogits[:, k : k + keys] * weights[:, j : j + 1], 0.0)
                slopes[j * rows : (j + 1) * rows, k : k + keys] = slope.astype(jnp.bfloat16)
        acc[...] = dot(slopes[...], near[...], NN)
        for z in range(pieces):
            for j in range(share):
                start = j * rows + z * span
                outs[i][z, pl.ds(j, span, stride=share), :] = acc[start : start + span]
            piece = wsum[z * few : (z + 1) * few]
            outs[i][z, share * span : share * span + few] = piece[:, 0:rows]
            outs[i][z, share * span + few :] = piece[:, rows : 2 * rows]


def query_gradient(offsets, place, got, kept, qh, weights, pieces):
    height, keys = got[0].shape
    heads, rows, depth = qh.shape
    share = heads // (RING * RING)
    extra = height - rows
    tall = share * (rows // pieces) + 2 * (extra // pieces)
    return call(
        functools.partial(query_kernel, offsets),
        "query_gradient",
        24,
        in_specs=[SMEM] + [VMEM] * (2 * RING + 2),
        out_specs=[VMEM] * len(offsets),
        out_shape=[f32(pieces, tall, depth)] * len(offsets),
        scratch_shapes=[
            pltpu.VMEM((share * rows, RING * keys), jnp.bfloat16),
            pltpu.VMEM((share * rows, depth), jnp.float32),
            pltpu.VMEM((RING * keys, depth), jnp.bfloat16),
            pltpu.VMEM((rows, RING * keys), jnp.float32),
        ],
    )(place, *got, *kept, qh, weights)


def exchange(x, axis):
    return lax.all_to_all(x, axis, split_axis=0, concat_axis=0, tiled=True)


def shift(x, d, across):
    pairs = []
    for a in range(RING):
        for b in range(RING):
            for row in range(2):
                if (row == 1) != across:
                    there = (a + d) % RING * RING + b
                else:
                    there = a * RING + (b + d) % RING
                pairs.append(((a * RING + b) * 2 + row, there * 2 + row))
    return lax.ppermute(x, ("head", "row"), pairs)


def shards(mla_query, mla_cache, index_query, index_keys, index_weight):
    key_count = lax.axis_size("key")
    head_count = lax.axis_size("head")
    rows = mla_query.shape[0]
    keys, depth = index_keys.shape
    heads = index_query.shape[1]
    share = heads // head_count
    head_index = lax.axis_index("head")
    row_index = lax.axis_index("row")
    x, y = head_index // RING, head_index % RING
    first = row_index == 0
    place = jnp.stack(
        [jnp.where(first, y, x), jnp.where(first, x, y), jnp.where(first, 1, RING), jnp.where(first, RING, 1)]
    ).astype(jnp.int32)

    weights = index_weight.T
    queries = jnp.transpose(mla_query, (1, 2, 0))
    cache = jnp.swapaxes(mla_cache, 1, 2)
    terms, tops, send1, logits, qh = scores_and_logits(queries, cache, index_query, index_keys, weights, key_count)
    send1, place = lax.optimization_barrier((send1, place))
    got1 = exchange(send1, "key")
    wide_keys = index_keys.astype(jnp.float32)
    (opposite,) = head_sum((2,), place, terms, tops, got1)
    others = head_sum((1, 3, 0), place, terms, tops, got1)
    got2 = [others[2], shift(others[0], 1, False), shift(opposite, 2, False), shift(others[1], 3, False)]
    wide_keys, _ = lax.optimization_barrier((wide_keys, others[0]))
    kept = [wide_keys] + [shift(wide_keys, d, False) for d in range(1, RING)]
    got2, kept = lax.optimization_barrier((got2, kept))
    send2 = partial_sum(place, got2)
    got2 = [send2[0]] + [shift(send2[d], d, True) for d in (1, 2, 3)]
    key_total = float(keys * head_count * key_count)
    send3, turned = dlogits_of(got2, logits, qh, index_keys, key_total)
    got3 = [send3] + [shift(send3, d, False) for d in range(1, RING)]
    keys_part = key_gradient(turned, qh, index_keys, weights)
    got3, keys_part = lax.optimization_barrier((got3, keys_part))

    half = keys // 2
    away = lax.dynamic_slice_in_dim(keys_part, (1 - row_index) * half, half, 0)
    near = lax.dynamic_slice_in_dim(keys_part, row_index * half, half, 0)
    key_grad = near + lax.ppermute(away, "row", [(0, 1), (1, 0)])

    (opposite,) = query_gradient((2,), place, got3, kept, qh, weights, key_count)
    opposite, got3 = lax.optimization_barrier((opposite, got3))
    others = query_gradient((1, 3, 0), place, got3, kept, qh, weights, key_count)
    opposite, one, three = shift(opposite, 2, True), shift(others[0], 1, True), shift(others[1], 3, True)
    send4 = others[2] + one + (opposite + three)
    got4 = jnp.sum(exchange(send4, "key"), axis=0)
    got5 = exchange(jnp.broadcast_to(got4[None], (key_count, *got4.shape)), "key")
    span = share * (rows // key_count)
    query_grad = got5[:, 0:span].reshape(rows, share, depth)
    few = (got4.shape[0] - span) // 2
    low = got5[:, span : span + few].reshape(heads // 2, rows)
    high = got5[:, span + few :].reshape(heads // 2, rows)
    weight_grad = jnp.concatenate([low, high], axis=0).T
    return (query_grad, key_grad, weight_grad)


def solution(mesh):
    placed = (
        P("row", "head", None),
        P(None, "key", None),
        P("row", None, None),
        P(("head", "key"), None),
        P("row", None),
    )
    return jax.shard_map(
        shards,
        mesh=mesh,
        in_specs=placed,
        out_specs=(P("row", "head", None), P(("head", "key", "row"), None), P("row", None)),
        check_vma=False,
    )
```

time: 143 us -> 145 us (1.014)
  blocking collectives: 13.3 us -> 32.1 us
  local copies, waits for them, and re-layouts: 13.6 us -> 2.53 us
  Pallas kernels: 29.2 us -> 39.9 us
  starting transfers between devices: 37.7 us -> 29 us
  waiting for transfers between devices: 45.4 us -> 38 us
    all_to_all x1 -> x2, blocking collectives: 13.3 us -> 32.1 us  [exchange(): return lax.all_to_all(x, axis, split_axis=0, concat_axis=0, tiled=True)]
    unnamed x18 -> x12, local copies, waits for them, and re-layouts: 12.2 us -> 1.07 us
    pallas_call x5 -> x7, Pallas kernels: 28.5 us -> 39.2 us  [the longest x1 18.7 us: scores_and_logits(): call(scores_kernel, 'scores_and_logits', 60, in_specs=[HBM] * 5, out_spec...]
    all_to_all x2 -> x1, starting transfers between devices: 13.3 us -> 5 us  [exchange(): return lax.all_to_all(x, axis, split_axis=0, concat_axis=0, tiled=True)]
    all_to_all x2 -> x1, waiting for transfers between devices: 14.5 us -> 7.41 us  [exchange(): return lax.all_to_all(x, axis, split_axis=0, concat_axis=0, tiled=True)]
  transfers between devices with their start and end apart: 18 -> 17, of which waited for: 12 -> 11; matrix products, arithmetic and copies ran while one was open for 1% -> 0% of each run, Pallas kernels for 0% -> 7%
where the time goes in v4:
time: 145 us; the launch traced here: 144 us
  Pallas kernels  39.9 us (28%)
  waiting for transfers between devices  38 us (26%)
  blocking collectives  32.1 us (22%)
  starting transfers between devices  29 us (20%)
  local copies, waits for them, and re-layouts  2.53 us (2%)
  other arithmetic  2.01 us (1%)
    all_to_all x2, blocking collectives, exchange(): return lax.all_to_all(x, axis, split_axis=0, concat_axis=0, tiled=True)  32.1 us
    ppermute x15, waiting for transfers between devices, shift(): return lax.ppermute(x, ('head', 'row'), pairs)  29.4 us
    ppermute x15, starting transfers between devices, shift(): return lax.ppermute(x, ('head', 'row'), pairs)  23.9 us
    pallas_call x1, Pallas kernels, scores_and_logits(): call(scores_kernel, 'scores_and_logits', 60, in_specs=[HBM] * 5, out_spec...  18.7 us
    pallas_call x2, Pallas kernels, head_sum(): call(functools.partial(headsum_kernel, offsets), 'head_sum', 56, in_specs...  9.77 us
    all_to_all x1, waiting for transfers between devices, exchange(): return lax.all_to_all(x, axis, split_axis=0, concat_axis=0, tiled=True)  7.41 us
    all_to_all x1, starting transfers between devices, exchange(): return lax.all_to_all(x, axis, split_axis=0, concat_axis=0, tiled=True)  5 us
    pallas_call x2, Pallas kernels, query_gradient(): call(functools.partial(query_kernel, offsets), 'query_gradient', 24, in_s...  4.03 us
  transfers between devices with their start and end apart: 17, of which 11 were waited for; matrix products, arithmetic and copies ran while one was open for 0% of the time, Pallas kernels for 7%

profile of v4, /device:TPU:32, one launch (start us, length us, event | category | flops | bytes accessed | tf_op | source)
XLA Modules:
  0.0 144.4 jit_solution(16146436260506529433)
XLA Ops:
  0.7 0.7 pad_add_fusion.place_ref
  1.3 18.7 %scores_and_logits.1 = (bf16[16,8,128,256]{3,2,1,0:T(8,128)(2,1)}, f32[1024,128]{1,0:T(8,128)}, f32[8,24,128]{2,1,0:T(8,128)}, f32[256,128]{1,0:T(8,128)}, bf16[64,128,128]{2,1,0:T(8,128)(2,1)}) custom-call(bf16[8,576,128]{2,1,0:T(8,128)(2,1)} %bitcast.17, bf16[16,576,256]{2,1,0:T(8,128)(2,1)} %bitcast.16, bf16[128,64,128]{2,1,0:T(8,128)(2,1)} %iq_hbm.1, ...), custom_call_target="tpu_custom_call" | custom-call | tf_op jit(solution)/shard_map/scores_and_logits/pallas_call | solution.py:157
  20.0 15.8 %all_to_all.15.got_ref = f32[8,24,128]{2,1,0:T(8,128)} all-to-all(f32[8,24,128]{2,1,0:T(8,128)} %get-tuple-element.45), channel_id=1, replica_groups=mesh['head'=16,'key'=8,'row'=2] {'key'}, dimensions={0} | all-to-all | bytes 196608 | tf_op jit(solution)/shard_map/all_to_all | solution.py:441
  35.9 3.9 %head_sum.3 = f32[4,136,256]{2,1,0:T(8,128)} custom-call(s32[4]{0:T(128)} %pad_add_fusion.place_ref, bf16[16,8,128,256]{3,2,1,0:T(8,128)(2,1)} %get-tuple-element.43.e_hbm, f32[1024,128]{1,0:T(8,128)} %get-tuple-element.44.tops_ref, f32[8,24,128]{2,1,0:T(8,128)} %all_to_all.15.got_ref), custom_call_target="tpu_custom_call" | custom-call | tf_op jit(solution)/shard_map/head_sum/pallas_call | solution.py:242
  39.7 0.0 copy-start.1
  39.7 3.3 %collective-permute-start.1 = (f32[4,136,256]{2,1,0:T(8,128)}, f32[4,136,256]{2,1,0:T(8,128)S(1)}, u32[]{:S(2)}, u32[]{:S(2)}) collective-permute-start(f32[4,136,256]{2,1,0:T(8,128)} %head_sum.3), channel_id=1, source_target_pairs={{0,32},{1,129},{16,48},{17,145},{32,0},{33,161},{48,16},{49,177},{... | collective-permute-start | bytes 1671176 | tf_op jit(solution)/shard_map/ppermute | solution.py:454
  43.0 5.9 %head_sum.2 = (f32[4,136,256]{2,1,0:T(8,128)}, f32[4,136,256]{2,1,0:T(8,128)}, f32[4,136,256]{2,1,0:T(8,128)}) custom-call(s32[4]{0:T(128)} %pad_add_fusion.place_ref, bf16[16,8,128,256]{3,2,1,0:T(8,128)(2,1)} %get-tuple-element.43.e_hbm, f32[1024,128]{1,0:T(8,128)} %get-tuple-element.44.tops_ref, f32[8,24,128]{2,1,0:T(8,128)} %all_to_all.15.got_ref), custom_call_target="tpu_custom_call" | custom-call | tf_op jit(solution)/shard_map/head_sum/pallas_call | solution.py:242
  49.0 0.8 collective-permute-start
  49.7 2.6 %collective-permute-start.2 = (f32[4,136,256]{2,1,0:T(8,128)}, f32[4,136,256]{2,1,0:T(8,128)S(1)}, u32[]{:S(2)}, u32[]{:S(2)}) collective-permute-start(f32[4,136,256]{2,1,0:T(8,128)} %get-tuple-element.48), channel_id=1, source_target_pairs={{0,48},{1,193},{16,0},{17,209},{32,16},{33,225},{48,32},{49,241},{... | collective-permute-start | bytes 1671176 | tf_op jit(solution)/shard_map/ppermute | solution.py:454
  52.3 0.1 collective-permute-start.3
  52.4 1.5 %collective-permute-start.4 = (f32[256,128]{1,0:T(8,128)S(1)}, f32[256,128]{1,0:T(8,128)S(1)}, u32[]{:S(2)}, u32[]{:S(2)}) collective-permute-start(f32[256,128]{1,0:T(8,128)S(1)} %convert_element_type.3.refs_4_), channel_id=1, source_target_pairs={{0,32},{1,129},{16,48},{17,145},{32,0},{33,161},{48,16},{49,177},{... | collective-permute-start | bytes 393224 | tf_op jit(solution)/shard_map/ppermute | solution.py:454
  53.8 9.0 %collective-permute-done.3.refs_5_ = f32[256,128]{1,0:T(8,128)S(1)} collective-permute-done((f32[256,128]{1,0:T(8,128)S(1)}, f32[256,128]{1,0:T(8,128)S(1)}, u32[]{:S(2)}, u32[]{:S(2)}) %collective-permute-start.3) | collective-permute-done | bytes 131104 | tf_op jit(solution)/shard_map/ppermute | solution.py:454
  62.8 0.0 collective-permute-start.5
  62.8 0.0 collective-permute-done.4.refs_6_
  62.8 5.0 %collective-permute-done.5.refs_7_ = f32[256,128]{1,0:T(8,128)S(1)} collective-permute-done((f32[256,128]{1,0:T(8,128)S(1)}, f32[256,128]{1,0:T(8,128)S(1)}, u32[]{:S(2)}, u32[]{:S(2)}) %collective-permute-start.5) | collective-permute-done | bytes 131104 | tf_op jit(solution)/shard_map/ppermute | solution.py:454
  67.8 0.0 collective-permute-done.1.refs_2_
  67.8 1.0 copy-done.2
  68.9 0.7 partial_sum.1
  69.5 1.6 %collective-permute-start.6 = (f32[136,256]{1,0:T(8,128)S(1)}, f32[136,256]{1,0:T(8,128)S(1)}, u32[]{:S(2)}, u32[]{:S(2)}) collective-permute-start(f32[136,256]{1,0:T(8,128)S(1)} %get-tuple-element.55), channel_id=1, source_target_pairs={{0,64},{1,17},{16,80},{17,33},{32,96},{33,49},{48,112},{49,1},{64,... | collective-permute-start | bytes 417800 | tf_op jit(solution)/shard_map/ppermute | solution.py:454
  71.1 2.8 %collective-permute-start.7 = (f32[136,256]{1,0:T(8,128)S(1)}, f32[136,256]{1,0:T(8,128)S(1)}, u32[]{:S(2)}, u32[]{:S(2)}) collective-permute-start(f32[136,256]{1,0:T(8,128)S(1)} %get-tuple-element.56), channel_id=1, source_target_pairs={{0,128},{1,33},{16,144},{17,49},{32,160},{33,1},{48,176},{49,17},{... | collective-permute-start | bytes 417800 | tf_op jit(solution)/shard_map/ppermute | solution.py:454
  73.8 2.5 %collective-permute-start.8 = (f32[136,256]{1,0:T(8,128)S(1)}, f32[136,256]{1,0:T(8,128)S(1)}, u32[]{:S(2)}, u32[]{:S(2)}) collective-permute-start(f32[136,256]{1,0:T(8,128)S(1)} %get-tuple-element.57), channel_id=1, source_target_pairs={{0,192},{1,49},{16,208},{17,1},{32,224},{33,17},{48,240},{49,33},{... | collective-permute-start | bytes 417800 | tf_op jit(solution)/shard_map/ppermute | solution.py:454
  76.4 2.0 %collective-permute-done.7.refs_2_ = f32[136,256]{1,0:T(8,128)S(1)} collective-permute-done((f32[136,256]{1,0:T(8,128)S(1)}, f32[136,256]{1,0:T(8,128)S(1)}, u32[]{:S(2)}, u32[]{:S(2)}) %collective-permute-start.7) | collective-permute-done | bytes 139296 | tf_op jit(solution)/shard_map/ppermute | solution.py:454
  78.3 2.6 %collective-permute-done.8.refs_3_ = f32[136,256]{1,0:T(8,128)S(1)} collective-permute-done((f32[136,256]{1,0:T(8,128)S(1)}, f32[136,256]{1,0:T(8,128)S(1)}, u32[]{:S(2)}, u32[]{:S(2)}) %collective-permute-start.8) | collective-permute-done | bytes 139296 | tf_op jit(solution)/shard_map/ppermute | solution.py:454
  80.9 2.7 %dlogits.1 = (f32[160,256]{1,0:T(8,128)S(1)}, f32[256,128]{1,0:T(8,128)S(1)}) custom-call(f32[136,256]{1,0:T(8,128)S(1)} %get-tuple-element.54.refs_0_, f32[136,256]{1,0:T(8,128)S(1)} %collective-permute-done.6.refs_1_, f32[136,256]{1,0:T(8,128)S(1)} %collective-permute-done.7.refs_2_, f32[136,256]{1,0:T(8,128)S(1)} %collective-permute-done.8.refs_3_, ...), custom_call_target="tpu_custom_call" | custom-call | tf_op jit(solution)/shard_map/dlogits/pallas_call | solution.py:336
  83.6 0.3 collective-permute-start.10
  83.9 0.2 collective-permute-start.11
  84.2 1.9 %collective-permute-start.9 = (f32[160,256]{1,0:T(8,128)S(1)}, f32[160,256]{1,0:T(8,128)S(1)}, u32[]{:S(2)}, u32[]{:S(2)}) collective-permute-start(f32[160,256]{1,0:T(8,128)S(1)} %get-tuple-element.70.refs_0_), channel_id=1, source_target_pairs={{0,16},{1,65},{16,32},{17,81},{32,48},{33,97},{48,0},{49,113},{64,... | collective-permute-start | bytes 491528 | tf_op jit(solution)/shard_map/ppermute | solution.py:454
  86.0 4.0 %key_gradient.1 = f32[256,128]{1,0:T(8,128)S(1)} custom-call(f32[256,128]{1,0:T(8,128)S(1)} %get-tuple-element.61.turned_ref, bf16[64,128,128]{2,1,0:T(8,128)(2,1)S(1)} %copy-done, bf16[256,128]{1,0:T(8,128)(2,1)S(1)} %copy-done.1, f32[64,128]{1,0:T(8,128)S(1)} %bitcast.13), custom_call_target="tpu_custom_call" | custom-call | tf_op jit(solution)/shard_map/key_gradient/pallas_call | solution.py:365
  90.0 0.8 collective-permute-done.10.refs_2_
  90.8 2.2 %collective-permute-done.9.refs_1_ = f32[160,256]{1,0:T(8,128)S(1)} collective-permute-done((f32[160,256]{1,0:T(8,128)S(1)}, f32[160,256]{1,0:T(8,128)S(1)}, u32[]{:S(2)}, u32[]{:S(2)}) %collective-permute-start.9) | collective-permute-done | bytes 163872 | tf_op jit(solution)/shard_map/ppermute | solution.py:454
  93.0 1.5 %query_gradient.2 = f32[8,72,128]{2,1,0:T(8,128)S(1)} custom-call(s32[4]{0:T(128)S(1)} %copy-done.5, f32[160,256]{1,0:T(8,128)S(1)} %get-tuple-element.70.refs_0_, f32[160,256]{1,0:T(8,128)S(1)} %collective-permute-done.9.refs_1_, f32[160,256]{1,0:T(8,128)S(1)} %collective-permute-done.10.refs_2_, f32[160,256]{1,0:T(8,128)S(1)} %collective-permute-done.11.refs_3_, ...), custom_call_target="tpu_custom_call" | custom-call | tf_op jit(solution)/shard_map/query_gradient/pallas_call | solution.py:424
  94.5 2.6 %query_gradient.3 = (f32[8,72,128]{2,1,0:T(8,128)S(1)}, f32[8,72,128]{2,1,0:T(8,128)S(1)}, f32[8,72,128]{2,1,0:T(8,128)S(1)}) custom-call(s32[4]{0:T(128)S(1)} %copy-done.5, f32[160,256]{1,0:T(8,128)S(1)} %get-tuple-element.70.refs_0_, f32[160,256]{1,0:T(8,128)S(1)} %collective-permute-done.9.refs_1_, f32[160,256]{1,0:T(8,128)S(1)} %collective-permute-done.10.refs_2_, ...), custom_call_target="tpu_custom_call" | custom-call | tf_op jit(solution)/shard_map/query_gradient/pallas_call | solution.py:424
  97.1 0.1 collective-permute-start.12
  97.2 5.1 %collective-permute-start.14 = (f32[8,72,128]{2,1,0:T(8,128)S(1)}, f32[8,72,128]{2,1,0:T(8,128)S(1)}, u32[]{:S(2)}, u32[]{:S(2)}) collective-permute-start(f32[8,72,128]{2,1,0:T(8,128)S(1)} %get-tuple-element.77), channel_id=1, source_target_pairs={{0,192},{1,49},{16,208},{17,1},{32,224},{33,17},{48,240},{49,33},{... | collective-permute-start | bytes 884744 | tf_op jit(solution)/shard_map/ppermute | solution.py:454
  102.2 1.4 collective-permute-start.13
  103.6 3.2 %collective-permute-done.12 = f32[8,72,128]{2,1,0:T(8,128)S(1)} collective-permute-done((f32[8,72,128]{2,1,0:T(8,128)S(1)}, f32[8,72,128]{2,1,0:T(8,128)S(1)}, u32[]{:S(2)}, u32[]{:S(2)}) %collective-permute-start.12) | collective-permute-done | bytes 294944 | tf_op jit(solution)/shard_map/ppermute | solution.py:454
  106.9 2.8 %collective-permute-done.14 = f32[8,72,128]{2,1,0:T(8,128)S(1)} collective-permute-done((f32[8,72,128]{2,1,0:T(8,128)S(1)}, f32[8,72,128]{2,1,0:T(8,128)S(1)}, u32[]{:S(2)}, u32[]{:S(2)}) %collective-permute-start.14) | collective-permute-done | bytes 294944 | tf_op jit(solution)/shard_map/ppermute | solution.py:454
  109.7 1.8 %collective-permute-done.13 = f32[8,72,128]{2,1,0:T(8,128)S(1)} collective-permute-done((f32[8,72,128]{2,1,0:T(8,128)S(1)}, f32[8,72,128]{2,1,0:T(8,128)S(1)}, u32[]{:S(2)}, u32[]{:S(2)}) %collective-permute-start.13) | collective-permute-done | bytes 294944 | tf_op jit(solution)/shard_map/ppermute | solution.py:454
  111.5 0.1 add_add_fusion
  111.5 16.3 %all_to_all.16 = f32[8,72,128]{2,1,0:T(8,128)S(1)} all-to-all(f32[8,72,128]{2,1,0:T(8,128)S(1)} %add_add_fusion), channel_id=1, replica_groups=mesh['head'=16,'key'=8,'row'=2] {'key'}, dimensions={0} | all-to-all | bytes 589824 | tf_op jit(solution)/shard_map/all_to_all | solution.py:441
  127.9 0.7 broadcast_in_dim.2
  128.6 5.0 %all-to-all-start.2 = ((f32[8,72,128]{2,1,0:T(8,128)}), f32[8,72,128]{2,1,0:T(8,128)S(1)}, u32[]{:S(2)}, u32[]{:S(2)}) async-start(f32[8,72,128]{2,1,0:T(8,128)} %broadcast_in_dim.2), calls=%async_computation.2 | async-start | bytes 589824 | tf_op jit(solution)/shard_map/all_to_all | solution.py:441
  133.6 0.1 collective-permute-start.15
  133.7 1.2 collective-permute-done.15
  135.0 0.6 dynamic-slice_add_fusion
  135.6 7.4 %all-to-all-done.2 = f32[8,72,128]{2,1,0:T(8,128)S(1)} async-done(((f32[8,72,128]{2,1,0:T(8,128)}), f32[8,72,128]{2,1,0:T(8,128)S(1)}, u32[]{:S(2)}, u32[]{:S(2)}) %all-to-all-start.2) | async-done | bytes 294944 | tf_op jit(solution)/shard_map/all_to_all | solution.py:441
  143.0 0.6 maximum_bitcast_fusion
  143.6 0.7 slice.12
  (18 shorter events, 0.1 us)
Async XLA Ops:
  39.7 12.6 %copy-start.1 = (bf16[256,128]{1,0:T(8,128)(2,1)S(1)}, bf16[256,128]{1,0:T(8,128)(2,1)}, u32[]{:S(2)}) copy-start(bf16[256,128]{1,0:T(8,128)(2,1)} %k_ref.1) | copy-start | bytes 196612
  39.7 28.1 %copy-start.5 = (s32[4]{0:T(128)S(1)}, s32[4]{0:T(128)}, u32[]{:S(2)}) copy-start(s32[4]{0:T(128)} %pad_add_fusion.place_ref) | copy-start | bytes 52
  39.7 28.0 %collective-permute-start.1 = (f32[4,136,256]{2,1,0:T(8,128)}, f32[4,136,256]{2,1,0:T(8,128)S(1)}, u32[]{:S(2)}, u32[]{:S(2)}) collective-permute-start(f32[4,136,256]{2,1,0:T(8,128)} %head_sum.3), channel_id=1, source_target_pairs={{0,32},{1,129},{16,48},{17,145},{32,0},{33,161},{48,16},{49,177},{... | collective-permute-start | bytes 1671176 | tf_op jit(solution)/shard_map/ppermute | solution.py:454
  43.0 37.9 %copy-start.4 = (f32[256,128]{1,0:T(8,128)S(1)}, f32[256,128]{1,0:T(8,128)}, u32[]{:S(2)}) copy-start(f32[256,128]{1,0:T(8,128)} %get-tuple-element.58.refs_4_) | copy-start | bytes 393220
  49.0 32.0 %copy-start = (bf16[64,128,128]{2,1,0:T(8,128)(2,1)S(1)}, bf16[64,128,128]{2,1,0:T(8,128)(2,1)}, u32[]{:S(2)}) copy-start(bf16[64,128,128]{2,1,0:T(8,128)(2,1)} %get-tuple-element.59.refs_5_.qh_ref.refs_8_) | copy-start | bytes 6291460
  49.0 18.8 %collective-permute-start = (f32[4,136,256]{2,1,0:T(8,128)}, f32[4,136,256]{2,1,0:T(8,128)S(1)}, u32[]{:S(2)}, u32[]{:S(2)}) collective-permute-start(f32[4,136,256]{2,1,0:T(8,128)} %get-tuple-element.47), channel_id=1, source_target_pairs={{0,16},{1,65},{16,32},{17,81},{32,48},{33,97},{48,0},{49,113},{64,... | collective-permute-start | bytes 1671176 | tf_op jit(solution)/shard_map/ppermute | solution.py:454
  49.7 18.1 %collective-permute-start.2 = (f32[4,136,256]{2,1,0:T(8,128)}, f32[4,136,256]{2,1,0:T(8,128)S(1)}, u32[]{:S(2)}, u32[]{:S(2)}) collective-permute-start(f32[4,136,256]{2,1,0:T(8,128)} %get-tuple-element.48), channel_id=1, source_target_pairs={{0,48},{1,193},{16,0},{17,209},{32,16},{33,225},{48,32},{49,241},{... | collective-permute-start | bytes 1671176 | tf_op jit(solution)/shard_map/ppermute | solution.py:454
  52.3 10.5 %collective-permute-start.3 = (f32[256,128]{1,0:T(8,128)S(1)}, f32[256,128]{1,0:T(8,128)S(1)}, u32[]{:S(2)}, u32[]{:S(2)}) collective-permute-start(f32[256,128]{1,0:T(8,128)S(1)} %convert_element_type.3.refs_4_), channel_id=1, source_target_pairs={{0,16},{1,65},{16,32},{17,81},{32,48},{33,97},{48,0},{49,113},{64,... | collective-permute-start | bytes 393224 | tf_op jit(solution)/shard_map/ppermute | solution.py:454
  52.4 10.4 %collective-permute-start.4 = (f32[256,128]{1,0:T(8,128)S(1)}, f32[256,128]{1,0:T(8,128)S(1)}, u32[]{:S(2)}, u32[]{:S(2)}) collective-permute-start(f32[256,128]{1,0:T(8,128)S(1)} %convert_element_type.3.refs_4_), channel_id=1, source_target_pairs={{0,32},{1,129},{16,48},{17,145},{32,0},{33,161},{48,16},{49,177},{... | collective-permute-start | bytes 393224 | tf_op jit(solution)/shard_map/ppermute | solution.py:454
  62.8 5.0 %collective-permute-start.5 = (f32[256,128]{1,0:T(8,128)S(1)}, f32[256,128]{1,0:T(8,128)S(1)}, u32[]{:S(2)}, u32[]{:S(2)}) collective-permute-start(f32[256,128]{1,0:T(8,128)S(1)} %convert_element_type.3.refs_4_), channel_id=1, source_target_pairs={{0,48},{1,193},{16,0},{17,209},{32,16},{33,225},{48,32},{49,241},{... | collective-permute-start | bytes 393224 | tf_op jit(solution)/shard_map/ppermute | solution.py:454
  67.8 1.1 copy-start.2
  68.9 17.2 %copy-start.3 = (f32[128,64]{0,1:T(8,128)S(1)}, f32[128,64]{0,1:T(8,128)}, u32[]{:S(2)}) copy-start(f32[128,64]{0,1:T(8,128)} %param.9) | copy-start | bytes 98308
  69.5 6.8 %collective-permute-start.6 = (f32[136,256]{1,0:T(8,128)S(1)}, f32[136,256]{1,0:T(8,128)S(1)}, u32[]{:S(2)}, u32[]{:S(2)}) collective-permute-start(f32[136,256]{1,0:T(8,128)S(1)} %get-tuple-element.55), channel_id=1, source_target_pairs={{0,64},{1,17},{16,80},{17,33},{32,96},{33,49},{48,112},{49,1},{64,... | collective-permute-start | bytes 417800 | tf_op jit(solution)/shard_map/ppermute | solution.py:454
  71.1 7.2 %collective-permute-start.7 = (f32[136,256]{1,0:T(8,128)S(1)}, f32[136,256]{1,0:T(8,128)S(1)}, u32[]{:S(2)}, u32[]{:S(2)}) collective-permute-start(f32[136,256]{1,0:T(8,128)S(1)} %get-tuple-element.56), channel_id=1, source_target_pairs={{0,128},{1,33},{16,144},{17,49},{32,160},{33,1},{48,176},{49,17},{... | collective-permute-start | bytes 417800 | tf_op jit(solution)/shard_map/ppermute | solution.py:454
  73.8 7.1 %collective-permute-start.8 = (f32[136,256]{1,0:T(8,128)S(1)}, f32[136,256]{1,0:T(8,128)S(1)}, u32[]{:S(2)}, u32[]{:S(2)}) collective-permute-start(f32[136,256]{1,0:T(8,128)S(1)} %get-tuple-element.57), channel_id=1, source_target_pairs={{0,192},{1,49},{16,208},{17,1},{32,224},{33,17},{48,240},{49,33},{... | collective-permute-start | bytes 417800 | tf_op jit(solution)/shard_map/ppermute | solution.py:454
  83.6 7.2 %collective-permute-start.10 = (f32[160,256]{1,0:T(8,128)S(1)}, f32[160,256]{1,0:T(8,128)S(1)}, u32[]{:S(2)}, u32[]{:S(2)}) collective-permute-start(f32[160,256]{1,0:T(8,128)S(1)} %get-tuple-element.70.refs_0_), channel_id=1, source_target_pairs={{0,32},{1,129},{16,48},{17,145},{32,0},{33,161},{48,16},{49,177},{... | collective-permute-start | bytes 491528 | tf_op jit(solution)/shard_map/ppermute | solution.py:454
  83.9 6.9 %collective-permute-start.11 = (f32[160,256]{1,0:T(8,128)S(1)}, f32[160,256]{1,0:T(8,128)S(1)}, u32[]{:S(2)}, u32[]{:S(2)}) collective-permute-start(f32[160,256]{1,0:T(8,128)S(1)} %get-tuple-element.70.refs_0_), channel_id=1, source_target_pairs={{0,48},{1,193},{16,0},{17,209},{32,16},{33,225},{48,32},{49,241},{... | collective-permute-start | bytes 491528 | tf_op jit(solution)/shard_map/ppermute | solution.py:454
  84.2 8.9 %collective-permute-start.9 = (f32[160,256]{1,0:T(8,128)S(1)}, f32[160,256]{1,0:T(8,128)S(1)}, u32[]{:S(2)}, u32[]{:S(2)}) collective-permute-start(f32[160,256]{1,0:T(8,128)S(1)} %get-tuple-element.70.refs_0_), channel_id=1, source_target_pairs={{0,16},{1,65},{16,32},{17,81},{32,48},{33,97},{48,0},{49,113},{64,... | collective-permute-start | bytes 491528 | tf_op jit(solution)/shard_map/ppermute | solution.py:454
  97.1 9.8 %collective-permute-start.12 = (f32[8,72,128]{2,1,0:T(8,128)S(1)}, f32[8,72,128]{2,1,0:T(8,128)S(1)}, u32[]{:S(2)}, u32[]{:S(2)}) collective-permute-start(f32[8,72,128]{2,1,0:T(8,128)S(1)} %get-tuple-element.75), channel_id=1, source_target_pairs={{0,64},{1,17},{16,80},{17,33},{32,96},{33,49},{48,112},{49,1},{64,... | collective-permute-start | bytes 884744 | tf_op jit(solution)/shard_map/ppermute | solution.py:454
  97.2 12.5 %collective-permute-start.14 = (f32[8,72,128]{2,1,0:T(8,128)S(1)}, f32[8,72,128]{2,1,0:T(8,128)S(1)}, u32[]{:S(2)}, u32[]{:S(2)}) collective-permute-start(f32[8,72,128]{2,1,0:T(8,128)S(1)} %get-tuple-element.77), channel_id=1, source_target_pairs={{0,192},{1,49},{16,208},{17,1},{32,224},{33,17},{48,240},{49,33},{... | collective-permute-start | bytes 884744 | tf_op jit(solution)/shard_map/ppermute | solution.py:454
  102.2 9.2 %collective-permute-start.13 = (f32[8,72,128]{2,1,0:T(8,128)S(1)}, f32[8,72,128]{2,1,0:T(8,128)S(1)}, u32[]{:S(2)}, u32[]{:S(2)}) collective-permute-start(f32[8,72,128]{2,1,0:T(8,128)S(1)} %query_gradient.2), channel_id=1, source_target_pairs={{0,128},{1,33},{16,144},{17,49},{32,160},{33,1},{48,176},{49,17},{... | collective-permute-start | bytes 884744 | tf_op jit(solution)/shard_map/ppermute | solution.py:454
  128.6 14.4 %all-to-all-start.2 = ((f32[8,72,128]{2,1,0:T(8,128)}), f32[8,72,128]{2,1,0:T(8,128)S(1)}, u32[]{:S(2)}, u32[]{:S(2)}) async-start(f32[8,72,128]{2,1,0:T(8,128)} %broadcast_in_dim.2), calls=%async_computation.2 | async-start | bytes 589824 | tf_op jit(solution)/shard_map/all_to_all | solution.py:441
  133.6 1.3 collective-permute-start.15

commit v5 on v4

v5 whole, which is shorter than its diff:
```python
import functools
import math

import jax
import jax.numpy as jnp
from jax import lax
from jax.experimental import pallas as pl
from jax.experimental.pallas import tpu as pltpu
from jax.sharding import PartitionSpec as P

MH = 128
LOG2E = 1.4426950408889634
SCORE2 = LOG2E / math.sqrt(192.0)
LANES = 128
NT = (((1,), (1,)), ((), ()))
TN = (((0,), (0,)), ((), ()))
NN = (((1,), (0,)), ((), ()))


def dot(a, b, dims):
    return lax.dot_general(a, b, dims, preferred_element_type=jnp.float32)


def lane_iota(rows):
    return lax.broadcasted_iota(jnp.int32, (rows, LANES), 1)


RING = 4
PART = 2
BESIDE = 4_000_000_000
VMEM = pl.BlockSpec(memory_space=pltpu.VMEM)
HBM = pl.BlockSpec(memory_space=pltpu.HBM)


def call(kernel, name, megabytes=32, flops=0, moved=0, **options):
    cost = pl.CostEstimate(flops=flops, bytes_accessed=moved, transcendentals=0) if flops else None
    return pl.pallas_call(
        kernel,
        name=name,
        compiler_params=pltpu.CompilerParams(vmem_limit_bytes=megabytes << 20),
        cost_estimate=cost,
        **options,
    )


def f32(*shape):
    return jax.ShapeDtypeStruct(shape, jnp.float32)


def bf16(*shape):
    return jax.ShapeDtypeStruct(shape, jnp.bfloat16)


def position():
    head, first = lax.axis_index("head"), lax.axis_index("row") == 0
    x, y = lax.div(head, RING), lax.rem(head, RING)
    return jnp.where(first, y, x), jnp.where(first, x, y), jnp.where(first, 1, RING), jnp.where(first, RING, 1)


def scores_kernel(
    q_hbm, c_hbm, iq_hbm, k_hbm, w_hbm,
    e_hbm, tops_ref, send_ref, logits_ref, qh_ref,
    e_ref, q_ref, c_ref, iq_ref, k_ref, w_ref, wide, total_ref, queries_ref, tops, sums, sems, out_sems,
):
    heads, width, rows = q_ref.shape
    blocks = c_ref.shape[0]
    steps = blocks // PART
    _, iheads, depth = iq_ref.shape
    keys = k_ref.shape[0]
    group = iheads // steps

    first = pltpu.make_async_copy(q_hbm, q_ref, sems.at[steps])
    first.start()

    def part_copy(step):
        span = pl.ds(step * PART, PART)
        return pltpu.make_async_copy(c_hbm.at[span], c_ref.at[span], sems.at[step])

    def terms_copy(step):
        span = pl.ds(step * PART, PART)
        return pltpu.make_async_copy(e_ref.at[span], e_hbm.at[span], out_sems.at[step])

    others = [(iq_hbm, iq_ref), (k_hbm, k_ref), (w_hbm, w_ref)]
    others = [pltpu.make_async_copy(src, dst, sems.at[steps + 1 + i]) for i, (src, dst) in enumerate(others)]
    for step in range(steps):
        part_copy(step).start()
    for copy in others:
        copy.start()

    tops[...] = jnp.zeros_like(tops)
    sums[...] = jnp.zeros_like(sums)
    first.wait()
    for h in range(heads):
        queries_ref[h * rows : (h + 1) * rows] = q_ref[h].T
    lane = lane_iota(rows)

    def score_step(step, carry):
        part_copy(step).wait()
        for h in range(0, heads, 2):
            queries = queries_ref[h * rows : (h + 2) * rows]
            scores = [dot(queries, c_ref[step * PART + j], NN) for j in range(PART)]
            top = scores[0]
            for score in scores[1:]:
                top = jnp.maximum(top, score)
            top = jnp.max(top, axis=1, keepdims=True)
            total = None
            for j, score in enumerate(scores):
                terms = jnp.exp2((score - top) * SCORE2)
                total = terms if total is None else total + terms
                e_ref[step * PART + j, h : h + 2] = terms.astype(jnp.bfloat16).reshape(2, rows, keys)
            total = jnp.sum(total, axis=1, keepdims=True)
            low, high = lane == h * steps + step, lane == (h + 1) * steps + step
            tops[...] = jnp.where(low, top[0:rows], jnp.where(high, top[rows:], tops[...]))
            sums[...] = jnp.where(low, total[0:rows], jnp.where(high, total[rows:], sums[...]))
        terms_copy(step).start()
        return carry

    lax.fori_loop(0, steps, score_step, 0)

    for copy in others:
        copy.wait()
    total_ref[...] = jnp.zeros_like(total_ref)
    wide[...] = iq_ref[...].astype(jnp.float32).reshape(rows * iheads, depth)
    columns = jnp.concatenate([w_ref[...], jnp.zeros((LANES - iheads, rows), jnp.float32)], axis=0).T

    def logit_step(step, carry):
        weights = pltpu.roll(columns, LANES - group * step, 1)
        for j in range(group):
            head = step * group + j
            qh_ref[head] = wide[pl.ds(head, rows, stride=iheads), :].astype(jnp.bfloat16)
        chunk = qh_ref[pl.ds(step * group, group)].reshape(group * rows, depth)
        products = dot(chunk, k_ref[...], NT)
        total = total_ref[...]
        for j in range(group):
            part = products[j * rows : (j + 1) * rows]
            total = total + jnp.maximum(part, 0.0) * weights[:, j : j + 1]
        total_ref[...] = total
        return carry

    lax.fori_loop(0, steps, logit_step, 0)

    turned_tops = tops[...].T[0 : heads * steps]
    turned_sums = sums[...].T[0 : heads * steps]
    tops_ref[...] = turned_tops
    for k in range(0, keys, rows):
        logits_ref[k : k + rows] = total_ref[:, k : k + rows].T * (1.0 / math.sqrt(depth))
    logits = logits_ref[...]
    ltop = jnp.max(logits, axis=0, keepdims=True)
    lsum = jnp.sum(jnp.exp(logits - ltop), axis=0, keepdims=True)
    flat = []
    for h in range(heads):
        span = slice(h * steps, (h + 1) * steps)
        top = jnp.max(turned_tops[span], axis=0, keepdims=True)
        scaled = turned_sums[span] * jnp.exp2((turned_tops[span] - top) * SCORE2)
        flat.append((top, jnp.sum(scaled, axis=0, keepdims=True)))
    flat = jnp.concatenate([top for top, _ in flat] + [total for _, total in flat], axis=0)
    for z in range(send_ref.shape[0]):
        send_ref[z, 0 : 2 * heads] = flat
        send_ref[z, 2 * heads :] = jnp.zeros((8, rows), jnp.float32)
        send_ref[z, 2 * heads : 2 * heads + 1] = ltop
        send_ref[z, 2 * heads + 1 : 2 * heads + 2] = lsum
    for step in range(steps):
        terms_copy(step).wait()


def scores_and_logits(queries, cache, index_query, index_keys, weights, key_count):
    heads, width, rows = queries.shape
    blocks, _, keys = cache.shape
    _, iheads, depth = index_query.shape
    steps = blocks // PART
    return call(
        scores_kernel,
        "scores_and_logits",
        60,
        in_specs=[HBM] * 5,
        out_specs=[HBM] + [VMEM] * 4,
        out_shape=(
            bf16(blocks, heads, rows, keys),
            f32(heads * steps, rows),
            f32(key_count, 2 * heads + 8, rows),
            f32(keys, rows),
            bf16(iheads, rows, depth),
        ),
        scratch_shapes=[
            pltpu.VMEM((blocks, heads, rows, keys), jnp.bfloat16),
            pltpu.VMEM(queries.shape, jnp.bfloat16),
            pltpu.VMEM(cache.shape, jnp.bfloat16),
            pltpu.VMEM(index_query.shape, jnp.bfloat16),
            pltpu.VMEM(index_keys.shape, jnp.bfloat16),
            pltpu.VMEM(weights.shape, jnp.float32),
            pltpu.VMEM((rows * iheads, depth), jnp.float32),
            pltpu.VMEM((rows, keys), jnp.float32),
            pltpu.VMEM((rows * heads, width), jnp.bfloat16),
            pltpu.VMEM((rows, LANES), jnp.float32),
            pltpu.VMEM((rows, LANES), jnp.float32),
            pltpu.SemaphoreType.DMA((steps + 4,)),
            pltpu.SemaphoreType.DMA((steps,)),
        ],
    )(queries, cache, index_query, index_keys, weights)


def headsum_kernel(offsets, e_hbm, tops_ref, got_ref, *refs):
    outs, e_ref, sums, sems, out_sems = refs[0 : len(offsets)], *refs[len(offsets) :]
    _, heads, rows, keys = e_ref.shape
    steps = tops_ref.shape[0] // heads
    near, _, near_stride, far_stride = position()

    def block_of(d, k):
        return lax.rem(near + d, RING) * near_stride + k * far_stride

    def block_copy(i, d, k):
        slot = i * RING + k
        return pltpu.make_async_copy(e_hbm.at[block_of(d, k)], e_ref.at[slot], sems.at[slot])

    def out_copy(i, k):
        slot = i * RING + k
        return pltpu.make_async_copy(sums.at[slot], outs[i].at[k], out_sems.at[slot])

    for i, d in enumerate(offsets):
        for k in range(RING):
            block_copy(i, d, k).start()

    tops = got_ref[:, 0:heads]
    top = jnp.max(tops, axis=0)
    total = jnp.sum(got_ref[:, heads : 2 * heads] * jnp.exp2((tops - top[None]) * SCORE2), axis=0)
    scale = (1.0 / MH) / total
    weights = []
    for h in range(heads):
        local = tops_ref[h * steps : (h + 1) * steps] - top[h : h + 1]
        weights.append(jnp.exp2(jnp.minimum(local * SCORE2, 0.0)) * scale[h : h + 1])
    weights = jnp.concatenate(weights + [jnp.zeros((LANES - heads * steps, rows), jnp.float32)], axis=0).T
    ltops = got_ref[:, 2 * heads : 2 * heads + 1]
    ltop = jnp.max(ltops, axis=0)
    lsum = jnp.sum(got_ref[:, 2 * heads + 1 : 2 * heads + 2] * jnp.exp(ltops - ltop[None]), axis=0)
    tail = jnp.concatenate([ltop, lsum, jnp.zeros((6, rows), jnp.float32)], axis=0)
    tail = jnp.concatenate([tail, jnp.zeros((8, keys - rows), jnp.float32)], axis=1)

    for i, d in enumerate(offsets):

        def body(k, carry):
            slot = i * RING + k
            columns = pltpu.roll(weights, LANES - lax.div(block_of(d, k), PART), 1)
            block_copy(i, d, k).wait()
            total = None
            for h in range(heads):
                term = e_ref[slot, h].astype(jnp.float32) * columns[:, h * steps : h * steps + 1]
                total = term if total is None else total + term
            sums[slot, 0:rows] = total
            sums[slot, rows:] = tail
            out_copy(i, k).start()
            return carry

        lax.fori_loop(0, RING, body, 0)
    for i, _ in enumerate(offsets):
        for k in range(RING):
            out_copy(i, k).wait()


def head_sum(offsets, terms, tops, got, flops=0):
    blocks, heads, rows, keys = terms.shape
    slots = len(offsets) * RING
    return call(
        functools.partial(headsum_kernel, offsets),
        "head_sum",
        56,
        flops,
        in_specs=[HBM] + [VMEM] * 2,
        out_specs=[HBM] * len(offsets),
        out_shape=[f32(blocks // RING, rows + 8, keys)] * len(offsets),
        scratch_shapes=[
            pltpu.VMEM((slots, heads, rows, keys), jnp.bfloat16),
            pltpu.VMEM((slots, rows + 8, keys), jnp.float32),
            pltpu.SemaphoreType.DMA((slots,)),
            pltpu.SemaphoreType.DMA((slots,)),
        ],
    )(terms, tops, got)


def merged_stats(tops, sums):
    top = tops[0]
    for other in tops[1:]:
        top = jnp.maximum(top, other)
    total = sums[0] * jnp.exp(tops[0] - top)
    for other, count in zip(tops[1:], sums[1:]):
        total = total + count * jnp.exp(other - top)
    return top, total


def partial_kernel(*refs):
    got, outs = refs[0:RING], refs[RING:]
    rows = outs[0].shape[0] - 8
    _, far, _, _ = position()
    top, total = merged_stats([r[0, rows : rows + 1] for r in got], [r[0, rows + 1 : rows + 2] for r in got])
    for d in range(RING):
        k = lax.rem(far + d, RING)
        outs[d][0:rows] = got[0][k, 0:rows] + got[1][k, 0:rows] + (got[2][k, 0:rows] + got[3][k, 0:rows])
        outs[d][rows:] = jnp.zeros_like(outs[d][rows:])
        outs[d][rows : rows + 1] = top
        outs[d][rows + 1 : rows + 2] = total


def partial_sum(got):
    _, height, keys = got[0].shape
    return call(
        partial_kernel,
        "partial_sum",
        in_specs=[VMEM] * RING,
        out_specs=[VMEM] * RING,
        out_shape=[f32(height, keys)] * RING,
    )(*got)


GROUP = 8


def dlogits_kernel(key_total, *refs):
    got = refs[0:RING]
    logits_ref, qh_ref, k_ref, send_ref, turned = refs[RING:]
    heads, rows, depth = qh_ref.shape
    keys = k_ref.shape[0]
    root = 1.0 / math.sqrt(depth)

    ltop, lsum = merged_stats(
        [r[rows : rows + 1, 0:rows] for r in got], [r[rows + 1 : rows + 2, 0:rows] for r in got]
    )
    target = got[0][0:rows] + got[1][0:rows] + (got[2][0:rows] + got[3][0:rows])
    soft = jnp.exp(logits_ref[...] - ltop) * (1.0 / lsum)
    for k in range(0, keys, rows):
        turned[k : k + rows] = key_total * (soft[k : k + rows] - target[:, k : k + rows].T)
        send_ref[0:rows, k : k + rows] = turned[k : k + rows].T
        send_ref[rows + heads // 2 :, k : k + rows] = k_ref[k : k + rows].astype(jnp.float32)

    def step(i, first, column):
        sums = []
        for j in range(GROUP):
            products = dot(k_ref[...], qh_ref[i * GROUP + j], NT)
            sums.append(jnp.sum(jnp.maximum(products, 0.0) * turned[...], axis=0, keepdims=True) * root)
        place = pl.ds(pl.multiple_of(rows + first, GROUP), GROUP)
        send_ref[place, column : column + rows] = jnp.concatenate(sums, axis=0)

    half = heads // 2 // GROUP

    def low(i, carry):
        step(i, i * GROUP, 0)
        return carry

    def high(i, carry):
        step(i + half, i * GROUP, rows)
        return carry

    lax.fori_loop(0, half, low, 0)
    lax.fori_loop(0, half, high, 0)


def dlogits_of(got, logits, qh, index_keys, key_total):
    heads, rows, depth = qh.shape
    keys = index_keys.shape[0]
    return call(
        functools.partial(dlogits_kernel, key_total),
        "dlogits",
        24,
        out_shape=f32(2 * rows + heads // 2, keys),
        scratch_shapes=[pltpu.VMEM((keys, rows), jnp.float32)],
    )(*got, logits, qh, index_keys)


def keys_kernel(dlogits_ref, qh_ref, k_ref, w_ref, keys_ref, slopes, turned):
    heads, rows, depth = qh_ref.shape
    root = 1.0 / math.sqrt(depth)
    for k in range(0, k_ref.shape[0], rows):
        turned[k : k + rows] = dlogits_ref[0:rows, k : k + rows].T
    keys_ref[...] = jnp.zeros_like(keys_ref)

    def step(i, carry):
        weights = w_ref[pl.ds(i * GROUP, GROUP)] * root
        for j in range(GROUP):
            products = dot(k_ref[...], qh_ref[i * GROUP + j], NT)
            slope = jnp.where(products > 0.0, turned[...] * weights[j : j + 1], 0.0)
            slopes[:, j * rows : (j + 1) * rows] = slope.astype(jnp.bfloat16)
        chunk = qh_ref[pl.ds(i * GROUP, GROUP)].reshape(GROUP * rows, depth)
        keys_ref[...] += dot(slopes[...], chunk, NN)
        return carry

    lax.fori_loop(0, heads // GROUP, step, 0)


def key_gradient(dlogits, qh, index_keys, weights):
    heads, rows, depth = qh.shape
    keys = index_keys.shape[0]
    return call(
        keys_kernel,
        "key_gradient",
        24,
        BESIDE,
        out_shape=f32(keys, depth),
        scratch_shapes=[pltpu.VMEM((keys, GROUP * rows), jnp.bfloat16), pltpu.VMEM((keys, rows), jnp.float32)],
    )(dlogits, qh, index_keys, weights)


def query_kernel(offsets, pieces, *refs):
    ring, count = RING, len(offsets)
    got = refs[0:ring]
    qh_ref, w_ref = refs[ring : ring + 2]
    outs = refs[ring + 2 : ring + 2 + count]
    slopes, acc, near, dlogits = refs[ring + 2 + count :]
    heads, rows, depth = qh_ref.shape
    keys = got[0].shape[1]
    share = heads // (ring * ring)
    extra = heads // 2
    root = 1.0 / math.sqrt(depth)
    near_at, far_at, near_stride, far_stride = position()
    span = rows // pieces
    few = extra // pieces

    wsum = got[0][rows : rows + extra]
    for d in range(1, ring):
        wsum = wsum + got[d][rows : rows + extra]
    for d in range(ring):
        for k in range(0, keys, rows):
            near[d * keys + k : d * keys + k + rows] = got[d][rows + extra :, k : k + rows].astype(jnp.bfloat16)
        dlogits[:, d * keys : (d + 1) * keys] = got[d][0:rows] * root
    columns = jnp.concatenate([w_ref[...], jnp.zeros((LANES - heads, rows), jnp.float32)], axis=0).T

    for i, d in enumerate(offsets):
        first = (lax.rem(far_at + d, ring) * far_stride + near_at * near_stride) * share
        weights = pltpu.roll(columns, LANES - first, 1)
        queries = qh_ref[pl.ds(first, share)].reshape(share * rows, depth)
        for k in range(0, ring * keys, keys):
            products = dot(queries, near[k : k + keys], NT)
            for j in range(share):
                part = products[j * rows : (j + 1) * rows]
                slope = jnp.where(part > 0.0, dlogits[:, k : k + keys] * weights[:, j : j + 1], 0.0)
                slopes[j * rows : (j + 1) * rows, k : k + keys] = slope.astype(jnp.bfloat16)
        acc[...] = dot(slopes[...], near[...], NN)
        for z in range(pieces):
            for j in range(share):
                start = j * rows + z * span
                outs[i][z, pl.ds(j, span, stride=share), :] = acc[start : start + span]
            piece = wsum[z * few : (z + 1) * few]
            outs[i][z, share * span : share * span + few] = piece[:, 0:rows]
            outs[i][z, share * span + few :] = piece[:, rows : 2 * rows]


def query_gradient(offsets, got, qh, weights, pieces, flops=0):
    keys = got[0].shape[1]
    heads, rows, depth = qh.shape
    share = heads // (RING * RING)
    tall = share * (rows // pieces) + heads // pieces
    return call(
        functools.partial(query_kernel, offsets, pieces),
        "query_gradient",
        24,
        flops,
        in_specs=[VMEM] * (RING + 2),
        out_specs=[VMEM] * len(offsets),
        out_shape=[f32(pieces, tall, depth)] * len(offsets),
        scratch_shapes=[
            pltpu.VMEM((share * rows, RING * keys), jnp.bfloat16),
            pltpu.VMEM((share * rows, depth), jnp.float32),
            pltpu.VMEM((RING * keys, depth), jnp.bfloat16),
            pltpu.VMEM((rows, RING * keys), jnp.float32),
        ],
    )(*got, qh, weights)


def results_kernel(got_ref, query_ref, weight_ref):
    pieces, tall, depth = got_ref.shape
    span = query_ref.shape[1]
    few = (tall - span) // 2
    query_ref[...] = got_ref[:, 0:span]
    for z in range(pieces):
        weight_ref[z * few : (z + 1) * few] = got_ref[z, span : span + few]
        weight_ref[(pieces + z) * few : (pieces + z + 1) * few] = got_ref[z, span + few :]


def results(got, heads, span):
    pieces, _, depth = got.shape
    return call(
        results_kernel,
        "results",
        16,
        out_shape=(f32(pieces, span, depth), f32(heads, depth)),
    )(got)


def exchange(x, axis):
    return lax.all_to_all(x, axis, split_axis=0, concat_axis=0, tiled=True)


def shift(x, d, across):
    pairs = []
    for a in range(RING):
        for b in range(RING):
            for row in range(2):
                if (row == 1) != across:
                    there = (a + d) % RING * RING + b
                else:
                    there = a * RING + (b + d) % RING
                pairs.append(((a * RING + b) * 2 + row, there * 2 + row))
    return lax.ppermute(x, ("head", "row"), pairs)


def shards(mla_query, mla_cache, index_query, index_keys, index_weight):
    key_count = lax.axis_size("key")
    head_count = lax.axis_size("head")
    rows = mla_query.shape[0]
    keys, depth = index_keys.shape
    heads = index_query.shape[1]
    share = heads // head_count
    row_index = lax.axis_index("row")
    weights = index_weight.T
    queries = jnp.transpose(mla_query, (1, 2, 0))
    cache = jnp.swapaxes(mla_cache, 1, 2)
    terms, tops, send1, logits, qh = scores_and_logits(queries, cache, index_query, index_keys, weights, key_count)
    got1 = exchange(send1, "key")
    sides = head_sum((1, 3), terms, tops, got1)
    rest = head_sum((2, 0), terms, tops, got1)
    got2 = [rest[1], shift(sides[0], 1, False), shift(rest[0], 2, False), shift(sides[1], 3, False)]
    send2 = partial_sum(got2)
    got2 = [send2[0]] + [shift(send2[d], d, True) for d in (1, 2, 3)]
    key_total = float(keys * head_count * key_count)
    send3 = dlogits_of(got2, logits, qh, index_keys, key_total)
    got3 = [send3] + [shift(send3, d, False) for d in range(1, RING)]
    keys_part = key_gradient(send3, qh, index_keys, weights)
    got3, keys_part = lax.optimization_barrier((got3, keys_part))

    half = keys // 2
    away = lax.dynamic_slice_in_dim(keys_part, (1 - row_index) * half, half, 0)
    near = lax.dynamic_slice_in_dim(keys_part, row_index * half, half, 0)
    key_grad = near + lax.ppermute(away, "row", [(0, 1), (1, 0)])

    sides = query_gradient((1, 3), got3, qh, weights, key_count)
    rest = query_gradient((2, 0), got3, qh, weights, key_count)
    one, three, two = shift(sides[0], 1, True), shift(sides[1], 3, True), shift(rest[0], 2, True)
    send4 = rest[1] + one + (two + three)
    got4 = jnp.sum(exchange(send4, "key"), axis=0)
    got5 = exchange(jnp.broadcast_to(got4[None], (key_count, *got4.shape)), "key")
    query_grad, weight_grad = results(got5, heads, share * (rows // key_count))
    return (query_grad.reshape(rows, share, depth), key_grad, weight_grad.T)


def solution(mesh):
    placed = (
        P("row", "head", None),
        P(None, "key", None),
        P("row", None, None),
        P(("head", "key"), None),
        P("row", None),
    )
    return jax.shard_map(
        shards,
        mesh=mesh,
        in_specs=placed,
        out_specs=(P("row", "head", None), P(("head", "key", "row"), None), P("row", None)),
        check_vma=False,
    )
```

time: 145 us -> 132 us (0.910)
  waiting for transfers between devices: 38 us -> 34.1 us
  starting transfers between devices: 29 us -> 25.3 us
  blocking collectives: 32.1 us -> 29.2 us
  Pallas kernels: 39.9 us -> 38.4 us
    ppermute x15 -> x12, waiting for transfers between devices: 29.4 us -> 25.5 us  [shift(): return lax.ppermute(x, ('head', 'row'), pairs)]
    ppermute x15 -> x12, starting transfers between devices: 23.9 us -> 20.4 us  [shift(): return lax.ppermute(x, ('head', 'row'), pairs)]
    all_to_all x2, blocking collectives: 32.1 us -> 29.2 us  [exchange(): return lax.all_to_all(x, axis, split_axis=0, concat_axis=0, tiled=True)]
    pallas_call x6 -> x7, Pallas kernels: 18.5 us -> 18.2 us  [the longest x2 10.4 us: head_sum(): call(functools.partial(headsum_kernel, offsets), 'head_sum', 56, flops, i...]
  transfers between devices with their start and end apart: 17 -> 14, of which waited for: 11 -> 12; matrix products, arithmetic and copies ran while one was open for 0% -> 0% of each run, Pallas kernels for 7% -> 7%
where the time goes in v5:
time: 132 us; the launch traced here: 130 us
  Pallas kernels  38.4 us (29%)
  waiting for transfers between devices  34.1 us (26%)
  blocking collectives  29.2 us (22%)
  starting transfers between devices  25.3 us (19%)
  local copies, waits for them, and re-layouts  1.81 us (1%)
    all_to_all x2, blocking collectives, exchange(): return lax.all_to_all(x, axis, split_axis=0, concat_axis=0, tiled=True)  29.2 us
    ppermute x12, waiting for transfers between devices, shift(): return lax.ppermute(x, ('head', 'row'), pairs)  25.5 us
    ppermute x12, starting transfers between devices, shift(): return lax.ppermute(x, ('head', 'row'), pairs)  20.4 us
    pallas_call x1, Pallas kernels, scores_and_logits(): call(scores_kernel, 'scores_and_logits', 60, in_specs=[HBM] * 5, out_spec...  17.5 us
    pallas_call x2, Pallas kernels, head_sum(): call(functools.partial(headsum_kernel, offsets), 'head_sum', 56, flops, i...  10.4 us
    all_to_all x1, waiting for transfers between devices, exchange(): return lax.all_to_all(x, axis, split_axis=0, concat_axis=0, tiled=True)  7.41 us
    all_to_all x1, starting transfers between devices, exchange(): return lax.all_to_all(x, axis, split_axis=0, concat_axis=0, tiled=True)  4.76 us
    pallas_call x1, Pallas kernels, key_gradient(): call(keys_kernel, 'key_gradient', 24, BESIDE, out_shape=f32(keys, depth),...  4 us
  transfers between devices with their start and end apart: 14, of which 12 were waited for; matrix products, arithmetic and copies ran while one was open for 0% of the time, Pallas kernels for 7%

profile of v5, /device:TPU:32, one launch (start us, length us, event | category | flops | bytes accessed | tf_op | source)
XLA Modules:
  0.0 130.2 jit_solution(1363057547128937103)
XLA Ops:
  0.6 17.5 %scores_and_logits.1 = (bf16[16,8,128,256]{3,2,1,0:T(8,128)(2,1)}, f32[64,128]{1,0:T(8,128)}, f32[8,24,128]{2,1,0:T(8,128)}, f32[256,128]{1,0:T(8,128)}, bf16[64,128,128]{2,1,0:T(8,128)(2,1)}) custom-call(bf16[8,576,128]{2,1,0:T(8,128)(2,1)} %bitcast.10, bf16[16,576,256]{2,1,0:T(8,128)(2,1)} %bitcast.9, bf16[128,64,128]{2,1,0:T(8,128)(2,1)} %iq_hbm.1, ...), custom_call_target="tpu_custom_call" | custom-call | tf_op jit(solution)/shard_map/scores_and_logits/pallas_call | solution.py:171
  18.2 15.8 %all_to_all.15.got_ref = f32[8,24,128]{2,1,0:T(8,128)} all-to-all(f32[8,24,128]{2,1,0:T(8,128)} %get-tuple-element.29), channel_id=1, replica_groups=mesh['head'=16,'key'=8,'row'=2] {'key'}, dimensions={0} | all-to-all | bytes 196608 | tf_op jit(solution)/shard_map/all_to_all | solution.py:487
  34.0 5.2 %head_sum.3 = (f32[4,136,256]{2,1,0:T(8,128)}, f32[4,136,256]{2,1,0:T(8,128)}) custom-call(bf16[16,8,128,256]{3,2,1,0:T(8,128)(2,1)} %get-tuple-element.27.e_hbm, f32[64,128]{1,0:T(8,128)} %get-tuple-element.28.tops_ref, f32[8,24,128]{2,1,0:T(8,128)} %all_to_all.15.got_ref), custom_call_target="tpu_custom_call" | custom-call | tf_op jit(solution)/shard_map/head_sum/pallas_call | solution.py:262
  39.2 1.7 %collective-permute-start = (f32[4,136,256]{2,1,0:T(8,128)}, f32[4,136,256]{2,1,0:T(8,128)S(1)}, u32[]{:S(2)}, u32[]{:S(2)}) collective-permute-start(f32[4,136,256]{2,1,0:T(8,128)} %get-tuple-element.31), channel_id=1, source_target_pairs={{0,16},{1,65},{16,32},{17,81},{32,48},{33,97},{48,0},{49,113},{64,... | collective-permute-start | bytes 1671176 | tf_op jit(solution)/shard_map/ppermute | solution.py:500
  40.8 1.7 %collective-permute-start.2 = (f32[4,136,256]{2,1,0:T(8,128)}, f32[4,136,256]{2,1,0:T(8,128)S(1)}, u32[]{:S(2)}, u32[]{:S(2)}) collective-permute-start(f32[4,136,256]{2,1,0:T(8,128)} %get-tuple-element.33), channel_id=1, source_target_pairs={{0,48},{1,193},{16,0},{17,209},{32,16},{33,225},{48,32},{49,241},{... | collective-permute-start | bytes 1671176 | tf_op jit(solution)/shard_map/ppermute | solution.py:500
  42.5 5.2 %head_sum.2 = (f32[4,136,256]{2,1,0:T(8,128)}, f32[4,136,256]{2,1,0:T(8,128)}) custom-call(bf16[16,8,128,256]{3,2,1,0:T(8,128)(2,1)} %get-tuple-element.27.e_hbm, f32[64,128]{1,0:T(8,128)} %get-tuple-element.28.tops_ref, f32[8,24,128]{2,1,0:T(8,128)} %all_to_all.15.got_ref), custom_call_target="tpu_custom_call" | custom-call | tf_op jit(solution)/shard_map/head_sum/pallas_call | solution.py:262
  47.7 0.0 copy-start
  47.7 2.1 %collective-permute-start.1 = (f32[4,136,256]{2,1,0:T(8,128)}, f32[4,136,256]{2,1,0:T(8,128)S(1)}, u32[]{:S(2)}, u32[]{:S(2)}) collective-permute-start(f32[4,136,256]{2,1,0:T(8,128)} %get-tuple-element.32), channel_id=1, source_target_pairs={{0,32},{1,129},{16,48},{17,145},{32,0},{33,161},{48,16},{49,177},{... | collective-permute-start | bytes 1671176 | tf_op jit(solution)/shard_map/ppermute | solution.py:500
  49.8 0.4 collective-permute-done.refs_1_
  50.2 0.4 collective-permute-done.2.refs_3_
  50.6 8.5 %collective-permute-done.1.refs_2_ = f32[4,136,256]{2,1,0:T(8,128)S(1)} collective-permute-done((f32[4,136,256]{2,1,0:T(8,128)}, f32[4,136,256]{2,1,0:T(8,128)S(1)}, u32[]{:S(2)}, u32[]{:S(2)}) %collective-permute-start.1) | collective-permute-done | bytes 557088 | tf_op jit(solution)/shard_map/ppermute | solution.py:500
  59.1 1.1 copy-done.1
  60.1 0.1 partial_sum.1
  60.3 0.0 copy-start.2
  60.3 1.6 %collective-permute-start.3 = (f32[136,256]{1,0:T(8,128)S(1)}, f32[136,256]{1,0:T(8,128)S(1)}, u32[]{:S(2)}, u32[]{:S(2)}) collective-permute-start(f32[136,256]{1,0:T(8,128)S(1)} %get-tuple-element.35), channel_id=1, source_target_pairs={{0,64},{1,17},{16,80},{17,33},{32,96},{33,49},{48,112},{49,1},{64,... | collective-permute-start | bytes 417800 | tf_op jit(solution)/shard_map/ppermute | solution.py:500
  61.8 2.7 %collective-permute-start.4 = (f32[136,256]{1,0:T(8,128)S(1)}, f32[136,256]{1,0:T(8,128)S(1)}, u32[]{:S(2)}, u32[]{:S(2)}) collective-permute-start(f32[136,256]{1,0:T(8,128)S(1)} %get-tuple-element.36), channel_id=1, source_target_pairs={{0,128},{1,33},{16,144},{17,49},{32,160},{33,1},{48,176},{49,17},{... | collective-permute-start | bytes 417800 | tf_op jit(solution)/shard_map/ppermute | solution.py:500
  64.6 1.4 %collective-permute-start.5 = (f32[136,256]{1,0:T(8,128)S(1)}, f32[136,256]{1,0:T(8,128)S(1)}, u32[]{:S(2)}, u32[]{:S(2)}) collective-permute-start(f32[136,256]{1,0:T(8,128)S(1)} %get-tuple-element.37), channel_id=1, source_target_pairs={{0,192},{1,49},{16,208},{17,1},{32,224},{33,17},{48,240},{49,33},{... | collective-permute-start | bytes 417800 | tf_op jit(solution)/shard_map/ppermute | solution.py:500
  66.0 0.6 collective-permute-done.3.refs_1_
  66.6 2.5 %collective-permute-done.4.refs_2_ = f32[136,256]{1,0:T(8,128)S(1)} collective-permute-done((f32[136,256]{1,0:T(8,128)S(1)}, f32[136,256]{1,0:T(8,128)S(1)}, u32[]{:S(2)}, u32[]{:S(2)}) %collective-permute-start.4) | collective-permute-done | bytes 139296 | tf_op jit(solution)/shard_map/ppermute | solution.py:500
  69.1 0.5 collective-permute-done.5.refs_3_
  69.6 0.0 copy-done.3
  69.6 0.0 copy-done.4
  69.6 2.7 %dlogits.1.dlogits_ref.refs_0_ = f32[288,256]{1,0:T(8,128)S(1)} custom-call(f32[136,256]{1,0:T(8,128)S(1)} %get-tuple-element.34.refs_0_, f32[136,256]{1,0:T(8,128)S(1)} %collective-permute-done.3.refs_1_, f32[136,256]{1,0:T(8,128)S(1)} %collective-permute-done.4.refs_2_, f32[136,256]{1,0:T(8,128)S(1)} %collective-permute-done.5.refs_3_, ...), custom_call_target="tpu_custom_call" | custom-call | tf_op jit(solution)/shard_map/dlogits/pallas_call | solution.py:358
  72.3 0.4 collective-permute-start.6
  72.8 2.9 %collective-permute-start.7 = (f32[288,256]{1,0:T(8,128)S(1)}, f32[288,256]{1,0:T(8,128)S(1)}, u32[]{:S(2)}, u32[]{:S(2)}) collective-permute-start(f32[288,256]{1,0:T(8,128)S(1)} %dlogits.1.dlogits_ref.refs_0_), channel_id=1, source_target_pairs={{0,32},{1,129},{16,48},{17,145},{32,0},{33,161},{48,16},{49,177},{... | collective-permute-start | bytes 884744 | tf_op jit(solution)/shard_map/ppermute | solution.py:500
  75.7 1.3 %collective-permute-start.8 = (f32[288,256]{1,0:T(8,128)S(1)}, f32[288,256]{1,0:T(8,128)S(1)}, u32[]{:S(2)}, u32[]{:S(2)}) collective-permute-start(f32[288,256]{1,0:T(8,128)S(1)} %dlogits.1.dlogits_ref.refs_0_), channel_id=1, source_target_pairs={{0,48},{1,193},{16,0},{17,209},{32,16},{33,225},{48,32},{49,241},{... | collective-permute-start | bytes 884744 | tf_op jit(solution)/shard_map/ppermute | solution.py:500
  77.0 0.0 copy-done.2
  77.0 4.0 %key_gradient.1 = f32[256,128]{1,0:T(8,128)S(1)} custom-call(f32[288,256]{1,0:T(8,128)S(1)} %dlogits.1.dlogits_ref.refs_0_, bf16[64,128,128]{2,1,0:T(8,128)(2,1)S(1)} %copy-done, bf16[256,128]{1,0:T(8,128)(2,1)S(1)} %copy-done.3, f32[64,128]{1,0:T(8,128)S(1)} %bitcast.6), custom_call_target="tpu_custom_call" | custom-call | flops 4000000000 | tf_op jit(solution)/shard_map/key_gradient/pallas_call | solution.py:390
  81.0 0.0 collective-permute-done.6.refs_1_
  81.0 2.5 %collective-permute-done.7.refs_2_ = f32[288,256]{1,0:T(8,128)S(1)} collective-permute-done((f32[288,256]{1,0:T(8,128)S(1)}, f32[288,256]{1,0:T(8,128)S(1)}, u32[]{:S(2)}, u32[]{:S(2)}) %collective-permute-start.7) | collective-permute-done | bytes 294944 | tf_op jit(solution)/shard_map/ppermute | solution.py:500
  83.5 0.9 collective-permute-done.8.refs_3_
  84.4 1.5 %query_gradient.3 = (f32[8,72,128]{2,1,0:T(8,128)S(1)}, f32[8,72,128]{2,1,0:T(8,128)S(1)}) custom-call(f32[288,256]{1,0:T(8,128)S(1)} %dlogits.1.dlogits_ref.refs_0_, f32[288,256]{1,0:T(8,128)S(1)} %collective-permute-done.6.refs_1_, f32[288,256]{1,0:T(8,128)S(1)} %collective-permute-done.7.refs_2_, f32[288,256]{1,0:T(8,128)S(1)} %collective-permute-done.8.refs_3_, ...), custom_call_target="tpu_custom_call" | custom-call | tf_op jit(solution)/shard_map/query_gradient/pallas_call | solution.py:449
  85.9 1.5 %query_gradient.2 = (f32[8,72,128]{2,1,0:T(8,128)S(1)}, f32[8,72,128]{2,1,0:T(8,128)S(1)}) custom-call(f32[288,256]{1,0:T(8,128)S(1)} %dlogits.1.dlogits_ref.refs_0_, f32[288,256]{1,0:T(8,128)S(1)} %collective-permute-done.6.refs_1_, f32[288,256]{1,0:T(8,128)S(1)} %collective-permute-done.7.refs_2_, f32[288,256]{1,0:T(8,128)S(1)} %collective-permute-done.8.refs_3_, ...), custom_call_target="tpu_custom_call" | custom-call | tf_op jit(solution)/shard_map/query_gradient/pallas_call | solution.py:449
  87.3 2.7 %collective-permute-start.11 = (f32[8,72,128]{2,1,0:T(8,128)S(1)}, f32[8,72,128]{2,1,0:T(8,128)S(1)}, u32[]{:S(2)}, u32[]{:S(2)}) collective-permute-start(f32[8,72,128]{2,1,0:T(8,128)S(1)} %get-tuple-element.47), channel_id=1, source_target_pairs={{0,192},{1,49},{16,208},{17,1},{32,224},{33,17},{48,240},{49,33},{... | collective-permute-start | bytes 884744 | tf_op jit(solution)/shard_map/ppermute | solution.py:500
  90.1 0.0 collective-permute-start.9
  90.1 1.9 %collective-permute-start.10 = (f32[8,72,128]{2,1,0:T(8,128)S(1)}, f32[8,72,128]{2,1,0:T(8,128)S(1)}, u32[]{:S(2)}, u32[]{:S(2)}) collective-permute-start(f32[8,72,128]{2,1,0:T(8,128)S(1)} %get-tuple-element.46), channel_id=1, source_target_pairs={{0,128},{1,33},{16,144},{17,49},{32,160},{33,1},{48,176},{49,17},{... | collective-permute-start | bytes 884744 | tf_op jit(solution)/shard_map/ppermute | solution.py:500
  91.9 2.4 %collective-permute-done.11 = f32[8,72,128]{2,1,0:T(8,128)S(1)} collective-permute-done((f32[8,72,128]{2,1,0:T(8,128)S(1)}, f32[8,72,128]{2,1,0:T(8,128)S(1)}, u32[]{:S(2)}, u32[]{:S(2)}) %collective-permute-start.11) | collective-permute-done | bytes 294944 | tf_op jit(solution)/shard_map/ppermute | solution.py:500
  94.3 6.9 %collective-permute-done.9 = f32[8,72,128]{2,1,0:T(8,128)S(1)} collective-permute-done((f32[8,72,128]{2,1,0:T(8,128)S(1)}, f32[8,72,128]{2,1,0:T(8,128)S(1)}, u32[]{:S(2)}, u32[]{:S(2)}) %collective-permute-start.9) | collective-permute-done | bytes 294944 | tf_op jit(solution)/shard_map/ppermute | solution.py:500
  101.1 0.0 collective-permute-done.10
  101.1 0.1 add_add_fusion
  101.2 13.4 %all_to_all.16 = f32[8,72,128]{2,1,0:T(8,128)S(1)} all-to-all(f32[8,72,128]{2,1,0:T(8,128)S(1)} %add_add_fusion), channel_id=1, replica_groups=mesh['head'=16,'key'=8,'row'=2] {'key'}, dimensions={0} | all-to-all | bytes 589824 | tf_op jit(solution)/shard_map/all_to_all | solution.py:487
  114.6 0.7 broadcast_in_dim.2
  115.3 4.8 %all-to-all-start.2 = ((f32[8,72,128]{2,1,0:T(8,128)}), f32[8,72,128]{2,1,0:T(8,128)S(1)}, u32[]{:S(2)}, u32[]{:S(2)}) async-start(f32[8,72,128]{2,1,0:T(8,128)} %broadcast_in_dim.2), calls=%async_computation.2 | async-start | bytes 589824 | tf_op jit(solution)/shard_map/all_to_all | solution.py:487
  120.1 0.1 collective-permute-start.12
  120.2 1.2 collective-permute-done.12
  121.4 0.6 dynamic-slice_add_fusion
  122.1 7.4 %all-to-all-done.2.got_ref = f32[8,72,128]{2,1,0:T(8,128)S(1)} async-done(((f32[8,72,128]{2,1,0:T(8,128)}), f32[8,72,128]{2,1,0:T(8,128)S(1)}, u32[]{:S(2)}, u32[]{:S(2)}) %all-to-all-start.2) | async-done | bytes 294944 | tf_op jit(solution)/shard_map/all_to_all | solution.py:487
  129.5 0.7 results.1
  (6 shorter events, 0.0 us)
Async XLA Ops:
  39.2 11.0 %collective-permute-start = (f32[4,136,256]{2,1,0:T(8,128)}, f32[4,136,256]{2,1,0:T(8,128)S(1)}, u32[]{:S(2)}, u32[]{:S(2)}) collective-permute-start(f32[4,136,256]{2,1,0:T(8,128)} %get-tuple-element.31), channel_id=1, source_target_pairs={{0,16},{1,65},{16,32},{17,81},{32,48},{33,97},{48,0},{49,113},{64,... | collective-permute-start | bytes 1671176 | tf_op jit(solution)/shard_map/ppermute | solution.py:500
  40.8 9.7 %collective-permute-start.2 = (f32[4,136,256]{2,1,0:T(8,128)}, f32[4,136,256]{2,1,0:T(8,128)S(1)}, u32[]{:S(2)}, u32[]{:S(2)}) collective-permute-start(f32[4,136,256]{2,1,0:T(8,128)} %get-tuple-element.33), channel_id=1, source_target_pairs={{0,48},{1,193},{16,0},{17,209},{32,16},{33,225},{48,32},{49,241},{... | collective-permute-start | bytes 1671176 | tf_op jit(solution)/shard_map/ppermute | solution.py:500
  42.5 27.1 %copy-start.3 = (bf16[256,128]{1,0:T(8,128)(2,1)S(1)}, bf16[256,128]{1,0:T(8,128)(2,1)}, u32[]{:S(2)}) copy-start(bf16[256,128]{1,0:T(8,128)(2,1)} %k_ref.1) | copy-start | bytes 196612
  42.5 27.1 %copy-start.4 = (f32[256,128]{1,0:T(8,128)S(1)}, f32[256,128]{1,0:T(8,128)}, u32[]{:S(2)}) copy-start(f32[256,128]{1,0:T(8,128)} %get-tuple-element.38.refs_4_) | copy-start | bytes 393220
  47.7 21.9 %copy-start = (bf16[64,128,128]{2,1,0:T(8,128)(2,1)S(1)}, bf16[64,128,128]{2,1,0:T(8,128)(2,1)}, u32[]{:S(2)}) copy-start(bf16[64,128,128]{2,1,0:T(8,128)(2,1)} %get-tuple-element.39.refs_5_.qh_ref.refs_4_) | copy-start | bytes 6291460
  47.7 11.3 %collective-permute-start.1 = (f32[4,136,256]{2,1,0:T(8,128)}, f32[4,136,256]{2,1,0:T(8,128)S(1)}, u32[]{:S(2)}, u32[]{:S(2)}) collective-permute-start(f32[4,136,256]{2,1,0:T(8,128)} %get-tuple-element.32), channel_id=1, source_target_pairs={{0,32},{1,129},{16,48},{17,145},{32,0},{33,161},{48,16},{49,177},{... | collective-permute-start | bytes 1671176 | tf_op jit(solution)/shard_map/ppermute | solution.py:500
  59.1 1.1 copy-start.1
  60.3 16.8 %copy-start.2 = (f32[128,64]{0,1:T(8,128)S(1)}, f32[128,64]{0,1:T(8,128)}, u32[]{:S(2)}) copy-start(f32[128,64]{0,1:T(8,128)} %param.9) | copy-start | bytes 98308
  60.3 6.3 %collective-permute-start.3 = (f32[136,256]{1,0:T(8,128)S(1)}, f32[136,256]{1,0:T(8,128)S(1)}, u32[]{:S(2)}, u32[]{:S(2)}) collective-permute-start(f32[136,256]{1,0:T(8,128)S(1)} %get-tuple-element.35), channel_id=1, source_target_pairs={{0,64},{1,17},{16,80},{17,33},{32,96},{33,49},{48,112},{49,1},{64,... | collective-permute-start | bytes 417800 | tf_op jit(solution)/shard_map/ppermute | solution.py:500
  61.8 7.2 %collective-permute-start.4 = (f32[136,256]{1,0:T(8,128)S(1)}, f32[136,256]{1,0:T(8,128)S(1)}, u32[]{:S(2)}, u32[]{:S(2)}) collective-permute-start(f32[136,256]{1,0:T(8,128)S(1)} %get-tuple-element.36), channel_id=1, source_target_pairs={{0,128},{1,33},{16,144},{17,49},{32,160},{33,1},{48,176},{49,17},{... | collective-permute-start | bytes 417800 | tf_op jit(solution)/shard_map/ppermute | solution.py:500
  64.6 5.1 %collective-permute-start.5 = (f32[136,256]{1,0:T(8,128)S(1)}, f32[136,256]{1,0:T(8,128)S(1)}, u32[]{:S(2)}, u32[]{:S(2)}) collective-permute-start(f32[136,256]{1,0:T(8,128)S(1)} %get-tuple-element.37), channel_id=1, source_target_pairs={{0,192},{1,49},{16,208},{17,1},{32,224},{33,17},{48,240},{49,33},{... | collective-permute-start | bytes 417800 | tf_op jit(solution)/shard_map/ppermute | solution.py:500
  72.3 8.7 %collective-permute-start.6 = (f32[288,256]{1,0:T(8,128)S(1)}, f32[288,256]{1,0:T(8,128)S(1)}, u32[]{:S(2)}, u32[]{:S(2)}) collective-permute-start(f32[288,256]{1,0:T(8,128)S(1)} %dlogits.1.dlogits_ref.refs_0_), channel_id=1, source_target_pairs={{0,16},{1,65},{16,32},{17,81},{32,48},{33,97},{48,0},{49,113},{64,... | collective-permute-start | bytes 884744 | tf_op jit(solution)/shard_map/ppermute | solution.py:500
  72.8 10.8 %collective-permute-start.7 = (f32[288,256]{1,0:T(8,128)S(1)}, f32[288,256]{1,0:T(8,128)S(1)}, u32[]{:S(2)}, u32[]{:S(2)}) collective-permute-start(f32[288,256]{1,0:T(8,128)S(1)} %dlogits.1.dlogits_ref.refs_0_), channel_id=1, source_target_pairs={{0,32},{1,129},{16,48},{17,145},{32,0},{33,161},{48,16},{49,177},{... | collective-permute-start | bytes 884744 | tf_op jit(solution)/shard_map/ppermute | solution.py:500
  75.7 8.7 %collective-permute-start.8 = (f32[288,256]{1,0:T(8,128)S(1)}, f32[288,256]{1,0:T(8,128)S(1)}, u32[]{:S(2)}, u32[]{:S(2)}) collective-permute-start(f32[288,256]{1,0:T(8,128)S(1)} %dlogits.1.dlogits_ref.refs_0_), channel_id=1, source_target_pairs={{0,48},{1,193},{16,0},{17,209},{32,16},{33,225},{48,32},{49,241},{... | collective-permute-start | bytes 884744 | tf_op jit(solution)/shard_map/ppermute | solution.py:500
  87.3 7.0 %collective-permute-start.11 = (f32[8,72,128]{2,1,0:T(8,128)S(1)}, f32[8,72,128]{2,1,0:T(8,128)S(1)}, u32[]{:S(2)}, u32[]{:S(2)}) collective-permute-start(f32[8,72,128]{2,1,0:T(8,128)S(1)} %get-tuple-element.47), channel_id=1, source_target_pairs={{0,192},{1,49},{16,208},{17,1},{32,224},{33,17},{48,240},{49,33},{... | collective-permute-start | bytes 884744 | tf_op jit(solution)/shard_map/ppermute | solution.py:500
  90.1 11.1 %collective-permute-start.9 = (f32[8,72,128]{2,1,0:T(8,128)S(1)}, f32[8,72,128]{2,1,0:T(8,128)S(1)}, u32[]{:S(2)}, u32[]{:S(2)}) collective-permute-start(f32[8,72,128]{2,1,0:T(8,128)S(1)} %get-tuple-element.45), channel_id=1, source_target_pairs={{0,64},{1,17},{16,80},{17,33},{32,96},{33,49},{48,112},{49,1},{64,... | collective-permute-start | bytes 884744 | tf_op jit(solution)/shard_map/ppermute | solution.py:500
  90.1 11.1 %collective-permute-start.10 = (f32[8,72,128]{2,1,0:T(8,128)S(1)}, f32[8,72,128]{2,1,0:T(8,128)S(1)}, u32[]{:S(2)}, u32[]{:S(2)}) collective-permute-start(f32[8,72,128]{2,1,0:T(8,128)S(1)} %get-tuple-element.46), channel_id=1, source_target_pairs={{0,128},{1,33},{16,144},{17,49},{32,160},{33,1},{48,176},{49,17},{... | collective-permute-start | bytes 884744 | tf_op jit(solution)/shard_map/ppermute | solution.py:500
  115.3 14.2 %all-to-all-start.2 = ((f32[8,72,128]{2,1,0:T(8,128)}), f32[8,72,128]{2,1,0:T(8,128)S(1)}, u32[]{:S(2)}, u32[]{:S(2)}) async-start(f32[8,72,128]{2,1,0:T(8,128)} %broadcast_in_dim.2), calls=%async_computation.2 | async-start | bytes 589824 | tf_op jit(solution)/shard_map/all_to_all | solution.py:487
  120.1 1.3 %collective-permute-start.12 = (f32[128,128]{1,0:T(8,128)S(1)}, f32[128,128]{1,0:T(8,128)S(1)}, u32[]{:S(2)}, u32[]{:S(2)}) collective-permute-start(f32[128,128]{1,0:T(8,128)S(1)} %constant_dynamic-slice_fusion), channel_id=1, source_target_pairs={{0,1},{1,0},{2,3},{3,2},{4,5},{5,4},{6,7},{7,6},{8,9},{9,8},{10,11... | collective-permute-start | bytes 196616 | tf_op jit(solution)/shard_map/ppermute | solution.py:530

commit v6 on v5

--- a/solution.py
+++ b/solution.py
@@ -26,19 +26,17 @@
 
 
 RING = 4
-PART = 2
-BESIDE = 4_000_000_000
+PART = 4
+GROUP = 8
 VMEM = pl.BlockSpec(memory_space=pltpu.VMEM)
 HBM = pl.BlockSpec(memory_space=pltpu.HBM)
 
 
-def call(kernel, name, megabytes=32, flops=0, moved=0, **options):
-    cost = pl.CostEstimate(flops=flops, bytes_accessed=moved, transcendentals=0) if flops else None
+def call(kernel, name, megabytes=32, **options):
     return pl.pallas_call(
         kernel,
         name=name,
         compiler_params=pltpu.CompilerParams(vmem_limit_bytes=megabytes << 20),
-        cost_estimate=cost,
         **options,
     )
 
@@ -67,7 +65,7 @@
     steps = blocks // PART
     _, iheads, depth = iq_ref.shape
     keys = k_ref.shape[0]
-    group = iheads // steps
+    group = GROUP
 
     first = pltpu.make_async_copy(q_hbm, q_ref, sems.at[steps])
     first.start()
@@ -137,7 +135,7 @@
         total_ref[...] = total
         return carry
 
-    lax.fori_loop(0, steps, logit_step, 0)
+    lax.fori_loop(0, iheads // group, logit_step, 0)
 
     turned_tops = tops[...].T[0 : heads * steps]
     turned_sums = sums[...].T[0 : heads * steps]
@@ -199,7 +197,7 @@
     )(queries, cache, index_query, index_keys, weights)
 
 
-def headsum_kernel(offsets, e_hbm, tops_ref, got_ref, *refs):
+def headsum_kernel(offsets, stays, e_hbm, tops_ref, got_ref, *refs):
     outs, e_ref, sums, sems, out_sems = refs[0 : len(offsets)], *refs[len(offsets) :]
     _, heads, rows, keys = e_ref.shape
     steps = tops_ref.shape[0] // heads
@@ -245,27 +243,28 @@
             for h in range(heads):
                 term = e_ref[slot, h].astype(jnp.float32) * columns[:, h * steps : h * steps + 1]
                 total = term if total is None else total + term
-            sums[slot, 0:rows] = total
-            sums[slot, rows:] = tail
-            out_copy(i, k).start()
+            place = outs[i].at[k] if stays else sums.at[slot]
+            place[0:rows] = total
+            place[rows:] = tail
+            if not stays:
+                out_copy(i, k).start()
             return carry
 
         lax.fori_loop(0, RING, body, 0)
     for i, _ in enumerate(offsets):
-        for k in range(RING):
+        for k in range(0 if stays else RING):
             out_copy(i, k).wait()
 
 
-def head_sum(offsets, terms, tops, got, flops=0):
+def head_sum(offsets, terms, tops, got, stays=False):
     blocks, heads, rows, keys = terms.shape
     slots = len(offsets) * RING
     return call(
-        functools.partial(headsum_kernel, offsets),
+        functools.partial(headsum_kernel, offsets, stays),
         "head_sum",
-        56,
-        flops,
+        53 if stays else 56,
         in_specs=[HBM] + [VMEM] * 2,
-        out_specs=[HBM] * len(offsets),
+        out_specs=[VMEM if stays else HBM] * len(offsets),
         out_shape=[f32(blocks // RING, rows + 8, keys)] * len(offsets),
         scratch_shapes=[
             pltpu.VMEM((slots, heads, rows, keys), jnp.bfloat16),
@@ -310,9 +309,6 @@
     )(*got)
 
 
-GROUP = 8
-
-
 def dlogits_kernel(key_total, *refs):
     got = refs[0:RING]
     logits_ref, qh_ref, k_ref, send_ref, turned = refs[RING:]
@@ -391,7 +387,6 @@
         keys_kernel,
         "key_gradient",
         24,
-        BESIDE,
         out_shape=f32(keys, depth),
         scratch_shapes=[pltpu.VMEM((keys, GROUP * rows), jnp.bfloat16), pltpu.VMEM((keys, rows), jnp.float32)],
     )(dlogits, qh, index_keys, weights)
@@ -441,7 +436,7 @@
             outs[i][z, share * span + few :] = piece[:, rows : 2 * rows]
 
 
-def query_gradient(offsets, got, qh, weights, pieces, flops=0):
+def query_gradient(offsets, got, qh, weights, pieces):
     keys = got[0].shape[1]
     heads, rows, depth = qh.shape
     share = heads // (RING * RING)
@@ -450,7 +445,6 @@
         functools.partial(query_kernel, offsets, pieces),
         "query_gradient",
         24,
-        flops,
         in_specs=[VMEM] * (RING + 2),
         out_specs=[VMEM] * len(offsets),
         out_shape=[f32(pieces, tall, depth)] * len(offsets),
@@ -513,9 +507,14 @@
     cache = jnp.swapaxes(mla_cache, 1, 2)
     terms, tops, send1, logits, qh = scores_and_logits(queries, cache, index_query, index_keys, weights, key_count)
     got1 = exchange(send1, "key")
+    (far_two,) = head_sum((2,), terms, tops, got1)
+    got1, _ = lax.optimization_barrier((got1, far_two))
     sides = head_sum((1, 3), terms, tops, got1)
-    rest = head_sum((2, 0), terms, tops, got1)
-    got2 = [rest[1], shift(sides[0], 1, False), shift(rest[0], 2, False), shift(sides[1], 3, False)]
+    (own,) = head_sum((0,), terms, tops, got1, True)
+    two = shift(far_two, 2, False)
+    one = shift(sides[0], 1, False)
+    three = shift(sides[1], 3, False)
+    got2 = [own, one, two, three]
     send2 = partial_sum(got2)
     got2 = [send2[0]] + [shift(send2[d], d, True) for d in (1, 2, 3)]
     key_total = float(keys * head_count * key_count)
@@ -529,10 +528,14 @@
     near = lax.dynamic_slice_in_dim(keys_part, row_index * half, half, 0)
     key_grad = near + lax.ppermute(away, "row", [(0, 1), (1, 0)])
 
+    (far_two,) = query_gradient((2,), got3, qh, weights, key_count)
+    got3, _ = lax.optimization_barrier((got3, far_two))
     sides = query_gradient((1, 3), got3, qh, weights, key_count)
-    rest = query_gradient((2, 0), got3, qh, weights, key_count)
-    one, three, two = shift(sides[0], 1, True), shift(sides[1], 3, True), shift(rest[0], 2, True)
-    send4 = rest[1] + one + (two + three)
+    (own,) = query_gradient((0,), got3, qh, weights, key_count)
+    two = shift(far_two, 2, True)
+    one = shift(sides[0], 1, True)
+    three = shift(sides[1], 3, True)
+    send4 = own + one + (two + three)
     got4 = jnp.sum(exchange(send4, "key"), axis=0)
     got5 = exchange(jnp.broadcast_to(got4[None], (key_count, *got4.shape)), "key")
     query_grad, weight_grad = results(got5, heads, share * (rows // key_count))

time: 132 us -> 134 us (1.015)
  the two profiles are of different devices: /device:TPU:32 before, /device:TPU:24 now
where the time goes in v6:
time: 134 us; the launch traced here: 133 us
  Pallas kernels  38.7 us (29%)
  blocking collectives  33.6 us (25%)
  waiting for transfers between devices  32.3 us (24%)
  starting transfers between devices  26.5 us (20%)
    all_to_all x2, blocking collectives, exchange(): return lax.all_to_all(x, axis, split_axis=0, concat_axis=0, tiled=True)  33.6 us
    ppermute x12, starting transfers between devices, shift(): return lax.ppermute(x, ('head', 'row'), pairs)  23 us
    ppermute x12, waiting for transfers between devices, shift(): return lax.ppermute(x, ('head', 'row'), pairs)  22.3 us
    pallas_call x1, Pallas kernels, scores_and_logits(): call(scores_kernel, 'scores_and_logits', 60, in_specs=[HBM] * 5, out_spec...  16.5 us
    pallas_call x3, Pallas kernels, head_sum(): call(functools.partial(headsum_kernel, offsets, stays), 'head_sum', 53 if...  11.4 us
    all_to_all x1, waiting for transfers between devices, exchange(): return lax.all_to_all(x, axis, split_axis=0, concat_axis=0, tiled=True)  8.73 us
    pallas_call x1, Pallas kernels, key_gradient(): call(keys_kernel, 'key_gradient', 24, out_shape=f32(keys, depth), scratch...  4 us
    all_to_all x1, starting transfers between devices, exchange(): return lax.all_to_all(x, axis, split_axis=0, concat_axis=0, tiled=True)  3.42 us
  transfers between devices with their start and end apart: 14, of which 12 were waited for; matrix products, arithmetic and copies ran while one was open for 0% of the time, Pallas kernels for 10%

profile of v6, /device:TPU:24, one launch (start us, length us, event | category | flops | bytes accessed | tf_op | source)
XLA Modules:
  0.0 133.3 jit_solution(5952985386244149827)
XLA Ops:
  0.6 16.5 %scores_and_logits.1 = (bf16[16,8,128,256]{3,2,1,0:T(8,128)(2,1)}, f32[32,128]{1,0:T(8,128)}, f32[8,24,128]{2,1,0:T(8,128)}, f32[256,128]{1,0:T(8,128)}, bf16[64,128,128]{2,1,0:T(8,128)(2,1)}) custom-call(bf16[8,576,128]{2,1,0:T(8,128)(2,1)} %bitcast.11, bf16[16,576,256]{2,1,0:T(8,128)(2,1)} %bitcast.10, bf16[128,64,128]{2,1,0:T(8,128)(2,1)} %iq_hbm.1, ...), custom_call_target="tpu_custom_call" | custom-call | tf_op jit(solution)/shard_map/scores_and_logits/pallas_call | solution.py:169
  17.1 17.3 %all_to_all.15.got_ref = f32[8,24,128]{2,1,0:T(8,128)} all-to-all(f32[8,24,128]{2,1,0:T(8,128)} %get-tuple-element.30), channel_id=1, replica_groups=mesh['head'=16,'key'=8,'row'=2] {'key'}, dimensions={0} | all-to-all | bytes 196608 | tf_op jit(solution)/shard_map/all_to_all | solution.py:481
  34.4 3.9 %head_sum.3 = f32[4,136,256]{2,1,0:T(8,128)} custom-call(bf16[16,8,128,256]{3,2,1,0:T(8,128)(2,1)} %get-tuple-element.28.e_hbm, f32[32,128]{1,0:T(8,128)} %get-tuple-element.29.tops_ref, f32[8,24,128]{2,1,0:T(8,128)} %all_to_all.15.got_ref), custom_call_target="tpu_custom_call" | custom-call | tf_op jit(solution)/shard_map/head_sum/pallas_call | solution.py:262
  38.3 0.0 copy-start.4
  38.3 1.3 collective-permute-start.1
  39.6 5.2 %head_sum.5 = (f32[4,136,256]{2,1,0:T(8,128)}, f32[4,136,256]{2,1,0:T(8,128)}) custom-call(bf16[16,8,128,256]{3,2,1,0:T(8,128)(2,1)} %get-tuple-element.28.e_hbm, f32[32,128]{1,0:T(8,128)} %get-tuple-element.29.tops_ref, f32[8,24,128]{2,1,0:T(8,128)} %all_to_all.15.got_ref), custom_call_target="tpu_custom_call" | custom-call | tf_op jit(solution)/shard_map/head_sum/pallas_call | solution.py:262
  44.8 2.3 %collective-permute-start = (f32[4,136,256]{2,1,0:T(8,128)}, f32[4,136,256]{2,1,0:T(8,128)S(1)}, u32[]{:S(2)}, u32[]{:S(2)}) collective-permute-start(f32[4,136,256]{2,1,0:T(8,128)} %get-tuple-element.32), channel_id=1, source_target_pairs={{0,16},{1,65},{16,32},{17,81},{32,48},{33,97},{48,0},{49,113},{64,... | collective-permute-start | bytes 1671176 | tf_op jit(solution)/shard_map/ppermute | solution.py:494
  47.1 0.0 collective-permute-start.2
  47.1 0.0 copy-start.5
  47.1 2.3 %head_sum.4.refs_0_ = f32[4,136,256]{2,1,0:T(8,128)S(1)} custom-call(bf16[16,8,128,256]{3,2,1,0:T(8,128)(2,1)} %get-tuple-element.28.e_hbm, f32[32,128]{1,0:T(8,128)S(1)} %copy-done.4, f32[8,24,128]{2,1,0:T(8,128)S(1)} %copy-done.1), custom_call_target="tpu_custom_call" | custom-call | tf_op jit(solution)/shard_map/head_sum/pallas_call | solution.py:262
  49.4 0.0 copy-start.3
  49.4 5.2 %collective-permute-done.refs_1_ = f32[4,136,256]{2,1,0:T(8,128)S(1)} collective-permute-done((f32[4,136,256]{2,1,0:T(8,128)}, f32[4,136,256]{2,1,0:T(8,128)S(1)}, u32[]{:S(2)}, u32[]{:S(2)}) %collective-permute-start) | collective-permute-done | bytes 557088 | tf_op jit(solution)/shard_map/ppermute | solution.py:494
  54.6 0.0 collective-permute-done.1.refs_2_
  54.6 3.4 %collective-permute-done.2.refs_3_ = f32[4,136,256]{2,1,0:T(8,128)S(1)} collective-permute-done((f32[4,136,256]{2,1,0:T(8,128)}, f32[4,136,256]{2,1,0:T(8,128)S(1)}, u32[]{:S(2)}, u32[]{:S(2)}) %collective-permute-start.2) | collective-permute-done | bytes 557088 | tf_op jit(solution)/shard_map/ppermute | solution.py:494
  58.0 0.1 partial_sum.1
  58.2 0.0 copy-start.2
  58.2 3.1 %collective-permute-start.3 = (f32[136,256]{1,0:T(8,128)S(1)}, f32[136,256]{1,0:T(8,128)S(1)}, u32[]{:S(2)}, u32[]{:S(2)}) collective-permute-start(f32[136,256]{1,0:T(8,128)S(1)} %get-tuple-element.35), channel_id=1, source_target_pairs={{0,64},{1,17},{16,80},{17,33},{32,96},{33,49},{48,112},{49,1},{64,... | collective-permute-start | bytes 417800 | tf_op jit(solution)/shard_map/ppermute | solution.py:494
  61.2 1.6 %collective-permute-start.4 = (f32[136,256]{1,0:T(8,128)S(1)}, f32[136,256]{1,0:T(8,128)S(1)}, u32[]{:S(2)}, u32[]{:S(2)}) collective-permute-start(f32[136,256]{1,0:T(8,128)S(1)} %get-tuple-element.36), channel_id=1, source_target_pairs={{0,128},{1,33},{16,144},{17,49},{32,160},{33,1},{48,176},{49,17},{... | collective-permute-start | bytes 417800 | tf_op jit(solution)/shard_map/ppermute | solution.py:494
  62.9 2.5 %collective-permute-start.5 = (f32[136,256]{1,0:T(8,128)S(1)}, f32[136,256]{1,0:T(8,128)S(1)}, u32[]{:S(2)}, u32[]{:S(2)}) collective-permute-start(f32[136,256]{1,0:T(8,128)S(1)} %get-tuple-element.37), channel_id=1, source_target_pairs={{0,192},{1,49},{16,208},{17,1},{32,224},{33,17},{48,240},{49,33},{... | collective-permute-start | bytes 417800 | tf_op jit(solution)/shard_map/ppermute | solution.py:494
  65.4 0.0 collective-permute-done.3.refs_1_
  65.4 2.4 %collective-permute-done.4.refs_2_ = f32[136,256]{1,0:T(8,128)S(1)} collective-permute-done((f32[136,256]{1,0:T(8,128)S(1)}, f32[136,256]{1,0:T(8,128)S(1)}, u32[]{:S(2)}, u32[]{:S(2)}) %collective-permute-start.4) | collective-permute-done | bytes 139296 | tf_op jit(solution)/shard_map/ppermute | solution.py:494
  67.8 0.2 collective-permute-done.5.refs_3_
  68.0 2.7 %dlogits.1.dlogits_ref.refs_0_ = f32[288,256]{1,0:T(8,128)S(1)} custom-call(f32[136,256]{1,0:T(8,128)S(1)} %get-tuple-element.34.refs_0_, f32[136,256]{1,0:T(8,128)S(1)} %collective-permute-done.3.refs_1_, f32[136,256]{1,0:T(8,128)S(1)} %collective-permute-done.4.refs_2_, f32[136,256]{1,0:T(8,128)S(1)} %collective-permute-done.5.refs_3_, ...), custom_call_target="tpu_custom_call" | custom-call | tf_op jit(solution)/shard_map/dlogits/pallas_call | solution.py:354
  70.7 0.1 collective-permute-start.6
  70.8 0.4 collective-permute-start.7
  71.2 1.6 %collective-permute-start.8 = (f32[288,256]{1,0:T(8,128)S(1)}, f32[288,256]{1,0:T(8,128)S(1)}, u32[]{:S(2)}, u32[]{:S(2)}) collective-permute-start(f32[288,256]{1,0:T(8,128)S(1)} %dlogits.1.dlogits_ref.refs_0_), channel_id=1, source_target_pairs={{0,48},{1,193},{16,0},{17,209},{32,16},{33,225},{48,32},{49,241},{... | collective-permute-start | bytes 884744 | tf_op jit(solution)/shard_map/ppermute | solution.py:494
  72.8 4.0 %key_gradient.1 = f32[256,128]{1,0:T(8,128)S(1)} custom-call(f32[288,256]{1,0:T(8,128)S(1)} %dlogits.1.dlogits_ref.refs_0_, bf16[64,128,128]{2,1,0:T(8,128)(2,1)S(1)} %copy-done, bf16[256,128]{1,0:T(8,128)(2,1)S(1)} %copy-done.3, f32[64,128]{1,0:T(8,128)S(1)} %bitcast.6), custom_call_target="tpu_custom_call" | custom-call | tf_op jit(solution)/shard_map/key_gradient/pallas_call | solution.py:386
  76.8 0.7 collective-permute-done.6.refs_1_
  77.5 1.7 %collective-permute-done.7.refs_2_ = f32[288,256]{1,0:T(8,128)S(1)} collective-permute-done((f32[288,256]{1,0:T(8,128)S(1)}, f32[288,256]{1,0:T(8,128)S(1)}, u32[]{:S(2)}, u32[]{:S(2)}) %collective-permute-start.7) | collective-permute-done | bytes 294944 | tf_op jit(solution)/shard_map/ppermute | solution.py:494
  79.2 3.7 %collective-permute-done.8.refs_3_ = f32[288,256]{1,0:T(8,128)S(1)} collective-permute-done((f32[288,256]{1,0:T(8,128)S(1)}, f32[288,256]{1,0:T(8,128)S(1)}, u32[]{:S(2)}, u32[]{:S(2)}) %collective-permute-start.8) | collective-permute-done | bytes 294944 | tf_op jit(solution)/shard_map/ppermute | solution.py:494
  82.9 0.9 query_gradient.3
  83.8 7.9 %collective-permute-start.10 = (f32[8,72,128]{2,1,0:T(8,128)S(1)}, f32[8,72,128]{2,1,0:T(8,128)S(1)}, u32[]{:S(2)}, u32[]{:S(2)}) collective-permute-start(f32[8,72,128]{2,1,0:T(8,128)S(1)} %query_gradient.3), channel_id=1, source_target_pairs={{0,128},{1,33},{16,144},{17,49},{32,160},{33,1},{48,176},{49,17},{... | collective-permute-start | bytes 884744 | tf_op jit(solution)/shard_map/ppermute | solution.py:494
  91.8 1.5 %query_gradient.5 = (f32[8,72,128]{2,1,0:T(8,128)S(1)}, f32[8,72,128]{2,1,0:T(8,128)S(1)}) custom-call(f32[288,256]{1,0:T(8,128)S(1)} %dlogits.1.dlogits_ref.refs_0_, f32[288,256]{1,0:T(8,128)S(1)} %collective-permute-done.6.refs_1_, f32[288,256]{1,0:T(8,128)S(1)} %collective-permute-done.7.refs_2_, f32[288,256]{1,0:T(8,128)S(1)} %collective-permute-done.8.refs_3_, ...), custom_call_target="tpu_custom_call" | custom-call | tf_op jit(solution)/shard_map/query_gradient/pallas_call | solution.py:444
  93.2 0.1 collective-permute-start.11
  93.3 2.0 %collective-permute-start.9 = (f32[8,72,128]{2,1,0:T(8,128)S(1)}, f32[8,72,128]{2,1,0:T(8,128)S(1)}, u32[]{:S(2)}, u32[]{:S(2)}) collective-permute-start(f32[8,72,128]{2,1,0:T(8,128)S(1)} %get-tuple-element.48), channel_id=1, source_target_pairs={{0,64},{1,17},{16,80},{17,33},{32,96},{33,49},{48,112},{49,1},{64,... | collective-permute-start | bytes 884744 | tf_op jit(solution)/shard_map/ppermute | solution.py:494
  95.3 0.9 query_gradient.4
  96.3 0.2 collective-permute-done.10
  96.5 3.6 %collective-permute-done.11 = f32[8,72,128]{2,1,0:T(8,128)S(1)} collective-permute-done((f32[8,72,128]{2,1,0:T(8,128)S(1)}, f32[8,72,128]{2,1,0:T(8,128)S(1)}, u32[]{:S(2)}, u32[]{:S(2)}) %collective-permute-start.11) | collective-permute-done | bytes 294944 | tf_op jit(solution)/shard_map/ppermute | solution.py:494
  100.0 1.3 collective-permute-done.9
  101.3 0.1 add_add_fusion
  101.4 16.3 %all_to_all.16 = f32[8,72,128]{2,1,0:T(8,128)S(1)} all-to-all(f32[8,72,128]{2,1,0:T(8,128)S(1)} %add_add_fusion), channel_id=1, replica_groups=mesh['head'=16,'key'=8,'row'=2] {'key'}, dimensions={0} | all-to-all | bytes 589824 | tf_op jit(solution)/shard_map/all_to_all | solution.py:481
  117.7 0.7 broadcast_in_dim.2
  118.4 3.4 %all-to-all-start.2 = ((f32[8,72,128]{2,1,0:T(8,128)}), f32[8,72,128]{2,1,0:T(8,128)S(1)}, u32[]{:S(2)}, u32[]{:S(2)}) async-start(f32[8,72,128]{2,1,0:T(8,128)} %broadcast_in_dim.2), calls=%async_computation.2 | async-start | bytes 589824 | tf_op jit(solution)/shard_map/all_to_all | solution.py:481
  121.9 0.1 collective-permute-start.12
  122.0 1.2 collective-permute-done.12
  123.2 0.6 dynamic-slice_add_fusion
  123.9 8.7 %all-to-all-done.2.got_ref = f32[8,72,128]{2,1,0:T(8,128)S(1)} async-done(((f32[8,72,128]{2,1,0:T(8,128)}), f32[8,72,128]{2,1,0:T(8,128)S(1)}, u32[]{:S(2)}, u32[]{:S(2)}) %all-to-all-start.2) | async-done | bytes 294944 | tf_op jit(solution)/shard_map/all_to_all | solution.py:481
  132.6 0.7 results.1
  (10 shorter events, 0.0 us)
Async XLA Ops:
  38.3 8.8 %copy-start.1 = (f32[8,24,128]{2,1,0:T(8,128)S(1)}, f32[8,24,128]{2,1,0:T(8,128)}, u32[]{:S(2)}) copy-start(f32[8,24,128]{2,1,0:T(8,128)} %all_to_all.15.got_ref) | copy-start | bytes 294916
  38.3 8.8 %copy-start.4 = (f32[32,128]{1,0:T(8,128)S(1)}, f32[32,128]{1,0:T(8,128)}, u32[]{:S(2)}) copy-start(f32[32,128]{1,0:T(8,128)} %get-tuple-element.29.tops_ref) | copy-start | bytes 49156
  38.3 16.3 %collective-permute-start.1 = (f32[4,136,256]{2,1,0:T(8,128)}, f32[4,136,256]{2,1,0:T(8,128)S(1)}, u32[]{:S(2)}, u32[]{:S(2)}) collective-permute-start(f32[4,136,256]{2,1,0:T(8,128)} %head_sum.3), channel_id=1, source_target_pairs={{0,32},{1,129},{16,48},{17,145},{32,0},{33,161},{48,16},{49,177},{... | collective-permute-start | bytes 1671176 | tf_op jit(solution)/shard_map/ppermute | solution.py:494
  44.8 9.8 %collective-permute-start = (f32[4,136,256]{2,1,0:T(8,128)}, f32[4,136,256]{2,1,0:T(8,128)S(1)}, u32[]{:S(2)}, u32[]{:S(2)}) collective-permute-start(f32[4,136,256]{2,1,0:T(8,128)} %get-tuple-element.32), channel_id=1, source_target_pairs={{0,16},{1,65},{16,32},{17,81},{32,48},{33,97},{48,0},{49,113},{64,... | collective-permute-start | bytes 1671176 | tf_op jit(solution)/shard_map/ppermute | solution.py:494
  47.1 11.0 %collective-permute-start.2 = (f32[4,136,256]{2,1,0:T(8,128)}, f32[4,136,256]{2,1,0:T(8,128)S(1)}, u32[]{:S(2)}, u32[]{:S(2)}) collective-permute-start(f32[4,136,256]{2,1,0:T(8,128)} %get-tuple-element.33), channel_id=1, source_target_pairs={{0,48},{1,193},{16,0},{17,209},{32,16},{33,225},{48,32},{49,241},{... | collective-permute-start | bytes 1671176 | tf_op jit(solution)/shard_map/ppermute | solution.py:494
  47.1 20.9 %copy-start.5 = (f32[256,128]{1,0:T(8,128)S(1)}, f32[256,128]{1,0:T(8,128)}, u32[]{:S(2)}) copy-start(f32[256,128]{1,0:T(8,128)} %get-tuple-element.38.refs_4_) | copy-start | bytes 393220
  49.4 18.6 %copy-start = (bf16[64,128,128]{2,1,0:T(8,128)(2,1)S(1)}, bf16[64,128,128]{2,1,0:T(8,128)(2,1)}, u32[]{:S(2)}) copy-start(bf16[64,128,128]{2,1,0:T(8,128)(2,1)} %get-tuple-element.39.refs_5_.qh_ref.refs_4_) | copy-start | bytes 6291460
  49.4 18.6 %copy-start.3 = (bf16[256,128]{1,0:T(8,128)(2,1)S(1)}, bf16[256,128]{1,0:T(8,128)(2,1)}, u32[]{:S(2)}) copy-start(bf16[256,128]{1,0:T(8,128)(2,1)} %k_ref.1) | copy-start | bytes 196612
  58.2 14.6 %copy-start.2 = (f32[128,64]{0,1:T(8,128)S(1)}, f32[128,64]{0,1:T(8,128)}, u32[]{:S(2)}) copy-start(f32[128,64]{0,1:T(8,128)} %param.9) | copy-start | bytes 98308
  58.2 7.2 %collective-permute-start.3 = (f32[136,256]{1,0:T(8,128)S(1)}, f32[136,256]{1,0:T(8,128)S(1)}, u32[]{:S(2)}, u32[]{:S(2)}) collective-permute-start(f32[136,256]{1,0:T(8,128)S(1)} %get-tuple-element.35), channel_id=1, source_target_pairs={{0,64},{1,17},{16,80},{17,33},{32,96},{33,49},{48,112},{49,1},{64,... | collective-permute-start | bytes 417800 | tf_op jit(solution)/shard_map/ppermute | solution.py:494
  61.2 6.6 %collective-permute-start.4 = (f32[136,256]{1,0:T(8,128)S(1)}, f32[136,256]{1,0:T(8,128)S(1)}, u32[]{:S(2)}, u32[]{:S(2)}) collective-permute-start(f32[136,256]{1,0:T(8,128)S(1)} %get-tuple-element.36), channel_id=1, source_target_pairs={{0,128},{1,33},{16,144},{17,49},{32,160},{33,1},{48,176},{49,17},{... | collective-permute-start | bytes 417800 | tf_op jit(solution)/shard_map/ppermute | solution.py:494
  62.9 5.1 %collective-permute-start.5 = (f32[136,256]{1,0:T(8,128)S(1)}, f32[136,256]{1,0:T(8,128)S(1)}, u32[]{:S(2)}, u32[]{:S(2)}) collective-permute-start(f32[136,256]{1,0:T(8,128)S(1)} %get-tuple-element.37), channel_id=1, source_target_pairs={{0,192},{1,49},{16,208},{17,1},{32,224},{33,17},{48,240},{49,33},{... | collective-permute-start | bytes 417800 | tf_op jit(solution)/shard_map/ppermute | solution.py:494
  70.7 6.8 %collective-permute-start.6 = (f32[288,256]{1,0:T(8,128)S(1)}, f32[288,256]{1,0:T(8,128)S(1)}, u32[]{:S(2)}, u32[]{:S(2)}) collective-permute-start(f32[288,256]{1,0:T(8,128)S(1)} %dlogits.1.dlogits_ref.refs_0_), channel_id=1, source_target_pairs={{0,16},{1,65},{16,32},{17,81},{32,48},{33,97},{48,0},{49,113},{64,... | collective-permute-start | bytes 884744 | tf_op jit(solution)/shard_map/ppermute | solution.py:494
  70.8 8.4 %collective-permute-start.7 = (f32[288,256]{1,0:T(8,128)S(1)}, f32[288,256]{1,0:T(8,128)S(1)}, u32[]{:S(2)}, u32[]{:S(2)}) collective-permute-start(f32[288,256]{1,0:T(8,128)S(1)} %dlogits.1.dlogits_ref.refs_0_), channel_id=1, source_target_pairs={{0,32},{1,129},{16,48},{17,145},{32,0},{33,161},{48,16},{49,177},{... | collective-permute-start | bytes 884744 | tf_op jit(solution)/shard_map/ppermute | solution.py:494
  71.2 11.7 %collective-permute-start.8 = (f32[288,256]{1,0:T(8,128)S(1)}, f32[288,256]{1,0:T(8,128)S(1)}, u32[]{:S(2)}, u32[]{:S(2)}) collective-permute-start(f32[288,256]{1,0:T(8,128)S(1)} %dlogits.1.dlogits_ref.refs_0_), channel_id=1, source_target_pairs={{0,48},{1,193},{16,0},{17,209},{32,16},{33,225},{48,32},{49,241},{... | collective-permute-start | bytes 884744 | tf_op jit(solution)/shard_map/ppermute | solution.py:494
  83.8 12.6 %collective-permute-start.10 = (f32[8,72,128]{2,1,0:T(8,128)S(1)}, f32[8,72,128]{2,1,0:T(8,128)S(1)}, u32[]{:S(2)}, u32[]{:S(2)}) collective-permute-start(f32[8,72,128]{2,1,0:T(8,128)S(1)} %query_gradient.3), channel_id=1, source_target_pairs={{0,128},{1,33},{16,144},{17,49},{32,160},{33,1},{48,176},{49,17},{... | collective-permute-start | bytes 884744 | tf_op jit(solution)/shard_map/ppermute | solution.py:494
  93.2 6.8 %collective-permute-start.11 = (f32[8,72,128]{2,1,0:T(8,128)S(1)}, f32[8,72,128]{2,1,0:T(8,128)S(1)}, u32[]{:S(2)}, u32[]{:S(2)}) collective-permute-start(f32[8,72,128]{2,1,0:T(8,128)S(1)} %get-tuple-element.49), channel_id=1, source_target_pairs={{0,192},{1,49},{16,208},{17,1},{32,224},{33,17},{48,240},{49,33},{... | collective-permute-start | bytes 884744 | tf_op jit(solution)/shard_map/ppermute | solution.py:494
  93.3 8.0 %collective-permute-start.9 = (f32[8,72,128]{2,1,0:T(8,128)S(1)}, f32[8,72,128]{2,1,0:T(8,128)S(1)}, u32[]{:S(2)}, u32[]{:S(2)}) collective-permute-start(f32[8,72,128]{2,1,0:T(8,128)S(1)} %get-tuple-element.48), channel_id=1, source_target_pairs={{0,64},{1,17},{16,80},{17,33},{32,96},{33,49},{48,112},{49,1},{64,... | collective-permute-start | bytes 884744 | tf_op jit(solution)/shard_map/ppermute | solution.py:494
  118.4 14.2 %all-to-all-start.2 = ((f32[8,72,128]{2,1,0:T(8,128)}), f32[8,72,128]{2,1,0:T(8,128)S(1)}, u32[]{:S(2)}, u32[]{:S(2)}) async-start(f32[8,72,128]{2,1,0:T(8,128)} %broadcast_in_dim.2), calls=%async_computation.2 | async-start | bytes 589824 | tf_op jit(solution)/shard_map/all_to_all | solution.py:481
  121.9 1.3 %collective-permute-start.12 = (f32[128,128]{1,0:T(8,128)S(1)}, f32[128,128]{1,0:T(8,128)S(1)}, u32[]{:S(2)}, u32[]{:S(2)}) collective-permute-start(f32[128,128]{1,0:T(8,128)S(1)} %constant_dynamic-slice_fusion), channel_id=1, source_target_pairs={{0,1},{1,0},{2,3},{3,2},{4,5},{5,4},{6,7},{7,6},{8,9},{9,8},{10,11... | collective-permute-start | bytes 196616 | tf_op jit(solution)/shard_map/ppermute | solution.py:529

commit v7 on v6

--- a/solution.py
+++ b/solution.py
@@ -41,6 +41,10 @@
     )
 
 
+def in_hbm(x):
+    return pltpu.with_memory_space_constraint(x, pltpu.HBM)
+
+
 def f32(*shape):
     return jax.ShapeDtypeStruct(shape, jnp.float32)
 
@@ -57,8 +61,8 @@
 
 def scores_kernel(
     q_hbm, c_hbm, iq_hbm, k_hbm, w_hbm,
-    e_hbm, tops_ref, send_ref, logits_ref, qh_ref,
-    e_ref, q_ref, c_ref, iq_ref, k_ref, w_ref, wide, total_ref, queries_ref, tops, sums, sems, out_sems,
+    e_ref, tops_ref, send_ref, logits_ref, qh_ref,
+    q_ref, c_ref, iq_ref, k_ref, w_ref, wide, total_ref, queries_ref, tops, sums, sems,
 ):
     heads, width, rows = q_ref.shape
     blocks = c_ref.shape[0]
@@ -73,10 +77,6 @@
     def part_copy(step):
         span = pl.ds(step * PART, PART)
         return pltpu.make_async_copy(c_hbm.at[span], c_ref.at[span], sems.at[step])
-
-    def terms_copy(step):
-        span = pl.ds(step * PART, PART)
-        return pltpu.make_async_copy(e_ref.at[span], e_hbm.at[span], out_sems.at[step])
 
     others = [(iq_hbm, iq_ref), (k_hbm, k_ref), (w_hbm, w_ref)]
     others = [pltpu.make_async_copy(src, dst, sems.at[steps + 1 + i]) for i, (src, dst) in enumerate(others)]
@@ -110,7 +110,6 @@
             low, high = lane == h * steps + step, lane == (h + 1) * steps + step
             tops[...] = jnp.where(low, top[0:rows], jnp.where(high, top[rows:], tops[...]))
             sums[...] = jnp.where(low, total[0:rows], jnp.where(high, total[rows:], sums[...]))
-        terms_copy(step).start()
         return carry
 
     lax.fori_loop(0, steps, score_step, 0)
@@ -157,8 +156,6 @@
         send_ref[z, 2 * heads :] = jnp.zeros((8, rows), jnp.float32)
         send_ref[z, 2 * heads : 2 * heads + 1] = ltop
         send_ref[z, 2 * heads + 1 : 2 * heads + 2] = lsum
-    for step in range(steps):
-        terms_copy(step).wait()
 
 
 def scores_and_logits(queries, cache, index_query, index_keys, weights, key_count):
@@ -169,9 +166,9 @@
     return call(
         scores_kernel,
         "scores_and_logits",
-        60,
+        32,
         in_specs=[HBM] * 5,
-        out_specs=[HBM] + [VMEM] * 4,
+        out_specs=[VMEM] * 5,
         out_shape=(
             bf16(blocks, heads, rows, keys),
             f32(heads * steps, rows),
@@ -180,7 +177,6 @@
             bf16(iheads, rows, depth),
         ),
         scratch_shapes=[
-            pltpu.VMEM((blocks, heads, rows, keys), jnp.bfloat16),
             pltpu.VMEM(queries.shape, jnp.bfloat16),
             pltpu.VMEM(cache.shape, jnp.bfloat16),
             pltpu.VMEM(index_query.shape, jnp.bfloat16),
@@ -192,31 +188,14 @@
             pltpu.VMEM((rows, LANES), jnp.float32),
             pltpu.VMEM((rows, LANES), jnp.float32),
             pltpu.SemaphoreType.DMA((steps + 4,)),
-            pltpu.SemaphoreType.DMA((steps,)),
         ],
-    )(queries, cache, index_query, index_keys, weights)
-
-
-def headsum_kernel(offsets, stays, e_hbm, tops_ref, got_ref, *refs):
-    outs, e_ref, sums, sems, out_sems = refs[0 : len(offsets)], *refs[len(offsets) :]
+    )(*[in_hbm(x) for x in (queries, cache, index_query, index_keys, weights)])
+
+
+def headsum_kernel(offsets, e_ref, tops_ref, got_ref, *outs):
     _, heads, rows, keys = e_ref.shape
     steps = tops_ref.shape[0] // heads
     near, _, near_stride, far_stride = position()
-
-    def block_of(d, k):
-        return lax.rem(near + d, RING) * near_stride + k * far_stride
-
-    def block_copy(i, d, k):
-        slot = i * RING + k
-        return pltpu.make_async_copy(e_hbm.at[block_of(d, k)], e_ref.at[slot], sems.at[slot])
-
-    def out_copy(i, k):
-        slot = i * RING + k
-        return pltpu.make_async_copy(sums.at[slot], outs[i].at[k], out_sems.at[slot])
-
-    for i, d in enumerate(offsets):
-        for k in range(RING):
-            block_copy(i, d, k).start()
 
     tops = got_ref[:, 0:heads]
     top = jnp.max(tops, axis=0)
@@ -236,42 +215,28 @@
     for i, d in enumerate(offsets):
 
         def body(k, carry):
-            slot = i * RING + k
-            columns = pltpu.roll(weights, LANES - lax.div(block_of(d, k), PART), 1)
-            block_copy(i, d, k).wait()
+            block = lax.rem(near + d, RING) * near_stride + k * far_stride
+            columns = pltpu.roll(weights, LANES - lax.div(block, PART), 1)
             total = None
             for h in range(heads):
-                term = e_ref[slot, h].astype(jnp.float32) * columns[:, h * steps : h * steps + 1]
+                term = e_ref[block, h].astype(jnp.float32) * columns[:, h * steps : h * steps + 1]
                 total = term if total is None else total + term
-            place = outs[i].at[k] if stays else sums.at[slot]
-            place[0:rows] = total
-            place[rows:] = tail
-            if not stays:
-                out_copy(i, k).start()
+            outs[i][k, 0:rows] = total
+            outs[i][k, rows:] = tail
             return carry
 
         lax.fori_loop(0, RING, body, 0)
-    for i, _ in enumerate(offsets):
-        for k in range(0 if stays else RING):
-            out_copy(i, k).wait()
-
-
-def head_sum(offsets, terms, tops, got, stays=False):
+
+
+def head_sum(offsets, terms, tops, got):
     blocks, heads, rows, keys = terms.shape
-    slots = len(offsets) * RING
-    return call(
-        functools.partial(headsum_kernel, offsets, stays),
+    return call(
+        functools.partial(headsum_kernel, offsets),
         "head_sum",
-        53 if stays else 56,
-        in_specs=[HBM] + [VMEM] * 2,
-        out_specs=[VMEM if stays else HBM] * len(offsets),
+        24,
+        in_specs=[VMEM] * 3,
+        out_specs=[VMEM] * len(offsets),
         out_shape=[f32(blocks // RING, rows + 8, keys)] * len(offsets),
-        scratch_shapes=[
-            pltpu.VMEM((slots, heads, rows, keys), jnp.bfloat16),
-            pltpu.VMEM((slots, rows + 8, keys), jnp.float32),
-            pltpu.SemaphoreType.DMA((slots,)),
-            pltpu.SemaphoreType.DMA((slots,)),
-        ],
     )(terms, tops, got)
 
 
@@ -510,7 +475,7 @@
     (far_two,) = head_sum((2,), terms, tops, got1)
     got1, _ = lax.optimization_barrier((got1, far_two))
     sides = head_sum((1, 3), terms, tops, got1)
-    (own,) = head_sum((0,), terms, tops, got1, True)
+    (own,) = head_sum((0,), terms, tops, got1)
     two = shift(far_two, 2, False)
     one = shift(sides[0], 1, False)
     three = shift(sides[1], 3, False)

time: 134 us -> 120 us (0.90)
  the two profiles are of different devices: /device:TPU:24 before, /device:TPU:32 now
where the time goes in v7:
time: 120 us; the launch traced here: 118 us
  Pallas kernels  31 us (26%)
  blocking collectives  28.9 us (24%)
  waiting for transfers between devices  28.3 us (24%)
  starting transfers between devices  27.4 us (23%)
    all_to_all x2, blocking collectives, exchange(): return lax.all_to_all(x, axis, split_axis=0, concat_axis=0, tiled=True)  28.9 us
    ppermute x12, starting transfers between devices, shift(): return lax.ppermute(x, ('head', 'row'), pairs)  22.5 us
    ppermute x12, waiting for transfers between devices, shift(): return lax.ppermute(x, ('head', 'row'), pairs)  19.6 us
    pallas_call x1, Pallas kernels, scores_and_logits(): call(scores_kernel, 'scores_and_logits', 32, in_specs=[HBM] * 5, out_spec...  14.9 us
    all_to_all x1, waiting for transfers between devices, exchange(): return lax.all_to_all(x, axis, split_axis=0, concat_axis=0, tiled=True)  7.41 us
    pallas_call x3, Pallas kernels, head_sum(): call(functools.partial(headsum_kernel, offsets), 'head_sum', 24, in_specs...  5.22 us
    all_to_all x1, starting transfers between devices, exchange(): return lax.all_to_all(x, axis, split_axis=0, concat_axis=0, tiled=True)  4.78 us
    pallas_call x1, Pallas kernels, key_gradient(): call(keys_kernel, 'key_gradient', 24, out_shape=f32(keys, depth), scratch...  4 us
  transfers between devices with their start and end apart: 14, of which 11 were waited for; matrix products, arithmetic and copies ran while one was open for 1% of the time, Pallas kernels for 9%

profile of v7, /device:TPU:32, one launch (start us, length us, event | category | flops | bytes accessed | tf_op | source)
XLA Modules:
  0.0 117.7 jit_solution(16786714799008861068)
XLA Ops:
  0.6 14.9 %scores_and_logits.1 = (bf16[16,8,128,256]{3,2,1,0:T(8,128)(2,1)S(1)}, f32[32,128]{1,0:T(8,128)S(1)}, f32[8,24,128]{2,1,0:T(8,128)S(1)}, f32[256,128]{1,0:T(8,128)S(1)}, bf16[64,128,128]{2,1,0:T(8,128)(2,1)S(1)}) custom-call(bf16[8,576,128]{2,1,0:T(8,128)(2,1)} %bitcast.11, bf16[16,576,256]{2,1,0:T(8,128)(2,1)} %bitcast.10, bf16[128,64,128]{2,1,0:T(8,128)(2,1)} %iq_hbm.1, ...), custom_call_target="tpu_custom_call" | custom-call | tf_op jit(solution)/shard_map/scores_and_logits/pallas_call | solution.py:166
  15.6 15.5 %all_to_all.15.got_ref = f32[8,24,128]{2,1,0:T(8,128)S(1)} all-to-all(f32[8,24,128]{2,1,0:T(8,128)S(1)} %get-tuple-element.30), channel_id=1, replica_groups=mesh['head'=16,'key'=8,'row'=2] {'key'}, dimensions={0} | all-to-all | bytes 196608 | tf_op jit(solution)/shard_map/all_to_all | solution.py:446
  31.1 1.3 %head_sum.3 = f32[4,136,256]{2,1,0:T(8,128)S(1)} custom-call(bf16[16,8,128,256]{3,2,1,0:T(8,128)(2,1)S(1)} %get-tuple-element.28.e_ref, f32[32,128]{1,0:T(8,128)S(1)} %get-tuple-element.29.tops_ref, f32[8,24,128]{2,1,0:T(8,128)S(1)} %all_to_all.15.got_ref), custom_call_target="tpu_custom_call" | custom-call | tf_op jit(solution)/shard_map/head_sum/pallas_call | solution.py:233
  32.4 3.3 %collective-permute-start.1 = (f32[4,136,256]{2,1,0:T(8,128)S(1)}, f32[4,136,256]{2,1,0:T(8,128)S(1)}, u32[]{:S(2)}, u32[]{:S(2)}) collective-permute-start(f32[4,136,256]{2,1,0:T(8,128)S(1)} %head_sum.3), channel_id=1, source_target_pairs={{0,32},{1,129},{16,48},{17,145},{32,0},{33,161},{48,16},{49,177},{... | collective-permute-start | bytes 1671176 | tf_op jit(solution)/shard_map/ppermute | solution.py:459
  35.7 2.5 %head_sum.5 = (f32[4,136,256]{2,1,0:T(8,128)S(1)}, f32[4,136,256]{2,1,0:T(8,128)S(1)}) custom-call(bf16[16,8,128,256]{3,2,1,0:T(8,128)(2,1)S(1)} %get-tuple-element.28.e_ref, f32[32,128]{1,0:T(8,128)S(1)} %get-tuple-element.29.tops_ref, f32[8,24,128]{2,1,0:T(8,128)S(1)} %all_to_all.15.got_ref), custom_call_target="tpu_custom_call" | custom-call | tf_op jit(solution)/shard_map/head_sum/pallas_call | solution.py:233
  38.3 0.8 collective-permute-start
  39.0 2.6 %collective-permute-start.2 = (f32[4,136,256]{2,1,0:T(8,128)S(1)}, f32[4,136,256]{2,1,0:T(8,128)S(1)}, u32[]{:S(2)}, u32[]{:S(2)}) collective-permute-start(f32[4,136,256]{2,1,0:T(8,128)S(1)} %get-tuple-element.33), channel_id=1, source_target_pairs={{0,48},{1,193},{16,0},{17,209},{32,16},{33,225},{48,32},{49,241},{... | collective-permute-start | bytes 1671176 | tf_op jit(solution)/shard_map/ppermute | solution.py:459
  41.6 1.3 %head_sum.4.refs_0_ = f32[4,136,256]{2,1,0:T(8,128)S(1)} custom-call(bf16[16,8,128,256]{3,2,1,0:T(8,128)(2,1)S(1)} %get-tuple-element.28.e_ref, f32[32,128]{1,0:T(8,128)S(1)} %get-tuple-element.29.tops_ref, f32[8,24,128]{2,1,0:T(8,128)S(1)} %all_to_all.15.got_ref), custom_call_target="tpu_custom_call" | custom-call | tf_op jit(solution)/shard_map/head_sum/pallas_call | solution.py:233
  42.9 0.0 copy-start.1
  42.9 6.6 %collective-permute-done.refs_1_ = f32[4,136,256]{2,1,0:T(8,128)S(1)} collective-permute-done((f32[4,136,256]{2,1,0:T(8,128)S(1)}, f32[4,136,256]{2,1,0:T(8,128)S(1)}, u32[]{:S(2)}, u32[]{:S(2)}) %collective-permute-start) | collective-permute-done | bytes 557088 | tf_op jit(solution)/shard_map/ppermute | solution.py:459
  49.5 0.0 collective-permute-done.1.refs_2_
  49.5 0.3 collective-permute-done.2.refs_3_
  49.9 0.1 partial_sum.1
  50.0 0.0 copy-start
  50.0 1.6 %collective-permute-start.3 = (f32[136,256]{1,0:T(8,128)S(1)}, f32[136,256]{1,0:T(8,128)S(1)}, u32[]{:S(2)}, u32[]{:S(2)}) collective-permute-start(f32[136,256]{1,0:T(8,128)S(1)} %get-tuple-element.35), channel_id=1, source_target_pairs={{0,64},{1,17},{16,80},{17,33},{32,96},{33,49},{48,112},{49,1},{64,... | collective-permute-start | bytes 417800 | tf_op jit(solution)/shard_map/ppermute | solution.py:459
  51.6 2.7 %collective-permute-start.4 = (f32[136,256]{1,0:T(8,128)S(1)}, f32[136,256]{1,0:T(8,128)S(1)}, u32[]{:S(2)}, u32[]{:S(2)}) collective-permute-start(f32[136,256]{1,0:T(8,128)S(1)} %get-tuple-element.36), channel_id=1, source_target_pairs={{0,128},{1,33},{16,144},{17,49},{32,160},{33,1},{48,176},{49,17},{... | collective-permute-start | bytes 417800 | tf_op jit(solution)/shard_map/ppermute | solution.py:459
  54.3 1.4 %collective-permute-start.5 = (f32[136,256]{1,0:T(8,128)S(1)}, f32[136,256]{1,0:T(8,128)S(1)}, u32[]{:S(2)}, u32[]{:S(2)}) collective-permute-start(f32[136,256]{1,0:T(8,128)S(1)} %get-tuple-element.37), channel_id=1, source_target_pairs={{0,192},{1,49},{16,208},{17,1},{32,224},{33,17},{48,240},{49,33},{... | collective-permute-start | bytes 417800 | tf_op jit(solution)/shard_map/ppermute | solution.py:459
  55.7 0.6 collective-permute-done.3.refs_1_
  56.3 2.5 %collective-permute-done.4.refs_2_ = f32[136,256]{1,0:T(8,128)S(1)} collective-permute-done((f32[136,256]{1,0:T(8,128)S(1)}, f32[136,256]{1,0:T(8,128)S(1)}, u32[]{:S(2)}, u32[]{:S(2)}) %collective-permute-start.4) | collective-permute-done | bytes 139296 | tf_op jit(solution)/shard_map/ppermute | solution.py:459
  58.8 0.5 collective-permute-done.5.refs_3_
  59.4 0.0 copy-done.1
  59.4 2.7 %dlogits.1.dlogits_ref.refs_0_ = f32[288,256]{1,0:T(8,128)S(1)} custom-call(f32[136,256]{1,0:T(8,128)S(1)} %get-tuple-element.34.refs_0_, f32[136,256]{1,0:T(8,128)S(1)} %collective-permute-done.3.refs_1_, f32[136,256]{1,0:T(8,128)S(1)} %collective-permute-done.4.refs_2_, f32[136,256]{1,0:T(8,128)S(1)} %collective-permute-done.5.refs_3_, ...), custom_call_target="tpu_custom_call" | custom-call | tf_op jit(solution)/shard_map/dlogits/pallas_call | solution.py:319
  62.0 1.5 %collective-permute-start.6 = (f32[288,256]{1,0:T(8,128)S(1)}, f32[288,256]{1,0:T(8,128)S(1)}, u32[]{:S(2)}, u32[]{:S(2)}) collective-permute-start(f32[288,256]{1,0:T(8,128)S(1)} %dlogits.1.dlogits_ref.refs_0_), channel_id=1, source_target_pairs={{0,16},{1,65},{16,32},{17,81},{32,48},{33,97},{48,0},{49,113},{64,... | collective-permute-start | bytes 884744 | tf_op jit(solution)/shard_map/ppermute | solution.py:459
  63.5 2.7 %collective-permute-start.7 = (f32[288,256]{1,0:T(8,128)S(1)}, f32[288,256]{1,0:T(8,128)S(1)}, u32[]{:S(2)}, u32[]{:S(2)}) collective-permute-start(f32[288,256]{1,0:T(8,128)S(1)} %dlogits.1.dlogits_ref.refs_0_), channel_id=1, source_target_pairs={{0,32},{1,129},{16,48},{17,145},{32,0},{33,161},{48,16},{49,177},{... | collective-permute-start | bytes 884744 | tf_op jit(solution)/shard_map/ppermute | solution.py:459
  66.2 1.4 %collective-permute-start.8 = (f32[288,256]{1,0:T(8,128)S(1)}, f32[288,256]{1,0:T(8,128)S(1)}, u32[]{:S(2)}, u32[]{:S(2)}) collective-permute-start(f32[288,256]{1,0:T(8,128)S(1)} %dlogits.1.dlogits_ref.refs_0_), channel_id=1, source_target_pairs={{0,48},{1,193},{16,0},{17,209},{32,16},{33,225},{48,32},{49,241},{... | collective-permute-start | bytes 884744 | tf_op jit(solution)/shard_map/ppermute | solution.py:459
  67.6 0.0 copy-done
  67.6 4.0 %key_gradient.1 = f32[256,128]{1,0:T(8,128)S(1)} custom-call(f32[288,256]{1,0:T(8,128)S(1)} %dlogits.1.dlogits_ref.refs_0_, bf16[64,128,128]{2,1,0:T(8,128)(2,1)S(1)} %get-tuple-element.39.refs_5_.qh_ref.refs_4_, bf16[256,128]{1,0:T(8,128)(2,1)S(1)} %copy-done.1, f32[64,128]{1,0:T(8,128)S(1)} %bitcast.6), custom_call_target="tpu_custom_call" | custom-call | tf_op jit(solution)/shard_map/key_gradient/pallas_call | solution.py:351
  71.6 0.0 collective-permute-done.6.refs_1_
  71.6 2.5 %collective-permute-done.7.refs_2_ = f32[288,256]{1,0:T(8,128)S(1)} collective-permute-done((f32[288,256]{1,0:T(8,128)S(1)}, f32[288,256]{1,0:T(8,128)S(1)}, u32[]{:S(2)}, u32[]{:S(2)}) %collective-permute-start.7) | collective-permute-done | bytes 294944 | tf_op jit(solution)/shard_map/ppermute | solution.py:459
  74.1 0.0 collective-permute-done.8.refs_3_
  74.1 0.9 query_gradient.3
  75.0 2.5 %collective-permute-start.10 = (f32[8,72,128]{2,1,0:T(8,128)S(1)}, f32[8,72,128]{2,1,0:T(8,128)S(1)}, u32[]{:S(2)}, u32[]{:S(2)}) collective-permute-start(f32[8,72,128]{2,1,0:T(8,128)S(1)} %query_gradient.3), channel_id=1, source_target_pairs={{0,128},{1,33},{16,144},{17,49},{32,160},{33,1},{48,176},{49,17},{... | collective-permute-start | bytes 884744 | tf_op jit(solution)/shard_map/ppermute | solution.py:459
  77.5 1.5 %query_gradient.5 = (f32[8,72,128]{2,1,0:T(8,128)S(1)}, f32[8,72,128]{2,1,0:T(8,128)S(1)}) custom-call(f32[288,256]{1,0:T(8,128)S(1)} %dlogits.1.dlogits_ref.refs_0_, f32[288,256]{1,0:T(8,128)S(1)} %collective-permute-done.6.refs_1_, f32[288,256]{1,0:T(8,128)S(1)} %collective-permute-done.7.refs_2_, f32[288,256]{1,0:T(8,128)S(1)} %collective-permute-done.8.refs_3_, ...), custom_call_target="tpu_custom_call" | custom-call | tf_op jit(solution)/shard_map/query_gradient/pallas_call | solution.py:409
  79.0 1.7 %collective-permute-start.11 = (f32[8,72,128]{2,1,0:T(8,128)S(1)}, f32[8,72,128]{2,1,0:T(8,128)S(1)}, u32[]{:S(2)}, u32[]{:S(2)}) collective-permute-start(f32[8,72,128]{2,1,0:T(8,128)S(1)} %get-tuple-element.49), channel_id=1, source_target_pairs={{0,192},{1,49},{16,208},{17,1},{32,224},{33,17},{48,240},{49,33},{... | collective-permute-start | bytes 884744 | tf_op jit(solution)/shard_map/ppermute | solution.py:459
  80.7 0.4 collective-permute-start.9
  81.1 0.9 query_gradient.4
  82.0 1.3 %collective-permute-done.10 = f32[8,72,128]{2,1,0:T(8,128)S(1)} collective-permute-done((f32[8,72,128]{2,1,0:T(8,128)S(1)}, f32[8,72,128]{2,1,0:T(8,128)S(1)}, u32[]{:S(2)}, u32[]{:S(2)}) %collective-permute-start.10) | collective-permute-done | bytes 294944 | tf_op jit(solution)/shard_map/ppermute | solution.py:459
  83.3 3.1 %collective-permute-done.11 = f32[8,72,128]{2,1,0:T(8,128)S(1)} collective-permute-done((f32[8,72,128]{2,1,0:T(8,128)S(1)}, f32[8,72,128]{2,1,0:T(8,128)S(1)}, u32[]{:S(2)}, u32[]{:S(2)}) %collective-permute-start.11) | collective-permute-done | bytes 294944 | tf_op jit(solution)/shard_map/ppermute | solution.py:459
  86.5 2.1 %collective-permute-done.9 = f32[8,72,128]{2,1,0:T(8,128)S(1)} collective-permute-done((f32[8,72,128]{2,1,0:T(8,128)S(1)}, f32[8,72,128]{2,1,0:T(8,128)S(1)}, u32[]{:S(2)}, u32[]{:S(2)}) %collective-permute-start.9) | collective-permute-done | bytes 294944 | tf_op jit(solution)/shard_map/ppermute | solution.py:459
  88.6 0.1 add_add_fusion
  88.7 13.3 %all_to_all.16 = f32[8,72,128]{2,1,0:T(8,128)S(1)} all-to-all(f32[8,72,128]{2,1,0:T(8,128)S(1)} %add_add_fusion), channel_id=1, replica_groups=mesh['head'=16,'key'=8,'row'=2] {'key'}, dimensions={0} | all-to-all | bytes 589824 | tf_op jit(solution)/shard_map/all_to_all | solution.py:446
  102.1 0.7 broadcast_in_dim.2
  102.8 4.8 %all-to-all-start.2 = ((f32[8,72,128]{2,1,0:T(8,128)}), f32[8,72,128]{2,1,0:T(8,128)S(1)}, u32[]{:S(2)}, u32[]{:S(2)}) async-start(f32[8,72,128]{2,1,0:T(8,128)} %broadcast_in_dim.2), calls=%async_computation.2 | async-start | bytes 589824 | tf_op jit(solution)/shard_map/all_to_all | solution.py:446
  107.6 0.1 collective-permute-start.12
  107.7 1.2 %collective-permute-done.12 = f32[128,128]{1,0:T(8,128)S(1)} collective-permute-done((f32[128,128]{1,0:T(8,128)S(1)}, f32[128,128]{1,0:T(8,128)S(1)}, u32[]{:S(2)}, u32[]{:S(2)}) %collective-permute-start.12) | collective-permute-done | bytes 65568 | tf_op jit(solution)/shard_map/ppermute | solution.py:494
  108.9 0.6 dynamic-slice_add_fusion
  109.6 7.4 %all-to-all-done.2.got_ref = f32[8,72,128]{2,1,0:T(8,128)S(1)} async-done(((f32[8,72,128]{2,1,0:T(8,128)}), f32[8,72,128]{2,1,0:T(8,128)S(1)}, u32[]{:S(2)}, u32[]{:S(2)}) %all-to-all-start.2) | async-done | bytes 294944 | tf_op jit(solution)/shard_map/all_to_all | solution.py:446
  117.0 0.7 results.1
  (2 shorter events, 0.0 us)
Async XLA Ops:
  32.4 17.1 %collective-permute-start.1 = (f32[4,136,256]{2,1,0:T(8,128)S(1)}, f32[4,136,256]{2,1,0:T(8,128)S(1)}, u32[]{:S(2)}, u32[]{:S(2)}) collective-permute-start(f32[4,136,256]{2,1,0:T(8,128)S(1)} %head_sum.3), channel_id=1, source_target_pairs={{0,32},{1,129},{16,48},{17,145},{32,0},{33,161},{48,16},{49,177},{... | collective-permute-start | bytes 1671176 | tf_op jit(solution)/shard_map/ppermute | solution.py:459
  38.3 11.3 %collective-permute-start = (f32[4,136,256]{2,1,0:T(8,128)S(1)}, f32[4,136,256]{2,1,0:T(8,128)S(1)}, u32[]{:S(2)}, u32[]{:S(2)}) collective-permute-start(f32[4,136,256]{2,1,0:T(8,128)S(1)} %get-tuple-element.32), channel_id=1, source_target_pairs={{0,16},{1,65},{16,32},{17,81},{32,48},{33,97},{48,0},{49,113},{64,... | collective-permute-start | bytes 1671176 | tf_op jit(solution)/shard_map/ppermute | solution.py:459
  39.0 10.8 %collective-permute-start.2 = (f32[4,136,256]{2,1,0:T(8,128)S(1)}, f32[4,136,256]{2,1,0:T(8,128)S(1)}, u32[]{:S(2)}, u32[]{:S(2)}) collective-permute-start(f32[4,136,256]{2,1,0:T(8,128)S(1)} %get-tuple-element.33), channel_id=1, source_target_pairs={{0,48},{1,193},{16,0},{17,209},{32,16},{33,225},{48,32},{49,241},{... | collective-permute-start | bytes 1671176 | tf_op jit(solution)/shard_map/ppermute | solution.py:459
  42.9 16.4 %copy-start.1 = (bf16[256,128]{1,0:T(8,128)(2,1)S(1)}, bf16[256,128]{1,0:T(8,128)(2,1)}, u32[]{:S(2)}) copy-start(bf16[256,128]{1,0:T(8,128)(2,1)} %k_ref.1) | copy-start | bytes 196612
  50.0 17.6 %copy-start = (f32[128,64]{0,1:T(8,128)S(1)}, f32[128,64]{0,1:T(8,128)}, u32[]{:S(2)}) copy-start(f32[128,64]{0,1:T(8,128)} %param.9) | copy-start | bytes 98308
  50.0 6.3 %collective-permute-start.3 = (f32[136,256]{1,0:T(8,128)S(1)}, f32[136,256]{1,0:T(8,128)S(1)}, u32[]{:S(2)}, u32[]{:S(2)}) collective-permute-start(f32[136,256]{1,0:T(8,128)S(1)} %get-tuple-element.35), channel_id=1, source_target_pairs={{0,64},{1,17},{16,80},{17,33},{32,96},{33,49},{48,112},{49,1},{64,... | collective-permute-start | bytes 417800 | tf_op jit(solution)/shard_map/ppermute | solution.py:459
  51.6 7.3 %collective-permute-start.4 = (f32[136,256]{1,0:T(8,128)S(1)}, f32[136,256]{1,0:T(8,128)S(1)}, u32[]{:S(2)}, u32[]{:S(2)}) collective-permute-start(f32[136,256]{1,0:T(8,128)S(1)} %get-tuple-element.36), channel_id=1, source_target_pairs={{0,128},{1,33},{16,144},{17,49},{32,160},{33,1},{48,176},{49,17},{... | collective-permute-start | bytes 417800 | tf_op jit(solution)/shard_map/ppermute | solution.py:459
  54.3 5.1 %collective-permute-start.5 = (f32[136,256]{1,0:T(8,128)S(1)}, f32[136,256]{1,0:T(8,128)S(1)}, u32[]{:S(2)}, u32[]{:S(2)}) collective-permute-start(f32[136,256]{1,0:T(8,128)S(1)} %get-tuple-element.37), channel_id=1, source_target_pairs={{0,192},{1,49},{16,208},{17,1},{32,224},{33,17},{48,240},{49,33},{... | collective-permute-start | bytes 417800 | tf_op jit(solution)/shard_map/ppermute | solution.py:459
  62.0 9.6 %collective-permute-start.6 = (f32[288,256]{1,0:T(8,128)S(1)}, f32[288,256]{1,0:T(8,128)S(1)}, u32[]{:S(2)}, u32[]{:S(2)}) collective-permute-start(f32[288,256]{1,0:T(8,128)S(1)} %dlogits.1.dlogits_ref.refs_0_), channel_id=1, source_target_pairs={{0,16},{1,65},{16,32},{17,81},{32,48},{33,97},{48,0},{49,113},{64,... | collective-permute-start | bytes 884744 | tf_op jit(solution)/shard_map/ppermute | solution.py:459
  63.5 10.6 %collective-permute-start.7 = (f32[288,256]{1,0:T(8,128)S(1)}, f32[288,256]{1,0:T(8,128)S(1)}, u32[]{:S(2)}, u32[]{:S(2)}) collective-permute-start(f32[288,256]{1,0:T(8,128)S(1)} %dlogits.1.dlogits_ref.refs_0_), channel_id=1, source_target_pairs={{0,32},{1,129},{16,48},{17,145},{32,0},{33,161},{48,16},{49,177},{... | collective-permute-start | bytes 884744 | tf_op jit(solution)/shard_map/ppermute | solution.py:459
  66.2 7.9 %collective-permute-start.8 = (f32[288,256]{1,0:T(8,128)S(1)}, f32[288,256]{1,0:T(8,128)S(1)}, u32[]{:S(2)}, u32[]{:S(2)}) collective-permute-start(f32[288,256]{1,0:T(8,128)S(1)} %dlogits.1.dlogits_ref.refs_0_), channel_id=1, source_target_pairs={{0,48},{1,193},{16,0},{17,209},{32,16},{33,225},{48,32},{49,241},{... | collective-permute-start | bytes 884744 | tf_op jit(solution)/shard_map/ppermute | solution.py:459
  75.0 8.3 %collective-permute-start.10 = (f32[8,72,128]{2,1,0:T(8,128)S(1)}, f32[8,72,128]{2,1,0:T(8,128)S(1)}, u32[]{:S(2)}, u32[]{:S(2)}) collective-permute-start(f32[8,72,128]{2,1,0:T(8,128)S(1)} %query_gradient.3), channel_id=1, source_target_pairs={{0,128},{1,33},{16,144},{17,49},{32,160},{33,1},{48,176},{49,17},{... | collective-permute-start | bytes 884744 | tf_op jit(solution)/shard_map/ppermute | solution.py:459
  79.0 7.5 %collective-permute-start.11 = (f32[8,72,128]{2,1,0:T(8,128)S(1)}, f32[8,72,128]{2,1,0:T(8,128)S(1)}, u32[]{:S(2)}, u32[]{:S(2)}) collective-permute-start(f32[8,72,128]{2,1,0:T(8,128)S(1)} %get-tuple-element.49), channel_id=1, source_target_pairs={{0,192},{1,49},{16,208},{17,1},{32,224},{33,17},{48,240},{49,33},{... | collective-permute-start | bytes 884744 | tf_op jit(solution)/shard_map/ppermute | solution.py:459
  80.7 7.9 %collective-permute-start.9 = (f32[8,72,128]{2,1,0:T(8,128)S(1)}, f32[8,72,128]{2,1,0:T(8,128)S(1)}, u32[]{:S(2)}, u32[]{:S(2)}) collective-permute-start(f32[8,72,128]{2,1,0:T(8,128)S(1)} %get-tuple-element.48), channel_id=1, source_target_pairs={{0,64},{1,17},{16,80},{17,33},{32,96},{33,49},{48,112},{49,1},{64,... | collective-permute-start | bytes 884744 | tf_op jit(solution)/shard_map/ppermute | solution.py:459
  102.8 14.2 %all-to-all-start.2 = ((f32[8,72,128]{2,1,0:T(8,128)}), f32[8,72,128]{2,1,0:T(8,128)S(1)}, u32[]{:S(2)}, u32[]{:S(2)}) async-start(f32[8,72,128]{2,1,0:T(8,128)} %broadcast_in_dim.2), calls=%async_computation.2 | async-start | bytes 589824 | tf_op jit(solution)/shard_map/all_to_all | solution.py:446
  107.6 1.3 %collective-permute-start.12 = (f32[128,128]{1,0:T(8,128)S(1)}, f32[128,128]{1,0:T(8,128)S(1)}, u32[]{:S(2)}, u32[]{:S(2)}) collective-permute-start(f32[128,128]{1,0:T(8,128)S(1)} %constant_dynamic-slice_fusion), channel_id=1, source_target_pairs={{0,1},{1,0},{2,3},{3,2},{4,5},{5,4},{6,7},{7,6},{8,9},{9,8},{10,11... | collective-permute-start | bytes 196616 | tf_op jit(solution)/shard_map/ppermute | solution.py:494

commit v8 on v7

--- a/solution.py
+++ b/solution.py
@@ -274,10 +274,27 @@
     )(*got)
 
 
+def active_kernel(qh_ref, k_ref, active_ref):
+    heads, rows, _ = qh_ref.shape
+
+    def step(i, carry):
+        for j in range(GROUP):
+            active_ref[i * GROUP + j] = jnp.maximum(dot(k_ref[...], qh_ref[i * GROUP + j], NT), 0.0)
+        return carry
+
+    lax.fori_loop(0, heads // GROUP, step, 0)
+
+
+def active_products(qh, index_keys):
+    heads, rows, _ = qh.shape
+    return call(active_kernel, "active_products", 24, out_shape=f32(heads, index_keys.shape[0], rows))(qh, index_keys)
+
+
 def dlogits_kernel(key_total, *refs):
     got = refs[0:RING]
-    logits_ref, qh_ref, k_ref, send_ref, turned = refs[RING:]
-    heads, rows, depth = qh_ref.shape
+    logits_ref, active_ref, k_ref, send_ref, turned = refs[RING:]
+    heads, _, rows = active_ref.shape
+    depth = k_ref.shape[1]
     keys = k_ref.shape[0]
     root = 1.0 / math.sqrt(depth)
 
@@ -294,8 +311,7 @@
     def step(i, first, column):
         sums = []
         for j in range(GROUP):
-            products = dot(k_ref[...], qh_ref[i * GROUP + j], NT)
-            sums.append(jnp.sum(jnp.maximum(products, 0.0) * turned[...], axis=0, keepdims=True) * root)
+            sums.append(jnp.sum(active_ref[i * GROUP + j] * turned[...], axis=0, keepdims=True) * root)
         place = pl.ds(pl.multiple_of(rows + first, GROUP), GROUP)
         send_ref[place, column : column + rows] = jnp.concatenate(sums, axis=0)
 
@@ -313,30 +329,28 @@
     lax.fori_loop(0, half, high, 0)
 
 
-def dlogits_of(got, logits, qh, index_keys, key_total):
-    heads, rows, depth = qh.shape
-    keys = index_keys.shape[0]
+def dlogits_of(got, logits, active, index_keys, key_total):
+    heads, keys, rows = active.shape
     return call(
         functools.partial(dlogits_kernel, key_total),
         "dlogits",
         24,
         out_shape=f32(2 * rows + heads // 2, keys),
         scratch_shapes=[pltpu.VMEM((keys, rows), jnp.float32)],
-    )(*got, logits, qh, index_keys)
-
-
-def keys_kernel(dlogits_ref, qh_ref, k_ref, w_ref, keys_ref, slopes, turned):
+    )(*got, logits, active, index_keys)
+
+
+def keys_kernel(dlogits_ref, active_ref, qh_ref, w_ref, keys_ref, slopes, turned):
     heads, rows, depth = qh_ref.shape
     root = 1.0 / math.sqrt(depth)
-    for k in range(0, k_ref.shape[0], rows):
+    for k in range(0, turned.shape[0], rows):
         turned[k : k + rows] = dlogits_ref[0:rows, k : k + rows].T
     keys_ref[...] = jnp.zeros_like(keys_ref)
 
     def step(i, carry):
         weights = w_ref[pl.ds(i * GROUP, GROUP)] * root
         for j in range(GROUP):
-            products = dot(k_ref[...], qh_ref[i * GROUP + j], NT)
-            slope = jnp.where(products > 0.0, turned[...] * weights[j : j + 1], 0.0)
+            slope = jnp.where(active_ref[i * GROUP + j] > 0.0, turned[...] * weights[j : j + 1], 0.0)
             slopes[:, j * rows : (j + 1) * rows] = slope.astype(jnp.bfloat16)
         chunk = qh_ref[pl.ds(i * GROUP, GROUP)].reshape(GROUP * rows, depth)
         keys_ref[...] += dot(slopes[...], chunk, NN)
@@ -345,16 +359,16 @@
     lax.fori_loop(0, heads // GROUP, step, 0)
 
 
-def key_gradient(dlogits, qh, index_keys, weights):
+def key_gradient(dlogits, active, qh, weights):
     heads, rows, depth = qh.shape
-    keys = index_keys.shape[0]
+    keys = active.shape[1]
     return call(
         keys_kernel,
         "key_gradient",
         24,
         out_shape=f32(keys, depth),
         scratch_shapes=[pltpu.VMEM((keys, GROUP * rows), jnp.bfloat16), pltpu.VMEM((keys, rows), jnp.float32)],
-    )(dlogits, qh, index_keys, weights)
+    )(dlogits, active, qh, weights)
 
 
 def query_kernel(offsets, pieces, *refs):
@@ -479,28 +493,32 @@
     two = shift(far_two, 2, False)
     one = shift(sides[0], 1, False)
     three = shift(sides[1], 3, False)
-    got2 = [own, one, two, three]
+    own, late = lax.optimization_barrier((own, qh))
+    active = active_products(late, index_keys)
+    got2, active = lax.optimization_barrier(([own, one, two, three], active))
     send2 = partial_sum(got2)
     got2 = [send2[0]] + [shift(send2[d], d, True) for d in (1, 2, 3)]
     key_total = float(keys * head_count * key_count)
-    send3 = dlogits_of(got2, logits, qh, index_keys, key_total)
+    send3 = dlogits_of(got2, logits, active, index_keys, key_total)
     got3 = [send3] + [shift(send3, d, False) for d in range(1, RING)]
-    keys_part = key_gradient(send3, qh, index_keys, weights)
-    got3, keys_part = lax.optimization_barrier((got3, keys_part))
-
-    half = keys // 2
-    away = lax.dynamic_slice_in_dim(keys_part, (1 - row_index) * half, half, 0)
-    near = lax.dynamic_slice_in_dim(keys_part, row_index * half, half, 0)
-    key_grad = near + lax.ppermute(away, "row", [(0, 1), (1, 0)])
 
     (far_two,) = query_gradient((2,), got3, qh, weights, key_count)
-    got3, _ = lax.optimization_barrier((got3, far_two))
+    got3, active, _ = lax.optimization_barrier((got3, active, far_two))
     sides = query_gradient((1, 3), got3, qh, weights, key_count)
     (own,) = query_gradient((0,), got3, qh, weights, key_count)
     two = shift(far_two, 2, True)
     one = shift(sides[0], 1, True)
     three = shift(sides[1], 3, True)
+    active, _ = lax.optimization_barrier((active, own))
+    keys_part = key_gradient(send3, active, qh, weights)
+    two, keys_part = lax.optimization_barrier((two, keys_part))
     send4 = own + one + (two + three)
+
+    half = keys // 2
+    away = lax.dynamic_slice_in_dim(keys_part, (1 - row_index) * half, half, 0)
+    near = lax.dynamic_slice_in_dim(keys_part, row_index * half, half, 0)
+    key_grad = near + lax.ppermute(away, "row", [(0, 1), (1, 0)])
+
     got4 = jnp.sum(exchange(send4, "key"), axis=0)
     got5 = exchange(jnp.broadcast_to(got4[None], (key_count, *got4.shape)), "key")
     query_grad, weight_grad = results(got5, heads, share * (rows // key_count))

time: 120 us -> 118 us (0.983)
  waiting for transfers between devices: 28.3 us -> 26.9 us
    pallas_call x0 -> x1, Pallas kernels: none -> 2.4 us  [active_products(): call(active_kernel, 'active_products', 24, out_shape=f32(heads, index_key...]
    pallas_call x1, Pallas kernels: 2.67 us -> 0.97 us  [dlogits_of(): call(functools.partial(dlogits_kernel, key_total), 'dlogits', 24, out_sha...]
    ppermute x12, waiting for transfers between devices: 19.6 us -> 18.3 us  [shift(): return lax.ppermute(x, ('head', 'row'), pairs)]
  transfers between devices with their start and end apart: 14 -> 14, of which waited for: 11 -> 11; matrix products, arithmetic and copies ran while one was open for 1% -> 1% of each run, Pallas kernels for 9% -> 10%
where the time goes in v8:
time: 118 us; the launch traced here: 116 us
  Pallas kernels  30.6 us (26%)
  blocking collectives  28.8 us (24%)
  starting transfers between devices  27.6 us (23%)
  waiting for transfers between devices  26.9 us (23%)
    all_to_all x2, blocking collectives, exchange(): return lax.all_to_all(x, axis, split_axis=0, concat_axis=0, tiled=True)  28.8 us
    ppermute x12, starting transfers between devices, shift(): return lax.ppermute(x, ('head', 'row'), pairs)  22.7 us
    ppermute x12, waiting for transfers between devices, shift(): return lax.ppermute(x, ('head', 'row'), pairs)  18.3 us
    pallas_call x1, Pallas kernels, scores_and_logits(): call(scores_kernel, 'scores_and_logits', 32, in_specs=[HBM] * 5, out_spec...  14.9 us
    all_to_all x1, waiting for transfers between devices, exchange(): return lax.all_to_all(x, axis, split_axis=0, concat_axis=0, tiled=True)  7.41 us
    pallas_call x3, Pallas kernels, head_sum(): call(functools.partial(headsum_kernel, offsets), 'head_sum', 24, in_specs...  5.22 us
    all_to_all x1, starting transfers between devices, exchange(): return lax.all_to_all(x, axis, split_axis=0, concat_axis=0, tiled=True)  4.78 us
    pallas_call x3, Pallas kernels, query_gradient(): call(functools.partial(query_kernel, offsets, pieces), 'query_gradient',...  3.29 us
  transfers between devices with their start and end apart: 14, of which 11 were waited for; matrix products, arithmetic and copies ran while one was open for 1% of the time, Pallas kernels for 10%

profile of v8, /device:TPU:32, one launch (start us, length us, event | category | flops | bytes accessed | tf_op | source)
XLA Modules:
  0.0 116.2 jit_solution(4761642582580800675)
XLA Ops:
  0.6 14.9 %scores_and_logits.1 = (bf16[16,8,128,256]{3,2,1,0:T(8,128)(2,1)S(1)}, f32[32,128]{1,0:T(8,128)S(1)}, f32[8,24,128]{2,1,0:T(8,128)S(1)}, f32[256,128]{1,0:T(8,128)S(1)}, bf16[64,128,128]{2,1,0:T(8,128)(2,1)S(1)}) custom-call(bf16[8,576,128]{2,1,0:T(8,128)(2,1)} %bitcast.11, bf16[16,576,256]{2,1,0:T(8,128)(2,1)} %bitcast.10, bf16[128,64,128]{2,1,0:T(8,128)(2,1)} %iq_hbm.1, ...), custom_call_target="tpu_custom_call" | custom-call | tf_op jit(solution)/shard_map/scores_and_logits/pallas_call | solution.py:166
  15.6 15.5 %all_to_all.15.got_ref = f32[8,24,128]{2,1,0:T(8,128)S(1)} all-to-all(f32[8,24,128]{2,1,0:T(8,128)S(1)} %get-tuple-element.36), channel_id=1, replica_groups=mesh['head'=16,'key'=8,'row'=2] {'key'}, dimensions={0} | all-to-all | bytes 196608 | tf_op jit(solution)/shard_map/all_to_all | solution.py:460
  31.1 1.3 %head_sum.3 = f32[4,136,256]{2,1,0:T(8,128)S(1)} custom-call(bf16[16,8,128,256]{3,2,1,0:T(8,128)(2,1)S(1)} %get-tuple-element.34.e_ref, f32[32,128]{1,0:T(8,128)S(1)} %get-tuple-element.35.tops_ref, f32[8,24,128]{2,1,0:T(8,128)S(1)} %all_to_all.15.got_ref), custom_call_target="tpu_custom_call" | custom-call | tf_op jit(solution)/shard_map/head_sum/pallas_call | solution.py:233
  32.4 3.3 %collective-permute-start.1 = (f32[4,136,256]{2,1,0:T(8,128)S(1)}, f32[4,136,256]{2,1,0:T(8,128)S(1)}, u32[]{:S(2)}, u32[]{:S(2)}) collective-permute-start(f32[4,136,256]{2,1,0:T(8,128)S(1)} %head_sum.3), channel_id=1, source_target_pairs={{0,32},{1,129},{16,48},{17,145},{32,0},{33,161},{48,16},{49,177},{... | collective-permute-start | bytes 1671176 | tf_op jit(solution)/shard_map/ppermute | solution.py:473
  35.7 2.5 %head_sum.5 = (f32[4,136,256]{2,1,0:T(8,128)S(1)}, f32[4,136,256]{2,1,0:T(8,128)S(1)}) custom-call(bf16[16,8,128,256]{3,2,1,0:T(8,128)(2,1)S(1)} %get-tuple-element.34.e_ref, f32[32,128]{1,0:T(8,128)S(1)} %get-tuple-element.35.tops_ref, f32[8,24,128]{2,1,0:T(8,128)S(1)} %all_to_all.15.got_ref), custom_call_target="tpu_custom_call" | custom-call | tf_op jit(solution)/shard_map/head_sum/pallas_call | solution.py:233
  38.3 0.0 copy-start.1
  38.3 0.8 collective-permute-start
  39.0 2.6 %collective-permute-start.2 = (f32[4,136,256]{2,1,0:T(8,128)S(1)}, f32[4,136,256]{2,1,0:T(8,128)S(1)}, u32[]{:S(2)}, u32[]{:S(2)}) collective-permute-start(f32[4,136,256]{2,1,0:T(8,128)S(1)} %get-tuple-element.41), channel_id=1, source_target_pairs={{0,48},{1,193},{16,0},{17,209},{32,16},{33,225},{48,32},{49,241},{... | collective-permute-start | bytes 1671176 | tf_op jit(solution)/shard_map/ppermute | solution.py:473
  41.6 1.3 %head_sum.4.refs_0_ = f32[4,136,256]{2,1,0:T(8,128)S(1)} custom-call(bf16[16,8,128,256]{3,2,1,0:T(8,128)(2,1)S(1)} %get-tuple-element.34.e_ref, f32[32,128]{1,0:T(8,128)S(1)} %get-tuple-element.35.tops_ref, f32[8,24,128]{2,1,0:T(8,128)S(1)} %all_to_all.15.got_ref), custom_call_target="tpu_custom_call" | custom-call | tf_op jit(solution)/shard_map/head_sum/pallas_call | solution.py:233
  42.9 0.0 copy-done.1
  42.9 2.4 %active_products.1.refs_5_.active_ref = f32[64,256,128]{2,1,0:T(8,128)S(1)} custom-call(bf16[64,128,128]{2,1,0:T(8,128)(2,1)S(1)} %get-tuple-element.42.qh_ref.refs_4_, bf16[256,128]{1,0:T(8,128)(2,1)S(1)} %copy-done.1), custom_call_target="tpu_custom_call" | custom-call | tf_op jit(solution)/shard_map/active_products/pallas_call | solution.py:290
  45.3 4.2 %collective-permute-done.refs_1_ = f32[4,136,256]{2,1,0:T(8,128)S(1)} collective-permute-done((f32[4,136,256]{2,1,0:T(8,128)S(1)}, f32[4,136,256]{2,1,0:T(8,128)S(1)}, u32[]{:S(2)}, u32[]{:S(2)}) %collective-permute-start) | collective-permute-done | bytes 557088 | tf_op jit(solution)/shard_map/ppermute | solution.py:473
  49.5 0.0 collective-permute-done.1.refs_2_
  49.5 0.3 collective-permute-done.2.refs_3_
  49.9 0.1 partial_sum.1
  50.0 1.6 %collective-permute-start.3 = (f32[136,256]{1,0:T(8,128)S(1)}, f32[136,256]{1,0:T(8,128)S(1)}, u32[]{:S(2)}, u32[]{:S(2)}) collective-permute-start(f32[136,256]{1,0:T(8,128)S(1)} %get-tuple-element.48), channel_id=1, source_target_pairs={{0,64},{1,17},{16,80},{17,33},{32,96},{33,49},{48,112},{49,1},{64,... | collective-permute-start | bytes 417800 | tf_op jit(solution)/shard_map/ppermute | solution.py:473
  51.6 2.7 %collective-permute-start.4 = (f32[136,256]{1,0:T(8,128)S(1)}, f32[136,256]{1,0:T(8,128)S(1)}, u32[]{:S(2)}, u32[]{:S(2)}) collective-permute-start(f32[136,256]{1,0:T(8,128)S(1)} %get-tuple-element.49), channel_id=1, source_target_pairs={{0,128},{1,33},{16,144},{17,49},{32,160},{33,1},{48,176},{49,17},{... | collective-permute-start | bytes 417800 | tf_op jit(solution)/shard_map/ppermute | solution.py:473
  54.3 1.4 %collective-permute-start.5 = (f32[136,256]{1,0:T(8,128)S(1)}, f32[136,256]{1,0:T(8,128)S(1)}, u32[]{:S(2)}, u32[]{:S(2)}) collective-permute-start(f32[136,256]{1,0:T(8,128)S(1)} %get-tuple-element.50), channel_id=1, source_target_pairs={{0,192},{1,49},{16,208},{17,1},{32,224},{33,17},{48,240},{49,33},{... | collective-permute-start | bytes 417800 | tf_op jit(solution)/shard_map/ppermute | solution.py:473
  55.7 0.6 collective-permute-done.3.refs_1_
  56.3 2.5 %collective-permute-done.4.refs_2_ = f32[136,256]{1,0:T(8,128)S(1)} collective-permute-done((f32[136,256]{1,0:T(8,128)S(1)}, f32[136,256]{1,0:T(8,128)S(1)}, u32[]{:S(2)}, u32[]{:S(2)}) %collective-permute-start.4) | collective-permute-done | bytes 139296 | tf_op jit(solution)/shard_map/ppermute | solution.py:473
  58.8 0.5 collective-permute-done.5.refs_3_
  59.3 1.0 dlogits.1.refs_0_.dlogits_ref
  60.3 1.5 %collective-permute-start.6 = (f32[288,256]{1,0:T(8,128)S(1)}, f32[288,256]{1,0:T(8,128)S(1)}, u32[]{:S(2)}, u32[]{:S(2)}) collective-permute-start(f32[288,256]{1,0:T(8,128)S(1)} %dlogits.1.refs_0_.dlogits_ref), channel_id=1, source_target_pairs={{0,16},{1,65},{16,32},{17,81},{32,48},{33,97},{48,0},{49,113},{64,... | collective-permute-start | bytes 884744 | tf_op jit(solution)/shard_map/ppermute | solution.py:473
  61.8 2.7 %collective-permute-start.7 = (f32[288,256]{1,0:T(8,128)S(1)}, f32[288,256]{1,0:T(8,128)S(1)}, u32[]{:S(2)}, u32[]{:S(2)}) collective-permute-start(f32[288,256]{1,0:T(8,128)S(1)} %dlogits.1.refs_0_.dlogits_ref), channel_id=1, source_target_pairs={{0,32},{1,129},{16,48},{17,145},{32,0},{33,161},{48,16},{49,177},{... | collective-permute-start | bytes 884744 | tf_op jit(solution)/shard_map/ppermute | solution.py:473
  64.5 1.4 %collective-permute-start.8 = (f32[288,256]{1,0:T(8,128)S(1)}, f32[288,256]{1,0:T(8,128)S(1)}, u32[]{:S(2)}, u32[]{:S(2)}) collective-permute-start(f32[288,256]{1,0:T(8,128)S(1)} %dlogits.1.refs_0_.dlogits_ref), channel_id=1, source_target_pairs={{0,48},{1,193},{16,0},{17,209},{32,16},{33,225},{48,32},{49,241},{... | collective-permute-start | bytes 884744 | tf_op jit(solution)/shard_map/ppermute | solution.py:473
  65.9 2.4 %collective-permute-done.6.refs_1_ = f32[288,256]{1,0:T(8,128)S(1)} collective-permute-done((f32[288,256]{1,0:T(8,128)S(1)}, f32[288,256]{1,0:T(8,128)S(1)}, u32[]{:S(2)}, u32[]{:S(2)}) %collective-permute-start.6) | collective-permute-done | bytes 294944 | tf_op jit(solution)/shard_map/ppermute | solution.py:473
  68.3 4.1 %collective-permute-done.7.refs_2_ = f32[288,256]{1,0:T(8,128)S(1)} collective-permute-done((f32[288,256]{1,0:T(8,128)S(1)}, f32[288,256]{1,0:T(8,128)S(1)}, u32[]{:S(2)}, u32[]{:S(2)}) %collective-permute-start.7) | collective-permute-done | bytes 294944 | tf_op jit(solution)/shard_map/ppermute | solution.py:473
  72.4 0.0 collective-permute-done.8.refs_3_
  72.4 0.0 copy-done
  72.4 0.9 query_gradient.3
  73.3 2.7 %collective-permute-start.10 = (f32[8,72,128]{2,1,0:T(8,128)S(1)}, f32[8,72,128]{2,1,0:T(8,128)S(1)}, u32[]{:S(2)}, u32[]{:S(2)}) collective-permute-start(f32[8,72,128]{2,1,0:T(8,128)S(1)} %query_gradient.3), channel_id=1, source_target_pairs={{0,128},{1,33},{16,144},{17,49},{32,160},{33,1},{48,176},{49,17},{... | collective-permute-start | bytes 884744 | tf_op jit(solution)/shard_map/ppermute | solution.py:473
  76.0 1.5 %query_gradient.5 = (f32[8,72,128]{2,1,0:T(8,128)S(1)}, f32[8,72,128]{2,1,0:T(8,128)S(1)}) custom-call(f32[288,256]{1,0:T(8,128)S(1)} %dlogits.1.refs_0_.dlogits_ref, f32[288,256]{1,0:T(8,128)S(1)} %collective-permute-done.6.refs_1_, f32[288,256]{1,0:T(8,128)S(1)} %collective-permute-done.7.refs_2_, f32[288,256]{1,0:T(8,128)S(1)} %collective-permute-done.8.refs_3_, ...), custom_call_target="tpu_custom_call" | custom-call | tf_op jit(solution)/shard_map/query_gradient/pallas_call | solution.py:423
  77.5 1.7 %collective-permute-start.11 = (f32[8,72,128]{2,1,0:T(8,128)S(1)}, f32[8,72,128]{2,1,0:T(8,128)S(1)}, u32[]{:S(2)}, u32[]{:S(2)}) collective-permute-start(f32[8,72,128]{2,1,0:T(8,128)S(1)} %get-tuple-element.61), channel_id=1, source_target_pairs={{0,192},{1,49},{16,208},{17,1},{32,224},{33,17},{48,240},{49,33},{... | collective-permute-start | bytes 884744 | tf_op jit(solution)/shard_map/ppermute | solution.py:473
  79.2 0.4 collective-permute-start.9
  79.6 0.9 query_gradient.4
  80.5 2.9 %key_gradient.1 = f32[256,128]{1,0:T(8,128)S(1)} custom-call(f32[288,256]{1,0:T(8,128)S(1)} %dlogits.1.refs_0_.dlogits_ref, f32[64,256,128]{2,1,0:T(8,128)S(1)} %active_products.1.refs_5_.active_ref, bf16[64,128,128]{2,1,0:T(8,128)(2,1)S(1)} %get-tuple-element.42.qh_ref.refs_4_, f32[64,128]{1,0:T(8,128)S(1)} %bitcast.9), custom_call_target="tpu_custom_call" | custom-call | tf_op jit(solution)/shard_map/key_gradient/pallas_call | solution.py:365
  83.4 0.0 collective-permute-done.10
  83.4 1.5 %collective-permute-done.11 = f32[8,72,128]{2,1,0:T(8,128)S(1)} collective-permute-done((f32[8,72,128]{2,1,0:T(8,128)S(1)}, f32[8,72,128]{2,1,0:T(8,128)S(1)}, u32[]{:S(2)}, u32[]{:S(2)}) %collective-permute-start.11) | collective-permute-done | bytes 294944 | tf_op jit(solution)/shard_map/ppermute | solution.py:473
  84.9 2.2 %collective-permute-done.9 = f32[8,72,128]{2,1,0:T(8,128)S(1)} collective-permute-done((f32[8,72,128]{2,1,0:T(8,128)S(1)}, f32[8,72,128]{2,1,0:T(8,128)S(1)}, u32[]{:S(2)}, u32[]{:S(2)}) %collective-permute-start.9) | collective-permute-done | bytes 294944 | tf_op jit(solution)/shard_map/ppermute | solution.py:473
  87.1 0.1 add_add_fusion
  87.2 13.3 %all_to_all.16 = f32[8,72,128]{2,1,0:T(8,128)S(1)} all-to-all(f32[8,72,128]{2,1,0:T(8,128)S(1)} %add_add_fusion), channel_id=1, replica_groups=mesh['head'=16,'key'=8,'row'=2] {'key'}, dimensions={0} | all-to-all | bytes 589824 | tf_op jit(solution)/shard_map/all_to_all | solution.py:460
  100.5 0.7 broadcast_in_dim.2
  101.3 4.8 %all-to-all-start.2 = ((f32[8,72,128]{2,1,0:T(8,128)}), f32[8,72,128]{2,1,0:T(8,128)S(1)}, u32[]{:S(2)}, u32[]{:S(2)}) async-start(f32[8,72,128]{2,1,0:T(8,128)} %broadcast_in_dim.2), calls=%async_computation.2 | async-start | bytes 589824 | tf_op jit(solution)/shard_map/all_to_all | solution.py:460
  106.0 0.1 collective-permute-start.12
  106.1 1.2 %collective-permute-done.12 = f32[128,128]{1,0:T(8,128)S(1)} collective-permute-done((f32[128,128]{1,0:T(8,128)S(1)}, f32[128,128]{1,0:T(8,128)S(1)}, u32[]{:S(2)}, u32[]{:S(2)}) %collective-permute-start.12) | collective-permute-done | bytes 65568 | tf_op jit(solution)/shard_map/ppermute | solution.py:520
  107.4 0.6 dynamic-slice_add_fusion
  108.0 7.4 %all-to-all-done.2.got_ref = f32[8,72,128]{2,1,0:T(8,128)S(1)} async-done(((f32[8,72,128]{2,1,0:T(8,128)}), f32[8,72,128]{2,1,0:T(8,128)S(1)}, u32[]{:S(2)}, u32[]{:S(2)}) %all-to-all-start.2) | async-done | bytes 294944 | tf_op jit(solution)/shard_map/all_to_all | solution.py:460
  115.4 0.7 results.1
  (3 shorter events, 0.0 us)
Async XLA Ops:
  32.4 17.1 %collective-permute-start.1 = (f32[4,136,256]{2,1,0:T(8,128)S(1)}, f32[4,136,256]{2,1,0:T(8,128)S(1)}, u32[]{:S(2)}, u32[]{:S(2)}) collective-permute-start(f32[4,136,256]{2,1,0:T(8,128)S(1)} %head_sum.3), channel_id=1, source_target_pairs={{0,32},{1,129},{16,48},{17,145},{32,0},{33,161},{48,16},{49,177},{... | collective-permute-start | bytes 1671176 | tf_op jit(solution)/shard_map/ppermute | solution.py:473
  38.3 4.7 %copy-start.1 = (bf16[256,128]{1,0:T(8,128)(2,1)S(1)}, bf16[256,128]{1,0:T(8,128)(2,1)}, u32[]{:S(2)}) copy-start(bf16[256,128]{1,0:T(8,128)(2,1)} %refs_6_.1) | copy-start | bytes 196612
  38.3 11.2 %collective-permute-start = (f32[4,136,256]{2,1,0:T(8,128)S(1)}, f32[4,136,256]{2,1,0:T(8,128)S(1)}, u32[]{:S(2)}, u32[]{:S(2)}) collective-permute-start(f32[4,136,256]{2,1,0:T(8,128)S(1)} %get-tuple-element.40), channel_id=1, source_target_pairs={{0,16},{1,65},{16,32},{17,81},{32,48},{33,97},{48,0},{49,113},{64,... | collective-permute-start | bytes 1671176 | tf_op jit(solution)/shard_map/ppermute | solution.py:473
  39.0 10.8 %collective-permute-start.2 = (f32[4,136,256]{2,1,0:T(8,128)S(1)}, f32[4,136,256]{2,1,0:T(8,128)S(1)}, u32[]{:S(2)}, u32[]{:S(2)}) collective-permute-start(f32[4,136,256]{2,1,0:T(8,128)S(1)} %get-tuple-element.41), channel_id=1, source_target_pairs={{0,48},{1,193},{16,0},{17,209},{32,16},{33,225},{48,32},{49,241},{... | collective-permute-start | bytes 1671176 | tf_op jit(solution)/shard_map/ppermute | solution.py:473
  50.0 6.3 %collective-permute-start.3 = (f32[136,256]{1,0:T(8,128)S(1)}, f32[136,256]{1,0:T(8,128)S(1)}, u32[]{:S(2)}, u32[]{:S(2)}) collective-permute-start(f32[136,256]{1,0:T(8,128)S(1)} %get-tuple-element.48), channel_id=1, source_target_pairs={{0,64},{1,17},{16,80},{17,33},{32,96},{33,49},{48,112},{49,1},{64,... | collective-permute-start | bytes 417800 | tf_op jit(solution)/shard_map/ppermute | solution.py:473
  51.6 7.3 %collective-permute-start.4 = (f32[136,256]{1,0:T(8,128)S(1)}, f32[136,256]{1,0:T(8,128)S(1)}, u32[]{:S(2)}, u32[]{:S(2)}) collective-permute-start(f32[136,256]{1,0:T(8,128)S(1)} %get-tuple-element.49), channel_id=1, source_target_pairs={{0,128},{1,33},{16,144},{17,49},{32,160},{33,1},{48,176},{49,17},{... | collective-permute-start | bytes 417800 | tf_op jit(solution)/shard_map/ppermute | solution.py:473
  54.3 5.1 %collective-permute-start.5 = (f32[136,256]{1,0:T(8,128)S(1)}, f32[136,256]{1,0:T(8,128)S(1)}, u32[]{:S(2)}, u32[]{:S(2)}) collective-permute-start(f32[136,256]{1,0:T(8,128)S(1)} %get-tuple-element.50), channel_id=1, source_target_pairs={{0,192},{1,49},{16,208},{17,1},{32,224},{33,17},{48,240},{49,33},{... | collective-permute-start | bytes 417800 | tf_op jit(solution)/shard_map/ppermute | solution.py:473
  59.3 13.1 %copy-start = (f32[128,64]{0,1:T(8,128)S(1)}, f32[128,64]{0,1:T(8,128)}, u32[]{:S(2)}) copy-start(f32[128,64]{0,1:T(8,128)} %param.9) | copy-start | bytes 98308
  60.3 8.0 %collective-permute-start.6 = (f32[288,256]{1,0:T(8,128)S(1)}, f32[288,256]{1,0:T(8,128)S(1)}, u32[]{:S(2)}, u32[]{:S(2)}) collective-permute-start(f32[288,256]{1,0:T(8,128)S(1)} %dlogits.1.refs_0_.dlogits_ref), channel_id=1, source_target_pairs={{0,16},{1,65},{16,32},{17,81},{32,48},{33,97},{48,0},{49,113},{64,... | collective-permute-start | bytes 884744 | tf_op jit(solution)/shard_map/ppermute | solution.py:473
  61.8 10.6 %collective-permute-start.7 = (f32[288,256]{1,0:T(8,128)S(1)}, f32[288,256]{1,0:T(8,128)S(1)}, u32[]{:S(2)}, u32[]{:S(2)}) collective-permute-start(f32[288,256]{1,0:T(8,128)S(1)} %dlogits.1.refs_0_.dlogits_ref), channel_id=1, source_target_pairs={{0,32},{1,129},{16,48},{17,145},{32,0},{33,161},{48,16},{49,177},{... | collective-permute-start | bytes 884744 | tf_op jit(solution)/shard_map/ppermute | solution.py:473
  64.5 7.9 %collective-permute-start.8 = (f32[288,256]{1,0:T(8,128)S(1)}, f32[288,256]{1,0:T(8,128)S(1)}, u32[]{:S(2)}, u32[]{:S(2)}) collective-permute-start(f32[288,256]{1,0:T(8,128)S(1)} %dlogits.1.refs_0_.dlogits_ref), channel_id=1, source_target_pairs={{0,48},{1,193},{16,0},{17,209},{32,16},{33,225},{48,32},{49,241},{... | collective-permute-start | bytes 884744 | tf_op jit(solution)/shard_map/ppermute | solution.py:473
  73.3 10.1 %collective-permute-start.10 = (f32[8,72,128]{2,1,0:T(8,128)S(1)}, f32[8,72,128]{2,1,0:T(8,128)S(1)}, u32[]{:S(2)}, u32[]{:S(2)}) collective-permute-start(f32[8,72,128]{2,1,0:T(8,128)S(1)} %query_gradient.3), channel_id=1, source_target_pairs={{0,128},{1,33},{16,144},{17,49},{32,160},{33,1},{48,176},{49,17},{... | collective-permute-start | bytes 884744 | tf_op jit(solution)/shard_map/ppermute | solution.py:473
  77.5 7.5 %collective-permute-start.11 = (f32[8,72,128]{2,1,0:T(8,128)S(1)}, f32[8,72,128]{2,1,0:T(8,128)S(1)}, u32[]{:S(2)}, u32[]{:S(2)}) collective-permute-start(f32[8,72,128]{2,1,0:T(8,128)S(1)} %get-tuple-element.61), channel_id=1, source_target_pairs={{0,192},{1,49},{16,208},{17,1},{32,224},{33,17},{48,240},{49,33},{... | collective-permute-start | bytes 884744 | tf_op jit(solution)/shard_map/ppermute | solution.py:473
  79.2 7.9 %collective-permute-start.9 = (f32[8,72,128]{2,1,0:T(8,128)S(1)}, f32[8,72,128]{2,1,0:T(8,128)S(1)}, u32[]{:S(2)}, u32[]{:S(2)}) collective-permute-start(f32[8,72,128]{2,1,0:T(8,128)S(1)} %get-tuple-element.57), channel_id=1, source_target_pairs={{0,64},{1,17},{16,80},{17,33},{32,96},{33,49},{48,112},{49,1},{64,... | collective-permute-start | bytes 884744 | tf_op jit(solution)/shard_map/ppermute | solution.py:473
  101.3 14.2 %all-to-all-start.2 = ((f32[8,72,128]{2,1,0:T(8,128)}), f32[8,72,128]{2,1,0:T(8,128)S(1)}, u32[]{:S(2)}, u32[]{:S(2)}) async-start(f32[8,72,128]{2,1,0:T(8,128)} %broadcast_in_dim.2), calls=%async_computation.2 | async-start | bytes 589824 | tf_op jit(solution)/shard_map/all_to_all | solution.py:460
  106.0 1.3 %collective-permute-start.12 = (f32[128,128]{1,0:T(8,128)S(1)}, f32[128,128]{1,0:T(8,128)S(1)}, u32[]{:S(2)}, u32[]{:S(2)}) collective-permute-start(f32[128,128]{1,0:T(8,128)S(1)} %constant_dynamic-slice_fusion), channel_id=1, source_target_pairs={{0,1},{1,0},{2,3},{3,2},{4,5},{5,4},{6,7},{7,6},{8,9},{9,8},{10,11... | collective-permute-start | bytes 196616 | tf_op jit(solution)/shard_map/ppermute | solution.py:520

commit v9 on v8

--- a/solution.py
+++ b/solution.py
@@ -70,6 +70,7 @@
     _, iheads, depth = iq_ref.shape
     keys = k_ref.shape[0]
     group = GROUP
+    pitch = wide.shape[0] // rows
 
     first = pltpu.make_async_copy(q_hbm, q_ref, sems.at[steps])
     first.start()
@@ -117,14 +118,15 @@
     for copy in others:
         copy.wait()
     total_ref[...] = jnp.zeros_like(total_ref)
-    wide[...] = iq_ref[...].astype(jnp.float32).reshape(rows * iheads, depth)
+    for t in range(rows):
+        wide[t * pitch : t * pitch + iheads] = iq_ref[t].astype(jnp.float32)
     columns = jnp.concatenate([w_ref[...], jnp.zeros((LANES - iheads, rows), jnp.float32)], axis=0).T
 
     def logit_step(step, carry):
         weights = pltpu.roll(columns, LANES - group * step, 1)
         for j in range(group):
             head = step * group + j
-            qh_ref[head] = wide[pl.ds(head, rows, stride=iheads), :].astype(jnp.bfloat16)
+            qh_ref[head] = wide[pl.ds(head, rows, stride=pitch), :].astype(jnp.bfloat16)
         chunk = qh_ref[pl.ds(step * group, group)].reshape(group * rows, depth)
         products = dot(chunk, k_ref[...], NT)
         total = total_ref[...]
@@ -182,7 +184,7 @@
             pltpu.VMEM(index_query.shape, jnp.bfloat16),
             pltpu.VMEM(index_keys.shape, jnp.bfloat16),
             pltpu.VMEM(weights.shape, jnp.float32),
-            pltpu.VMEM((rows * iheads, depth), jnp.float32),
+            pltpu.VMEM((rows * (iheads + 8), depth), jnp.float32),
             pltpu.VMEM((rows, keys), jnp.float32),
             pltpu.VMEM((rows * heads, width), jnp.bfloat16),
             pltpu.VMEM((rows, LANES), jnp.float32),
@@ -221,11 +223,11 @@
             for h in range(heads):
                 term = e_ref[block, h].astype(jnp.float32) * columns[:, h * steps : h * steps + 1]
                 total = term if total is None else total + term
-            outs[i][k, 0:rows] = total
-            outs[i][k, rows:] = tail
+            outs[i][pl.ds(pl.multiple_of(k * rows, rows), rows)] = total
             return carry
 
         lax.fori_loop(0, RING, body, 0)
+        outs[i][RING * rows :] = tail
 
 
 def head_sum(offsets, terms, tops, got):
@@ -236,7 +238,7 @@
         24,
         in_specs=[VMEM] * 3,
         out_specs=[VMEM] * len(offsets),
-        out_shape=[f32(blocks // RING, rows + 8, keys)] * len(offsets),
+        out_shape=[f32(blocks // RING * rows + 8, keys)] * len(offsets),
     )(terms, tops, got)
 
 
@@ -254,17 +256,19 @@
     got, outs = refs[0:RING], refs[RING:]
     rows = outs[0].shape[0] - 8
     _, far, _, _ = position()
-    top, total = merged_stats([r[0, rows : rows + 1] for r in got], [r[0, rows + 1 : rows + 2] for r in got])
+    last = RING * rows
+    top, total = merged_stats([r[last : last + 1] for r in got], [r[last + 1 : last + 2] for r in got])
     for d in range(RING):
-        k = lax.rem(far + d, RING)
-        outs[d][0:rows] = got[0][k, 0:rows] + got[1][k, 0:rows] + (got[2][k, 0:rows] + got[3][k, 0:rows])
+        place = pl.ds(pl.multiple_of(lax.rem(far + d, RING) * rows, rows), rows)
+        outs[d][0:rows] = got[0][place] + got[1][place] + (got[2][place] + got[3][place])
         outs[d][rows:] = jnp.zeros_like(outs[d][rows:])
         outs[d][rows : rows + 1] = top
         outs[d][rows + 1 : rows + 2] = total
 
 
 def partial_sum(got):
-    _, height, keys = got[0].shape
+    height, keys = got[0].shape
+    height = (height - 8) // RING + 8
     return call(
         partial_kernel,
         "partial_sum",
@@ -497,10 +501,12 @@
     active = active_products(late, index_keys)
     got2, active = lax.optimization_barrier(([own, one, two, three], active))
     send2 = partial_sum(got2)
-    got2 = [send2[0]] + [shift(send2[d], d, True) for d in (1, 2, 3)]
+    two, one, three = [shift(send2[d], d, True) for d in (2, 1, 3)]
+    got2 = [send2[0], one, two, three]
     key_total = float(keys * head_count * key_count)
     send3 = dlogits_of(got2, logits, active, index_keys, key_total)
-    got3 = [send3] + [shift(send3, d, False) for d in range(1, RING)]
+    two, one, three = [shift(send3, d, False) for d in (2, 1, 3)]
+    got3 = [send3, one, two, three]
 
     (far_two,) = query_gradient((2,), got3, qh, weights, key_count)
     got3, active, _ = lax.optimization_barrier((got3, active, far_two))

time: 118 us -> 116 us (0.983)
  Pallas kernels: 30.6 us -> 28.8 us
    pallas_call x1, Pallas kernels: 14.9 us -> 13.1 us  [scores_and_logits(): call(scores_kernel, 'scores_and_logits', 32, in_specs=[HBM] * 5, out_spec...]
where the time goes in v9:
time: 116 us; the launch traced here: 114 us
  Pallas kernels  28.8 us (25%)
  blocking collectives  28.8 us (25%)
  starting transfers between devices  27.5 us (24%)
  waiting for transfers between devices  26.5 us (23%)
    all_to_all x2, blocking collectives, exchange(): return lax.all_to_all(x, axis, split_axis=0, concat_axis=0, tiled=True)  28.8 us
    ppermute x12, starting transfers between devices, shift(): return lax.ppermute(x, ('head', 'row'), pairs)  22.7 us
    ppermute x12, waiting for transfers between devices, shift(): return lax.ppermute(x, ('head', 'row'), pairs)  17.8 us
    pallas_call x1, Pallas kernels, scores_and_logits(): call(scores_kernel, 'scores_and_logits', 32, in_specs=[HBM] * 5, out_spec...  13.1 us
    all_to_all x1, waiting for transfers between devices, exchange(): return lax.all_to_all(x, axis, split_axis=0, concat_axis=0, tiled=True)  7.41 us
    pallas_call x3, Pallas kernels, head_sum(): call(functools.partial(headsum_kernel, offsets), 'head_sum', 24, in_specs...  5.23 us
    all_to_all x1, starting transfers between devices, exchange(): return lax.all_to_all(x, axis, split_axis=0, concat_axis=0, tiled=True)  4.78 us
    pallas_call x3, Pallas kernels, query_gradient(): call(functools.partial(query_kernel, offsets, pieces), 'query_gradient',...  3.29 us
  transfers between devices with their start and end apart: 14, of which 11 were waited for; matrix products, arithmetic and copies ran while one was open for 1% of the time, Pallas kernels for 10%

profile of v9, /device:TPU:32, one launch (start us, length us, event | category | flops | bytes accessed | tf_op | source)
XLA Modules:
  0.0 113.9 jit_solution(15478234831587245974)
XLA Ops:
  0.6 13.1 %scores_and_logits.1 = (bf16[16,8,128,256]{3,2,1,0:T(8,128)(2,1)S(1)}, f32[32,128]{1,0:T(8,128)S(1)}, f32[8,24,128]{2,1,0:T(8,128)S(1)}, f32[256,128]{1,0:T(8,128)S(1)}, bf16[64,128,128]{2,1,0:T(8,128)(2,1)S(1)}) custom-call(bf16[8,576,128]{2,1,0:T(8,128)(2,1)} %bitcast.11, bf16[16,576,256]{2,1,0:T(8,128)(2,1)} %bitcast.10, bf16[128,64,128]{2,1,0:T(8,128)(2,1)} %iq_hbm.1, ...), custom_call_target="tpu_custom_call" | custom-call | tf_op jit(solution)/shard_map/scores_and_logits/pallas_call | solution.py:168
  13.8 15.5 %all_to_all.15.got_ref = f32[8,24,128]{2,1,0:T(8,128)S(1)} all-to-all(f32[8,24,128]{2,1,0:T(8,128)S(1)} %get-tuple-element.36), channel_id=1, replica_groups=mesh['head'=16,'key'=8,'row'=2] {'key'}, dimensions={0} | all-to-all | bytes 196608 | tf_op jit(solution)/shard_map/all_to_all | solution.py:464
  29.3 1.3 %head_sum.3 = f32[520,256]{1,0:T(8,128)S(1)} custom-call(bf16[16,8,128,256]{3,2,1,0:T(8,128)(2,1)S(1)} %get-tuple-element.34.e_ref, f32[32,128]{1,0:T(8,128)S(1)} %get-tuple-element.35.tops_ref, f32[8,24,128]{2,1,0:T(8,128)S(1)} %all_to_all.15.got_ref), custom_call_target="tpu_custom_call" | custom-call | tf_op jit(solution)/shard_map/head_sum/pallas_call | solution.py:235
  30.6 3.3 %collective-permute-start.1 = (f32[520,256]{1,0:T(8,128)S(1)}, f32[520,256]{1,0:T(8,128)S(1)}, u32[]{:S(2)}, u32[]{:S(2)}) collective-permute-start(f32[520,256]{1,0:T(8,128)S(1)} %head_sum.3), channel_id=1, source_target_pairs={{0,32},{1,129},{16,48},{17,145},{32,0},{33,161},{48,16},{49,177},{... | collective-permute-start | bytes 1597448 | tf_op jit(solution)/shard_map/ppermute | solution.py:477
  33.9 2.5 %head_sum.5 = (f32[520,256]{1,0:T(8,128)S(1)}, f32[520,256]{1,0:T(8,128)S(1)}) custom-call(bf16[16,8,128,256]{3,2,1,0:T(8,128)(2,1)S(1)} %get-tuple-element.34.e_ref, f32[32,128]{1,0:T(8,128)S(1)} %get-tuple-element.35.tops_ref, f32[8,24,128]{2,1,0:T(8,128)S(1)} %all_to_all.15.got_ref), custom_call_target="tpu_custom_call" | custom-call | tf_op jit(solution)/shard_map/head_sum/pallas_call | solution.py:235
  36.5 0.0 copy-start.1
  36.5 0.8 collective-permute-start
  37.2 2.6 %collective-permute-start.2 = (f32[520,256]{1,0:T(8,128)S(1)}, f32[520,256]{1,0:T(8,128)S(1)}, u32[]{:S(2)}, u32[]{:S(2)}) collective-permute-start(f32[520,256]{1,0:T(8,128)S(1)} %get-tuple-element.41), channel_id=1, source_target_pairs={{0,48},{1,193},{16,0},{17,209},{32,16},{33,225},{48,32},{49,241},{... | collective-permute-start | bytes 1597448 | tf_op jit(solution)/shard_map/ppermute | solution.py:477
  39.8 1.3 %head_sum.4.refs_0_ = f32[520,256]{1,0:T(8,128)S(1)} custom-call(bf16[16,8,128,256]{3,2,1,0:T(8,128)(2,1)S(1)} %get-tuple-element.34.e_ref, f32[32,128]{1,0:T(8,128)S(1)} %get-tuple-element.35.tops_ref, f32[8,24,128]{2,1,0:T(8,128)S(1)} %all_to_all.15.got_ref), custom_call_target="tpu_custom_call" | custom-call | tf_op jit(solution)/shard_map/head_sum/pallas_call | solution.py:235
  41.1 0.0 copy-done.1
  41.1 2.4 %active_products.1.refs_5_.active_ref = f32[64,256,128]{2,1,0:T(8,128)S(1)} custom-call(bf16[64,128,128]{2,1,0:T(8,128)(2,1)S(1)} %get-tuple-element.42.qh_ref.refs_4_, bf16[256,128]{1,0:T(8,128)(2,1)S(1)} %copy-done.1), custom_call_target="tpu_custom_call" | custom-call | tf_op jit(solution)/shard_map/active_products/pallas_call | solution.py:294
  43.5 3.6 %collective-permute-done.refs_1_ = f32[520,256]{1,0:T(8,128)S(1)} collective-permute-done((f32[520,256]{1,0:T(8,128)S(1)}, f32[520,256]{1,0:T(8,128)S(1)}, u32[]{:S(2)}, u32[]{:S(2)}) %collective-permute-start) | collective-permute-done | bytes 532512 | tf_op jit(solution)/shard_map/ppermute | solution.py:477
  47.2 0.0 collective-permute-done.1.refs_2_
  47.2 0.3 collective-permute-done.2.refs_3_
  47.5 0.1 partial_sum.1
  47.7 1.6 %collective-permute-start.3 = (f32[136,256]{1,0:T(8,128)S(1)}, f32[136,256]{1,0:T(8,128)S(1)}, u32[]{:S(2)}, u32[]{:S(2)}) collective-permute-start(f32[136,256]{1,0:T(8,128)S(1)} %get-tuple-element.48), channel_id=1, source_target_pairs={{0,64},{1,17},{16,80},{17,33},{32,96},{33,49},{48,112},{49,1},{64,... | collective-permute-start | bytes 417800 | tf_op jit(solution)/shard_map/ppermute | solution.py:477
  49.2 2.7 %collective-permute-start.4 = (f32[136,256]{1,0:T(8,128)S(1)}, f32[136,256]{1,0:T(8,128)S(1)}, u32[]{:S(2)}, u32[]{:S(2)}) collective-permute-start(f32[136,256]{1,0:T(8,128)S(1)} %get-tuple-element.49), channel_id=1, source_target_pairs={{0,128},{1,33},{16,144},{17,49},{32,160},{33,1},{48,176},{49,17},{... | collective-permute-start | bytes 417800 | tf_op jit(solution)/shard_map/ppermute | solution.py:477
  52.0 1.4 %collective-permute-start.5 = (f32[136,256]{1,0:T(8,128)S(1)}, f32[136,256]{1,0:T(8,128)S(1)}, u32[]{:S(2)}, u32[]{:S(2)}) collective-permute-start(f32[136,256]{1,0:T(8,128)S(1)} %get-tuple-element.50), channel_id=1, source_target_pairs={{0,192},{1,49},{16,208},{17,1},{32,224},{33,17},{48,240},{49,33},{... | collective-permute-start | bytes 417800 | tf_op jit(solution)/shard_map/ppermute | solution.py:477
  53.4 0.6 collective-permute-done.3.refs_1_
  54.0 2.5 %collective-permute-done.4.refs_2_ = f32[136,256]{1,0:T(8,128)S(1)} collective-permute-done((f32[136,256]{1,0:T(8,128)S(1)}, f32[136,256]{1,0:T(8,128)S(1)}, u32[]{:S(2)}, u32[]{:S(2)}) %collective-permute-start.4) | collective-permute-done | bytes 139296 | tf_op jit(solution)/shard_map/ppermute | solution.py:477
  56.5 0.5 collective-permute-done.5.refs_3_
  57.0 1.0 dlogits.1.refs_0_.dlogits_ref
  58.0 1.5 %collective-permute-start.6 = (f32[288,256]{1,0:T(8,128)S(1)}, f32[288,256]{1,0:T(8,128)S(1)}, u32[]{:S(2)}, u32[]{:S(2)}) collective-permute-start(f32[288,256]{1,0:T(8,128)S(1)} %dlogits.1.refs_0_.dlogits_ref), channel_id=1, source_target_pairs={{0,16},{1,65},{16,32},{17,81},{32,48},{33,97},{48,0},{49,113},{64,... | collective-permute-start | bytes 884744 | tf_op jit(solution)/shard_map/ppermute | solution.py:477
  59.5 2.8 %collective-permute-start.7 = (f32[288,256]{1,0:T(8,128)S(1)}, f32[288,256]{1,0:T(8,128)S(1)}, u32[]{:S(2)}, u32[]{:S(2)}) collective-permute-start(f32[288,256]{1,0:T(8,128)S(1)} %dlogits.1.refs_0_.dlogits_ref), channel_id=1, source_target_pairs={{0,32},{1,129},{16,48},{17,145},{32,0},{33,161},{48,16},{49,177},{... | collective-permute-start | bytes 884744 | tf_op jit(solution)/shard_map/ppermute | solution.py:477
  62.3 1.3 %collective-permute-start.8 = (f32[288,256]{1,0:T(8,128)S(1)}, f32[288,256]{1,0:T(8,128)S(1)}, u32[]{:S(2)}, u32[]{:S(2)}) collective-permute-start(f32[288,256]{1,0:T(8,128)S(1)} %dlogits.1.refs_0_.dlogits_ref), channel_id=1, source_target_pairs={{0,48},{1,193},{16,0},{17,209},{32,16},{33,225},{48,32},{49,241},{... | collective-permute-start | bytes 884744 | tf_op jit(solution)/shard_map/ppermute | solution.py:477
  63.6 2.4 %collective-permute-done.6.refs_1_ = f32[288,256]{1,0:T(8,128)S(1)} collective-permute-done((f32[288,256]{1,0:T(8,128)S(1)}, f32[288,256]{1,0:T(8,128)S(1)}, u32[]{:S(2)}, u32[]{:S(2)}) %collective-permute-start.6) | collective-permute-done | bytes 294944 | tf_op jit(solution)/shard_map/ppermute | solution.py:477
  66.0 4.1 %collective-permute-done.7.refs_2_ = f32[288,256]{1,0:T(8,128)S(1)} collective-permute-done((f32[288,256]{1,0:T(8,128)S(1)}, f32[288,256]{1,0:T(8,128)S(1)}, u32[]{:S(2)}, u32[]{:S(2)}) %collective-permute-start.7) | collective-permute-done | bytes 294944 | tf_op jit(solution)/shard_map/ppermute | solution.py:477
  70.1 0.0 collective-permute-done.8.refs_3_
  70.1 0.0 copy-done
  70.1 0.9 query_gradient.3
  71.1 2.7 %collective-permute-start.10 = (f32[8,72,128]{2,1,0:T(8,128)S(1)}, f32[8,72,128]{2,1,0:T(8,128)S(1)}, u32[]{:S(2)}, u32[]{:S(2)}) collective-permute-start(f32[8,72,128]{2,1,0:T(8,128)S(1)} %query_gradient.3), channel_id=1, source_target_pairs={{0,128},{1,33},{16,144},{17,49},{32,160},{33,1},{48,176},{49,17},{... | collective-permute-start | bytes 884744 | tf_op jit(solution)/shard_map/ppermute | solution.py:477
  73.7 1.5 %query_gradient.5 = (f32[8,72,128]{2,1,0:T(8,128)S(1)}, f32[8,72,128]{2,1,0:T(8,128)S(1)}) custom-call(f32[288,256]{1,0:T(8,128)S(1)} %dlogits.1.refs_0_.dlogits_ref, f32[288,256]{1,0:T(8,128)S(1)} %collective-permute-done.6.refs_1_, f32[288,256]{1,0:T(8,128)S(1)} %collective-permute-done.7.refs_2_, f32[288,256]{1,0:T(8,128)S(1)} %collective-permute-done.8.refs_3_, ...), custom_call_target="tpu_custom_call" | custom-call | tf_op jit(solution)/shard_map/query_gradient/pallas_call | solution.py:427
  75.2 1.7 %collective-permute-start.11 = (f32[8,72,128]{2,1,0:T(8,128)S(1)}, f32[8,72,128]{2,1,0:T(8,128)S(1)}, u32[]{:S(2)}, u32[]{:S(2)}) collective-permute-start(f32[8,72,128]{2,1,0:T(8,128)S(1)} %get-tuple-element.61), channel_id=1, source_target_pairs={{0,192},{1,49},{16,208},{17,1},{32,224},{33,17},{48,240},{49,33},{... | collective-permute-start | bytes 884744 | tf_op jit(solution)/shard_map/ppermute | solution.py:477
  76.9 0.4 collective-permute-start.9
  77.3 0.9 query_gradient.4
  78.2 2.9 %key_gradient.1 = f32[256,128]{1,0:T(8,128)S(1)} custom-call(f32[288,256]{1,0:T(8,128)S(1)} %dlogits.1.refs_0_.dlogits_ref, f32[64,256,128]{2,1,0:T(8,128)S(1)} %active_products.1.refs_5_.active_ref, bf16[64,128,128]{2,1,0:T(8,128)(2,1)S(1)} %get-tuple-element.42.qh_ref.refs_4_, f32[64,128]{1,0:T(8,128)S(1)} %bitcast.9), custom_call_target="tpu_custom_call" | custom-call | tf_op jit(solution)/shard_map/key_gradient/pallas_call | solution.py:369
  81.2 0.0 collective-permute-done.10
  81.2 1.5 %collective-permute-done.11 = f32[8,72,128]{2,1,0:T(8,128)S(1)} collective-permute-done((f32[8,72,128]{2,1,0:T(8,128)S(1)}, f32[8,72,128]{2,1,0:T(8,128)S(1)}, u32[]{:S(2)}, u32[]{:S(2)}) %collective-permute-start.11) | collective-permute-done | bytes 294944 | tf_op jit(solution)/shard_map/ppermute | solution.py:477
  82.7 2.2 %collective-permute-done.9 = f32[8,72,128]{2,1,0:T(8,128)S(1)} collective-permute-done((f32[8,72,128]{2,1,0:T(8,128)S(1)}, f32[8,72,128]{2,1,0:T(8,128)S(1)}, u32[]{:S(2)}, u32[]{:S(2)}) %collective-permute-start.9) | collective-permute-done | bytes 294944 | tf_op jit(solution)/shard_map/ppermute | solution.py:477
  84.9 0.1 add_add_fusion
  84.9 13.3 %all_to_all.16 = f32[8,72,128]{2,1,0:T(8,128)S(1)} all-to-all(f32[8,72,128]{2,1,0:T(8,128)S(1)} %add_add_fusion), channel_id=1, replica_groups=mesh['head'=16,'key'=8,'row'=2] {'key'}, dimensions={0} | all-to-all | bytes 589824 | tf_op jit(solution)/shard_map/all_to_all | solution.py:464
  98.3 0.7 broadcast_in_dim.2
  99.0 4.8 %all-to-all-start.2 = ((f32[8,72,128]{2,1,0:T(8,128)}), f32[8,72,128]{2,1,0:T(8,128)S(1)}, u32[]{:S(2)}, u32[]{:S(2)}) async-start(f32[8,72,128]{2,1,0:T(8,128)} %broadcast_in_dim.2), calls=%async_computation.2 | async-start | bytes 589824 | tf_op jit(solution)/shard_map/all_to_all | solution.py:464
  103.8 0.1 collective-permute-start.12
  103.9 1.2 %collective-permute-done.12 = f32[128,128]{1,0:T(8,128)S(1)} collective-permute-done((f32[128,128]{1,0:T(8,128)S(1)}, f32[128,128]{1,0:T(8,128)S(1)}, u32[]{:S(2)}, u32[]{:S(2)}) %collective-permute-start.12) | collective-permute-done | bytes 65568 | tf_op jit(solution)/shard_map/ppermute | solution.py:526
  105.1 0.6 dynamic-slice_add_fusion
  105.8 7.4 %all-to-all-done.2.got_ref = f32[8,72,128]{2,1,0:T(8,128)S(1)} async-done(((f32[8,72,128]{2,1,0:T(8,128)}), f32[8,72,128]{2,1,0:T(8,128)S(1)}, u32[]{:S(2)}, u32[]{:S(2)}) %all-to-all-start.2) | async-done | bytes 294944 | tf_op jit(solution)/shard_map/all_to_all | solution.py:464
  113.2 0.7 results.1
  (3 shorter events, 0.0 us)
Async XLA Ops:
  30.6 16.6 %collective-permute-start.1 = (f32[520,256]{1,0:T(8,128)S(1)}, f32[520,256]{1,0:T(8,128)S(1)}, u32[]{:S(2)}, u32[]{:S(2)}) collective-permute-start(f32[520,256]{1,0:T(8,128)S(1)} %head_sum.3), channel_id=1, source_target_pairs={{0,32},{1,129},{16,48},{17,145},{32,0},{33,161},{48,16},{49,177},{... | collective-permute-start | bytes 1597448 | tf_op jit(solution)/shard_map/ppermute | solution.py:477
  36.5 4.7 %copy-start.1 = (bf16[256,128]{1,0:T(8,128)(2,1)S(1)}, bf16[256,128]{1,0:T(8,128)(2,1)}, u32[]{:S(2)}) copy-start(bf16[256,128]{1,0:T(8,128)(2,1)} %refs_6_.1) | copy-start | bytes 196612
  36.5 10.7 %collective-permute-start = (f32[520,256]{1,0:T(8,128)S(1)}, f32[520,256]{1,0:T(8,128)S(1)}, u32[]{:S(2)}, u32[]{:S(2)}) collective-permute-start(f32[520,256]{1,0:T(8,128)S(1)} %get-tuple-element.40), channel_id=1, source_target_pairs={{0,16},{1,65},{16,32},{17,81},{32,48},{33,97},{48,0},{49,113},{64,... | collective-permute-start | bytes 1597448 | tf_op jit(solution)/shard_map/ppermute | solution.py:477
  37.2 10.3 %collective-permute-start.2 = (f32[520,256]{1,0:T(8,128)S(1)}, f32[520,256]{1,0:T(8,128)S(1)}, u32[]{:S(2)}, u32[]{:S(2)}) collective-permute-start(f32[520,256]{1,0:T(8,128)S(1)} %get-tuple-element.41), channel_id=1, source_target_pairs={{0,48},{1,193},{16,0},{17,209},{32,16},{33,225},{48,32},{49,241},{... | collective-permute-start | bytes 1597448 | tf_op jit(solution)/shard_map/ppermute | solution.py:477
  47.7 6.3 %collective-permute-start.3 = (f32[136,256]{1,0:T(8,128)S(1)}, f32[136,256]{1,0:T(8,128)S(1)}, u32[]{:S(2)}, u32[]{:S(2)}) collective-permute-start(f32[136,256]{1,0:T(8,128)S(1)} %get-tuple-element.48), channel_id=1, source_target_pairs={{0,64},{1,17},{16,80},{17,33},{32,96},{33,49},{48,112},{49,1},{64,... | collective-permute-start | bytes 417800 | tf_op jit(solution)/shard_map/ppermute | solution.py:477
  49.2 7.3 %collective-permute-start.4 = (f32[136,256]{1,0:T(8,128)S(1)}, f32[136,256]{1,0:T(8,128)S(1)}, u32[]{:S(2)}, u32[]{:S(2)}) collective-permute-start(f32[136,256]{1,0:T(8,128)S(1)} %get-tuple-element.49), channel_id=1, source_target_pairs={{0,128},{1,33},{16,144},{17,49},{32,160},{33,1},{48,176},{49,17},{... | collective-permute-start | bytes 417800 | tf_op jit(solution)/shard_map/ppermute | solution.py:477
  52.0 5.1 %collective-permute-start.5 = (f32[136,256]{1,0:T(8,128)S(1)}, f32[136,256]{1,0:T(8,128)S(1)}, u32[]{:S(2)}, u32[]{:S(2)}) collective-permute-start(f32[136,256]{1,0:T(8,128)S(1)} %get-tuple-element.50), channel_id=1, source_target_pairs={{0,192},{1,49},{16,208},{17,1},{32,224},{33,17},{48,240},{49,33},{... | collective-permute-start | bytes 417800 | tf_op jit(solution)/shard_map/ppermute | solution.py:477
  57.0 13.1 %copy-start = (f32[128,64]{0,1:T(8,128)S(1)}, f32[128,64]{0,1:T(8,128)}, u32[]{:S(2)}) copy-start(f32[128,64]{0,1:T(8,128)} %param.9) | copy-start | bytes 98308
  58.0 8.0 %collective-permute-start.6 = (f32[288,256]{1,0:T(8,128)S(1)}, f32[288,256]{1,0:T(8,128)S(1)}, u32[]{:S(2)}, u32[]{:S(2)}) collective-permute-start(f32[288,256]{1,0:T(8,128)S(1)} %dlogits.1.refs_0_.dlogits_ref), channel_id=1, source_target_pairs={{0,16},{1,65},{16,32},{17,81},{32,48},{33,97},{48,0},{49,113},{64,... | collective-permute-start | bytes 884744 | tf_op jit(solution)/shard_map/ppermute | solution.py:477
  59.5 10.7 %collective-permute-start.7 = (f32[288,256]{1,0:T(8,128)S(1)}, f32[288,256]{1,0:T(8,128)S(1)}, u32[]{:S(2)}, u32[]{:S(2)}) collective-permute-start(f32[288,256]{1,0:T(8,128)S(1)} %dlogits.1.refs_0_.dlogits_ref), channel_id=1, source_target_pairs={{0,32},{1,129},{16,48},{17,145},{32,0},{33,161},{48,16},{49,177},{... | collective-permute-start | bytes 884744 | tf_op jit(solution)/shard_map/ppermute | solution.py:477
  62.3 7.9 %collective-permute-start.8 = (f32[288,256]{1,0:T(8,128)S(1)}, f32[288,256]{1,0:T(8,128)S(1)}, u32[]{:S(2)}, u32[]{:S(2)}) collective-permute-start(f32[288,256]{1,0:T(8,128)S(1)} %dlogits.1.refs_0_.dlogits_ref), channel_id=1, source_target_pairs={{0,48},{1,193},{16,0},{17,209},{32,16},{33,225},{48,32},{49,241},{... | collective-permute-start | bytes 884744 | tf_op jit(solution)/shard_map/ppermute | solution.py:477
  71.1 10.1 %collective-permute-start.10 = (f32[8,72,128]{2,1,0:T(8,128)S(1)}, f32[8,72,128]{2,1,0:T(8,128)S(1)}, u32[]{:S(2)}, u32[]{:S(2)}) collective-permute-start(f32[8,72,128]{2,1,0:T(8,128)S(1)} %query_gradient.3), channel_id=1, source_target_pairs={{0,128},{1,33},{16,144},{17,49},{32,160},{33,1},{48,176},{49,17},{... | collective-permute-start | bytes 884744 | tf_op jit(solution)/shard_map/ppermute | solution.py:477
  75.2 7.5 %collective-permute-start.11 = (f32[8,72,128]{2,1,0:T(8,128)S(1)}, f32[8,72,128]{2,1,0:T(8,128)S(1)}, u32[]{:S(2)}, u32[]{:S(2)}) collective-permute-start(f32[8,72,128]{2,1,0:T(8,128)S(1)} %get-tuple-element.61), channel_id=1, source_target_pairs={{0,192},{1,49},{16,208},{17,1},{32,224},{33,17},{48,240},{49,33},{... | collective-permute-start | bytes 884744 | tf_op jit(solution)/shard_map/ppermute | solution.py:477
  76.9 7.9 %collective-permute-start.9 = (f32[8,72,128]{2,1,0:T(8,128)S(1)}, f32[8,72,128]{2,1,0:T(8,128)S(1)}, u32[]{:S(2)}, u32[]{:S(2)}) collective-permute-start(f32[8,72,128]{2,1,0:T(8,128)S(1)} %get-tuple-element.57), channel_id=1, source_target_pairs={{0,64},{1,17},{16,80},{17,33},{32,96},{33,49},{48,112},{49,1},{64,... | collective-permute-start | bytes 884744 | tf_op jit(solution)/shard_map/ppermute | solution.py:477
  99.0 14.2 %all-to-all-start.2 = ((f32[8,72,128]{2,1,0:T(8,128)}), f32[8,72,128]{2,1,0:T(8,128)S(1)}, u32[]{:S(2)}, u32[]{:S(2)}) async-start(f32[8,72,128]{2,1,0:T(8,128)} %broadcast_in_dim.2), calls=%async_computation.2 | async-start | bytes 589824 | tf_op jit(solution)/shard_map/all_to_all | solution.py:464
  103.8 1.3 %collective-permute-start.12 = (f32[128,128]{1,0:T(8,128)S(1)}, f32[128,128]{1,0:T(8,128)S(1)}, u32[]{:S(2)}, u32[]{:S(2)}) collective-permute-start(f32[128,128]{1,0:T(8,128)S(1)} %constant_dynamic-slice_fusion), channel_id=1, source_target_pairs={{0,1},{1,0},{2,3},{3,2},{4,5},{5,4},{6,7},{7,6},{8,9},{9,8},{10,11... | collective-permute-start | bytes 196616 | tf_op jit(solution)/shard_map/ppermute | solution.py:526

commit v10 on v9

--- a/solution.py
+++ b/solution.py
@@ -69,7 +69,7 @@
     steps = blocks // PART
     _, iheads, depth = iq_ref.shape
     keys = k_ref.shape[0]
-    group = GROUP
+    group = iheads
     pitch = wide.shape[0] // rows
 
     first = pltpu.make_async_copy(q_hbm, q_ref, sems.at[steps])

time: 116 us -> 115 us (level)
  no operation moved by 1% of the time
where the time goes in v10:
time: 115 us; the launch traced here: 113 us
  blocking collectives  28.8 us (25%)
  Pallas kernels  28.2 us (25%)
  starting transfers between devices  27.4 us (24%)
  waiting for transfers between devices  26.5 us (23%)
    all_to_all x2, blocking collectives, exchange(): return lax.all_to_all(x, axis, split_axis=0, concat_axis=0, tiled=True)  28.8 us
    ppermute x12, starting transfers between devices, shift(): return lax.ppermute(x, ('head', 'row'), pairs)  22.5 us
    ppermute x12, waiting for transfers between devices, shift(): return lax.ppermute(x, ('head', 'row'), pairs)  17.8 us
    pallas_call x1, Pallas kernels, scores_and_logits(): call(scores_kernel, 'scores_and_logits', 32, in_specs=[HBM] * 5, out_spec...  12.6 us
    all_to_all x1, waiting for transfers between devices, exchange(): return lax.all_to_all(x, axis, split_axis=0, concat_axis=0, tiled=True)  7.41 us
    pallas_call x3, Pallas kernels, head_sum(): call(functools.partial(headsum_kernel, offsets), 'head_sum', 24, in_specs...  5.23 us
    all_to_all x1, starting transfers between devices, exchange(): return lax.all_to_all(x, axis, split_axis=0, concat_axis=0, tiled=True)  4.78 us
    pallas_call x3, Pallas kernels, query_gradient(): call(functools.partial(query_kernel, offsets, pieces), 'query_gradient',...  3.29 us
  transfers between devices with their start and end apart: 14, of which 11 were waited for; matrix products, arithmetic and copies ran while one was open for 1% of the time, Pallas kernels for 10%

profile of v10, /device:TPU:32, one launch (start us, length us, event | category | flops | bytes accessed | tf_op | source)
XLA Modules:
  0.0 113.2 jit_solution(14026909300653185495)
XLA Ops:
  0.6 12.6 %scores_and_logits.1 = (bf16[16,8,128,256]{3,2,1,0:T(8,128)(2,1)S(1)}, f32[32,128]{1,0:T(8,128)S(1)}, f32[8,24,128]{2,1,0:T(8,128)S(1)}, f32[256,128]{1,0:T(8,128)S(1)}, bf16[64,128,128]{2,1,0:T(8,128)(2,1)S(1)}) custom-call(bf16[8,576,128]{2,1,0:T(8,128)(2,1)} %bitcast.11, bf16[16,576,256]{2,1,0:T(8,128)(2,1)} %bitcast.10, bf16[128,64,128]{2,1,0:T(8,128)(2,1)} %iq_hbm.1, ...), custom_call_target="tpu_custom_call" | custom-call | tf_op jit(solution)/shard_map/scores_and_logits/pallas_call | solution.py:168
  13.2 15.5 %all_to_all.15.got_ref = f32[8,24,128]{2,1,0:T(8,128)S(1)} all-to-all(f32[8,24,128]{2,1,0:T(8,128)S(1)} %get-tuple-element.36), channel_id=1, replica_groups=mesh['head'=16,'key'=8,'row'=2] {'key'}, dimensions={0} | all-to-all | bytes 196608 | tf_op jit(solution)/shard_map/all_to_all | solution.py:464
  28.7 1.3 %head_sum.3 = f32[520,256]{1,0:T(8,128)S(1)} custom-call(bf16[16,8,128,256]{3,2,1,0:T(8,128)(2,1)S(1)} %get-tuple-element.34.e_ref, f32[32,128]{1,0:T(8,128)S(1)} %get-tuple-element.35.tops_ref, f32[8,24,128]{2,1,0:T(8,128)S(1)} %all_to_all.15.got_ref), custom_call_target="tpu_custom_call" | custom-call | tf_op jit(solution)/shard_map/head_sum/pallas_call | solution.py:235
  30.0 3.3 %collective-permute-start.1 = (f32[520,256]{1,0:T(8,128)S(1)}, f32[520,256]{1,0:T(8,128)S(1)}, u32[]{:S(2)}, u32[]{:S(2)}) collective-permute-start(f32[520,256]{1,0:T(8,128)S(1)} %head_sum.3), channel_id=1, source_target_pairs={{0,32},{1,129},{16,48},{17,145},{32,0},{33,161},{48,16},{49,177},{... | collective-permute-start | bytes 1597448 | tf_op jit(solution)/shard_map/ppermute | solution.py:477
  33.3 2.5 %head_sum.5 = (f32[520,256]{1,0:T(8,128)S(1)}, f32[520,256]{1,0:T(8,128)S(1)}) custom-call(bf16[16,8,128,256]{3,2,1,0:T(8,128)(2,1)S(1)} %get-tuple-element.34.e_ref, f32[32,128]{1,0:T(8,128)S(1)} %get-tuple-element.35.tops_ref, f32[8,24,128]{2,1,0:T(8,128)S(1)} %all_to_all.15.got_ref), custom_call_target="tpu_custom_call" | custom-call | tf_op jit(solution)/shard_map/head_sum/pallas_call | solution.py:235
  35.9 0.0 copy-start.1
  35.9 0.8 collective-permute-start
  36.6 2.6 %collective-permute-start.2 = (f32[520,256]{1,0:T(8,128)S(1)}, f32[520,256]{1,0:T(8,128)S(1)}, u32[]{:S(2)}, u32[]{:S(2)}) collective-permute-start(f32[520,256]{1,0:T(8,128)S(1)} %get-tuple-element.41), channel_id=1, source_target_pairs={{0,48},{1,193},{16,0},{17,209},{32,16},{33,225},{48,32},{49,241},{... | collective-permute-start | bytes 1597448 | tf_op jit(solution)/shard_map/ppermute | solution.py:477
  39.2 1.3 %head_sum.4.refs_0_ = f32[520,256]{1,0:T(8,128)S(1)} custom-call(bf16[16,8,128,256]{3,2,1,0:T(8,128)(2,1)S(1)} %get-tuple-element.34.e_ref, f32[32,128]{1,0:T(8,128)S(1)} %get-tuple-element.35.tops_ref, f32[8,24,128]{2,1,0:T(8,128)S(1)} %all_to_all.15.got_ref), custom_call_target="tpu_custom_call" | custom-call | tf_op jit(solution)/shard_map/head_sum/pallas_call | solution.py:235
  40.6 0.0 copy-done.1
  40.6 2.4 %active_products.1.refs_5_.active_ref = f32[64,256,128]{2,1,0:T(8,128)S(1)} custom-call(bf16[64,128,128]{2,1,0:T(8,128)(2,1)S(1)} %get-tuple-element.42.qh_ref.refs_4_, bf16[256,128]{1,0:T(8,128)(2,1)S(1)} %copy-done.1), custom_call_target="tpu_custom_call" | custom-call | tf_op jit(solution)/shard_map/active_products/pallas_call | solution.py:294
  43.0 3.6 %collective-permute-done.refs_1_ = f32[520,256]{1,0:T(8,128)S(1)} collective-permute-done((f32[520,256]{1,0:T(8,128)S(1)}, f32[520,256]{1,0:T(8,128)S(1)}, u32[]{:S(2)}, u32[]{:S(2)}) %collective-permute-start) | collective-permute-done | bytes 532512 | tf_op jit(solution)/shard_map/ppermute | solution.py:477
  46.6 0.0 collective-permute-done.1.refs_2_
  46.6 0.3 collective-permute-done.2.refs_3_
  47.0 0.1 partial_sum.1
  47.1 1.6 %collective-permute-start.3 = (f32[136,256]{1,0:T(8,128)S(1)}, f32[136,256]{1,0:T(8,128)S(1)}, u32[]{:S(2)}, u32[]{:S(2)}) collective-permute-start(f32[136,256]{1,0:T(8,128)S(1)} %get-tuple-element.48), channel_id=1, source_target_pairs={{0,64},{1,17},{16,80},{17,33},{32,96},{33,49},{48,112},{49,1},{64,... | collective-permute-start | bytes 417800 | tf_op jit(solution)/shard_map/ppermute | solution.py:477
  48.7 2.7 %collective-permute-start.4 = (f32[136,256]{1,0:T(8,128)S(1)}, f32[136,256]{1,0:T(8,128)S(1)}, u32[]{:S(2)}, u32[]{:S(2)}) collective-permute-start(f32[136,256]{1,0:T(8,128)S(1)} %get-tuple-element.49), channel_id=1, source_target_pairs={{0,128},{1,33},{16,144},{17,49},{32,160},{33,1},{48,176},{49,17},{... | collective-permute-start | bytes 417800 | tf_op jit(solution)/shard_map/ppermute | solution.py:477
  51.4 1.4 %collective-permute-start.5 = (f32[136,256]{1,0:T(8,128)S(1)}, f32[136,256]{1,0:T(8,128)S(1)}, u32[]{:S(2)}, u32[]{:S(2)}) collective-permute-start(f32[136,256]{1,0:T(8,128)S(1)} %get-tuple-element.50), channel_id=1, source_target_pairs={{0,192},{1,49},{16,208},{17,1},{32,224},{33,17},{48,240},{49,33},{... | collective-permute-start | bytes 417800 | tf_op jit(solution)/shard_map/ppermute | solution.py:477
  52.8 0.6 collective-permute-done.3.refs_1_
  53.4 2.5 %collective-permute-done.4.refs_2_ = f32[136,256]{1,0:T(8,128)S(1)} collective-permute-done((f32[136,256]{1,0:T(8,128)S(1)}, f32[136,256]{1,0:T(8,128)S(1)}, u32[]{:S(2)}, u32[]{:S(2)}) %collective-permute-start.4) | collective-permute-done | bytes 139296 | tf_op jit(solution)/shard_map/ppermute | solution.py:477
  55.9 0.5 collective-permute-done.5.refs_3_
  56.5 1.0 dlogits.1.refs_0_.dlogits_ref
  57.4 1.5 %collective-permute-start.6 = (f32[288,256]{1,0:T(8,128)S(1)}, f32[288,256]{1,0:T(8,128)S(1)}, u32[]{:S(2)}, u32[]{:S(2)}) collective-permute-start(f32[288,256]{1,0:T(8,128)S(1)} %dlogits.1.refs_0_.dlogits_ref), channel_id=1, source_target_pairs={{0,16},{1,65},{16,32},{17,81},{32,48},{33,97},{48,0},{49,113},{64,... | collective-permute-start | bytes 884744 | tf_op jit(solution)/shard_map/ppermute | solution.py:477
  58.9 2.8 %collective-permute-start.7 = (f32[288,256]{1,0:T(8,128)S(1)}, f32[288,256]{1,0:T(8,128)S(1)}, u32[]{:S(2)}, u32[]{:S(2)}) collective-permute-start(f32[288,256]{1,0:T(8,128)S(1)} %dlogits.1.refs_0_.dlogits_ref), channel_id=1, source_target_pairs={{0,32},{1,129},{16,48},{17,145},{32,0},{33,161},{48,16},{49,177},{... | collective-permute-start | bytes 884744 | tf_op jit(solution)/shard_map/ppermute | solution.py:477
  61.7 1.3 %collective-permute-start.8 = (f32[288,256]{1,0:T(8,128)S(1)}, f32[288,256]{1,0:T(8,128)S(1)}, u32[]{:S(2)}, u32[]{:S(2)}) collective-permute-start(f32[288,256]{1,0:T(8,128)S(1)} %dlogits.1.refs_0_.dlogits_ref), channel_id=1, source_target_pairs={{0,48},{1,193},{16,0},{17,209},{32,16},{33,225},{48,32},{49,241},{... | collective-permute-start | bytes 884744 | tf_op jit(solution)/shard_map/ppermute | solution.py:477
  63.0 2.4 %collective-permute-done.6.refs_1_ = f32[288,256]{1,0:T(8,128)S(1)} collective-permute-done((f32[288,256]{1,0:T(8,128)S(1)}, f32[288,256]{1,0:T(8,128)S(1)}, u32[]{:S(2)}, u32[]{:S(2)}) %collective-permute-start.6) | collective-permute-done | bytes 294944 | tf_op jit(solution)/shard_map/ppermute | solution.py:477
  65.4 4.1 %collective-permute-done.7.refs_2_ = f32[288,256]{1,0:T(8,128)S(1)} collective-permute-done((f32[288,256]{1,0:T(8,128)S(1)}, f32[288,256]{1,0:T(8,128)S(1)}, u32[]{:S(2)}, u32[]{:S(2)}) %collective-permute-start.7) | collective-permute-done | bytes 294944 | tf_op jit(solution)/shard_map/ppermute | solution.py:477
  69.6 0.0 collective-permute-done.8.refs_3_
  69.6 0.0 copy-done
  69.6 0.9 query_gradient.3
  70.5 2.5 %collective-permute-start.10 = (f32[8,72,128]{2,1,0:T(8,128)S(1)}, f32[8,72,128]{2,1,0:T(8,128)S(1)}, u32[]{:S(2)}, u32[]{:S(2)}) collective-permute-start(f32[8,72,128]{2,1,0:T(8,128)S(1)} %query_gradient.3), channel_id=1, source_target_pairs={{0,128},{1,33},{16,144},{17,49},{32,160},{33,1},{48,176},{49,17},{... | collective-permute-start | bytes 884744 | tf_op jit(solution)/shard_map/ppermute | solution.py:477
  73.0 1.5 %query_gradient.5 = (f32[8,72,128]{2,1,0:T(8,128)S(1)}, f32[8,72,128]{2,1,0:T(8,128)S(1)}) custom-call(f32[288,256]{1,0:T(8,128)S(1)} %dlogits.1.refs_0_.dlogits_ref, f32[288,256]{1,0:T(8,128)S(1)} %collective-permute-done.6.refs_1_, f32[288,256]{1,0:T(8,128)S(1)} %collective-permute-done.7.refs_2_, f32[288,256]{1,0:T(8,128)S(1)} %collective-permute-done.8.refs_3_, ...), custom_call_target="tpu_custom_call" | custom-call | tf_op jit(solution)/shard_map/query_gradient/pallas_call | solution.py:427
  74.5 1.7 %collective-permute-start.11 = (f32[8,72,128]{2,1,0:T(8,128)S(1)}, f32[8,72,128]{2,1,0:T(8,128)S(1)}, u32[]{:S(2)}, u32[]{:S(2)}) collective-permute-start(f32[8,72,128]{2,1,0:T(8,128)S(1)} %get-tuple-element.61), channel_id=1, source_target_pairs={{0,192},{1,49},{16,208},{17,1},{32,224},{33,17},{48,240},{49,33},{... | collective-permute-start | bytes 884744 | tf_op jit(solution)/shard_map/ppermute | solution.py:477
  76.2 0.4 collective-permute-start.9
  76.6 0.9 query_gradient.4
  77.5 2.9 %key_gradient.1 = f32[256,128]{1,0:T(8,128)S(1)} custom-call(f32[288,256]{1,0:T(8,128)S(1)} %dlogits.1.refs_0_.dlogits_ref, f32[64,256,128]{2,1,0:T(8,128)S(1)} %active_products.1.refs_5_.active_ref, bf16[64,128,128]{2,1,0:T(8,128)(2,1)S(1)} %get-tuple-element.42.qh_ref.refs_4_, f32[64,128]{1,0:T(8,128)S(1)} %bitcast.9), custom_call_target="tpu_custom_call" | custom-call | tf_op jit(solution)/shard_map/key_gradient/pallas_call | solution.py:369
  80.4 0.0 collective-permute-done.10
  80.4 1.5 %collective-permute-done.11 = f32[8,72,128]{2,1,0:T(8,128)S(1)} collective-permute-done((f32[8,72,128]{2,1,0:T(8,128)S(1)}, f32[8,72,128]{2,1,0:T(8,128)S(1)}, u32[]{:S(2)}, u32[]{:S(2)}) %collective-permute-start.11) | collective-permute-done | bytes 294944 | tf_op jit(solution)/shard_map/ppermute | solution.py:477
  81.9 2.2 %collective-permute-done.9 = f32[8,72,128]{2,1,0:T(8,128)S(1)} collective-permute-done((f32[8,72,128]{2,1,0:T(8,128)S(1)}, f32[8,72,128]{2,1,0:T(8,128)S(1)}, u32[]{:S(2)}, u32[]{:S(2)}) %collective-permute-start.9) | collective-permute-done | bytes 294944 | tf_op jit(solution)/shard_map/ppermute | solution.py:477
  84.1 0.1 add_add_fusion
  84.2 13.3 %all_to_all.16 = f32[8,72,128]{2,1,0:T(8,128)S(1)} all-to-all(f32[8,72,128]{2,1,0:T(8,128)S(1)} %add_add_fusion), channel_id=1, replica_groups=mesh['head'=16,'key'=8,'row'=2] {'key'}, dimensions={0} | all-to-all | bytes 589824 | tf_op jit(solution)/shard_map/all_to_all | solution.py:464
  97.5 0.7 broadcast_in_dim.2
  98.3 4.8 %all-to-all-start.2 = ((f32[8,72,128]{2,1,0:T(8,128)}), f32[8,72,128]{2,1,0:T(8,128)S(1)}, u32[]{:S(2)}, u32[]{:S(2)}) async-start(f32[8,72,128]{2,1,0:T(8,128)} %broadcast_in_dim.2), calls=%async_computation.2 | async-start | bytes 589824 | tf_op jit(solution)/shard_map/all_to_all | solution.py:464
  103.0 0.1 collective-permute-start.12
  103.1 1.2 %collective-permute-done.12 = f32[128,128]{1,0:T(8,128)S(1)} collective-permute-done((f32[128,128]{1,0:T(8,128)S(1)}, f32[128,128]{1,0:T(8,128)S(1)}, u32[]{:S(2)}, u32[]{:S(2)}) %collective-permute-start.12) | collective-permute-done | bytes 65568 | tf_op jit(solution)/shard_map/ppermute | solution.py:526
  104.4 0.6 dynamic-slice_add_fusion
  105.0 7.4 %all-to-all-done.2.got_ref = f32[8,72,128]{2,1,0:T(8,128)S(1)} async-done(((f32[8,72,128]{2,1,0:T(8,128)}), f32[8,72,128]{2,1,0:T(8,128)S(1)}, u32[]{:S(2)}, u32[]{:S(2)}) %all-to-all-start.2) | async-done | bytes 294944 | tf_op jit(solution)/shard_map/all_to_all | solution.py:464
  112.4 0.7 results.1
  (3 shorter events, 0.0 us)
Async XLA Ops:
  30.0 16.6 %collective-permute-start.1 = (f32[520,256]{1,0:T(8,128)S(1)}, f32[520,256]{1,0:T(8,128)S(1)}, u32[]{:S(2)}, u32[]{:S(2)}) collective-permute-start(f32[520,256]{1,0:T(8,128)S(1)} %head_sum.3), channel_id=1, source_target_pairs={{0,32},{1,129},{16,48},{17,145},{32,0},{33,161},{48,16},{49,177},{... | collective-permute-start | bytes 1597448 | tf_op jit(solution)/shard_map/ppermute | solution.py:477
  35.9 4.7 %copy-start.1 = (bf16[256,128]{1,0:T(8,128)(2,1)S(1)}, bf16[256,128]{1,0:T(8,128)(2,1)}, u32[]{:S(2)}) copy-start(bf16[256,128]{1,0:T(8,128)(2,1)} %refs_6_.1) | copy-start | bytes 196612
  35.9 10.7 %collective-permute-start = (f32[520,256]{1,0:T(8,128)S(1)}, f32[520,256]{1,0:T(8,128)S(1)}, u32[]{:S(2)}, u32[]{:S(2)}) collective-permute-start(f32[520,256]{1,0:T(8,128)S(1)} %get-tuple-element.40), channel_id=1, source_target_pairs={{0,16},{1,65},{16,32},{17,81},{32,48},{33,97},{48,0},{49,113},{64,... | collective-permute-start | bytes 1597448 | tf_op jit(solution)/shard_map/ppermute | solution.py:477
  36.6 10.3 %collective-permute-start.2 = (f32[520,256]{1,0:T(8,128)S(1)}, f32[520,256]{1,0:T(8,128)S(1)}, u32[]{:S(2)}, u32[]{:S(2)}) collective-permute-start(f32[520,256]{1,0:T(8,128)S(1)} %get-tuple-element.41), channel_id=1, source_target_pairs={{0,48},{1,193},{16,0},{17,209},{32,16},{33,225},{48,32},{49,241},{... | collective-permute-start | bytes 1597448 | tf_op jit(solution)/shard_map/ppermute | solution.py:477
  47.1 6.3 %collective-permute-start.3 = (f32[136,256]{1,0:T(8,128)S(1)}, f32[136,256]{1,0:T(8,128)S(1)}, u32[]{:S(2)}, u32[]{:S(2)}) collective-permute-start(f32[136,256]{1,0:T(8,128)S(1)} %get-tuple-element.48), channel_id=1, source_target_pairs={{0,64},{1,17},{16,80},{17,33},{32,96},{33,49},{48,112},{49,1},{64,... | collective-permute-start | bytes 417800 | tf_op jit(solution)/shard_map/ppermute | solution.py:477
  48.7 7.3 %collective-permute-start.4 = (f32[136,256]{1,0:T(8,128)S(1)}, f32[136,256]{1,0:T(8,128)S(1)}, u32[]{:S(2)}, u32[]{:S(2)}) collective-permute-start(f32[136,256]{1,0:T(8,128)S(1)} %get-tuple-element.49), channel_id=1, source_target_pairs={{0,128},{1,33},{16,144},{17,49},{32,160},{33,1},{48,176},{49,17},{... | collective-permute-start | bytes 417800 | tf_op jit(solution)/shard_map/ppermute | solution.py:477
  51.4 5.1 %collective-permute-start.5 = (f32[136,256]{1,0:T(8,128)S(1)}, f32[136,256]{1,0:T(8,128)S(1)}, u32[]{:S(2)}, u32[]{:S(2)}) collective-permute-start(f32[136,256]{1,0:T(8,128)S(1)} %get-tuple-element.50), channel_id=1, source_target_pairs={{0,192},{1,49},{16,208},{17,1},{32,224},{33,17},{48,240},{49,33},{... | collective-permute-start | bytes 417800 | tf_op jit(solution)/shard_map/ppermute | solution.py:477
  56.5 13.1 %copy-start = (f32[128,64]{0,1:T(8,128)S(1)}, f32[128,64]{0,1:T(8,128)}, u32[]{:S(2)}) copy-start(f32[128,64]{0,1:T(8,128)} %param.9) | copy-start | bytes 98308
  57.4 8.0 %collective-permute-start.6 = (f32[288,256]{1,0:T(8,128)S(1)}, f32[288,256]{1,0:T(8,128)S(1)}, u32[]{:S(2)}, u32[]{:S(2)}) collective-permute-start(f32[288,256]{1,0:T(8,128)S(1)} %dlogits.1.refs_0_.dlogits_ref), channel_id=1, source_target_pairs={{0,16},{1,65},{16,32},{17,81},{32,48},{33,97},{48,0},{49,113},{64,... | collective-permute-start | bytes 884744 | tf_op jit(solution)/shard_map/ppermute | solution.py:477
  58.9 10.7 %collective-permute-start.7 = (f32[288,256]{1,0:T(8,128)S(1)}, f32[288,256]{1,0:T(8,128)S(1)}, u32[]{:S(2)}, u32[]{:S(2)}) collective-permute-start(f32[288,256]{1,0:T(8,128)S(1)} %dlogits.1.refs_0_.dlogits_ref), channel_id=1, source_target_pairs={{0,32},{1,129},{16,48},{17,145},{32,0},{33,161},{48,16},{49,177},{... | collective-permute-start | bytes 884744 | tf_op jit(solution)/shard_map/ppermute | solution.py:477
  61.7 7.9 %collective-permute-start.8 = (f32[288,256]{1,0:T(8,128)S(1)}, f32[288,256]{1,0:T(8,128)S(1)}, u32[]{:S(2)}, u32[]{:S(2)}) collective-permute-start(f32[288,256]{1,0:T(8,128)S(1)} %dlogits.1.refs_0_.dlogits_ref), channel_id=1, source_target_pairs={{0,48},{1,193},{16,0},{17,209},{32,16},{33,225},{48,32},{49,241},{... | collective-permute-start | bytes 884744 | tf_op jit(solution)/shard_map/ppermute | solution.py:477
  70.5 9.9 %collective-permute-start.10 = (f32[8,72,128]{2,1,0:T(8,128)S(1)}, f32[8,72,128]{2,1,0:T(8,128)S(1)}, u32[]{:S(2)}, u32[]{:S(2)}) collective-permute-start(f32[8,72,128]{2,1,0:T(8,128)S(1)} %query_gradient.3), channel_id=1, source_target_pairs={{0,128},{1,33},{16,144},{17,49},{32,160},{33,1},{48,176},{49,17},{... | collective-permute-start | bytes 884744 | tf_op jit(solution)/shard_map/ppermute | solution.py:477
  74.5 7.5 %collective-permute-start.11 = (f32[8,72,128]{2,1,0:T(8,128)S(1)}, f32[8,72,128]{2,1,0:T(8,128)S(1)}, u32[]{:S(2)}, u32[]{:S(2)}) collective-permute-start(f32[8,72,128]{2,1,0:T(8,128)S(1)} %get-tuple-element.61), channel_id=1, source_target_pairs={{0,192},{1,49},{16,208},{17,1},{32,224},{33,17},{48,240},{49,33},{... | collective-permute-start | bytes 884744 | tf_op jit(solution)/shard_map/ppermute | solution.py:477
  76.2 7.9 %collective-permute-start.9 = (f32[8,72,128]{2,1,0:T(8,128)S(1)}, f32[8,72,128]{2,1,0:T(8,128)S(1)}, u32[]{:S(2)}, u32[]{:S(2)}) collective-permute-start(f32[8,72,128]{2,1,0:T(8,128)S(1)} %get-tuple-element.57), channel_id=1, source_target_pairs={{0,64},{1,17},{16,80},{17,33},{32,96},{33,49},{48,112},{49,1},{64,... | collective-permute-start | bytes 884744 | tf_op jit(solution)/shard_map/ppermute | solution.py:477
  98.3 14.2 %all-to-all-start.2 = ((f32[8,72,128]{2,1,0:T(8,128)}), f32[8,72,128]{2,1,0:T(8,128)S(1)}, u32[]{:S(2)}, u32[]{:S(2)}) async-start(f32[8,72,128]{2,1,0:T(8,128)} %broadcast_in_dim.2), calls=%async_computation.2 | async-start | bytes 589824 | tf_op jit(solution)/shard_map/all_to_all | solution.py:464
  103.0 1.3 %collective-permute-start.12 = (f32[128,128]{1,0:T(8,128)S(1)}, f32[128,128]{1,0:T(8,128)S(1)}, u32[]{:S(2)}, u32[]{:S(2)}) collective-permute-start(f32[128,128]{1,0:T(8,128)S(1)} %constant_dynamic-slice_fusion), channel_id=1, source_target_pairs={{0,1},{1,0},{2,3},{3,2},{4,5},{5,4},{6,7},{7,6},{8,9},{9,8},{10,11... | collective-permute-start | bytes 196616 | tf_op jit(solution)/shard_map/ppermute | solution.py:526

commit v11 on v10

--- a/solution.py
+++ b/solution.py
@@ -27,7 +27,7 @@
 
 RING = 4
 PART = 4
-GROUP = 8
+GROUP = 16
 VMEM = pl.BlockSpec(memory_space=pltpu.VMEM)
 HBM = pl.BlockSpec(memory_space=pltpu.HBM)
 

time: 115 us -> 115 us (level)
  transfers between devices with their start and end apart: 14 -> 14, of which waited for: 11 -> 11; matrix products, arithmetic and copies ran while one was open for 1% -> 1% of each run, Pallas kernels for 10% -> 9%
where the time goes in v11:
time: 115 us; the launch traced here: 113 us
  blocking collectives  28.8 us (25%)
  waiting for transfers between devices  27.5 us (24%)
  starting transfers between devices  27.4 us (24%)
  Pallas kernels  27.1 us (24%)
    all_to_all x2, blocking collectives, exchange(): return lax.all_to_all(x, axis, split_axis=0, concat_axis=0, tiled=True)  28.8 us
    ppermute x12, starting transfers between devices, shift(): return lax.ppermute(x, ('head', 'row'), pairs)  22.5 us
    ppermute x12, waiting for transfers between devices, shift(): return lax.ppermute(x, ('head', 'row'), pairs)  18.9 us
    pallas_call x1, Pallas kernels, scores_and_logits(): call(scores_kernel, 'scores_and_logits', 32, in_specs=[HBM] * 5, out_spec...  12.6 us
    all_to_all x1, waiting for transfers between devices, exchange(): return lax.all_to_all(x, axis, split_axis=0, concat_axis=0, tiled=True)  7.41 us
    pallas_call x3, Pallas kernels, head_sum(): call(functools.partial(headsum_kernel, offsets), 'head_sum', 24, in_specs...  5.23 us
    all_to_all x1, starting transfers between devices, exchange(): return lax.all_to_all(x, axis, split_axis=0, concat_axis=0, tiled=True)  4.78 us
    pallas_call x3, Pallas kernels, query_gradient(): call(functools.partial(query_kernel, offsets, pieces), 'query_gradient',...  3.29 us
  transfers between devices with their start and end apart: 14, of which 11 were waited for; matrix products, arithmetic and copies ran while one was open for 1% of the time, Pallas kernels for 9%

profile of v11, /device:TPU:32, one launch (start us, length us, event | category | flops | bytes accessed | tf_op | source)
XLA Modules:
  0.0 113.1 jit_solution(1893261765369776149)
XLA Ops:
  0.6 12.6 %scores_and_logits.1 = (bf16[16,8,128,256]{3,2,1,0:T(8,128)(2,1)S(1)}, f32[32,128]{1,0:T(8,128)S(1)}, f32[8,24,128]{2,1,0:T(8,128)S(1)}, f32[256,128]{1,0:T(8,128)S(1)}, bf16[64,128,128]{2,1,0:T(8,128)(2,1)S(1)}) custom-call(bf16[8,576,128]{2,1,0:T(8,128)(2,1)} %bitcast.11, bf16[16,576,256]{2,1,0:T(8,128)(2,1)} %bitcast.10, bf16[128,64,128]{2,1,0:T(8,128)(2,1)} %iq_hbm.1, ...), custom_call_target="tpu_custom_call" | custom-call | tf_op jit(solution)/shard_map/scores_and_logits/pallas_call | solution.py:168
  13.2 15.5 %all_to_all.15.got_ref = f32[8,24,128]{2,1,0:T(8,128)S(1)} all-to-all(f32[8,24,128]{2,1,0:T(8,128)S(1)} %get-tuple-element.36), channel_id=1, replica_groups=mesh['head'=16,'key'=8,'row'=2] {'key'}, dimensions={0} | all-to-all | bytes 196608 | tf_op jit(solution)/shard_map/all_to_all | solution.py:464
  28.7 1.3 %head_sum.3 = f32[520,256]{1,0:T(8,128)S(1)} custom-call(bf16[16,8,128,256]{3,2,1,0:T(8,128)(2,1)S(1)} %get-tuple-element.34.e_ref, f32[32,128]{1,0:T(8,128)S(1)} %get-tuple-element.35.tops_ref, f32[8,24,128]{2,1,0:T(8,128)S(1)} %all_to_all.15.got_ref), custom_call_target="tpu_custom_call" | custom-call | tf_op jit(solution)/shard_map/head_sum/pallas_call | solution.py:235
  30.0 3.3 %collective-permute-start.1 = (f32[520,256]{1,0:T(8,128)S(1)}, f32[520,256]{1,0:T(8,128)S(1)}, u32[]{:S(2)}, u32[]{:S(2)}) collective-permute-start(f32[520,256]{1,0:T(8,128)S(1)} %head_sum.3), channel_id=1, source_target_pairs={{0,32},{1,129},{16,48},{17,145},{32,0},{33,161},{48,16},{49,177},{... | collective-permute-start | bytes 1597448 | tf_op jit(solution)/shard_map/ppermute | solution.py:477
  33.3 2.5 %head_sum.5 = (f32[520,256]{1,0:T(8,128)S(1)}, f32[520,256]{1,0:T(8,128)S(1)}) custom-call(bf16[16,8,128,256]{3,2,1,0:T(8,128)(2,1)S(1)} %get-tuple-element.34.e_ref, f32[32,128]{1,0:T(8,128)S(1)} %get-tuple-element.35.tops_ref, f32[8,24,128]{2,1,0:T(8,128)S(1)} %all_to_all.15.got_ref), custom_call_target="tpu_custom_call" | custom-call | tf_op jit(solution)/shard_map/head_sum/pallas_call | solution.py:235
  35.9 0.0 copy-start.1
  35.9 0.8 collective-permute-start
  36.6 2.6 %collective-permute-start.2 = (f32[520,256]{1,0:T(8,128)S(1)}, f32[520,256]{1,0:T(8,128)S(1)}, u32[]{:S(2)}, u32[]{:S(2)}) collective-permute-start(f32[520,256]{1,0:T(8,128)S(1)} %get-tuple-element.41), channel_id=1, source_target_pairs={{0,48},{1,193},{16,0},{17,209},{32,16},{33,225},{48,32},{49,241},{... | collective-permute-start | bytes 1597448 | tf_op jit(solution)/shard_map/ppermute | solution.py:477
  39.2 1.3 %head_sum.4.refs_0_ = f32[520,256]{1,0:T(8,128)S(1)} custom-call(bf16[16,8,128,256]{3,2,1,0:T(8,128)(2,1)S(1)} %get-tuple-element.34.e_ref, f32[32,128]{1,0:T(8,128)S(1)} %get-tuple-element.35.tops_ref, f32[8,24,128]{2,1,0:T(8,128)S(1)} %all_to_all.15.got_ref), custom_call_target="tpu_custom_call" | custom-call | tf_op jit(solution)/shard_map/head_sum/pallas_call | solution.py:235
  40.6 0.0 copy-done.1
  40.6 1.8 %active_products.1.refs_5_.active_ref = f32[64,256,128]{2,1,0:T(8,128)S(1)} custom-call(bf16[64,128,128]{2,1,0:T(8,128)(2,1)S(1)} %get-tuple-element.42.qh_ref.refs_4_, bf16[256,128]{1,0:T(8,128)(2,1)S(1)} %copy-done.1), custom_call_target="tpu_custom_call" | custom-call | tf_op jit(solution)/shard_map/active_products/pallas_call | solution.py:294
  42.3 4.3 %collective-permute-done.refs_1_ = f32[520,256]{1,0:T(8,128)S(1)} collective-permute-done((f32[520,256]{1,0:T(8,128)S(1)}, f32[520,256]{1,0:T(8,128)S(1)}, u32[]{:S(2)}, u32[]{:S(2)}) %collective-permute-start) | collective-permute-done | bytes 532512 | tf_op jit(solution)/shard_map/ppermute | solution.py:477
  46.6 0.0 collective-permute-done.1.refs_2_
  46.6 0.3 collective-permute-done.2.refs_3_
  47.0 0.1 partial_sum.1
  47.1 1.6 %collective-permute-start.3 = (f32[136,256]{1,0:T(8,128)S(1)}, f32[136,256]{1,0:T(8,128)S(1)}, u32[]{:S(2)}, u32[]{:S(2)}) collective-permute-start(f32[136,256]{1,0:T(8,128)S(1)} %get-tuple-element.48), channel_id=1, source_target_pairs={{0,64},{1,17},{16,80},{17,33},{32,96},{33,49},{48,112},{49,1},{64,... | collective-permute-start | bytes 417800 | tf_op jit(solution)/shard_map/ppermute | solution.py:477
  48.7 2.7 %collective-permute-start.4 = (f32[136,256]{1,0:T(8,128)S(1)}, f32[136,256]{1,0:T(8,128)S(1)}, u32[]{:S(2)}, u32[]{:S(2)}) collective-permute-start(f32[136,256]{1,0:T(8,128)S(1)} %get-tuple-element.49), channel_id=1, source_target_pairs={{0,128},{1,33},{16,144},{17,49},{32,160},{33,1},{48,176},{49,17},{... | collective-permute-start | bytes 417800 | tf_op jit(solution)/shard_map/ppermute | solution.py:477
  51.4 1.4 %collective-permute-start.5 = (f32[136,256]{1,0:T(8,128)S(1)}, f32[136,256]{1,0:T(8,128)S(1)}, u32[]{:S(2)}, u32[]{:S(2)}) collective-permute-start(f32[136,256]{1,0:T(8,128)S(1)} %get-tuple-element.50), channel_id=1, source_target_pairs={{0,192},{1,49},{16,208},{17,1},{32,224},{33,17},{48,240},{49,33},{... | collective-permute-start | bytes 417800 | tf_op jit(solution)/shard_map/ppermute | solution.py:477
  52.8 0.6 collective-permute-done.3.refs_1_
  53.4 2.5 %collective-permute-done.4.refs_2_ = f32[136,256]{1,0:T(8,128)S(1)} collective-permute-done((f32[136,256]{1,0:T(8,128)S(1)}, f32[136,256]{1,0:T(8,128)S(1)}, u32[]{:S(2)}, u32[]{:S(2)}) %collective-permute-start.4) | collective-permute-done | bytes 139296 | tf_op jit(solution)/shard_map/ppermute | solution.py:477
  55.9 0.5 collective-permute-done.5.refs_3_
  56.5 0.9 dlogits.1.refs_0_.dlogits_ref
  57.4 1.5 %collective-permute-start.6 = (f32[288,256]{1,0:T(8,128)S(1)}, f32[288,256]{1,0:T(8,128)S(1)}, u32[]{:S(2)}, u32[]{:S(2)}) collective-permute-start(f32[288,256]{1,0:T(8,128)S(1)} %dlogits.1.refs_0_.dlogits_ref), channel_id=1, source_target_pairs={{0,16},{1,65},{16,32},{17,81},{32,48},{33,97},{48,0},{49,113},{64,... | collective-permute-start | bytes 884744 | tf_op jit(solution)/shard_map/ppermute | solution.py:477
  58.8 2.8 %collective-permute-start.7 = (f32[288,256]{1,0:T(8,128)S(1)}, f32[288,256]{1,0:T(8,128)S(1)}, u32[]{:S(2)}, u32[]{:S(2)}) collective-permute-start(f32[288,256]{1,0:T(8,128)S(1)} %dlogits.1.refs_0_.dlogits_ref), channel_id=1, source_target_pairs={{0,32},{1,129},{16,48},{17,145},{32,0},{33,161},{48,16},{49,177},{... | collective-permute-start | bytes 884744 | tf_op jit(solution)/shard_map/ppermute | solution.py:477
  61.6 1.3 %collective-permute-start.8 = (f32[288,256]{1,0:T(8,128)S(1)}, f32[288,256]{1,0:T(8,128)S(1)}, u32[]{:S(2)}, u32[]{:S(2)}) collective-permute-start(f32[288,256]{1,0:T(8,128)S(1)} %dlogits.1.refs_0_.dlogits_ref), channel_id=1, source_target_pairs={{0,48},{1,193},{16,0},{17,209},{32,16},{33,225},{48,32},{49,241},{... | collective-permute-start | bytes 884744 | tf_op jit(solution)/shard_map/ppermute | solution.py:477
  62.9 2.4 %collective-permute-done.6.refs_1_ = f32[288,256]{1,0:T(8,128)S(1)} collective-permute-done((f32[288,256]{1,0:T(8,128)S(1)}, f32[288,256]{1,0:T(8,128)S(1)}, u32[]{:S(2)}, u32[]{:S(2)}) %collective-permute-start.6) | collective-permute-done | bytes 294944 | tf_op jit(solution)/shard_map/ppermute | solution.py:477
  65.4 4.1 %collective-permute-done.7.refs_2_ = f32[288,256]{1,0:T(8,128)S(1)} collective-permute-done((f32[288,256]{1,0:T(8,128)S(1)}, f32[288,256]{1,0:T(8,128)S(1)}, u32[]{:S(2)}, u32[]{:S(2)}) %collective-permute-start.7) | collective-permute-done | bytes 294944 | tf_op jit(solution)/shard_map/ppermute | solution.py:477
  69.5 0.0 collective-permute-done.8.refs_3_
  69.5 0.0 copy-done
  69.5 0.9 query_gradient.3
  70.4 2.5 %collective-permute-start.10 = (f32[8,72,128]{2,1,0:T(8,128)S(1)}, f32[8,72,128]{2,1,0:T(8,128)S(1)}, u32[]{:S(2)}, u32[]{:S(2)}) collective-permute-start(f32[8,72,128]{2,1,0:T(8,128)S(1)} %query_gradient.3), channel_id=1, source_target_pairs={{0,128},{1,33},{16,144},{17,49},{32,160},{33,1},{48,176},{49,17},{... | collective-permute-start | bytes 884744 | tf_op jit(solution)/shard_map/ppermute | solution.py:477
  72.9 1.5 %query_gradient.5 = (f32[8,72,128]{2,1,0:T(8,128)S(1)}, f32[8,72,128]{2,1,0:T(8,128)S(1)}) custom-call(f32[288,256]{1,0:T(8,128)S(1)} %dlogits.1.refs_0_.dlogits_ref, f32[288,256]{1,0:T(8,128)S(1)} %collective-permute-done.6.refs_1_, f32[288,256]{1,0:T(8,128)S(1)} %collective-permute-done.7.refs_2_, f32[288,256]{1,0:T(8,128)S(1)} %collective-permute-done.8.refs_3_, ...), custom_call_target="tpu_custom_call" | custom-call | tf_op jit(solution)/shard_map/query_gradient/pallas_call | solution.py:427
  74.4 1.7 %collective-permute-start.11 = (f32[8,72,128]{2,1,0:T(8,128)S(1)}, f32[8,72,128]{2,1,0:T(8,128)S(1)}, u32[]{:S(2)}, u32[]{:S(2)}) collective-permute-start(f32[8,72,128]{2,1,0:T(8,128)S(1)} %get-tuple-element.61), channel_id=1, source_target_pairs={{0,192},{1,49},{16,208},{17,1},{32,224},{33,17},{48,240},{49,33},{... | collective-permute-start | bytes 884744 | tf_op jit(solution)/shard_map/ppermute | solution.py:477
  76.1 0.4 collective-permute-start.9
  76.5 0.9 query_gradient.4
  77.4 2.6 %key_gradient.1 = f32[256,128]{1,0:T(8,128)S(1)} custom-call(f32[288,256]{1,0:T(8,128)S(1)} %dlogits.1.refs_0_.dlogits_ref, f32[64,256,128]{2,1,0:T(8,128)S(1)} %active_products.1.refs_5_.active_ref, bf16[64,128,128]{2,1,0:T(8,128)(2,1)S(1)} %get-tuple-element.42.qh_ref.refs_4_, f32[64,128]{1,0:T(8,128)S(1)} %bitcast.9), custom_call_target="tpu_custom_call" | custom-call | tf_op jit(solution)/shard_map/key_gradient/pallas_call | solution.py:369
  80.0 0.0 collective-permute-done.10
  80.0 1.9 %collective-permute-done.11 = f32[8,72,128]{2,1,0:T(8,128)S(1)} collective-permute-done((f32[8,72,128]{2,1,0:T(8,128)S(1)}, f32[8,72,128]{2,1,0:T(8,128)S(1)}, u32[]{:S(2)}, u32[]{:S(2)}) %collective-permute-start.11) | collective-permute-done | bytes 294944 | tf_op jit(solution)/shard_map/ppermute | solution.py:477
  81.9 2.2 %collective-permute-done.9 = f32[8,72,128]{2,1,0:T(8,128)S(1)} collective-permute-done((f32[8,72,128]{2,1,0:T(8,128)S(1)}, f32[8,72,128]{2,1,0:T(8,128)S(1)}, u32[]{:S(2)}, u32[]{:S(2)}) %collective-permute-start.9) | collective-permute-done | bytes 294944 | tf_op jit(solution)/shard_map/ppermute | solution.py:477
  84.0 0.1 add_add_fusion
  84.1 13.3 %all_to_all.16 = f32[8,72,128]{2,1,0:T(8,128)S(1)} all-to-all(f32[8,72,128]{2,1,0:T(8,128)S(1)} %add_add_fusion), channel_id=1, replica_groups=mesh['head'=16,'key'=8,'row'=2] {'key'}, dimensions={0} | all-to-all | bytes 589824 | tf_op jit(solution)/shard_map/all_to_all | solution.py:464
  97.4 0.7 broadcast_in_dim.2
  98.2 4.8 %all-to-all-start.2 = ((f32[8,72,128]{2,1,0:T(8,128)}), f32[8,72,128]{2,1,0:T(8,128)S(1)}, u32[]{:S(2)}, u32[]{:S(2)}) async-start(f32[8,72,128]{2,1,0:T(8,128)} %broadcast_in_dim.2), calls=%async_computation.2 | async-start | bytes 589824 | tf_op jit(solution)/shard_map/all_to_all | solution.py:464
  103.0 0.1 collective-permute-start.12
  103.1 1.2 %collective-permute-done.12 = f32[128,128]{1,0:T(8,128)S(1)} collective-permute-done((f32[128,128]{1,0:T(8,128)S(1)}, f32[128,128]{1,0:T(8,128)S(1)}, u32[]{:S(2)}, u32[]{:S(2)}) %collective-permute-start.12) | collective-permute-done | bytes 65568 | tf_op jit(solution)/shard_map/ppermute | solution.py:526
  104.3 0.6 dynamic-slice_add_fusion
  104.9 7.4 %all-to-all-done.2.got_ref = f32[8,72,128]{2,1,0:T(8,128)S(1)} async-done(((f32[8,72,128]{2,1,0:T(8,128)}), f32[8,72,128]{2,1,0:T(8,128)S(1)}, u32[]{:S(2)}, u32[]{:S(2)}) %all-to-all-start.2) | async-done | bytes 294944 | tf_op jit(solution)/shard_map/all_to_all | solution.py:464
  112.4 0.7 results.1
  (3 shorter events, 0.0 us)
Async XLA Ops:
  30.0 16.6 %collective-permute-start.1 = (f32[520,256]{1,0:T(8,128)S(1)}, f32[520,256]{1,0:T(8,128)S(1)}, u32[]{:S(2)}, u32[]{:S(2)}) collective-permute-start(f32[520,256]{1,0:T(8,128)S(1)} %head_sum.3), channel_id=1, source_target_pairs={{0,32},{1,129},{16,48},{17,145},{32,0},{33,161},{48,16},{49,177},{... | collective-permute-start | bytes 1597448 | tf_op jit(solution)/shard_map/ppermute | solution.py:477
  35.9 4.7 %copy-start.1 = (bf16[256,128]{1,0:T(8,128)(2,1)S(1)}, bf16[256,128]{1,0:T(8,128)(2,1)}, u32[]{:S(2)}) copy-start(bf16[256,128]{1,0:T(8,128)(2,1)} %refs_6_.1) | copy-start | bytes 196612
  35.9 10.7 %collective-permute-start = (f32[520,256]{1,0:T(8,128)S(1)}, f32[520,256]{1,0:T(8,128)S(1)}, u32[]{:S(2)}, u32[]{:S(2)}) collective-permute-start(f32[520,256]{1,0:T(8,128)S(1)} %get-tuple-element.40), channel_id=1, source_target_pairs={{0,16},{1,65},{16,32},{17,81},{32,48},{33,97},{48,0},{49,113},{64,... | collective-permute-start | bytes 1597448 | tf_op jit(solution)/shard_map/ppermute | solution.py:477
  36.6 10.3 %collective-permute-start.2 = (f32[520,256]{1,0:T(8,128)S(1)}, f32[520,256]{1,0:T(8,128)S(1)}, u32[]{:S(2)}, u32[]{:S(2)}) collective-permute-start(f32[520,256]{1,0:T(8,128)S(1)} %get-tuple-element.41), channel_id=1, source_target_pairs={{0,48},{1,193},{16,0},{17,209},{32,16},{33,225},{48,32},{49,241},{... | collective-permute-start | bytes 1597448 | tf_op jit(solution)/shard_map/ppermute | solution.py:477
  47.1 6.3 %collective-permute-start.3 = (f32[136,256]{1,0:T(8,128)S(1)}, f32[136,256]{1,0:T(8,128)S(1)}, u32[]{:S(2)}, u32[]{:S(2)}) collective-permute-start(f32[136,256]{1,0:T(8,128)S(1)} %get-tuple-element.48), channel_id=1, source_target_pairs={{0,64},{1,17},{16,80},{17,33},{32,96},{33,49},{48,112},{49,1},{64,... | collective-permute-start | bytes 417800 | tf_op jit(solution)/shard_map/ppermute | solution.py:477
  48.7 7.3 %collective-permute-start.4 = (f32[136,256]{1,0:T(8,128)S(1)}, f32[136,256]{1,0:T(8,128)S(1)}, u32[]{:S(2)}, u32[]{:S(2)}) collective-permute-start(f32[136,256]{1,0:T(8,128)S(1)} %get-tuple-element.49), channel_id=1, source_target_pairs={{0,128},{1,33},{16,144},{17,49},{32,160},{33,1},{48,176},{49,17},{... | collective-permute-start | bytes 417800 | tf_op jit(solution)/shard_map/ppermute | solution.py:477
  51.4 5.1 %collective-permute-start.5 = (f32[136,256]{1,0:T(8,128)S(1)}, f32[136,256]{1,0:T(8,128)S(1)}, u32[]{:S(2)}, u32[]{:S(2)}) collective-permute-start(f32[136,256]{1,0:T(8,128)S(1)} %get-tuple-element.50), channel_id=1, source_target_pairs={{0,192},{1,49},{16,208},{17,1},{32,224},{33,17},{48,240},{49,33},{... | collective-permute-start | bytes 417800 | tf_op jit(solution)/shard_map/ppermute | solution.py:477
  56.5 13.0 %copy-start = (f32[128,64]{0,1:T(8,128)S(1)}, f32[128,64]{0,1:T(8,128)}, u32[]{:S(2)}) copy-start(f32[128,64]{0,1:T(8,128)} %param.9) | copy-start | bytes 98308
  57.4 8.0 %collective-permute-start.6 = (f32[288,256]{1,0:T(8,128)S(1)}, f32[288,256]{1,0:T(8,128)S(1)}, u32[]{:S(2)}, u32[]{:S(2)}) collective-permute-start(f32[288,256]{1,0:T(8,128)S(1)} %dlogits.1.refs_0_.dlogits_ref), channel_id=1, source_target_pairs={{0,16},{1,65},{16,32},{17,81},{32,48},{33,97},{48,0},{49,113},{64,... | collective-permute-start | bytes 884744 | tf_op jit(solution)/shard_map/ppermute | solution.py:477
  58.8 10.7 %collective-permute-start.7 = (f32[288,256]{1,0:T(8,128)S(1)}, f32[288,256]{1,0:T(8,128)S(1)}, u32[]{:S(2)}, u32[]{:S(2)}) collective-permute-start(f32[288,256]{1,0:T(8,128)S(1)} %dlogits.1.refs_0_.dlogits_ref), channel_id=1, source_target_pairs={{0,32},{1,129},{16,48},{17,145},{32,0},{33,161},{48,16},{49,177},{... | collective-permute-start | bytes 884744 | tf_op jit(solution)/shard_map/ppermute | solution.py:477
  61.6 7.9 %collective-permute-start.8 = (f32[288,256]{1,0:T(8,128)S(1)}, f32[288,256]{1,0:T(8,128)S(1)}, u32[]{:S(2)}, u32[]{:S(2)}) collective-permute-start(f32[288,256]{1,0:T(8,128)S(1)} %dlogits.1.refs_0_.dlogits_ref), channel_id=1, source_target_pairs={{0,48},{1,193},{16,0},{17,209},{32,16},{33,225},{48,32},{49,241},{... | collective-permute-start | bytes 884744 | tf_op jit(solution)/shard_map/ppermute | solution.py:477
  70.4 9.5 %collective-permute-start.10 = (f32[8,72,128]{2,1,0:T(8,128)S(1)}, f32[8,72,128]{2,1,0:T(8,128)S(1)}, u32[]{:S(2)}, u32[]{:S(2)}) collective-permute-start(f32[8,72,128]{2,1,0:T(8,128)S(1)} %query_gradient.3), channel_id=1, source_target_pairs={{0,128},{1,33},{16,144},{17,49},{32,160},{33,1},{48,176},{49,17},{... | collective-permute-start | bytes 884744 | tf_op jit(solution)/shard_map/ppermute | solution.py:477
  74.4 7.5 %collective-permute-start.11 = (f32[8,72,128]{2,1,0:T(8,128)S(1)}, f32[8,72,128]{2,1,0:T(8,128)S(1)}, u32[]{:S(2)}, u32[]{:S(2)}) collective-permute-start(f32[8,72,128]{2,1,0:T(8,128)S(1)} %get-tuple-element.61), channel_id=1, source_target_pairs={{0,192},{1,49},{16,208},{17,1},{32,224},{33,17},{48,240},{49,33},{... | collective-permute-start | bytes 884744 | tf_op jit(solution)/shard_map/ppermute | solution.py:477
  76.1 7.9 %collective-permute-start.9 = (f32[8,72,128]{2,1,0:T(8,128)S(1)}, f32[8,72,128]{2,1,0:T(8,128)S(1)}, u32[]{:S(2)}, u32[]{:S(2)}) collective-permute-start(f32[8,72,128]{2,1,0:T(8,128)S(1)} %get-tuple-element.57), channel_id=1, source_target_pairs={{0,64},{1,17},{16,80},{17,33},{32,96},{33,49},{48,112},{49,1},{64,... | collective-permute-start | bytes 884744 | tf_op jit(solution)/shard_map/ppermute | solution.py:477
  98.2 14.2 %all-to-all-start.2 = ((f32[8,72,128]{2,1,0:T(8,128)}), f32[8,72,128]{2,1,0:T(8,128)S(1)}, u32[]{:S(2)}, u32[]{:S(2)}) async-start(f32[8,72,128]{2,1,0:T(8,128)} %broadcast_in_dim.2), calls=%async_computation.2 | async-start | bytes 589824 | tf_op jit(solution)/shard_map/all_to_all | solution.py:464
  103.0 1.3 %collective-permute-start.12 = (f32[128,128]{1,0:T(8,128)S(1)}, f32[128,128]{1,0:T(8,128)S(1)}, u32[]{:S(2)}, u32[]{:S(2)}) collective-permute-start(f32[128,128]{1,0:T(8,128)S(1)} %constant_dynamic-slice_fusion), channel_id=1, source_target_pairs={{0,1},{1,0},{2,3},{3,2},{4,5},{5,4},{6,7},{7,6},{8,9},{9,8},{10,11... | collective-permute-start | bytes 196616 | tf_op jit(solution)/shard_map/ppermute | solution.py:526
